TPU v7x, 32 devices: a whole 2x2x4 slice. The times are simulated.
32 devices in a mesh: groups: 2 (over x), space: 16 (over z, y, core).
Axes of the slice: x: 2, y: 2, z: 4, core: 2. Of those that a mesh axis runs over, the one named last changes fastest.
Arguments:
- volume: bfloat16 [64, 64, 32, 64], P(('groups', 'space')), parts along dimension 0, may hold values from -6 to 6
- weight_one: bfloat16 [3, 3, 3, 64, 64], replicated, may hold values from -0.15625 to 0.15625
- weight_two: bfloat16 [3, 3, 3, 64, 128], replicated, may hold values from -0.15625 to 0.15625
- cotangent: bfloat16 [64, 64, 32, 128], P(('groups', 'space')), parts along dimension 0, may hold values from -6 to 6
Outputs:
- output: float32 [64, 64, 32, 128], P(('groups', 'space')), parts along dimension 0
- grad_volume: float32 [64, 64, 32, 64], P(('groups', 'space')), parts along dimension 0
- grad_one: float32 [6, 3, 3, 64, 64], P('groups', None, None, None, 'space'), parts along dimension 0
- grad_two: float32 [6, 3, 3, 64, 128], P('groups', None, None, None, 'space'), parts along dimension 0
There are 2 independent parts, one for each index of `groups`. A program takes and returns all parts, laid end to end along the dimension named above; an argument that names none is the same for every part. Nothing has to cross between parts.
All inputs are finite; a program needn't handle non-finite values.
Results may differ from a plain program's by a relative error of at most 0.0029.
Values may be sent and summed in bfloat16 or wider, within the bound.
No kernel may reach another device: no remote copies, remote signals or barrier semaphores. Data moves between devices by JAX's collectives and lax.ppermute only.
A program may use at most 64 MiB of HBM per device.

v0:
```python
import functools
import math

import jax
import jax.numpy as jnp
from jax import lax
from jax.experimental import pallas as pl
from jax.experimental.pallas import tpu as pltpu
from jax.sharding import PartitionSpec as P

F32, BF16 = jnp.float32, jnp.bfloat16
STEP = 256
VMEM_LIMIT = 48 * 2**20
NT = (((1,), (1,)), ((), ()))

ENTER = ((1, 2, 0, None), (0, 1, None, 2))
LEAVE = ((1, 2), (0, 1), (2, None), (None, 0))


def call(body, outs, ins, scratch=(), flops=0, name=None, smem=()):
    moved = sum(math.prod(s.shape) * s.dtype.itemsize for s in (*outs, *ins))
    return pl.pallas_call(
        body,
        out_shape=list(outs),
        in_specs=[
            pl.BlockSpec(memory_space=pltpu.SMEM if i in smem else pltpu.VMEM)
            for i in range(len(ins))
        ],
        out_specs=[pl.BlockSpec(memory_space=pltpu.VMEM)] * len(outs),
        scratch_shapes=list(scratch),
        compiler_params=pltpu.CompilerParams(vmem_limit_bytes=VMEM_LIMIT),
        cost_estimate=pl.CostEstimate(flops=flops, bytes_accessed=moved, transcendentals=0),
        name=name,
    )(*ins)


def lanes_low(x):
    return lax.broadcasted_iota(jnp.int32, x.shape, 1) < 64


def swap(x):
    return pltpu.roll(x, 64, 1)


def pick(low, high):
    return jnp.where(lanes_low(low), low, high)


def fill_windows(windows, start, lane, chunk, columns, stride):
    size = chunk.shape[0]
    column = lax.broadcasted_iota(jnp.int32, chunk.shape, 0) % columns
    before = jnp.where(column == 0, 0.0, pltpu.roll(chunk, 1, 0))
    after = jnp.where(column == columns - 1, 0.0, pltpu.roll(chunk, size - 1, 0))
    at = pl.ds(pl.multiple_of(columns + start, 32), size)
    for tap, part in enumerate((before, chunk, after)):
        first = tap * stride + lane
        windows[at, first : first + chunk.shape[1]] = part.astype(BF16)


def clear_edges(windows, columns):
    rows, lanes = windows.shape
    windows[0:columns, :] = jnp.zeros((columns, lanes), BF16)
    windows[rows - columns : rows, :] = jnp.zeros((columns, lanes), BF16)


def four_planes(windows, own, below, above, columns):
    half = own.shape[0] // 2

    def step(i, carry):
        start = pl.multiple_of(i * STEP, STEP)
        low, high = pl.ds(start, STEP), pl.ds(start + half, STEP)
        fill_windows(windows, start, 0, own[low, :].astype(F32), columns, 256)
        fill_windows(windows, start + half, 0, own[high, :].astype(F32), columns, 256)
        from_below, from_above = below[low, :].astype(F32), above[low, :].astype(F32)
        fill_windows(windows, start, 128, pick(from_below, swap(from_above)), columns, 256)
        fill_windows(windows, start + half, 128, pick(swap(from_below), from_above), columns, 256)
        return carry

    clear_edges(windows, columns)
    lax.fori_loop(0, half // STEP, step, 0)


def window_dot(windows, weights, start, columns, dims):
    total = None
    for tap in range(3):
        rows = pl.ds(pl.multiple_of(start + tap * columns, 32), STEP)
        term = lax.dot_general(windows[rows, :], weights[tap], dims, preferred_element_type=F32)
        total = term if total is None else total + term
    return total


def packed(low, high):
    return pick(low, swap(high)), pick(swap(low), high)


def pack_body(volume, own, up, down):
    cells = own.shape[0]
    half = cells // 2

    def step(i, carry):
        start = pl.multiple_of(i * STEP, STEP)
        low, high = pl.ds(start, STEP), pl.ds(start + half, STEP)
        pairs = []
        for rows in (low, high):
            pair = jnp.concatenate([volume[0, rows, :], volume[1, rows, :]], axis=1)
            own[rows, :] = pair
            pairs.append(pair.astype(F32))
        first, second = packed(*pairs)
        down[low, :] = first.astype(BF16)
        up[low, :] = second.astype(BF16)
        return carry

    lax.fori_loop(0, half // STEP, step, 0)


def leave_body(columns, cotangent, weight, own, up, down, windows, taps):
    half = cotangent.shape[1] // 2
    for row in range(3):
        for plane, enters in enumerate(LEAVE):
            for column in range(3):
                for source, depth in enumerate(enters):
                    first = column * 256 + source * 128
                    taps[row, plane * 64 : plane * 64 + 64, first : first + 128] = (
                        jnp.zeros((64, 128), BF16)
                        if depth is None
                        else weight[(2 - depth) * 9 + (2 - row) * 3 + 2 - column]
                    )

    def fill(i, carry):
        start = pl.multiple_of(i * STEP, STEP)
        for plane in range(2):
            chunk = cotangent[plane, pl.ds(start, STEP), :].astype(F32)
            fill_windows(windows, start, plane * 128, chunk, columns, 256)
        return carry

    clear_edges(windows, columns)
    lax.fori_loop(0, 2 * half // STEP, fill, 0)

    def step(i, carry):
        start = pl.multiple_of(i * STEP, STEP)
        sides = []
        for first in (start, start + half):
            term = window_dot(windows, taps, first, columns, NT)
            own[pl.ds(first, STEP), :] = term[:, :128]
            sides.append(term[:, 128:])
        lower, upper = packed(*sides)
        down[pl.ds(start, STEP), :] = lower.astype(BF16)
        up[pl.ds(start, STEP), :] = upper.astype(BF16)
        return carry

    lax.fori_loop(0, half // STEP, step, 0)


def hidden_body(columns, own, below, above, weight, activation, up, down, slope, windows, taps):
    half = own.shape[0] // 2
    zero = jnp.zeros((64, 64), BF16)
    for row in range(3):
        for column in range(3):
            for source in range(4):
                first = column * 256 + source * 64
                pair = [
                    zero if ENTER[plane][source] is None
                    else weight[ENTER[plane][source] * 9 + row * 3 + column]
                    for plane in range(2)
                ]
                taps[row, first : first + 64, :] = jnp.concatenate(pair, axis=1)
    four_planes(windows, own, below, above, columns)

    def step(i, carry):
        start = pl.multiple_of(i * STEP, STEP)
        sides = []
        for first in (start, start + half):
            hidden = window_dot(windows, taps, first, columns, (((1,), (0,)), ((), ())))
            gate = jax.nn.sigmoid(hidden)
            act = (hidden * gate).astype(BF16)
            activation[pl.ds(first, STEP), :] = act
            slope[pl.ds(first, STEP), :] = gate * (1.0 + hidden * (1.0 - gate))
            sides.append(act.astype(F32))
        lower, upper = packed(*sides)
        down[pl.ds(start, STEP), :] = lower.astype(BF16)
        up[pl.ds(start, STEP), :] = upper.astype(BF16)
        return carry

    lax.fori_loop(0, half // STEP, step, 0)


def slope_body(terms, below, above, slope, grad, up, down):
    half = terms.shape[0] // 2

    def step(i, carry):
        start = pl.multiple_of(i * STEP, STEP)
        low, high = pl.ds(start, STEP), pl.ds(start + half, STEP)
        from_below, from_above = below[low, :].astype(F32), above[low, :].astype(F32)
        arrived = (pick(from_below, swap(from_above)), pick(swap(from_below), from_above))
        sides = []
        for rows, extra in zip((low, high), arrived):
            value = ((terms[rows, :] + extra) * slope[rows, :]).astype(BF16)
            grad[rows, :] = value
            sides.append(value.astype(F32))
        lower, upper = packed(*sides)
        down[low, :] = lower.astype(BF16)
        up[low, :] = upper.astype(BF16)
        return carry

    lax.fori_loop(0, half // STEP, step, 0)


def kernel_terms(columns, out_channels, windows, turned, terms):
    cells = turned.shape[1]
    for row in range(3):
        for column in range(3):
            tap = row * 3 + column
            product = jnp.dot(
                turned[...],
                windows[row * columns : row * columns + cells, column * 256 : column * 256 + 256],
                preferred_element_type=F32,
            )
            first, second = product[:out_channels], product[out_channels:]
            terms[:, tap * 128 : tap * 128 + 128] = first[:, :128] + pick(
                swap(second[:, :128]), second[:, 128:]
            )
            zeroth = first[:, 128:] + second[:, :128]
            group = 9 + tap // 2
            here = slice(group * 128, group * 128 + 128)
            if tap % 2 == 0:
                terms[:, here] = zeroth
            else:
                terms[:, here] = pick(terms[:, here], swap(zeroth))


def turn(source, target, first):
    for start in range(0, source.shape[0], STEP):
        chunk = source[start : start + STEP, :].astype(F32)
        target[first : first + chunk.shape[1], start : start + STEP] = chunk.T.astype(BF16)


def grad_one_body(columns, own, below, above, grad, terms, windows, turned):
    four_planes(windows, own, below, above, columns)
    turn(grad, turned, 0)
    kernel_terms(columns, 64, windows, turned, terms)


def grad_two_body(
    columns, count, me, own, below, above, cotangent, other, sent, kept, windows, turned, terms
):
    four_planes(windows, own, below, above, columns)
    turn(cotangent.at[0], turned, 0)
    turn(cotangent.at[1], turned, 128)
    kernel_terms(columns, 128, windows, turned, terms)
    half = terms.shape[1] // 2
    odd = me[0] % 2 == 1

    def share(owner):
        parts = []
        for source in (other, terms):
            each = source.shape[0] // count
            block = source[owner * each : owner * each + each, :]
            parts += [block[:, :half], block[:, half:]]
        return jnp.concatenate(parts, axis=0)

    for pair in range(count // 2):
        even_share, odd_share = share(2 * pair), share(2 * pair + 1)
        sent[pair] = jnp.where(odd, even_share, odd_share).astype(BF16)
        kept[pair] = jnp.where(odd, odd_share, even_share)


def halve_body(me, mine, arrived, sent, kept):
    odd = (me[0] // 2) % 2
    for pair in range(sent.shape[0]):
        keep, give = 2 * pair + odd, 2 * pair + 1 - odd
        sent[pair] = (mine[give] + arrived[give].astype(F32)).astype(BF16)
        kept[pair] = mine[keep] + arrived[keep].astype(F32)


def finish_body(scale, sizes, mine, *refs):
    arrived, (grad_one, grad_two) = refs[:-2], refs[-2:]
    total = mine[...]
    for part in arrived:
        total = total + part[...].astype(F32)
    total = total * scale
    half = total.shape[1]
    first = 0
    for size, out in zip(sizes, (grad_one, grad_two)):
        blocks = (total[first : first + size], total[first + size : first + 2 * size])
        first += 2 * size
        for tap in range(9):
            for depth, group, side in ((0, 9 + tap // 2, tap % 2), (1, tap, 0), (2, tap, 1)):
                lane = group * 128 + side * 64
                block, lane = (blocks[0], lane) if lane < half else (blocks[1], lane - half)
                out[depth * 9 + tap] = block[:, lane : lane + 64]


def output_body(columns, own, below, above, weight, output, windows, taps):
    for row in range(3):
        for column in range(3):
            for source in range(4):
                first = column * 256 + source * 64
                for plane in range(2):
                    depth = ENTER[plane][source]
                    taps[row, first : first + 64, plane * 128 : plane * 128 + 128] = (
                        jnp.zeros((64, 128), BF16)
                        if depth is None
                        else weight[depth * 9 + row * 3 + column]
                    )
    four_planes(windows, own, below, above, columns)

    def step(i, carry):
        start = pl.multiple_of(i * STEP, STEP)
        value = window_dot(windows, taps, start, columns, (((1,), (0,)), ((), ())))
        output[0, pl.ds(start, STEP), :] = value[:, :128]
        output[1, pl.ds(start, STEP), :] = value[:, 128:]
        return carry

    lax.fori_loop(0, own.shape[0] // STEP, step, 0)


def grad_volume_body(columns, own, below, above, weight, output, windows, taps):
    zero = jnp.zeros((64, 64), BF16)
    for row in range(3):
        for column in range(3):
            for plane in range(2):
                pieces = [
                    zero if depth is None
                    else weight[(2 - depth) * 9 + (2 - row) * 3 + 2 - column]
                    for depth in ENTER[plane]
                ]
                for pair in range(2):
                    first = column * 256 + pair * 128
                    taps[row, plane * 64 : plane * 64 + 64, first : first + 128] = (
                        jnp.concatenate(pieces[2 * pair : 2 * pair + 2], axis=1)
                    )
    four_planes(windows, own, below, above, columns)

    def step(i, carry):
        start = pl.multiple_of(i * STEP, STEP)
        value = window_dot(windows, taps, start, columns, NT)
        output[0, pl.ds(start, STEP), :] = value[:, :64]
        output[1, pl.ds(start, STEP), :] = value[:, 64:]
        return carry

    lax.fori_loop(0, own.shape[0] // STEP, step, 0)


def shards(volume, weight_one, weight_two, cotangent):
    count = lax.axis_size("space")
    planes, rows, columns, channels = volume.shape
    cells = rows * columns
    scale = 1.0 / math.sqrt(planes * count * cells)
    mid, wide = weight_two.shape[3], weight_two.shape[4]
    me = lax.axis_index("space").astype(jnp.int32).reshape(1)
    shape = jax.ShapeDtypeStruct
    flat, pack = shape((cells, 128), BF16), shape((cells // 2, 128), BF16)
    windows = pltpu.VMEM((cells + 2 * columns, 768), BF16)
    lanes = 14 * 64
    chunk = 2 * (mid + wide) // count

    def upward(x):
        return lax.ppermute(x, "space", [(i, i + 1) for i in range(count - 1)])

    def downward(x):
        return lax.ppermute(x, "space", [(i + 1, i) for i in range(count - 1)])

    volume = volume.reshape(planes, cells, channels)
    cotangent = cotangent.reshape(planes, cells, wide)
    weight_one = weight_one.reshape(27, channels, mid)
    weight_two = weight_two.reshape(27, mid, wide)
    one_flops = 2 * planes * cells * 27 * channels * mid
    two_flops = 2 * planes * cells * 27 * mid * wide

    own, up, down = call(pack_body, (flat, pack, pack), (volume,), name="pack_volume")
    vol_halo = (upward(up), downward(down))
    terms, up, down = call(
        functools.partial(leave_body, columns),
        (shape((cells, 128), F32), pack, pack),
        (cotangent, weight_two),
        (windows, pltpu.VMEM((3, 256, 768), BF16)),
        two_flops, "grad_act_terms",
    )
    act_terms_halo = (upward(up), downward(down))
    activation, up, down, slope = call(
        functools.partial(hidden_body, columns),
        (flat, pack, pack, shape((cells, 128), F32)),
        (own, *vol_halo, weight_one),
        (windows, pltpu.VMEM((3, 768, 128), BF16)),
        one_flops, "hidden",
    )
    act_halo = (upward(up), downward(down))
    grad_hidden, up, down = call(
        slope_body, (flat, pack, pack), (terms, *act_terms_halo, slope), name="grad_hidden"
    )
    grad_halo = (upward(up), downward(down))
    terms_one, = call(
        functools.partial(grad_one_body, columns),
        (shape((mid, 2 * lanes), F32),),
        (own, *vol_halo, grad_hidden),
        (windows, pltpu.VMEM((128, cells), BF16)),
        one_flops, "grad_one_terms",
    )
    sent, kept = call(
        functools.partial(grad_two_body, columns, count),
        (shape((count // 2, chunk, lanes), BF16), shape((count // 2, chunk, lanes), F32)),
        (me, activation, *act_halo, cotangent, terms_one),
        (windows, pltpu.VMEM((256, cells), BF16), pltpu.VMEM((wide, 2 * lanes), F32)),
        two_flops, "grad_two_terms", (0,),
    )
    arrived = lax.ppermute(sent, "space", [(i, i ^ 1) for i in range(count)])
    output, = call(
        functools.partial(output_body, columns),
        (shape((planes, cells, wide), F32),),
        (activation, *act_halo, weight_two),
        (windows, pltpu.VMEM((3, 768, 256), BF16)),
        two_flops, "output",
    )
    sent, kept = call(
        halve_body,
        (shape((count // 4, chunk, lanes), BF16), shape((count // 4, chunk, lanes), F32)),
        (me, kept, arrived), name="halve", smem=(0,),
    )
    arrived = lax.ppermute(sent, "space", [(i, i ^ 2) for i in range(count)])
    grad_volume, = call(
        functools.partial(grad_volume_body, columns),
        (shape((planes, cells, channels), F32),),
        (grad_hidden, *grad_halo, weight_one),
        (windows, pltpu.VMEM((3, 128, 768), BF16)),
        one_flops, "grad_volume",
    )
    summed = kept + arrived.astype(F32)
    ring = count // 4
    place = lax.axis_index("space") // 4
    rest = []
    for hop in range(1, ring):
        part = lax.dynamic_index_in_dim(summed, (place + hop) % ring, 0, False).astype(BF16)
        rest.append(lax.ppermute(part, "space", [(i, (i + 4 * hop) % count) for i in range(count)]))
    mine = lax.dynamic_index_in_dim(summed, place, 0, False)
    grad_one, grad_two = call(
        functools.partial(finish_body, scale, (mid // count, wide // count)),
        (shape((27, mid // count, channels), F32), shape((27, wide // count, mid), F32)),
        (mine, *rest), name="finish",
    )
    return (
        output.reshape(planes, rows, columns, wide),
        grad_volume.reshape(planes, rows, columns, channels),
        jnp.swapaxes(grad_one, 1, 2).reshape(3, 3, 3, channels, mid // count),
        jnp.swapaxes(grad_two, 1, 2).reshape(3, 3, 3, mid, wide // count),
    )


def solution(mesh):
    cells = P(("groups", "space"), None, None, None)
    kernel = P("groups", None, None, None, "space")
    return jax.shard_map(
        shards,
        mesh=mesh,
        in_specs=(cells, P(), P(), cells),
        out_specs=(cells, cells, kernel, kernel),
        check_vma=False,
    )
```

profile of v0, /device:TPU:0, one launch (start us, length us, event | category | flops | bytes accessed | tf_op | source)
XLA Modules:
  0.0 81.4 jit_solution(12463838007891480795)
XLA Ops:
  0.6 1.2 %copy-done = bf16[2,64,32,64]{3,2,1,0:T(8,128)(2,1)S(1)} copy-done((bf16[2,64,32,64]{3,2,1,0:T(8,128)(2,1)S(1)}, bf16[2,64,32,64]{3,2,1,0:T(8,128)(2,1)}, u32[]{:S(2)}) %copy-start) | copy-done | bytes 524312
  1.9 0.7 pack_volume.1
  2.6 2.4 %collective-permute-start = (bf16[1024,128]{1,0:T(8,128)(2,1)S(1)}, bf16[1024,128]{1,0:T(8,128)(2,1)S(1)}, u32[]{:S(2)}, u32[]{:S(2)}) collective-permute-start(bf16[1024,128]{1,0:T(8,128)(2,1)S(1)} %get-tuple-element.24), channel_id=1, source_target_pairs={{0,1},{1,2},{2,3},{3,4},{4,5},{5,6},{6,7},{7,8},{8,9},{9,10},{10,1... | collective-permute-start | bytes 786440 | tf_op jit(solution)/shard_map/ppermute | solution.py:358
  5.0 1.3 %collective-permute-start.1 = (bf16[1024,128]{1,0:T(8,128)(2,1)S(1)}, bf16[1024,128]{1,0:T(8,128)(2,1)S(1)}, u32[]{:S(2)}, u32[]{:S(2)}) collective-permute-start(bf16[1024,128]{1,0:T(8,128)(2,1)S(1)} %get-tuple-element.25), channel_id=1, source_target_pairs={{1,0},{2,1},{3,2},{4,3},{5,4},{6,5},{7,6},{8,7},{9,8},{10,9},{11,1... | collective-permute-start | bytes 786440 | tf_op jit(solution)/shard_map/ppermute | solution.py:361
  6.3 1.2 %copy-done.4 = bf16[2,64,32,128]{3,2,1,0:T(8,128)(2,1)S(1)} copy-done((bf16[2,64,32,128]{3,2,1,0:T(8,128)(2,1)S(1)}, bf16[2,64,32,128]{3,2,1,0:T(8,128)(2,1)}, u32[]{:S(2)}) %copy-start.4) | copy-done | bytes 1048600
  7.5 1.0 %copy-done.8 = bf16[3,3,3,64,128]{4,3,2,1,0:T(8,128)(2,1)S(1)} copy-done((bf16[3,3,3,64,128]{4,3,2,1,0:T(8,128)(2,1)S(1)}, bf16[3,3,3,64,128]{4,3,2,1,0:T(8,128)(2,1)}, u32[]{:S(2)}) %copy-start.8) | copy-done | bytes 442392
  8.5 5.2 %grad_act_terms.1 = (f32[2048,128]{1,0:T(8,128)S(1)}, bf16[1024,128]{1,0:T(8,128)(2,1)}, bf16[1024,128]{1,0:T(8,128)(2,1)}) custom-call(bf16[2,2048,128]{2,1,0:T(8,128)(2,1)S(1)} %bitcast.24, bf16[27,64,128]{2,1,0:T(8,128)(2,1)S(1)} %bitcast.26), custom_call_target="tpu_custom_call" | custom-call | flops 1811939328 | bytes 3063808 | tf_op jit(solution)/shard_map/grad_act_terms/pallas_call | solution.py:22
  13.7 5.2 %collective-permute-start.4 = (bf16[1024,128]{1,0:T(8,128)(2,1)}, bf16[1024,128]{1,0:T(8,128)(2,1)S(1)}, u32[]{:S(2)}, u32[]{:S(2)}) collective-permute-start(bf16[1024,128]{1,0:T(8,128)(2,1)} %get-tuple-element.30), channel_id=1, source_target_pairs={{0,1},{1,2},{2,3},{3,4},{4,5},{5,6},{6,7},{7,8},{8,9},{9,10},{10,1... | collective-permute-start | bytes 786440 | tf_op jit(solution)/shard_map/ppermute | solution.py:358
  18.8 1.3 %collective-permute-start.5 = (bf16[1024,128]{1,0:T(8,128)(2,1)}, bf16[1024,128]{1,0:T(8,128)(2,1)S(1)}, u32[]{:S(2)}, u32[]{:S(2)}) collective-permute-start(bf16[1024,128]{1,0:T(8,128)(2,1)} %get-tuple-element.31), channel_id=1, source_target_pairs={{1,0},{2,1},{3,2},{4,3},{5,4},{6,5},{7,6},{8,7},{9,8},{10,9},{11,1... | collective-permute-start | bytes 786440 | tf_op jit(solution)/shard_map/ppermute | solution.py:361
  20.2 5.3 %hidden.1 = (bf16[2048,128]{1,0:T(8,128)(2,1)S(1)}, bf16[1024,128]{1,0:T(8,128)(2,1)}, bf16[1024,128]{1,0:T(8,128)(2,1)}, f32[2048,128]{1,0:T(8,128)S(1)}) custom-call(bf16[2048,128]{1,0:T(8,128)(2,1)S(1)} %get-tuple-element.23.own, bf16[1024,128]{1,0:T(8,128)(2,1)S(1)} %collective-permute-done.below, bf16[1024,128]{1,0:T(8,128)(2,1)S(1)} %collective-permute-done.1.above, ...), custom_call_target="tpu_custom_call" | custom-call | flops 905969664 | bytes 3366912 | tf_op jit(solution)/shard_map/hidden/pallas_call | solution.py:22
  25.5 0.8 copy-done.14
  26.2 5.0 %collective-permute-start.2 = (bf16[1024,128]{1,0:T(8,128)(2,1)}, bf16[1024,128]{1,0:T(8,128)(2,1)}, u32[]{:S(2)}, u32[]{:S(2)}) collective-permute-start(bf16[1024,128]{1,0:T(8,128)(2,1)} %get-tuple-element.27), channel_id=1, source_target_pairs={{0,1},{1,2},{2,3},{3,4},{4,5},{5,6},{6,7},{7,8},{8,9},{9,10},{10,1... | collective-permute-start | bytes 786440 | tf_op jit(solution)/shard_map/ppermute | solution.py:358
  31.2 1.3 %collective-permute-start.3 = (bf16[1024,128]{1,0:T(8,128)(2,1)}, bf16[1024,128]{1,0:T(8,128)(2,1)}, u32[]{:S(2)}, u32[]{:S(2)}) collective-permute-start(bf16[1024,128]{1,0:T(8,128)(2,1)} %get-tuple-element.28), channel_id=1, source_target_pairs={{1,0},{2,1},{3,2},{4,3},{5,4},{6,5},{7,6},{8,7},{9,8},{10,9},{11,1... | collective-permute-start | bytes 786440 | tf_op jit(solution)/shard_map/ppermute | solution.py:361
  32.5 0.7 copy-done.2
  33.2 0.9 %copy-done.3 = bf16[1024,128]{1,0:T(8,128)(2,1)S(1)} copy-done((bf16[1024,128]{1,0:T(8,128)(2,1)S(1)}, bf16[1024,128]{1,0:T(8,128)(2,1)}, u32[]{:S(2)}) %copy-start.3) | copy-done | bytes 262168
  34.2 1.6 %grad_hidden.1 = (bf16[2048,128]{1,0:T(8,128)(2,1)S(1)}, bf16[1024,128]{1,0:T(8,128)(2,1)}, bf16[1024,128]{1,0:T(8,128)(2,1)}) custom-call(f32[2048,128]{1,0:T(8,128)S(1)} %get-tuple-element.29.terms, bf16[1024,128]{1,0:T(8,128)(2,1)S(1)} %collective-permute-done.4.below, bf16[1024,128]{1,0:T(8,128)(2,1)S(1)} %copy-done.3, ...), custom_call_target="tpu_custom_call" | custom-call | bytes 3670016 | tf_op jit(solution)/shard_map/grad_hidden/pallas_call | solution.py:22
  35.8 2.4 %grad_one_terms.1.other = f32[64,1792]{1,0:T(8,128)S(1)} custom-call(bf16[2048,128]{1,0:T(8,128)(2,1)S(1)} %copy-done.7, bf16[1024,128]{1,0:T(8,128)(2,1)S(1)} %copy-done.11, bf16[1024,128]{1,0:T(8,128)(2,1)S(1)} %copy-done.13, bf16[2048,128]{1,0:T(8,128)(2,1)S(1)} %get-tuple-element.33.own.grad), custom_call_target="tpu_custom_call" | custom-call | flops 905969664 | bytes 2031616 | tf_op jit(solution)/shard_map/grad_one_terms/pallas_call | solution.py:22
  38.3 4.7 %grad_two_terms.1 = (bf16[8,24,896]{2,1,0:T(8,128)(2,1)S(1)}, f32[8,24,896]{2,1,0:T(8,128)S(1)}) custom-call(s32[1]{0:T(128)} %bitcast.6.me, bf16[2048,128]{1,0:T(8,128)(2,1)S(1)} %copy-done.15, bf16[1024,128]{1,0:T(8,128)(2,1)} %collective-permute-done.2.below, bf16[1024,128]{1,0:T(8,128)(2,1)} %collective-permute-done.3.above, ...), custom_call_target="tpu_custom_call" | custom-call | flops 1811939328 | bytes 3588100 | tf_op jit(solution)/shard_map/grad_two_terms/pallas_call | solution.py:22
  42.9 2.1 %collective-permute-start.8 = (bf16[8,24,896]{2,1,0:T(8,128)(2,1)S(1)}, bf16[8,24,896]{2,1,0:T(8,128)(2,1)S(1)}, u32[]{:S(2)}, u32[]{:S(2)}) collective-permute-start(bf16[8,24,896]{2,1,0:T(8,128)(2,1)S(1)} %get-tuple-element.37), channel_id=1, source_target_pairs={{0,1},{1,0},{2,3},{3,2},{4,5},{5,4},{6,7},{7,6},{8,9},{9,8},{10,11... | collective-permute-start | bytes 1032200 | tf_op jit(solution)/shard_map/ppermute | solution.py:406
  45.0 1.9 %collective-permute-start.6 = (bf16[1024,128]{1,0:T(8,128)(2,1)}, bf16[1024,128]{1,0:T(8,128)(2,1)S(1)}, u32[]{:S(2)}, u32[]{:S(2)}) collective-permute-start(bf16[1024,128]{1,0:T(8,128)(2,1)} %get-tuple-element.34), channel_id=1, source_target_pairs={{0,1},{1,2},{2,3},{3,4},{4,5},{5,6},{6,7},{7,8},{8,9},{9,10},{10,1... | collective-permute-start | bytes 786440 | tf_op jit(solution)/shard_map/ppermute | solution.py:358
  46.9 1.3 %collective-permute-start.7 = (bf16[1024,128]{1,0:T(8,128)(2,1)}, bf16[1024,128]{1,0:T(8,128)(2,1)S(1)}, u32[]{:S(2)}, u32[]{:S(2)}) collective-permute-start(bf16[1024,128]{1,0:T(8,128)(2,1)} %get-tuple-element.35), channel_id=1, source_target_pairs={{1,0},{2,1},{3,2},{4,3},{5,4},{6,5},{7,6},{8,7},{9,8},{10,9},{11,1... | collective-permute-start | bytes 786440 | tf_op jit(solution)/shard_map/ppermute | solution.py:361
  48.3 0.1 halve.1
  48.4 6.6 %collective-permute-start.9 = (bf16[4,24,896]{2,1,0:T(8,128)(2,1)S(1)}, bf16[4,24,896]{2,1,0:T(8,128)(2,1)S(1)}, u32[]{:S(2)}, u32[]{:S(2)}) collective-permute-start(bf16[4,24,896]{2,1,0:T(8,128)(2,1)S(1)} %get-tuple-element.39), channel_id=1, source_target_pairs={{0,2},{1,3},{2,0},{3,1},{4,6},{5,7},{6,4},{7,5},{8,10},{9,11},{10,... | collective-permute-start | bytes 516104 | tf_op jit(solution)/shard_map/ppermute | solution.py:419
  55.0 6.6 %grad_volume.1 = f32[2,2048,64]{2,1,0:T(8,128)} custom-call(bf16[2048,128]{1,0:T(8,128)(2,1)S(1)} %get-tuple-element.33.own.grad, bf16[1024,128]{1,0:T(8,128)(2,1)S(1)} %collective-permute-done.6.below, bf16[1024,128]{1,0:T(8,128)(2,1)S(1)} %collective-permute-done.7.above, bf16[27,64,64]{2,1,0:T(8,128)(2,1)S(1)} %bitcast.23), custom_call_target="tpu_custom_call" | custom-call | flops 905969664 | bytes 2318336 | tf_op jit(solution)/shard_map/grad_volume/pallas_call | solution.py:22
  61.7 7.2 %output.1 = f32[2,2048,128]{2,1,0:T(8,128)} custom-call(bf16[2048,128]{1,0:T(8,128)(2,1)S(1)} %copy-done.16, bf16[1024,128]{1,0:T(8,128)(2,1)} %collective-permute-done.2.below, bf16[1024,128]{1,0:T(8,128)(2,1)} %collective-permute-done.3.above, bf16[27,64,128]{2,1,0:T(8,128)(2,1)S(1)} %bitcast.27), custom_call_target="tpu_custom_call" | custom-call | flops 1811939328 | bytes 3588096 | tf_op jit(solution)/shard_map/output/pallas_call | solution.py:22
  69.0 4.8 %collective-permute-start.10 = (bf16[24,896]{1,0:T(8,128)(2,1)S(1)}, bf16[24,896]{1,0:T(8,128)(2,1)S(1)}, u32[]{:S(2)}, u32[]{:S(2)}) collective-permute-start(bf16[24,896]{1,0:T(8,128)(2,1)S(1)} %get-tuple-element.44), channel_id=1, source_target_pairs={{0,4},{1,5},{2,6},{3,7},{4,8},{5,9},{6,10},{7,11},{8,12},{9,13},{1... | collective-permute-start | bytes 129032 | tf_op jit(solution)/shard_map/ppermute | solution.py:433
  73.8 2.6 %collective-permute-start.11 = (bf16[24,896]{1,0:T(8,128)(2,1)S(1)}, bf16[24,896]{1,0:T(8,128)(2,1)S(1)}, u32[]{:S(2)}, u32[]{:S(2)}) collective-permute-start(bf16[24,896]{1,0:T(8,128)(2,1)S(1)} %get-tuple-element.43), channel_id=1, source_target_pairs={{0,8},{1,9},{2,10},{3,11},{4,12},{5,13},{6,14},{7,15},{8,0},{9,1},... | collective-permute-start | bytes 129032 | tf_op jit(solution)/shard_map/ppermute | solution.py:433
  76.3 1.3 %collective-permute-start.12 = (bf16[24,896]{1,0:T(8,128)(2,1)S(1)}, bf16[24,896]{1,0:T(8,128)(2,1)S(1)}, u32[]{:S(2)}, u32[]{:S(2)}) collective-permute-start(bf16[24,896]{1,0:T(8,128)(2,1)S(1)} %get-tuple-element.42), channel_id=1, source_target_pairs={{0,12},{1,13},{2,14},{3,15},{4,0},{5,1},{6,2},{7,3},{8,4},{9,5},{1... | collective-permute-start | bytes 129032 | tf_op jit(solution)/shard_map/ppermute | solution.py:433
  77.7 0.1 collective-permute-done.10.refs_0_
  77.8 0.9 %collective-permute-done.11.refs_1_ = bf16[24,896]{1,0:T(8,128)(2,1)S(1)} collective-permute-done((bf16[24,896]{1,0:T(8,128)(2,1)S(1)}, bf16[24,896]{1,0:T(8,128)(2,1)S(1)}, u32[]{:S(2)}, u32[]{:S(2)}) %collective-permute-start.11) | collective-permute-done | bytes 43040 | tf_op jit(solution)/shard_map/ppermute | solution.py:433
  78.7 2.0 %collective-permute-done.12.refs_2_ = bf16[24,896]{1,0:T(8,128)(2,1)S(1)} collective-permute-done((bf16[24,896]{1,0:T(8,128)(2,1)S(1)}, bf16[24,896]{1,0:T(8,128)(2,1)S(1)}, u32[]{:S(2)}, u32[]{:S(2)}) %collective-permute-start.12) | collective-permute-done | bytes 43040 | tf_op jit(solution)/shard_map/ppermute | solution.py:433
  80.7 0.7 finish.1
  (41 shorter events, 0.2 us)
Async XLA Ops:
  0.6 1.2 %copy-start = (bf16[2,64,32,64]{3,2,1,0:T(8,128)(2,1)S(1)}, bf16[2,64,32,64]{3,2,1,0:T(8,128)(2,1)}, u32[]{:S(2)}) copy-start(bf16[2,64,32,64]{3,2,1,0:T(8,128)(2,1)} %param.4) | copy-start | bytes 1572868
  2.6 17.6 %copy-start.6 = (bf16[2048,128]{1,0:T(8,128)(2,1)}, bf16[2048,128]{1,0:T(8,128)(2,1)S(1)}, u32[]{:S(2)}) copy-start(bf16[2048,128]{1,0:T(8,128)(2,1)S(1)} %get-tuple-element.23.own) | copy-start | bytes 1572868
  2.6 17.6 %collective-permute-start = (bf16[1024,128]{1,0:T(8,128)(2,1)S(1)}, bf16[1024,128]{1,0:T(8,128)(2,1)S(1)}, u32[]{:S(2)}, u32[]{:S(2)}) collective-permute-start(bf16[1024,128]{1,0:T(8,128)(2,1)S(1)} %get-tuple-element.24), channel_id=1, source_target_pairs={{0,1},{1,2},{2,3},{3,4},{4,5},{5,6},{6,7},{7,8},{8,9},{9,10},{10,1... | collective-permute-start | bytes 786440 | tf_op jit(solution)/shard_map/ppermute | solution.py:358
  5.0 15.2 %collective-permute-start.1 = (bf16[1024,128]{1,0:T(8,128)(2,1)S(1)}, bf16[1024,128]{1,0:T(8,128)(2,1)S(1)}, u32[]{:S(2)}, u32[]{:S(2)}) collective-permute-start(bf16[1024,128]{1,0:T(8,128)(2,1)S(1)} %get-tuple-element.25), channel_id=1, source_target_pairs={{1,0},{2,1},{3,2},{4,3},{5,4},{6,5},{7,6},{8,7},{9,8},{10,9},{11,1... | collective-permute-start | bytes 786440 | tf_op jit(solution)/shard_map/ppermute | solution.py:361
  6.3 1.2 %copy-start.4 = (bf16[2,64,32,128]{3,2,1,0:T(8,128)(2,1)S(1)}, bf16[2,64,32,128]{3,2,1,0:T(8,128)(2,1)}, u32[]{:S(2)}) copy-start(bf16[2,64,32,128]{3,2,1,0:T(8,128)(2,1)} %param.7) | copy-start | bytes 3145732
  7.5 1.0 %copy-start.8 = (bf16[3,3,3,64,128]{4,3,2,1,0:T(8,128)(2,1)S(1)}, bf16[3,3,3,64,128]{4,3,2,1,0:T(8,128)(2,1)}, u32[]{:S(2)}) copy-start(bf16[3,3,3,64,128]{4,3,2,1,0:T(8,128)(2,1)} %param.6) | copy-start | bytes 1327108
  8.5 11.7 %copy-start.1 = (bf16[3,3,3,64,64]{4,3,2,1,0:T(8,128)(2,1)S(1)}, bf16[3,3,3,64,64]{4,3,2,1,0:T(8,128)(2,1)}, u32[]{:S(2)}) copy-start(bf16[3,3,3,64,64]{4,3,2,1,0:T(8,128)(2,1)} %param.5) | copy-start | bytes 663556
  13.7 18.8 %collective-permute-start.4 = (bf16[1024,128]{1,0:T(8,128)(2,1)}, bf16[1024,128]{1,0:T(8,128)(2,1)S(1)}, u32[]{:S(2)}, u32[]{:S(2)}) collective-permute-start(bf16[1024,128]{1,0:T(8,128)(2,1)} %get-tuple-element.30), channel_id=1, source_target_pairs={{0,1},{1,2},{2,3},{3,4},{4,5},{5,6},{6,7},{7,8},{8,9},{9,10},{10,1... | collective-permute-start | bytes 786440 | tf_op jit(solution)/shard_map/ppermute | solution.py:358
  18.8 13.7 %collective-permute-start.5 = (bf16[1024,128]{1,0:T(8,128)(2,1)}, bf16[1024,128]{1,0:T(8,128)(2,1)S(1)}, u32[]{:S(2)}, u32[]{:S(2)}) collective-permute-start(bf16[1024,128]{1,0:T(8,128)(2,1)} %get-tuple-element.31), channel_id=1, source_target_pairs={{1,0},{2,1},{3,2},{4,3},{5,4},{6,5},{7,6},{8,7},{9,8},{10,9},{11,1... | collective-permute-start | bytes 786440 | tf_op jit(solution)/shard_map/ppermute | solution.py:361
  20.1 5.3 %copy-start.10 = (bf16[1024,128]{1,0:T(8,128)(2,1)}, bf16[1024,128]{1,0:T(8,128)(2,1)S(1)}, u32[]{:S(2)}) copy-start(bf16[1024,128]{1,0:T(8,128)(2,1)S(1)} %collective-permute-done.below) | copy-start | bytes 786436
  20.2 6.1 %copy-start.12 = (bf16[1024,128]{1,0:T(8,128)(2,1)}, bf16[1024,128]{1,0:T(8,128)(2,1)S(1)}, u32[]{:S(2)}) copy-start(bf16[1024,128]{1,0:T(8,128)(2,1)S(1)} %collective-permute-done.1.above) | copy-start | bytes 786436
  25.5 0.8 copy-start.14
  26.2 12.0 %collective-permute-start.2 = (bf16[1024,128]{1,0:T(8,128)(2,1)}, bf16[1024,128]{1,0:T(8,128)(2,1)}, u32[]{:S(2)}, u32[]{:S(2)}) collective-permute-start(bf16[1024,128]{1,0:T(8,128)(2,1)} %get-tuple-element.27), channel_id=1, source_target_pairs={{0,1},{1,2},{2,3},{3,4},{4,5},{5,6},{6,7},{7,8},{8,9},{9,10},{10,1... | collective-permute-start | bytes 786440 | tf_op jit(solution)/shard_map/ppermute | solution.py:358
  31.2 7.0 %collective-permute-start.3 = (bf16[1024,128]{1,0:T(8,128)(2,1)}, bf16[1024,128]{1,0:T(8,128)(2,1)}, u32[]{:S(2)}, u32[]{:S(2)}) collective-permute-start(bf16[1024,128]{1,0:T(8,128)(2,1)} %get-tuple-element.28), channel_id=1, source_target_pairs={{1,0},{2,1},{3,2},{4,3},{5,4},{6,5},{7,6},{8,7},{9,8},{10,9},{11,1... | collective-permute-start | bytes 786440 | tf_op jit(solution)/shard_map/ppermute | solution.py:361
  32.5 0.7 copy-start.2
  33.2 0.9 %copy-start.3 = (bf16[1024,128]{1,0:T(8,128)(2,1)S(1)}, bf16[1024,128]{1,0:T(8,128)(2,1)}, u32[]{:S(2)}) copy-start(bf16[1024,128]{1,0:T(8,128)(2,1)} %copy-done.2) | copy-start | bytes 786436
  34.2 1.6 %copy-start.7 = (bf16[2048,128]{1,0:T(8,128)(2,1)S(1)}, bf16[2048,128]{1,0:T(8,128)(2,1)}, u32[]{:S(2)}) copy-start(bf16[2048,128]{1,0:T(8,128)(2,1)} %copy-done.6) | copy-start | bytes 1572868
  34.2 1.6 %copy-start.11 = (bf16[1024,128]{1,0:T(8,128)(2,1)S(1)}, bf16[1024,128]{1,0:T(8,128)(2,1)}, u32[]{:S(2)}) copy-start(bf16[1024,128]{1,0:T(8,128)(2,1)} %copy-done.10) | copy-start | bytes 786436
  34.2 1.6 %copy-start.13 = (bf16[1024,128]{1,0:T(8,128)(2,1)S(1)}, bf16[1024,128]{1,0:T(8,128)(2,1)}, u32[]{:S(2)}) copy-start(bf16[1024,128]{1,0:T(8,128)(2,1)} %copy-done.12) | copy-start | bytes 786436
  35.8 2.5 %copy-start.5 = (bf16[2,64,32,128]{3,2,1,0:T(8,128)(2,1)S(1)}, bf16[2,64,32,128]{3,2,1,0:T(8,128)(2,1)}, u32[]{:S(2)}) copy-start(bf16[2,64,32,128]{3,2,1,0:T(8,128)(2,1)} %param.7) | copy-start | bytes 3145732
  35.8 2.5 %copy-start.15 = (bf16[2048,128]{1,0:T(8,128)(2,1)S(1)}, bf16[2048,128]{1,0:T(8,128)(2,1)}, u32[]{:S(2)}) copy-start(bf16[2048,128]{1,0:T(8,128)(2,1)} %copy-done.14) | copy-start | bytes 1572868
  42.9 5.4 %collective-permute-start.8 = (bf16[8,24,896]{2,1,0:T(8,128)(2,1)S(1)}, bf16[8,24,896]{2,1,0:T(8,128)(2,1)S(1)}, u32[]{:S(2)}, u32[]{:S(2)}) collective-permute-start(bf16[8,24,896]{2,1,0:T(8,128)(2,1)S(1)} %get-tuple-element.37), channel_id=1, source_target_pairs={{0,1},{1,0},{2,3},{3,2},{4,5},{5,4},{6,7},{7,6},{8,9},{9,8},{10,11... | collective-permute-start | bytes 1032200 | tf_op jit(solution)/shard_map/ppermute | solution.py:406
  45.0 10.0 %collective-permute-start.6 = (bf16[1024,128]{1,0:T(8,128)(2,1)}, bf16[1024,128]{1,0:T(8,128)(2,1)S(1)}, u32[]{:S(2)}, u32[]{:S(2)}) collective-permute-start(bf16[1024,128]{1,0:T(8,128)(2,1)} %get-tuple-element.34), channel_id=1, source_target_pairs={{0,1},{1,2},{2,3},{3,4},{4,5},{5,6},{6,7},{7,8},{8,9},{9,10},{10,1... | collective-permute-start | bytes 786440 | tf_op jit(solution)/shard_map/ppermute | solution.py:358
  46.9 8.1 %collective-permute-start.7 = (bf16[1024,128]{1,0:T(8,128)(2,1)}, bf16[1024,128]{1,0:T(8,128)(2,1)S(1)}, u32[]{:S(2)}, u32[]{:S(2)}) collective-permute-start(bf16[1024,128]{1,0:T(8,128)(2,1)} %get-tuple-element.35), channel_id=1, source_target_pairs={{1,0},{2,1},{3,2},{4,3},{5,4},{6,5},{7,6},{8,7},{9,8},{10,9},{11,1... | collective-permute-start | bytes 786440 | tf_op jit(solution)/shard_map/ppermute | solution.py:361
  48.3 13.3 %copy-start.9 = (bf16[3,3,3,64,128]{4,3,2,1,0:T(8,128)(2,1)S(1)}, bf16[3,3,3,64,128]{4,3,2,1,0:T(8,128)(2,1)}, u32[]{:S(2)}) copy-start(bf16[3,3,3,64,128]{4,3,2,1,0:T(8,128)(2,1)} %param.6) | copy-start | bytes 1327108
  48.3 13.3 %copy-start.16 = (bf16[2048,128]{1,0:T(8,128)(2,1)S(1)}, bf16[2048,128]{1,0:T(8,128)(2,1)}, u32[]{:S(2)}) copy-start(bf16[2048,128]{1,0:T(8,128)(2,1)} %copy-done.14) | copy-start | bytes 1572868
  48.4 20.5 %collective-permute-start.9 = (bf16[4,24,896]{2,1,0:T(8,128)(2,1)S(1)}, bf16[4,24,896]{2,1,0:T(8,128)(2,1)S(1)}, u32[]{:S(2)}, u32[]{:S(2)}) collective-permute-start(bf16[4,24,896]{2,1,0:T(8,128)(2,1)S(1)} %get-tuple-element.39), channel_id=1, source_target_pairs={{0,2},{1,3},{2,0},{3,1},{4,6},{5,7},{6,4},{7,5},{8,10},{9,11},{10,... | collective-permute-start | bytes 516104 | tf_op jit(solution)/shard_map/ppermute | solution.py:419
  69.0 8.8 %collective-permute-start.10 = (bf16[24,896]{1,0:T(8,128)(2,1)S(1)}, bf16[24,896]{1,0:T(8,128)(2,1)S(1)}, u32[]{:S(2)}, u32[]{:S(2)}) collective-permute-start(bf16[24,896]{1,0:T(8,128)(2,1)S(1)} %get-tuple-element.44), channel_id=1, source_target_pairs={{0,4},{1,5},{2,6},{3,7},{4,8},{5,9},{6,10},{7,11},{8,12},{9,13},{1... | collective-permute-start | bytes 129032 | tf_op jit(solution)/shard_map/ppermute | solution.py:433
  73.8 4.9 %collective-permute-start.11 = (bf16[24,896]{1,0:T(8,128)(2,1)S(1)}, bf16[24,896]{1,0:T(8,128)(2,1)S(1)}, u32[]{:S(2)}, u32[]{:S(2)}) collective-permute-start(bf16[24,896]{1,0:T(8,128)(2,1)S(1)} %get-tuple-element.43), channel_id=1, source_target_pairs={{0,8},{1,9},{2,10},{3,11},{4,12},{5,13},{6,14},{7,15},{8,0},{9,1},... | collective-permute-start | bytes 129032 | tf_op jit(solution)/shard_map/ppermute | solution.py:433
  76.3 4.3 %collective-permute-start.12 = (bf16[24,896]{1,0:T(8,128)(2,1)S(1)}, bf16[24,896]{1,0:T(8,128)(2,1)S(1)}, u32[]{:S(2)}, u32[]{:S(2)}) collective-permute-start(bf16[24,896]{1,0:T(8,128)(2,1)S(1)} %get-tuple-element.42), channel_id=1, source_target_pairs={{0,12},{1,13},{2,14},{3,15},{4,0},{5,1},{6,2},{7,3},{8,4},{9,5},{1... | collective-permute-start | bytes 129032 | tf_op jit(solution)/shard_map/ppermute | solution.py:433
where the time goes:
time: 82.2 us; the launch traced here: 81.4 us
  starting transfers between devices  36.9 us (45%)
  Pallas kernels  34.5 us (42%)
  local copies, waits for them, and re-layouts  5.99 us (7%)
  waiting for transfers between devices  3.02 us (4%)
  between operations  0.99 us (1%)
    pallas_call x10, Pallas kernels, call(): pl.pallas_call(body, out_shape=list(outs), in_specs=[pl.BlockSpec(memory_...  34.5 us
    ppermute x4, starting transfers between devices, upward(): return lax.ppermute(x, 'space', [(i, i + 1) for i in range(count - 1)])  14.4 us
    ppermute x3, starting transfers between devices, shards(): lax.ppermute(part, 'space', [(i, (i + 4 * hop) % count) for i in range(co...  8.72 us
    ppermute x1, starting transfers between devices, shards(): arrived = lax.ppermute(sent, 'space', [(i, i ^ 2) for i in range(count)])  6.6 us
    unnamed x34, local copies, waits for them, and re-layouts  5.94 us
    ppermute x4, starting transfers between devices, downward(): return lax.ppermute(x, 'space', [(i + 1, i) for i in range(count - 1)])  5.16 us
    ppermute x3, waiting for transfers between devices, shards(): lax.ppermute(part, 'space', [(i, (i + 4 * hop) % count) for i in range(co...  2.99 us
    ppermute x1, starting transfers between devices, shards(): arrived = lax.ppermute(sent, 'space', [(i, i ^ 1) for i in range(count)])  2.05 us
  transfers between devices with their start and end apart: 13, of which 3 were waited for; matrix products, arithmetic and copies ran while one was open for 0% of the time, Pallas kernels for 35%

commit v1 on v0

v1 whole, which is shorter than its diff:
```python
import functools
import math

import jax
import jax.numpy as jnp
from jax import lax
from jax.experimental import pallas as pl
from jax.experimental.pallas import tpu as pltpu
from jax.sharding import PartitionSpec as P

F32, BF16 = jnp.float32, jnp.bfloat16
STEP, BLOCK = 256, 512
VMEM_LIMIT = 24 * 2**20
NN = (((1,), (0,)), ((), ()))
NT = (((1,), (1,)), ((), ()))

PLANES = (0, 1, 2, -1, -2, 3)


def depth_tap(source, target):
    tap = source - target + 1
    return tap if 0 <= tap <= 2 else None


def call(body, outs, ins, scratch=(), flops=0, name=None, smem=()):
    moved = sum(math.prod(s.shape) * s.dtype.itemsize for s in (*outs, *ins))
    return pl.pallas_call(
        body,
        out_shape=list(outs),
        in_specs=[
            pl.BlockSpec(memory_space=pltpu.SMEM if i in smem else pltpu.VMEM)
            for i in range(len(ins))
        ],
        out_specs=[pl.BlockSpec(memory_space=pltpu.VMEM)] * len(outs),
        scratch_shapes=list(scratch),
        compiler_params=pltpu.CompilerParams(vmem_limit_bytes=VMEM_LIMIT),
        cost_estimate=pl.CostEstimate(flops=flops, bytes_accessed=moved, transcendentals=0),
        name=name,
    )(*ins)


def lanes_low(x):
    return lax.broadcasted_iota(jnp.int32, x.shape, 1) < 64


def swap(x):
    return pltpu.roll(x, 64, 1)


def pick(low, high):
    return jnp.where(lanes_low(low), low, high)


def fill_windows(windows, start, lane, chunk, columns, stride):
    size = chunk.shape[0]
    column = lax.broadcasted_iota(jnp.int32, chunk.shape, 0) % columns
    before = jnp.where(column == 0, 0.0, pltpu.roll(chunk, 1, 0))
    after = jnp.where(column == columns - 1, 0.0, pltpu.roll(chunk, size - 1, 0))
    at = pl.ds(pl.multiple_of(columns + start, 32), size)
    for tap, part in enumerate((before, chunk, after)):
        first = tap * stride + lane
        windows[at, first : first + chunk.shape[1]] = part.astype(BF16)


def clear_edges(windows, columns):
    rows, lanes = windows.shape
    windows[0:columns, :] = jnp.zeros((columns, lanes), BF16)
    windows[rows - columns : rows, :] = jnp.zeros((columns, lanes), BF16)


def window_dot(windows, weights, start, columns, dims):
    rows = jnp.concatenate(
        [windows[start + tap * columns : start + tap * columns + BLOCK, :] for tap in range(3)],
        axis=1,
    )
    return lax.dot_general(rows, weights[...], dims, preferred_element_type=F32)


def packed(low, high):
    return pick(low, swap(high)), pick(swap(low), high)


def unpacked(first, second):
    return packed(first, second)


def pack_body(volume, own):
    def step(i, carry):
        rows = pl.ds(pl.multiple_of(i * STEP, STEP), STEP)
        own[rows, :] = jnp.concatenate([volume[0, rows, :], volume[1, rows, :]], axis=1)
        return carry

    lax.fori_loop(0, own.shape[0] // STEP, step, 0)


def leave_body(columns, cotangent, weight, own, up, down, windows, taps):
    half = cotangent.shape[1] // 2
    for row in range(3):
        for column in range(3):
            for source in range(2):
                first = row * 768 + column * 256 + source * 128
                for at, target in enumerate(PLANES[:4]):
                    depth = depth_tap(source, target)
                    taps[at * 64 : at * 64 + 64, first : first + 128] = (
                        jnp.zeros((64, 128), BF16)
                        if depth is None
                        else weight[(2 - depth) * 9 + (2 - row) * 3 + 2 - column]
                    )

    def fill(i, carry):
        start = pl.multiple_of(i * STEP, STEP)
        for plane in range(2):
            chunk = cotangent[plane, pl.ds(start, STEP), :].astype(F32)
            fill_windows(windows, start, plane * 128, chunk, columns, 256)
        return carry

    clear_edges(windows, columns)
    lax.fori_loop(0, 2 * half // STEP, fill, 0)
    for start in range(0, half, BLOCK):
        sides = []
        for first in (start, start + half):
            term = window_dot(windows, taps, first, columns, NT)
            own[first : first + BLOCK, :] = term[:, :128]
            sides.append(term[:, 128:])
        upper, lower = packed(*sides)
        up[start : start + BLOCK, :] = upper.astype(BF16)
        down[start : start + BLOCK, :] = lower.astype(BF16)


def hidden_body(
    columns, count, me, own, below, above, weight, act_windows, slope, windows, taps
):
    cells = own.shape[0]
    zero = jnp.zeros((64, 64), BF16)
    for row in range(3):
        for column in range(3):
            for at, source in enumerate(PLANES):
                first = row * 1152 + column * 384 + at * 64
                depths = [depth_tap(source, target) for target in PLANES[:4]]
                parts = [
                    zero if d is None else weight[d * 9 + row * 3 + column] for d in depths
                ]
                taps[first : first + 64, :128] = jnp.concatenate(parts[:2], axis=1)
                taps[first : first + 64, 128:] = jnp.concatenate(parts[2:], axis=1)

    def fill(i, carry):
        start = pl.multiple_of(i * STEP, STEP)
        rows = pl.ds(start, STEP)
        lower, upper = below[rows, :].astype(F32), above[rows, :].astype(F32)
        fill_windows(windows, start, 0, own[rows, :].astype(F32), columns, 384)
        fill_windows(windows, start, 128, pick(upper, lower), columns, 384)
        fill_windows(windows, start, 256, pick(lower, upper), columns, 384)
        return carry

    clear_edges(windows, columns)
    clear_edges(act_windows, columns)
    lax.fori_loop(0, cells // STEP, fill, 0)
    lanes = lax.broadcasted_iota(jnp.int32, (BLOCK, 128), 1)
    edges = [jnp.where(me[0] == end, 0.0, 1.0).astype(F32) for end in (count - 1, 0)]
    inside = jnp.where(lanes < 64, edges[0], edges[1])
    for start in range(0, cells, BLOCK):
        hidden = window_dot(windows, taps, start, columns, NN)
        gate = jax.nn.sigmoid(hidden)
        act = (hidden * gate).astype(BF16).astype(F32)
        fill_windows(act_windows, start, 0, act[:, :128], columns, 256)
        fill_windows(act_windows, start, 128, act[:, 128:] * inside, columns, 256)
        hidden, gate = hidden[:, :128], gate[:, :128]
        slope[start : start + BLOCK, :] = gate * (1.0 + hidden * (1.0 - gate))


def slope_body(terms, below, above, slope, grad, up, down):
    half = terms.shape[0] // 2

    def step(i, carry):
        start = pl.multiple_of(i * STEP, STEP)
        low, high = pl.ds(start, STEP), pl.ds(start + half, STEP)
        arrived = unpacked(below[low, :].astype(F32), above[low, :].astype(F32))
        sides = []
        for rows, extra in zip((low, high), arrived):
            value = ((terms[rows, :] + extra) * slope[rows, :]).astype(BF16)
            grad[rows, :] = value
            sides.append(value.astype(F32))
        lower, upper = packed(*sides)
        down[low, :] = lower.astype(BF16)
        up[low, :] = upper.astype(BF16)
        return carry

    lax.fori_loop(0, half // STEP, step, 0)


def kernel_terms(columns, out_channels, windows, stride, turned, terms):
    cells = turned.shape[1]
    for row in range(3):
        for column in range(3):
            tap = row * 3 + column
            product = jnp.dot(
                turned[...],
                windows[
                    row * columns : row * columns + cells, column * stride : column * stride + 256
                ],
                preferred_element_type=F32,
            )
            first, second = product[:out_channels], product[out_channels:]
            terms[:, tap * 128 : tap * 128 + 128] = first[:, :128] + swap(
                pick(second[:, 128:], second[:, :128])
            )
            group = 9 + tap // 2
            here = slice(group * 128, group * 128 + 128)
            if tap % 2 == 0:
                terms[:, here] = swap(first[:, 128:]) + second[:, :128]
            else:
                terms[:, here] = pick(terms[:, here], first[:, 128:] + swap(second[:, :128]))


def turn(source, target, first):
    for start in range(0, source.shape[0], STEP):
        chunk = source[start : start + STEP, :].astype(F32)
        target[first : first + chunk.shape[1], start : start + STEP] = chunk.T.astype(BF16)


def grad_two_body(columns, act_windows, cotangent, terms, turned):
    turn(cotangent.at[0], turned, 0)
    turn(cotangent.at[1], turned, 128)
    kernel_terms(columns, 128, act_windows, 256, turned, terms)


def coded(value, split):
    head = value[:split].astype(BF16)
    rest = (value[:split] - head.astype(F32)).astype(BF16)
    return jnp.concatenate([head, rest, value[split:].astype(BF16)], axis=0)


def decoded(value, split):
    value = value.astype(F32)
    return jnp.concatenate([value[:split] + value[split : 2 * split], value[2 * split :]], axis=0)


def grad_one_body(
    columns, count, me, own, below, above, grad, other, sent, kept, windows, turned, terms
):
    def fill(i, carry):
        start = pl.multiple_of(i * STEP, STEP)
        rows = pl.ds(start, STEP)
        sides = pick(above[rows, :].astype(F32), below[rows, :].astype(F32))
        fill_windows(windows, start, 0, own[rows, :].astype(F32), columns, 256)
        fill_windows(windows, start, 128, sides, columns, 256)
        return carry

    clear_edges(windows, columns)
    lax.fori_loop(0, own.shape[0] // STEP, fill, 0)
    turn(grad, turned, 0)
    kernel_terms(columns, 64, windows, 256, turned, terms)
    half = terms.shape[1] // 2
    odd = me[0] % 2 == 1

    def share(owner):
        parts = []
        for source in (terms, other):
            each = source.shape[0] // count
            block = source[owner * each : owner * each + each, :]
            parts += [block[:, :half], block[:, half:]]
        return jnp.concatenate(parts, axis=0)

    split = 2 * terms.shape[0] // count
    for pair in range(count // 2):
        even_share, odd_share = share(2 * pair), share(2 * pair + 1)
        sent[pair] = coded(jnp.where(odd, even_share, odd_share), split)
        kept[pair] = jnp.where(odd, odd_share, even_share)


def halve_body(split, me, mine, arrived, sent, kept):
    odd = (me[0] // 2) % 2
    for pair in range(sent.shape[0]):
        keep, give = 2 * pair + odd, 2 * pair + 1 - odd
        sent[pair] = coded(mine[give] + decoded(arrived[give], split), split)
        kept[pair] = mine[keep] + decoded(arrived[keep], split)


def spread_body(split, me, mine, arrived, kept, *sent):
    ring = mine.shape[0]
    place = me[0] // 4
    kept[...] = mine[place] + decoded(arrived[place], split)
    for hop, out in enumerate(sent):
        there = (place + hop + 1) % ring
        out[...] = coded(mine[there] + decoded(arrived[there], split), split)


def finish_body(scale, split, sizes, mine, *refs):
    arrived, (grad_one, grad_two) = refs[:-2], refs[-2:]
    total = mine[...]
    for part in arrived:
        total = total + decoded(part[...], split)
    total = total * scale
    half = total.shape[1]
    first = 0
    for size, out in zip(sizes, (grad_one, grad_two)):
        blocks = (total[first : first + size], total[first + size : first + 2 * size])
        first += 2 * size
        for tap in range(9):
            for depth, group, side in ((0, 9 + tap // 2, tap % 2), (1, tap, 0), (2, tap, 1)):
                lane = group * 128 + side * 64
                block, lane = (blocks[0], lane) if lane < half else (blocks[1], lane - half)
                out[depth * 9 + tap] = block[:, lane : lane + 64]


def output_body(columns, act_windows, weight, output, taps):
    for row in range(3):
        for column in range(3):
            for at, source in enumerate(PLANES[:4]):
                first = row * 768 + column * 256 + at * 64
                for plane in range(2):
                    depth = depth_tap(source, plane)
                    taps[first : first + 64, plane * 128 : plane * 128 + 128] = (
                        jnp.zeros((64, 128), BF16)
                        if depth is None
                        else weight[depth * 9 + row * 3 + column]
                    )
    for start in range(0, output.shape[1], BLOCK):
        value = window_dot(act_windows, taps, start, columns, NN)
        output[0, start : start + BLOCK, :] = value[:, :128]
        output[1, start : start + BLOCK, :] = value[:, 128:]


def grad_volume_body(columns, own, below, above, weight, output, windows, taps):
    zero = jnp.zeros((64, 64), BF16)
    half = own.shape[0] // 2
    for row in range(3):
        for column in range(3):
            for plane in range(2):
                pieces = []
                for source in PLANES[:4]:
                    depth = depth_tap(source, plane)
                    pieces.append(
                        zero if depth is None
                        else weight[(2 - depth) * 9 + (2 - row) * 3 + 2 - column]
                    )
                for pair in range(2):
                    first = row * 768 + column * 256 + pair * 128
                    taps[plane * 64 : plane * 64 + 64, first : first + 128] = (
                        jnp.concatenate(pieces[2 * pair : 2 * pair + 2], axis=1)
                    )

    def fill(i, carry):
        start = pl.multiple_of(i * STEP, STEP)
        sides = unpacked(
            above[pl.ds(start, STEP), :].astype(F32), below[pl.ds(start, STEP), :].astype(F32)
        )
        for first, side in zip((start, start + half), sides):
            fill_windows(windows, first, 0, own[pl.ds(first, STEP), :].astype(F32), columns, 256)
            fill_windows(windows, first, 128, side, columns, 256)
        return carry

    clear_edges(windows, columns)
    lax.fori_loop(0, half // STEP, fill, 0)
    for start in range(0, 2 * half, BLOCK):
        value = window_dot(windows, taps, start, columns, NT)
        output[0, start : start + BLOCK, :] = value[:, :64]
        output[1, start : start + BLOCK, :] = value[:, 64:]


def shards(volume, weight_one, weight_two, cotangent):
    count = lax.axis_size("space")
    planes, rows, columns, channels = volume.shape
    cells = rows * columns
    scale = 1.0 / math.sqrt(planes * count * cells)
    mid, wide = weight_two.shape[3], weight_two.shape[4]
    me = lax.axis_index("space").astype(jnp.int32).reshape(1)
    shape = jax.ShapeDtypeStruct
    flat, pack = shape((cells, 128), BF16), shape((cells // 2, 128), BF16)
    slab = (cells + 2 * columns, 768)
    windows = pltpu.VMEM(slab, BF16)
    lanes = 14 * 64
    split = 2 * mid // count
    chunk = 2 * (mid + wide) // count

    def upward(x):
        return lax.ppermute(x, "space", [(i, i + 1) for i in range(count - 1)])

    def downward(x):
        return lax.ppermute(x, "space", [(i + 1, i) for i in range(count - 1)])

    def shares(*lead):
        return shape((*lead, chunk + split, lanes), BF16), shape((*lead, chunk, lanes), F32)

    volume = volume.reshape(planes, cells, channels)
    cotangent = cotangent.reshape(planes, cells, wide)
    weight_one = weight_one.reshape(27, channels, mid)
    weight_two = weight_two.reshape(27, mid, wide)
    one_flops = 2 * planes * cells * 27 * channels * mid
    two_flops = 2 * planes * cells * 27 * mid * wide

    own, = call(pack_body, (flat,), (volume,), name="pack_volume")
    vol_halo = (upward(own), downward(own))
    terms, up, down = call(
        functools.partial(leave_body, columns),
        (shape((cells, 128), F32), pack, pack),
        (cotangent, weight_two),
        (windows, pltpu.VMEM((256, 3 * 768), BF16)),
        two_flops, "grad_act_terms",
    )
    act_terms_halo = (upward(up), downward(down))
    act_windows, slope = call(
        functools.partial(hidden_body, columns, count),
        (shape(slab, BF16), shape((cells, 128), F32)),
        (me, own, *vol_halo, weight_one),
        (pltpu.VMEM((slab[0], 3 * 384), BF16), pltpu.VMEM((9 * 384, 256), BF16)),
        2 * one_flops, "hidden", (0,),
    )
    terms_two, = call(
        functools.partial(grad_two_body, columns),
        (shape((wide, 2 * lanes), F32),),
        (act_windows, cotangent),
        (pltpu.VMEM((256, cells), BF16),),
        two_flops, "grad_two_terms",
    )
    grad_hidden, up, down = call(
        slope_body, (flat, pack, pack), (terms, *act_terms_halo, slope), name="grad_hidden"
    )
    grad_halo = (upward(up), downward(down))
    sent, kept = call(
        functools.partial(grad_one_body, columns, count),
        shares(count // 2),
        (me, own, *vol_halo, grad_hidden, terms_two),
        (windows, pltpu.VMEM((128, cells), BF16), pltpu.VMEM((mid, 2 * lanes), F32)),
        one_flops, "grad_one_terms", (0,),
    )
    arrived = lax.ppermute(sent, "space", [(i, i ^ 1) for i in range(count)])
    sent, kept = call(
        functools.partial(halve_body, split), shares(count // 4),
        (me, kept, arrived), name="halve", smem=(0,),
    )
    sent, act_windows = lax.optimization_barrier((sent, act_windows))
    arrived = lax.ppermute(sent, "space", [(i, i ^ 2) for i in range(count)])
    output, = call(
        functools.partial(output_body, columns),
        (shape((planes, cells, wide), F32),),
        (act_windows, weight_two),
        (pltpu.VMEM((3 * 768, 256), BF16),),
        two_flops, "output",
    )
    ring = count // 4
    out, mine = shares()
    mine, *sent = call(
        functools.partial(spread_body, split), (mine, *[out] * (ring - 1)),
        (me, kept, arrived), name="spread", smem=(0,),
    )
    sent, grad_hidden = lax.optimization_barrier((sent, grad_hidden))
    rest = [
        lax.ppermute(x, "space", [(i, (i + 4 * hop + 4) % count) for i in range(count)])
        for hop, x in enumerate(sent)
    ]
    grad_volume, = call(
        functools.partial(grad_volume_body, columns),
        (shape((planes, cells, channels), F32),),
        (grad_hidden, *grad_halo, weight_one),
        (windows, pltpu.VMEM((128, 3 * 768), BF16)),
        one_flops, "grad_volume",
    )
    grad_one, grad_two = call(
        functools.partial(finish_body, scale, split, (mid // count, wide // count)),
        (shape((27, mid // count, channels), F32), shape((27, wide // count, mid), F32)),
        (mine, *rest), name="finish",
    )
    return (
        output.reshape(planes, rows, columns, wide),
        grad_volume.reshape(planes, rows, columns, channels),
        jnp.swapaxes(grad_one, 1, 2).reshape(3, 3, 3, channels, mid // count),
        jnp.swapaxes(grad_two, 1, 2).reshape(3, 3, 3, mid, wide // count),
    )


def solution(mesh):
    cells = P(("groups", "space"), None, None, None)
    kernel = P("groups", None, None, None, "space")
    return jax.shard_map(
        shards,
        mesh=mesh,
        in_specs=(cells, P(), P(), cells),
        out_specs=(cells, cells, kernel, kernel),
        check_vma=False,
    )
```

time: 82.2 us -> 64.5 us (0.78)
  starting transfers between devices: 36.9 us -> 25.4 us
  Pallas kernels: 34.5 us -> 29.4 us
  local copies, waits for them, and re-layouts: 5.99 us -> 3.47 us
  waiting for transfers between devices: 3.02 us -> 5.08 us
    pallas_call x10 -> x11, Pallas kernels: 34.5 us -> 29.4 us  [call(): pl.pallas_call(body, out_shape=list(outs), in_specs=[pl.BlockSpec(memory_...]
    ppermute x1, waiting for transfers between devices: 0.01 us -> 5.06 us  [shards(): arrived = lax.ppermute(sent, 'space', [(i, i ^ 2) for i in range(count)])]
    ppermute x4 -> x3, starting transfers between devices: 14.4 us -> 9.48 us  [upward(): return lax.ppermute(x, 'space', [(i, i + 1) for i in range(count - 1)])]
    ppermute x3, waiting for transfers between devices: 2.99 us -> 0.01 us  [shards(): lax.ppermute(x, 'space', [(i, (i + 4 * hop + 4) % count) for i in range(c...]
    ppermute x3, starting transfers between devices: 8.72 us -> 6.11 us  [shards(): lax.ppermute(x, 'space', [(i, (i + 4 * hop + 4) % count) for i in range(c...]
    unnamed x34 -> x12, local copies, waits for them, and re-layouts: 5.94 us -> 3.47 us
    ppermute x1, starting transfers between devices: 6.6 us -> 4.74 us  [shards(): arrived = lax.ppermute(sent, 'space', [(i, i ^ 2) for i in range(count)])]
    ppermute x4 -> x3, starting transfers between devices: 5.16 us -> 3.88 us  [downward(): return lax.ppermute(x, 'space', [(i + 1, i) for i in range(count - 1)])]
  transfers between devices with their start and end apart: 13 -> 11, of which waited for: 3 -> 1; matrix products, arithmetic and copies ran while one was open for 0% -> 0% of each run, Pallas kernels for 35% -> 37%
where the time goes in v1:
time: 64.5 us; the launch traced here: 64.1 us
  Pallas kernels  29.4 us (46%)
  starting transfers between devices  25.4 us (39%)
  waiting for transfers between devices  5.08 us (8%)
  local copies, waits for them, and re-layouts  3.47 us (5%)
  between operations  0.81 us (1%)
    pallas_call x11, Pallas kernels, call(): pl.pallas_call(body, out_shape=list(outs), in_specs=[pl.BlockSpec(memory_...  29.4 us
    ppermute x3, starting transfers between devices, upward(): return lax.ppermute(x, 'space', [(i, i + 1) for i in range(count - 1)])  9.48 us
    ppermute x3, starting transfers between devices, shards(): lax.ppermute(x, 'space', [(i, (i + 4 * hop + 4) % count) for i in range(c...  6.11 us
    ppermute x1, waiting for transfers between devices, shards(): arrived = lax.ppermute(sent, 'space', [(i, i ^ 2) for i in range(count)])  5.06 us
    ppermute x1, starting transfers between devices, shards(): arrived = lax.ppermute(sent, 'space', [(i, i ^ 2) for i in range(count)])  4.74 us
    ppermute x3, starting transfers between devices, downward(): return lax.ppermute(x, 'space', [(i + 1, i) for i in range(count - 1)])  3.88 us
    unnamed x12, local copies, waits for them, and re-layouts  3.47 us
  transfers between devices with their start and end apart: 11, of which 1 were waited for; matrix products, arithmetic and copies ran while one was open for 0% of the time, Pallas kernels for 37%

profile of v1, /device:TPU:0, one launch (start us, length us, event | category | flops | bytes accessed | tf_op | source)
XLA Modules:
  0.0 64.1 jit_solution(16713503407799796137)
XLA Ops:
  0.6 1.2 %copy-done = bf16[2,64,32,64]{3,2,1,0:T(8,128)(2,1)S(1)} copy-done((bf16[2,64,32,64]{3,2,1,0:T(8,128)(2,1)S(1)}, bf16[2,64,32,64]{3,2,1,0:T(8,128)(2,1)}, u32[]{:S(2)}) %copy-start) | copy-done | bytes 524312
  1.9 0.7 %pack_volume.1.own = bf16[2048,128]{1,0:T(8,128)(2,1)S(1)} custom-call(bf16[2,2048,64]{2,1,0:T(8,128)(2,1)S(1)} %bitcast.13), custom_call_target="tpu_custom_call" | custom-call | bytes 1048576 | tf_op jit(solution)/shard_map/pack_volume/pallas_call | solution.py:27
  2.5 1.3 %collective-permute-start.1 = (bf16[2048,128]{1,0:T(8,128)(2,1)S(1)}, bf16[2048,128]{1,0:T(8,128)(2,1)S(1)}, u32[]{:S(2)}, u32[]{:S(2)}) collective-permute-start(bf16[2048,128]{1,0:T(8,128)(2,1)S(1)} %pack_volume.1.own), channel_id=1, source_target_pairs={{1,0},{2,1},{3,2},{4,3},{5,4},{6,5},{7,6},{8,7},{9,8},{10,9},{11,1... | collective-permute-start | bytes 1572872 | tf_op jit(solution)/shard_map/ppermute | solution.py:380
  3.8 3.8 %collective-permute-start = (bf16[2048,128]{1,0:T(8,128)(2,1)S(1)}, bf16[2048,128]{1,0:T(8,128)(2,1)}, u32[]{:S(2)}, u32[]{:S(2)}) collective-permute-start(bf16[2048,128]{1,0:T(8,128)(2,1)S(1)} %pack_volume.1.own), channel_id=1, source_target_pairs={{0,1},{1,2},{2,3},{3,4},{4,5},{5,6},{6,7},{7,8},{8,9},{9,10},{10,1... | collective-permute-start | bytes 1572872 | tf_op jit(solution)/shard_map/ppermute | solution.py:377
  7.7 1.2 %copy-done.2 = bf16[2,64,32,128]{3,2,1,0:T(8,128)(2,1)S(1)} copy-done((bf16[2,64,32,128]{3,2,1,0:T(8,128)(2,1)S(1)}, bf16[2,64,32,128]{3,2,1,0:T(8,128)(2,1)}, u32[]{:S(2)}) %copy-start.2) | copy-done | bytes 1048600
  8.9 1.0 %copy-done.4 = bf16[3,3,3,64,128]{4,3,2,1,0:T(8,128)(2,1)S(1)} copy-done((bf16[3,3,3,64,128]{4,3,2,1,0:T(8,128)(2,1)S(1)}, bf16[3,3,3,64,128]{4,3,2,1,0:T(8,128)(2,1)}, u32[]{:S(2)}) %copy-start.4) | copy-done | bytes 442392
  9.9 4.3 %grad_act_terms.1 = (f32[2048,128]{1,0:T(8,128)S(1)}, bf16[1024,128]{1,0:T(8,128)(2,1)}, bf16[1024,128]{1,0:T(8,128)(2,1)S(1)}) custom-call(bf16[2,2048,128]{2,1,0:T(8,128)(2,1)S(1)} %bitcast.16, bf16[27,64,128]{2,1,0:T(8,128)(2,1)S(1)} %bitcast.18), custom_call_target="tpu_custom_call" | custom-call | flops 1811939328 | bytes 3063808 | tf_op jit(solution)/shard_map/grad_act_terms/pallas_call | solution.py:27
  14.2 3.7 %collective-permute-start.2 = (bf16[1024,128]{1,0:T(8,128)(2,1)}, bf16[1024,128]{1,0:T(8,128)(2,1)S(1)}, u32[]{:S(2)}, u32[]{:S(2)}) collective-permute-start(bf16[1024,128]{1,0:T(8,128)(2,1)} %get-tuple-element.29), channel_id=1, source_target_pairs={{0,1},{1,2},{2,3},{3,4},{4,5},{5,6},{6,7},{7,8},{8,9},{9,10},{10,1... | collective-permute-start | bytes 786440 | tf_op jit(solution)/shard_map/ppermute | solution.py:377
  17.9 1.3 %collective-permute-start.3 = (bf16[1024,128]{1,0:T(8,128)(2,1)S(1)}, bf16[1024,128]{1,0:T(8,128)(2,1)S(1)}, u32[]{:S(2)}, u32[]{:S(2)}) collective-permute-start(bf16[1024,128]{1,0:T(8,128)(2,1)S(1)} %get-tuple-element.30), channel_id=1, source_target_pairs={{1,0},{2,1},{3,2},{4,3},{5,4},{6,5},{7,6},{8,7},{9,8},{10,9},{11,1... | collective-permute-start | bytes 786440 | tf_op jit(solution)/shard_map/ppermute | solution.py:380
  19.2 0.0 collective-permute-done.below
  19.2 0.0 copy-start.3
  19.3 7.4 %hidden.1 = (bf16[2112,768]{1,0:T(8,128)(2,1)S(1)}, f32[2048,128]{1,0:T(8,128)S(1)}) custom-call(s32[1]{0:T(128)} %bitcast.me, bf16[2048,128]{1,0:T(8,128)(2,1)S(1)} %pack_volume.1.own, bf16[2048,128]{1,0:T(8,128)(2,1)} %collective-permute-done.below, bf16[2048,128]{1,0:T(8,128)(2,1)S(1)} %collective-permute-done.1.above, bf16[27,64,64]{2,1,0:T(8,128)(2,1)S(1)} %bitcast.14), custom_call_target="tpu_custom_call" | custom-call | flops 1811939328 | bytes 6086660 | tf_op jit(solution)/shard_map/hidden/pallas_call | solution.py:27
  26.7 2.8 %grad_two_terms.1.other = f32[128,1792]{1,0:T(8,128)S(1)} custom-call(bf16[2112,768]{1,0:T(8,128)(2,1)S(1)} %get-tuple-element.37.act_windows, bf16[2,2048,128]{2,1,0:T(8,128)(2,1)S(1)} %bitcast.17), custom_call_target="tpu_custom_call" | custom-call | flops 1811939328 | bytes 5210112 | tf_op jit(solution)/shard_map/grad_two_terms/pallas_call | solution.py:27
  29.5 0.0 collective-permute-done.2.below
  29.5 0.9 %grad_hidden.1 = (bf16[2048,128]{1,0:T(8,128)(2,1)S(1)}, bf16[1024,128]{1,0:T(8,128)(2,1)S(1)}, bf16[1024,128]{1,0:T(8,128)(2,1)S(1)}) custom-call(f32[2048,128]{1,0:T(8,128)S(1)} %get-tuple-element.28.terms, bf16[1024,128]{1,0:T(8,128)(2,1)S(1)} %collective-permute-done.2.below, bf16[1024,128]{1,0:T(8,128)(2,1)S(1)} %collective-permute-done.3.above, ...), custom_call_target="tpu_custom_call" | custom-call | bytes 3670016 | tf_op jit(solution)/shard_map/grad_hidden/pallas_call | solution.py:27
  30.4 0.0 copy-start.5
  30.4 3.5 %grad_one_terms.1 = (bf16[8,32,896]{2,1,0:T(8,128)(2,1)S(1)}, f32[8,24,896]{2,1,0:T(8,128)S(1)}) custom-call(s32[1]{0:T(128)} %bitcast.me, bf16[2048,128]{1,0:T(8,128)(2,1)S(1)} %pack_volume.1.own, bf16[2048,128]{1,0:T(8,128)(2,1)} %collective-permute-done.below, bf16[2048,128]{1,0:T(8,128)(2,1)S(1)} %collective-permute-done.1.above, ...), custom_call_target="tpu_custom_call" | custom-call | flops 905969664 | bytes 4161540 | tf_op jit(solution)/shard_map/grad_one_terms/pallas_call | solution.py:27
  33.9 1.2 %collective-permute-start.4 = (bf16[8,32,896]{2,1,0:T(8,128)(2,1)S(1)}, bf16[8,32,896]{2,1,0:T(8,128)(2,1)S(1)}, u32[]{:S(2)}, u32[]{:S(2)}) collective-permute-start(bf16[8,32,896]{2,1,0:T(8,128)(2,1)S(1)} %get-tuple-element.35), channel_id=1, source_target_pairs={{0,1},{1,0},{2,3},{3,2},{4,5},{5,4},{6,7},{7,6},{8,9},{9,8},{10,11... | collective-permute-start | bytes 1376264 | tf_op jit(solution)/shard_map/ppermute | solution.py:427
  35.1 1.9 %collective-permute-start.6 = (bf16[1024,128]{1,0:T(8,128)(2,1)S(1)}, bf16[1024,128]{1,0:T(8,128)(2,1)S(1)}, u32[]{:S(2)}, u32[]{:S(2)}) collective-permute-start(bf16[1024,128]{1,0:T(8,128)(2,1)S(1)} %get-tuple-element.44), channel_id=1, source_target_pairs={{0,1},{1,2},{2,3},{3,4},{4,5},{5,6},{6,7},{7,8},{8,9},{9,10},{10,1... | collective-permute-start | bytes 786440 | tf_op jit(solution)/shard_map/ppermute | solution.py:377
  37.0 1.3 %collective-permute-start.7 = (bf16[1024,128]{1,0:T(8,128)(2,1)S(1)}, bf16[1024,128]{1,0:T(8,128)(2,1)S(1)}, u32[]{:S(2)}, u32[]{:S(2)}) collective-permute-start(bf16[1024,128]{1,0:T(8,128)(2,1)S(1)} %get-tuple-element.45), channel_id=1, source_target_pairs={{1,0},{2,1},{3,2},{4,3},{5,4},{6,5},{7,6},{8,7},{9,8},{10,9},{11,1... | collective-permute-start | bytes 786440 | tf_op jit(solution)/shard_map/ppermute | solution.py:380
  38.3 0.1 halve.1
  38.4 4.7 %collective-permute-start.5 = (bf16[4,32,896]{2,1,0:T(8,128)(2,1)S(1)}, bf16[4,32,896]{2,1,0:T(8,128)(2,1)S(1)}, u32[]{:S(2)}, u32[]{:S(2)}) collective-permute-start(bf16[4,32,896]{2,1,0:T(8,128)(2,1)S(1)} %get-tuple-element.39), channel_id=1, source_target_pairs={{0,2},{1,3},{2,0},{3,1},{4,6},{5,7},{6,4},{7,5},{8,10},{9,11},{10,... | collective-permute-start | bytes 688136 | tf_op jit(solution)/shard_map/ppermute | solution.py:433
  43.2 4.0 %output.1 = f32[2,2048,128]{2,1,0:T(8,128)} custom-call(bf16[2112,768]{1,0:T(8,128)(2,1)S(1)} %get-tuple-element.37.act_windows, bf16[27,64,128]{2,1,0:T(8,128)(2,1)S(1)} %bitcast.19), custom_call_target="tpu_custom_call" | custom-call | flops 1811939328 | bytes 5783552 | tf_op jit(solution)/shard_map/output/pallas_call | solution.py:27
  47.1 5.1 %collective-permute-done.5.arrived = bf16[4,32,896]{2,1,0:T(8,128)(2,1)S(1)} collective-permute-done((bf16[4,32,896]{2,1,0:T(8,128)(2,1)S(1)}, bf16[4,32,896]{2,1,0:T(8,128)(2,1)S(1)}, u32[]{:S(2)}, u32[]{:S(2)}) %collective-permute-start.5) | collective-permute-done | bytes 229408 | tf_op jit(solution)/shard_map/ppermute | solution.py:433
  52.2 0.1 spread.1
  52.3 2.2 %collective-permute-start.8 = (bf16[32,896]{1,0:T(8,128)(2,1)S(1)}, bf16[32,896]{1,0:T(8,128)(2,1)S(1)}, u32[]{:S(2)}, u32[]{:S(2)}) collective-permute-start(bf16[32,896]{1,0:T(8,128)(2,1)S(1)} %get-tuple-element.47), channel_id=1, source_target_pairs={{0,4},{1,5},{2,6},{3,7},{4,8},{5,9},{6,10},{7,11},{8,12},{9,13},{1... | collective-permute-start | bytes 172040 | tf_op jit(solution)/shard_map/ppermute | solution.py:449
  54.4 2.6 %collective-permute-start.9 = (bf16[32,896]{1,0:T(8,128)(2,1)S(1)}, bf16[32,896]{1,0:T(8,128)(2,1)S(1)}, u32[]{:S(2)}, u32[]{:S(2)}) collective-permute-start(bf16[32,896]{1,0:T(8,128)(2,1)S(1)} %get-tuple-element.48), channel_id=1, source_target_pairs={{0,8},{1,9},{2,10},{3,11},{4,12},{5,13},{6,14},{7,15},{8,0},{9,1},... | collective-permute-start | bytes 172040 | tf_op jit(solution)/shard_map/ppermute | solution.py:449
  57.0 1.4 %collective-permute-start.10 = (bf16[32,896]{1,0:T(8,128)(2,1)S(1)}, bf16[32,896]{1,0:T(8,128)(2,1)S(1)}, u32[]{:S(2)}, u32[]{:S(2)}) collective-permute-start(bf16[32,896]{1,0:T(8,128)(2,1)S(1)} %get-tuple-element.49), channel_id=1, source_target_pairs={{0,12},{1,13},{2,14},{3,15},{4,0},{5,1},{6,2},{7,3},{8,4},{9,5},{1... | collective-permute-start | bytes 172040 | tf_op jit(solution)/shard_map/ppermute | solution.py:449
  58.4 0.0 collective-permute-done.6.below
  58.4 0.0 collective-permute-done.7.above
  58.4 5.0 %grad_volume.1 = f32[2,2048,64]{2,1,0:T(8,128)} custom-call(bf16[2048,128]{1,0:T(8,128)(2,1)S(1)} %get-tuple-element.43.grad.own, bf16[1024,128]{1,0:T(8,128)(2,1)S(1)} %collective-permute-done.6.below, bf16[1024,128]{1,0:T(8,128)(2,1)S(1)} %collective-permute-done.7.above, bf16[27,64,64]{2,1,0:T(8,128)(2,1)S(1)} %bitcast.15), custom_call_target="tpu_custom_call" | custom-call | flops 905969664 | bytes 2318336 | tf_op jit(solution)/shard_map/grad_volume/pallas_call | solution.py:27
  63.4 0.8 %finish.1 = (f32[27,4,64]{2,1,0:T(4,128)}, f32[27,8,64]{2,1,0:T(8,128)}) custom-call(f32[24,896]{1,0:T(8,128)S(1)} %get-tuple-element.46.mine, bf16[32,896]{1,0:T(8,128)(2,1)S(1)} %collective-permute-done.8.refs_0_, bf16[32,896]{1,0:T(8,128)(2,1)S(1)} %collective-permute-done.9.refs_1_, bf16[32,896]{1,0:T(8,128)(2,1)S(1)} %collective-permute-done.10.refs_2_), custom_call_target="tpu_custom_call" | custom-call | bytes 340992 | tf_op jit(solution)/shard_map/finish/pallas_call | solution.py:27
  (13 shorter events, 0.0 us)
Async XLA Ops:
  0.6 1.2 %copy-start = (bf16[2,64,32,64]{3,2,1,0:T(8,128)(2,1)S(1)}, bf16[2,64,32,64]{3,2,1,0:T(8,128)(2,1)}, u32[]{:S(2)}) copy-start(bf16[2,64,32,64]{3,2,1,0:T(8,128)(2,1)} %param.4) | copy-start | bytes 1572868
  2.5 16.7 %collective-permute-start.1 = (bf16[2048,128]{1,0:T(8,128)(2,1)S(1)}, bf16[2048,128]{1,0:T(8,128)(2,1)S(1)}, u32[]{:S(2)}, u32[]{:S(2)}) collective-permute-start(bf16[2048,128]{1,0:T(8,128)(2,1)S(1)} %pack_volume.1.own), channel_id=1, source_target_pairs={{1,0},{2,1},{3,2},{4,3},{5,4},{6,5},{7,6},{8,7},{9,8},{10,9},{11,1... | collective-permute-start | bytes 1572872 | tf_op jit(solution)/shard_map/ppermute | solution.py:380
  3.8 15.4 %collective-permute-start = (bf16[2048,128]{1,0:T(8,128)(2,1)S(1)}, bf16[2048,128]{1,0:T(8,128)(2,1)}, u32[]{:S(2)}, u32[]{:S(2)}) collective-permute-start(bf16[2048,128]{1,0:T(8,128)(2,1)S(1)} %pack_volume.1.own), channel_id=1, source_target_pairs={{0,1},{1,2},{2,3},{3,4},{4,5},{5,6},{6,7},{7,8},{8,9},{9,10},{10,1... | collective-permute-start | bytes 1572872 | tf_op jit(solution)/shard_map/ppermute | solution.py:377
  7.7 1.2 %copy-start.2 = (bf16[2,64,32,128]{3,2,1,0:T(8,128)(2,1)S(1)}, bf16[2,64,32,128]{3,2,1,0:T(8,128)(2,1)}, u32[]{:S(2)}) copy-start(bf16[2,64,32,128]{3,2,1,0:T(8,128)(2,1)} %param.7) | copy-start | bytes 3145732
  8.9 1.0 %copy-start.4 = (bf16[3,3,3,64,128]{4,3,2,1,0:T(8,128)(2,1)S(1)}, bf16[3,3,3,64,128]{4,3,2,1,0:T(8,128)(2,1)}, u32[]{:S(2)}) copy-start(bf16[3,3,3,64,128]{4,3,2,1,0:T(8,128)(2,1)} %param.6) | copy-start | bytes 1327108
  9.9 9.3 %copy-start.1 = (bf16[3,3,3,64,64]{4,3,2,1,0:T(8,128)(2,1)S(1)}, bf16[3,3,3,64,64]{4,3,2,1,0:T(8,128)(2,1)}, u32[]{:S(2)}) copy-start(bf16[3,3,3,64,64]{4,3,2,1,0:T(8,128)(2,1)} %param.5) | copy-start | bytes 663556
  14.2 15.3 %collective-permute-start.2 = (bf16[1024,128]{1,0:T(8,128)(2,1)}, bf16[1024,128]{1,0:T(8,128)(2,1)S(1)}, u32[]{:S(2)}, u32[]{:S(2)}) collective-permute-start(bf16[1024,128]{1,0:T(8,128)(2,1)} %get-tuple-element.29), channel_id=1, source_target_pairs={{0,1},{1,2},{2,3},{3,4},{4,5},{5,6},{6,7},{7,8},{8,9},{9,10},{10,1... | collective-permute-start | bytes 786440 | tf_op jit(solution)/shard_map/ppermute | solution.py:377
  17.9 11.6 %collective-permute-start.3 = (bf16[1024,128]{1,0:T(8,128)(2,1)S(1)}, bf16[1024,128]{1,0:T(8,128)(2,1)S(1)}, u32[]{:S(2)}, u32[]{:S(2)}) collective-permute-start(bf16[1024,128]{1,0:T(8,128)(2,1)S(1)} %get-tuple-element.30), channel_id=1, source_target_pairs={{1,0},{2,1},{3,2},{4,3},{5,4},{6,5},{7,6},{8,7},{9,8},{10,9},{11,1... | collective-permute-start | bytes 786440 | tf_op jit(solution)/shard_map/ppermute | solution.py:380
  19.2 7.4 %copy-start.3 = (bf16[2,64,32,128]{3,2,1,0:T(8,128)(2,1)S(1)}, bf16[2,64,32,128]{3,2,1,0:T(8,128)(2,1)}, u32[]{:S(2)}) copy-start(bf16[2,64,32,128]{3,2,1,0:T(8,128)(2,1)} %param.7) | copy-start | bytes 3145732
  30.4 12.8 %copy-start.5 = (bf16[3,3,3,64,128]{4,3,2,1,0:T(8,128)(2,1)S(1)}, bf16[3,3,3,64,128]{4,3,2,1,0:T(8,128)(2,1)}, u32[]{:S(2)}) copy-start(bf16[3,3,3,64,128]{4,3,2,1,0:T(8,128)(2,1)} %param.6) | copy-start | bytes 1327108
  33.9 4.4 %collective-permute-start.4 = (bf16[8,32,896]{2,1,0:T(8,128)(2,1)S(1)}, bf16[8,32,896]{2,1,0:T(8,128)(2,1)S(1)}, u32[]{:S(2)}, u32[]{:S(2)}) collective-permute-start(bf16[8,32,896]{2,1,0:T(8,128)(2,1)S(1)} %get-tuple-element.35), channel_id=1, source_target_pairs={{0,1},{1,0},{2,3},{3,2},{4,5},{5,4},{6,7},{7,6},{8,9},{9,8},{10,11... | collective-permute-start | bytes 1376264 | tf_op jit(solution)/shard_map/ppermute | solution.py:427
  35.1 23.3 %collective-permute-start.6 = (bf16[1024,128]{1,0:T(8,128)(2,1)S(1)}, bf16[1024,128]{1,0:T(8,128)(2,1)S(1)}, u32[]{:S(2)}, u32[]{:S(2)}) collective-permute-start(bf16[1024,128]{1,0:T(8,128)(2,1)S(1)} %get-tuple-element.44), channel_id=1, source_target_pairs={{0,1},{1,2},{2,3},{3,4},{4,5},{5,6},{6,7},{7,8},{8,9},{9,10},{10,1... | collective-permute-start | bytes 786440 | tf_op jit(solution)/shard_map/ppermute | solution.py:377
  37.0 21.4 %collective-permute-start.7 = (bf16[1024,128]{1,0:T(8,128)(2,1)S(1)}, bf16[1024,128]{1,0:T(8,128)(2,1)S(1)}, u32[]{:S(2)}, u32[]{:S(2)}) collective-permute-start(bf16[1024,128]{1,0:T(8,128)(2,1)S(1)} %get-tuple-element.45), channel_id=1, source_target_pairs={{1,0},{2,1},{3,2},{4,3},{5,4},{6,5},{7,6},{8,7},{9,8},{10,9},{11,1... | collective-permute-start | bytes 786440 | tf_op jit(solution)/shard_map/ppermute | solution.py:380
  38.4 13.8 %collective-permute-start.5 = (bf16[4,32,896]{2,1,0:T(8,128)(2,1)S(1)}, bf16[4,32,896]{2,1,0:T(8,128)(2,1)S(1)}, u32[]{:S(2)}, u32[]{:S(2)}) collective-permute-start(bf16[4,32,896]{2,1,0:T(8,128)(2,1)S(1)} %get-tuple-element.39), channel_id=1, source_target_pairs={{0,2},{1,3},{2,0},{3,1},{4,6},{5,7},{6,4},{7,5},{8,10},{9,11},{10,... | collective-permute-start | bytes 688136 | tf_op jit(solution)/shard_map/ppermute | solution.py:433
  52.3 11.1 %collective-permute-start.8 = (bf16[32,896]{1,0:T(8,128)(2,1)S(1)}, bf16[32,896]{1,0:T(8,128)(2,1)S(1)}, u32[]{:S(2)}, u32[]{:S(2)}) collective-permute-start(bf16[32,896]{1,0:T(8,128)(2,1)S(1)} %get-tuple-element.47), channel_id=1, source_target_pairs={{0,4},{1,5},{2,6},{3,7},{4,8},{5,9},{6,10},{7,11},{8,12},{9,13},{1... | collective-permute-start | bytes 172040 | tf_op jit(solution)/shard_map/ppermute | solution.py:449
  54.4 9.0 %collective-permute-start.9 = (bf16[32,896]{1,0:T(8,128)(2,1)S(1)}, bf16[32,896]{1,0:T(8,128)(2,1)S(1)}, u32[]{:S(2)}, u32[]{:S(2)}) collective-permute-start(bf16[32,896]{1,0:T(8,128)(2,1)S(1)} %get-tuple-element.48), channel_id=1, source_target_pairs={{0,8},{1,9},{2,10},{3,11},{4,12},{5,13},{6,14},{7,15},{8,0},{9,1},... | collective-permute-start | bytes 172040 | tf_op jit(solution)/shard_map/ppermute | solution.py:449
  57.0 6.4 %collective-permute-start.10 = (bf16[32,896]{1,0:T(8,128)(2,1)S(1)}, bf16[32,896]{1,0:T(8,128)(2,1)S(1)}, u32[]{:S(2)}, u32[]{:S(2)}) collective-permute-start(bf16[32,896]{1,0:T(8,128)(2,1)S(1)} %get-tuple-element.49), channel_id=1, source_target_pairs={{0,12},{1,13},{2,14},{3,15},{4,0},{5,1},{6,2},{7,3},{8,4},{9,5},{1... | collective-permute-start | bytes 172040 | tf_op jit(solution)/shard_map/ppermute | solution.py:449

commit v2 on v1

v2 whole, which is shorter than its diff:
```python
import functools
import math

import jax
import jax.numpy as jnp
from jax import lax
from jax.experimental import pallas as pl
from jax.experimental.pallas import tpu as pltpu
from jax.sharding import PartitionSpec as P

F32, BF16 = jnp.float32, jnp.bfloat16
STEP, BLOCK = 256, 512
VMEM_LIMIT = 24 * 2**20
NN = (((1,), (0,)), ((), ()))
NT = (((1,), (1,)), ((), ()))

PLANES = (0, 1, 2, -1, -2, 3)


def depth_tap(source, target):
    tap = source - target + 1
    return tap if 0 <= tap <= 2 else None


def call(body, outs, ins, scratch=(), flops=0, name=None, smem=(), apart=()):
    return pl.pallas_call(
        body,
        out_shape=list(outs),
        in_specs=[
            pl.BlockSpec(
                memory_space=pltpu.SMEM if i in smem else pl.ANY if i in apart else pltpu.VMEM
            )
            for i in range(len(ins))
        ],
        out_specs=[pl.BlockSpec(memory_space=pltpu.VMEM)] * len(outs),
        scratch_shapes=list(scratch),
        compiler_params=pltpu.CompilerParams(vmem_limit_bytes=VMEM_LIMIT),
        cost_estimate=pl.CostEstimate(flops=1, bytes_accessed=1, transcendentals=0),
        name=name,
    )(*ins)


def lanes_low(x):
    return lax.broadcasted_iota(jnp.int32, x.shape, 1) < 64


def swap(x):
    return pltpu.roll(x, 64, 1)


def pick(low, high):
    return jnp.where(lanes_low(low), low, high)


def fill_windows(windows, start, lane, chunk, columns, stride):
    size = chunk.shape[0]
    column = lax.broadcasted_iota(jnp.int32, chunk.shape, 0) % columns
    before = jnp.where(column == 0, 0.0, pltpu.roll(chunk, 1, 0))
    after = jnp.where(column == columns - 1, 0.0, pltpu.roll(chunk, size - 1, 0))
    at = pl.ds(pl.multiple_of(columns + start, 32), size)
    for tap, part in enumerate((before, chunk, after)):
        first = tap * stride + lane
        windows[at, first : first + chunk.shape[1]] = part.astype(BF16)


def clear_edges(windows, columns):
    rows, lanes = windows.shape
    windows[0:columns, :] = jnp.zeros((columns, lanes), BF16)
    windows[rows - columns : rows, :] = jnp.zeros((columns, lanes), BF16)


def row_windows(windows, start, columns, lanes=slice(None)):
    return [
        windows[start + tap * columns : start + tap * columns + BLOCK, lanes] for tap in range(3)
    ]


def window_dot(windows, weights, start, columns, dims):
    rows = jnp.concatenate(row_windows(windows, start, columns), axis=1)
    return lax.dot_general(rows, weights[...], dims, preferred_element_type=F32)


def packed(low, high):
    return pick(low, swap(high)), pick(swap(low), high)


def unpacked(first, second):
    return packed(first, second)


def by_side(odd, inner, outer):
    return jnp.where(odd, inner, outer), jnp.where(odd, outer, inner)


def pieces_of(source, target, sems, parts):
    size = target.shape[1] // parts
    return [
        pltpu.make_async_copy(
            source.at[:, pl.ds(i * size, size), :], target.at[:, pl.ds(i * size, size), :], sems.at[i]
        )
        for i in range(parts)
    ]


def pack_body(volume, own, held, sems):
    copies = pieces_of(volume, held, sems, sems.shape[0])
    size = own.shape[0] // len(copies)
    for copy in copies:
        copy.start()
    for i, copy in enumerate(copies):
        copy.wait()
        rows = slice(i * size, i * size + size)
        own[rows, :] = jnp.concatenate([held[0, rows, :], held[1, rows, :]], axis=1)


def leave_body(
    columns, me, cotangent, weight, own, inner, outer, windows, taps, held, kernel, sems, sem
):
    half = held.shape[1] // 2
    odd = me[0] % 2 == 1
    fetch = pltpu.make_async_copy(weight, kernel, sem)
    fetch.start()
    copies = pieces_of(cotangent, held, sems, sems.shape[0])
    for copy in copies:
        copy.start()
    clear_edges(windows, columns)
    fetch.wait()
    for row in range(3):
        for column in range(3):
            for source in range(2):
                first = row * 768 + column * 256 + source * 128
                for at, target in enumerate(PLANES[:4]):
                    depth = depth_tap(source, target)
                    taps[at * 64 : at * 64 + 64, first : first + 128] = (
                        jnp.zeros((64, 128), BF16)
                        if depth is None
                        else kernel[(2 - depth) * 9 + (2 - row) * 3 + 2 - column]
                    )
    size = 2 * half // len(copies)
    for i, copy in enumerate(copies):
        copy.wait()

        def fill(j, carry):
            start = pl.multiple_of(i * size + j * STEP, STEP)
            for plane in range(2):
                chunk = held[plane, pl.ds(start, STEP), :].astype(F32)
                fill_windows(windows, start, plane * 128, chunk, columns, 256)
            return carry

        lax.fori_loop(0, size // STEP, fill, 0)
    for start in range(0, half, BLOCK):
        sides = []
        for first in (start, start + half):
            term = window_dot(windows, taps, first, columns, NT)
            own[first : first + BLOCK, :] = term[:, :128]
            sides.append(term[:, 128:])
        upper, lower = packed(*sides)
        inner[start : start + BLOCK, :] = jnp.where(odd, lower, upper).astype(BF16)
        outer[start : start + BLOCK, :] = jnp.where(odd, upper, lower).astype(BF16)


def prepare_body(
    columns, own, weight_one, weight_two, cotangent,
    own_windows, hidden, side_taps, out_taps, back_taps, turned, own_taps,
):
    turn(cotangent.at[0], turned, 0)
    turn(cotangent.at[1], turned, 128)
    zero, wide_zero = jnp.zeros((64, 64), BF16), jnp.zeros((64, 128), BF16)
    for row in range(3):
        for column in range(3):
            tap = row * 3 + column
            for at, source in enumerate(PLANES):
                depths = [depth_tap(source, target) for target in PLANES[:4]]
                parts = [zero if d is None else weight_one[d * 9 + tap] for d in depths]
                if at < 2:
                    target, first = own_taps, tap * 128 + at * 64
                else:
                    target, first = side_taps, tap * 256 + (at - 2) * 64
                target[first : first + 64, :128] = jnp.concatenate(parts[:2], axis=1)
                target[first : first + 64, 128:] = jnp.concatenate(parts[2:], axis=1)
            for at, source in enumerate(PLANES[:4]):
                first = tap * 256 + at * 64
                for plane in range(2):
                    depth = depth_tap(source, plane)
                    out_taps[first : first + 64, plane * 128 : plane * 128 + 128] = (
                        wide_zero if depth is None else weight_two[depth * 9 + tap]
                    )
            for plane in range(2):
                depths = [depth_tap(source, plane) for source in PLANES[:4]]
                parts = [
                    zero if d is None else weight_one[(2 - d) * 9 + 8 - tap] for d in depths
                ]
                for pair in range(2):
                    first = tap * 256 + pair * 128
                    back_taps[plane * 64 : plane * 64 + 64, first : first + 128] = (
                        jnp.concatenate(parts[2 * pair : 2 * pair + 2], axis=1)
                    )

    def fill(i, carry):
        start = pl.multiple_of(i * STEP, STEP)
        chunk = own[pl.ds(start, STEP), :].astype(F32)
        fill_windows(own_windows, start, 0, chunk, columns, 128)
        return carry

    clear_edges(own_windows, columns)
    lax.fori_loop(0, own.shape[0] // STEP, fill, 0)
    for start in range(0, own.shape[0], BLOCK):
        hidden[start : start + BLOCK, :] = window_dot(own_windows, own_taps, start, columns, NN)


def hidden_body(
    columns, count, me, inner, outer, part, side_taps, side_windows, act_windows, slope
):
    cells = inner.shape[0]
    odd = me[0] % 2 == 1

    def fill(i, carry):
        start = pl.multiple_of(i * STEP, STEP)
        rows = pl.ds(start, STEP)
        below, above = by_side(odd, inner[rows, :].astype(F32), outer[rows, :].astype(F32))
        fill_windows(side_windows, start, 0, pick(above, below), columns, 256)
        fill_windows(side_windows, start, 128, pick(below, above), columns, 256)
        return carry

    clear_edges(side_windows, columns)
    clear_edges(act_windows, columns)
    lax.fori_loop(0, cells // STEP, fill, 0)
    lanes = lax.broadcasted_iota(jnp.int32, (BLOCK, 128), 1)
    edges = [jnp.where(me[0] == end, 0.0, 1.0).astype(F32) for end in (count - 1, 0)]
    inside = jnp.where(lanes < 64, edges[0], edges[1])
    for start in range(0, cells, BLOCK):
        hidden = part[start : start + BLOCK, :]
        hidden = hidden + window_dot(side_windows, side_taps, start, columns, NN)
        gate = jax.nn.sigmoid(hidden)
        act = (hidden * gate).astype(BF16).astype(F32)
        fill_windows(act_windows, start, 0, act[:, :128], columns, 256)
        fill_windows(act_windows, start, 128, act[:, 128:] * inside, columns, 256)
        hidden, gate = hidden[:, :128], gate[:, :128]
        slope[start : start + BLOCK, :] = gate * (1.0 + hidden * (1.0 - gate))


def slope_body(me, terms, inner, outer, slope, grad, to_inner, to_outer):
    half = terms.shape[0] // 2
    odd = me[0] % 2 == 1

    def step(i, carry):
        start = pl.multiple_of(i * STEP, STEP)
        low, high = pl.ds(start, STEP), pl.ds(start + half, STEP)
        arrived = unpacked(
            *by_side(odd, inner[low, :].astype(F32), outer[low, :].astype(F32))
        )
        sides = []
        for rows, extra in zip((low, high), arrived):
            value = ((terms[rows, :] + extra) * slope[rows, :]).astype(BF16)
            grad[rows, :] = value
            sides.append(value.astype(F32))
        lower, upper = packed(*sides)
        to_inner[low, :] = jnp.where(odd, lower, upper).astype(BF16)
        to_outer[low, :] = jnp.where(odd, upper, lower).astype(BF16)
        return carry

    lax.fori_loop(0, half // STEP, step, 0)


def kernel_terms(columns, out_channels, slices, turned, terms):
    for row in range(3):
        for column in range(3):
            tap = row * 3 + column
            product = jnp.dot(turned[...], slices(row, column), preferred_element_type=F32)
            first, second = product[:out_channels], product[out_channels:]
            terms[:, tap * 128 : tap * 128 + 128] = first[:, :128] + swap(
                pick(second[:, 128:], second[:, :128])
            )
            group = 9 + tap // 2
            here = slice(group * 128, group * 128 + 128)
            if tap % 2 == 0:
                terms[:, here] = swap(first[:, 128:]) + second[:, :128]
            else:
                terms[:, here] = pick(terms[:, here], first[:, 128:] + swap(second[:, :128]))


def turn(source, target, first):
    for start in range(0, source.shape[0], STEP):
        chunk = source[start : start + STEP, :].astype(F32)
        target[first : first + chunk.shape[1], start : start + STEP] = chunk.T.astype(BF16)


def grad_two_body(columns, act_windows, turned, terms):
    cells = turned.shape[1]

    def slices(row, column):
        rows = slice(row * columns, row * columns + cells)
        return act_windows[rows, column * 256 : column * 256 + 256]

    kernel_terms(columns, 128, slices, turned, terms)


def coded(value, split):
    head = value[:split].astype(BF16)
    rest = (value[:split] - head.astype(F32)).astype(BF16)
    return jnp.concatenate([head, rest, value[split:].astype(BF16)], axis=0)


def decoded(value, split):
    value = value.astype(F32)
    return jnp.concatenate([value[:split] + value[split : 2 * split], value[2 * split :]], axis=0)


def grad_one_body(
    columns, count, me, own_windows, side_windows, grad, other, sent, kept, turned, terms
):
    cells = grad.shape[0]

    def slices(row, column):
        rows = slice(row * columns, row * columns + cells)
        return jnp.concatenate(
            [
                own_windows[rows, column * 128 : column * 128 + 128],
                side_windows[rows, column * 256 : column * 256 + 128],
            ],
            axis=1,
        )

    turn(grad, turned, 0)
    kernel_terms(columns, 64, slices, turned, terms)
    half = terms.shape[1] // 2
    odd = me[0] % 2 == 1

    def share(owner):
        parts = []
        for source in (terms, other):
            each = source.shape[0] // count
            block = source[owner * each : owner * each + each, :]
            parts += [block[:, :half], block[:, half:]]
        return jnp.concatenate(parts, axis=0)

    split = 2 * terms.shape[0] // count
    for pair in range(count // 2):
        even_share, odd_share = share(2 * pair), share(2 * pair + 1)
        sent[pair] = coded(jnp.where(odd, even_share, odd_share), split)
        kept[pair] = jnp.where(odd, odd_share, even_share)


def sum_body(split, me, mine, arrived, sent, kept):
    place = me[0] // 2
    for at in range(mine.shape[0]):
        sent[at] = coded(mine[at] + decoded(arrived[at], split), split)
    kept[...] = mine[place] + decoded(arrived[place], split)


def finish_body(scale, split, sizes, me, mine, arrived, grad_one, grad_two):
    total = mine[...]
    for at in range(arrived.shape[0]):
        total = total + jnp.where(at == me[0] // 2, 0.0, decoded(arrived[at], split))
    total = total * scale
    half = total.shape[1]
    first = 0
    for size, out in zip(sizes, (grad_one, grad_two)):
        blocks = (total[first : first + size], total[first + size : first + 2 * size])
        first += 2 * size
        for tap in range(9):
            for depth, group, side in ((0, 9 + tap // 2, tap % 2), (1, tap, 0), (2, tap, 1)):
                lane = group * 128 + side * 64
                block, lane = (blocks[0], lane) if lane < half else (blocks[1], lane - half)
                out[depth * 9 + tap] = block[:, lane : lane + 64]


def output_body(columns, act_windows, taps, output):
    for start in range(0, output.shape[1], BLOCK):
        value = window_dot(act_windows, taps, start, columns, NN)
        output[0, start : start + BLOCK, :] = value[:, :128]
        output[1, start : start + BLOCK, :] = value[:, 128:]


def grad_volume_body(columns, me, own, inner, outer, taps, output, windows):
    half = own.shape[0] // 2
    odd = me[0] % 2 == 1

    def fill(i, carry):
        start = pl.multiple_of(i * STEP, STEP)
        rows = pl.ds(start, STEP)
        below, above = by_side(odd, inner[rows, :].astype(F32), outer[rows, :].astype(F32))
        for first, side in zip((start, start + half), unpacked(above, below)):
            fill_windows(windows, first, 0, own[pl.ds(first, STEP), :].astype(F32), columns, 256)
            fill_windows(windows, first, 128, side, columns, 256)
        return carry

    clear_edges(windows, columns)
    lax.fori_loop(0, half // STEP, fill, 0)
    for start in range(0, 2 * half, BLOCK):
        value = window_dot(windows, taps, start, columns, NT)
        output[0, start : start + BLOCK, :] = value[:, :64]
        output[1, start : start + BLOCK, :] = value[:, 64:]


def shards(volume, weight_one, weight_two, cotangent):
    count = lax.axis_size("space")
    planes, rows, columns, channels = volume.shape
    cells = rows * columns
    scale = 1.0 / math.sqrt(planes * count * cells)
    mid, wide = weight_two.shape[3], weight_two.shape[4]
    me = lax.axis_index("space").astype(jnp.int32).reshape(1)
    shape = jax.ShapeDtypeStruct
    flat, pack = shape((cells, 128), BF16), shape((cells // 2, 128), BF16)
    slab = (cells + 2 * columns, 768)
    windows = pltpu.VMEM(slab, BF16)
    lanes = 14 * 64
    split = 2 * mid // count
    chunk = 2 * (mid + wide) // count

    within = [(i, i ^ 1) for i in range(count)]
    across = [(i, i + 1) for i in range(1, count - 1, 2)]
    across += [(j, i) for i, j in across]

    def exchange(inner, outer):
        outer = lax.ppermute(outer, "space", across)
        return lax.ppermute(inner, "space", within), outer

    def shares(*lead):
        return shape((*lead, chunk + split, lanes), BF16), shape((*lead, chunk, lanes), F32)

    volume = volume.reshape(planes, cells, channels)
    cotangent = cotangent.reshape(planes, cells, wide)
    weight_one = weight_one.reshape(27, channels, mid)
    weight_two = weight_two.reshape(27, mid, wide)
    one_flops = 2 * planes * cells * 27 * channels * mid
    two_flops = 2 * planes * cells * 27 * mid * wide

    dma = pltpu.SemaphoreType.DMA
    own, = call(
        pack_body, (flat,), (volume,),
        (pltpu.VMEM((planes, cells, channels), BF16), dma((4,))),
        name="pack_volume", apart=(0,),
    )
    vol_halo = exchange(own, own)
    terms, inner, outer = call(
        functools.partial(leave_body, columns),
        (shape((cells, 128), F32), pack, pack),
        (me, cotangent, weight_two),
        (
            windows, pltpu.VMEM((256, 3 * 768), BF16), pltpu.VMEM(cotangent.shape, BF16),
            pltpu.VMEM(weight_two.shape, BF16), dma((4,)), dma,
        ),
        two_flops, "grad_act_terms", (0,), (1, 2),
    )
    own_windows, part, side_taps, out_taps, back_taps, turned = call(
        functools.partial(prepare_body, columns),
        (
            shape((slab[0], 384), BF16), shape((cells, 256), F32), shape((9 * 256, 256), BF16),
            shape((9 * 256, 256), BF16), shape((128, 9 * 256), BF16), shape((256, cells), BF16),
        ),
        (own, weight_one, weight_two, cotangent),
        (pltpu.VMEM((9 * 128, 256), BF16),),
        one_flops, "prepare",
    )
    inner, outer, part = lax.optimization_barrier((inner, outer, part))
    act_terms_halo = exchange(inner, outer)
    side_windows, act_windows, slope = call(
        functools.partial(hidden_body, columns, count),
        (shape(slab, BF16), shape(slab, BF16), shape((cells, 128), F32)),
        (me, *vol_halo, part, side_taps),
        (), 2 * one_flops, "hidden", (0,),
    )
    grad_hidden, inner, outer = call(
        slope_body, (flat, pack, pack), (me, terms, *act_terms_halo, slope),
        name="grad_hidden", smem=(0,),
    )
    inner, outer, act_windows = lax.optimization_barrier((inner, outer, act_windows))
    grad_halo = exchange(inner, outer)
    terms_two, = call(
        functools.partial(grad_two_body, columns),
        (shape((wide, 2 * lanes), F32),),
        (act_windows, turned), (), two_flops, "grad_two_terms",
    )
    sent, kept = call(
        functools.partial(grad_one_body, columns, count),
        shares(count // 2),
        (me, own_windows, side_windows, grad_hidden, terms_two),
        (pltpu.VMEM((128, cells), BF16), pltpu.VMEM((mid, 2 * lanes), F32)),
        one_flops, "grad_one_terms", (0,),
    )
    sent, grad_halo = lax.optimization_barrier((sent, grad_halo))
    arrived = lax.ppermute(sent, "space", within)
    sent, mine = call(
        functools.partial(sum_body, split), (shares(count // 2)[0], shares()[1]),
        (me, kept, arrived), name="sum_pair", smem=(0,),
    )
    sent, act_windows, grad_hidden = lax.optimization_barrier((sent, act_windows, grad_hidden))
    arrived = lax.all_to_all(
        sent, "space", 0, 0, tiled=True,
        axis_index_groups=[list(range(core, count, 2)) for core in range(2)],
    )
    output, = call(
        functools.partial(output_body, columns),
        (shape((planes, cells, wide), F32),),
        (act_windows, out_taps), (), two_flops, "output",
    )
    grad_volume, = call(
        functools.partial(grad_volume_body, columns),
        (shape((planes, cells, channels), F32),),
        (me, grad_hidden, *grad_halo, back_taps),
        (windows,), one_flops, "grad_volume", (0,),
    )
    grad_one, grad_two = call(
        functools.partial(finish_body, scale, split, (mid // count, wide // count)),
        (shape((27, mid // count, channels), F32), shape((27, wide // count, mid), F32)),
        (me, mine, arrived), name="finish", smem=(0,),
    )
    return (
        output.reshape(planes, rows, columns, wide),
        grad_volume.reshape(planes, rows, columns, channels),
        jnp.swapaxes(grad_one, 1, 2).reshape(3, 3, 3, channels, mid // count),
        jnp.swapaxes(grad_two, 1, 2).reshape(3, 3, 3, mid, wide // count),
    )


def solution(mesh):
    cells = P(("groups", "space"), None, None, None)
    kernel = P("groups", None, None, None, "space")
    return jax.shard_map(
        shards,
        mesh=mesh,
        in_specs=(cells, P(), P(), cells),
        out_specs=(cells, cells, kernel, kernel),
        check_vma=False,
    )
```

time: 64.5 us -> 63.7 us (0.988)
  local copies, waits for them, and re-layouts: 3.47 us -> 9.69 us
  starting transfers between devices: 25.4 us -> 20 us
  Pallas kernels: 29.4 us -> 27.5 us
    ppermute x11 -> x7, starting transfers between devices: 25.4 us -> 14 us  [the longest x3 7.31 us: exchange(): return (lax.ppermute(inner, 'space', within), outer)]
    unnamed x12 -> x38, local copies, waits for them, and re-layouts: 3.47 us -> 9.69 us
    all_to_all x0 -> x1, starting transfers between devices: none -> 6.04 us  [shards(): lax.all_to_all(sent, 'space', 0, 0, tiled=True, axis_index_groups=[list(r...]
    all_to_all x0 -> x1, waiting for transfers between devices: none -> 3.66 us  [shards(): lax.all_to_all(sent, 'space', 0, 0, tiled=True, axis_index_groups=[list(r...]
    ppermute x11 -> x7, waiting for transfers between devices: 5.08 us -> 1.46 us  [the longest x1 1.44 us: shards(): arrived = lax.ppermute(sent, 'space', within)]
    pallas_call x11, Pallas kernels: 29.4 us -> 27.5 us  [call(): pl.pallas_call(body, out_shape=list(outs), in_specs=[pl.BlockSpec(memory_...]
  transfers between devices with their start and end apart: 11 -> 8, of which waited for: 1 -> 2; matrix products, arithmetic and copies ran while one was open for 0% -> 0% of each run, Pallas kernels for 37% -> 38%
where the time goes in v2:
time: 63.7 us; the launch traced here: 63.2 us
  Pallas kernels  27.5 us (43%)
  starting transfers between devices  20 us (31%)
  local copies, waits for them, and re-layouts  9.69 us (15%)
  waiting for transfers between devices  5.12 us (8%)
  between operations  0.86 us (1%)
    pallas_call x11, Pallas kernels, call(): pl.pallas_call(body, out_shape=list(outs), in_specs=[pl.BlockSpec(memory_...  27.5 us
    unnamed x38, local copies, waits for them, and re-layouts  9.69 us
    ppermute x3, starting transfers between devices, exchange(): return (lax.ppermute(inner, 'space', within), outer)  7.31 us
    all_to_all x1, starting transfers between devices, shards(): lax.all_to_all(sent, 'space', 0, 0, tiled=True, axis_index_groups=[list(r...  6.04 us
    ppermute x1, starting transfers between devices, shards(): arrived = lax.ppermute(sent, 'space', within)  4.65 us
    all_to_all x1, waiting for transfers between devices, shards(): lax.all_to_all(sent, 'space', 0, 0, tiled=True, axis_index_groups=[list(r...  3.66 us
    ppermute x3, starting transfers between devices, exchange(): outer = lax.ppermute(outer, 'space', across)  2.02 us
    ppermute x1, waiting for transfers between devices, shards(): arrived = lax.ppermute(sent, 'space', within)  1.44 us
  transfers between devices with their start and end apart: 8, of which 2 were waited for; matrix products, arithmetic and copies ran while one was open for 0% of the time, Pallas kernels for 38%

profile of v2, /device:TPU:0, one launch (start us, length us, event | category | flops | bytes accessed | tf_op | source)
XLA Modules:
  0.0 63.2 jit_solution(10445139222130399197)
XLA Ops:
  0.7 1.3 %copy-done.6 = bf16[2,64,32,64]{3,2,1,0:T(8,128)(2,1)S(1)} copy-done((bf16[2,64,32,64]{3,2,1,0:T(8,128)(2,1)S(1)}, bf16[2,64,32,64]{3,2,1,0:T(8,128)(2,1)}, u32[]{:S(2)}) %copy-start.6) | copy-done | bytes 524312
  2.0 0.5 pack_volume.1.own
  2.5 0.7 %collective-permute-start.1 = (bf16[2048,128]{1,0:T(8,128)(2,1)S(1)}, bf16[2048,128]{1,0:T(8,128)(2,1)S(1)}, u32[]{:S(2)}, u32[]{:S(2)}) collective-permute-start(bf16[2048,128]{1,0:T(8,128)(2,1)S(1)} %pack_volume.1.own), channel_id=1, source_target_pairs={{1,2},{3,4},{5,6},{7,8},{9,10},{11,12},{13,14},{2,1},{4,3},{6,5},{... | collective-permute-start | bytes 1572872 | tf_op jit(solution)/shard_map/ppermute | solution.py:416
  3.2 4.4 %collective-permute-start = (bf16[2048,128]{1,0:T(8,128)(2,1)S(1)}, bf16[2048,128]{1,0:T(8,128)(2,1)S(1)}, u32[]{:S(2)}, u32[]{:S(2)}) collective-permute-start(bf16[2048,128]{1,0:T(8,128)(2,1)S(1)} %pack_volume.1.own), channel_id=1, source_target_pairs={{0,1},{1,0},{2,3},{3,2},{4,5},{5,4},{6,7},{7,6},{8,9},{9,8},{10,11... | collective-permute-start | bytes 1572872 | tf_op jit(solution)/shard_map/ppermute | solution.py:417
  7.6 1.0 %copy-done.3 = bf16[3,3,3,64,128]{4,3,2,1,0:T(8,128)(2,1)S(1)} copy-done((bf16[3,3,3,64,128]{4,3,2,1,0:T(8,128)(2,1)S(1)}, bf16[3,3,3,64,128]{4,3,2,1,0:T(8,128)(2,1)}, u32[]{:S(2)}) %copy-start.3) | copy-done | bytes 442392
  8.6 3.9 %grad_act_terms.1 = (f32[2048,128]{1,0:T(8,128)S(1)}, bf16[1024,128]{1,0:T(8,128)(2,1)S(1)}, bf16[1024,128]{1,0:T(8,128)(2,1)S(1)}) custom-call(s32[1]{0:T(128)} %bitcast.me, bf16[2,2048,128]{2,1,0:T(8,128)(2,1)S(1)} %bitcast.13, bf16[27,64,128]{2,1,0:T(8,128)(2,1)S(1)} %bitcast.15), custom_call_target="tpu_custom_call" | custom-call | flops 1 | bytes 1 | tf_op jit(solution)/shard_map/grad_act_terms/pallas_call | solution.py:26
  12.5 2.9 %prepare.1 = (bf16[2112,384]{1,0:T(8,128)(2,1)S(1)}, f32[2048,256]{1,0:T(8,128)S(1)}, bf16[2304,256]{1,0:T(8,128)(2,1)S(1)}, bf16[2304,256]{1,0:T(8,128)(2,1)S(1...) custom-call(bf16[2048,128]{1,0:T(8,128)(2,1)S(1)} %pack_volume.1.own, bf16[27,64,64]{2,1,0:T(8,128)(2,1)S(1)} %bitcast.18, ...), custom_call_target="tpu_custom_call" | custom-call | flops 1 | bytes 1 | tf_op jit(solution)/shard_map/prepare/pallas_call | solution.py:26
  15.4 0.0 copy-start.4
  15.4 1.0 %copy-done.4 = bf16[2304,256]{1,0:T(8,128)(2,1)} copy-done((bf16[2304,256]{1,0:T(8,128)(2,1)}, bf16[2304,256]{1,0:T(8,128)(2,1)S(1)}, u32[]{:S(2)}) %copy-start.4) | copy-done | bytes 1179672
  16.4 0.0 collective-permute-start.2
  16.4 0.7 %collective-permute-start.3 = (bf16[1024,128]{1,0:T(8,128)(2,1)S(1)}, bf16[1024,128]{1,0:T(8,128)(2,1)S(1)}, u32[]{:S(2)}, u32[]{:S(2)}) collective-permute-start(bf16[1024,128]{1,0:T(8,128)(2,1)S(1)} %get-tuple-element.46), channel_id=1, source_target_pairs={{1,2},{3,4},{5,6},{7,8},{9,10},{11,12},{13,14},{2,1},{4,3},{6,5},{... | collective-permute-start | bytes 786440 | tf_op jit(solution)/shard_map/ppermute | solution.py:416
  17.1 0.8 %copy-done.9 = bf16[2048,128]{1,0:T(8,128)(2,1)} copy-done((bf16[2048,128]{1,0:T(8,128)(2,1)}, bf16[2048,128]{1,0:T(8,128)(2,1)S(1)}, u32[]{:S(2)}) %copy-start.9) | copy-done | bytes 524312
  17.9 0.8 %copy-done.11 = bf16[2048,128]{1,0:T(8,128)(2,1)} copy-done((bf16[2048,128]{1,0:T(8,128)(2,1)}, bf16[2048,128]{1,0:T(8,128)(2,1)S(1)}, u32[]{:S(2)}) %copy-start.11) | copy-done | bytes 524312
  18.7 1.0 %copy-done.10 = bf16[2048,128]{1,0:T(8,128)(2,1)S(1)} copy-done((bf16[2048,128]{1,0:T(8,128)(2,1)S(1)}, bf16[2048,128]{1,0:T(8,128)(2,1)}, u32[]{:S(2)}) %copy-start.10) | copy-done | bytes 524312
  19.8 1.0 %copy-done.12 = bf16[2048,128]{1,0:T(8,128)(2,1)S(1)} copy-done((bf16[2048,128]{1,0:T(8,128)(2,1)S(1)}, bf16[2048,128]{1,0:T(8,128)(2,1)}, u32[]{:S(2)}) %copy-start.12) | copy-done | bytes 524312
  20.8 4.3 %hidden.1 = (bf16[2112,768]{1,0:T(8,128)(2,1)S(1)}, bf16[2112,768]{1,0:T(8,128)(2,1)S(1)}, f32[2048,128]{1,0:T(8,128)S(1)}) custom-call(s32[1]{0:T(128)} %bitcast.me, bf16[2048,128]{1,0:T(8,128)(2,1)S(1)} %copy-done.12, bf16[2048,128]{1,0:T(8,128)(2,1)S(1)} %copy-done.10, f32[2048,256]{1,0:T(8,128)S(1)} %get-tuple-element.41.part, ...), custom_call_target="tpu_custom_call" | custom-call | flops 1 | bytes 1 | tf_op jit(solution)/shard_map/hidden/pallas_call | solution.py:26
  25.1 0.8 %grad_hidden.1 = (bf16[2048,128]{1,0:T(8,128)(2,1)S(1)}, bf16[1024,128]{1,0:T(8,128)(2,1)S(1)}, bf16[1024,128]{1,0:T(8,128)(2,1)S(1)}) custom-call(s32[1]{0:T(128)} %bitcast.me, f32[2048,128]{1,0:T(8,128)S(1)} %get-tuple-element.44.terms, bf16[1024,128]{1,0:T(8,128)(2,1)S(1)} %collective-permute-done.2.inner, ...), custom_call_target="tpu_custom_call" | custom-call | flops 1 | bytes 1 | tf_op jit(solution)/shard_map/grad_hidden/pallas_call | solution.py:26
  26.0 2.9 %collective-permute-start.4 = (bf16[1024,128]{1,0:T(8,128)(2,1)S(1)}, bf16[1024,128]{1,0:T(8,128)(2,1)S(1)}, u32[]{:S(2)}, u32[]{:S(2)}) collective-permute-start(bf16[1024,128]{1,0:T(8,128)(2,1)S(1)} %get-tuple-element.56), channel_id=1, source_target_pairs={{0,1},{1,0},{2,3},{3,2},{4,5},{5,4},{6,7},{7,6},{8,9},{9,8},{10,11... | collective-permute-start | bytes 786440 | tf_op jit(solution)/shard_map/ppermute | solution.py:417
  28.9 0.7 %collective-permute-start.5 = (bf16[1024,128]{1,0:T(8,128)(2,1)S(1)}, bf16[1024,128]{1,0:T(8,128)(2,1)S(1)}, u32[]{:S(2)}, u32[]{:S(2)}) collective-permute-start(bf16[1024,128]{1,0:T(8,128)(2,1)S(1)} %get-tuple-element.57), channel_id=1, source_target_pairs={{1,2},{3,4},{5,6},{7,8},{9,10},{11,12},{13,14},{2,1},{4,3},{6,5},{... | collective-permute-start | bytes 786440 | tf_op jit(solution)/shard_map/ppermute | solution.py:416
  29.6 2.7 %grad_two_terms.1.other = f32[128,1792]{1,0:T(8,128)S(1)} custom-call(bf16[2112,768]{1,0:T(8,128)(2,1)S(1)} %get-tuple-element.60.act_windows, bf16[256,2048]{1,0:T(8,128)(2,1)S(1)} %get-tuple-element.53.turned), custom_call_target="tpu_custom_call" | custom-call | flops 1 | bytes 1 | tf_op jit(solution)/shard_map/grad_two_terms/pallas_call | solution.py:26
  32.3 1.7 %grad_one_terms.1 = (bf16[8,32,896]{2,1,0:T(8,128)(2,1)S(1)}, f32[8,24,896]{2,1,0:T(8,128)S(1)}) custom-call(s32[1]{0:T(128)} %bitcast.me, bf16[2112,384]{1,0:T(8,128)(2,1)S(1)} %get-tuple-element.37.own_windows, bf16[2112,768]{1,0:T(8,128)(2,1)S(1)} %get-tuple-element.43.side_windows, bf16[2048,128]{1,0:T(8,128)(2,1)S(1)} %get-tuple-element.62.grad.own, ...), custom_call_target="tpu_custom_call" | custom-call | flops 1 | bytes 1 | tf_op jit(solution)/shard_map/grad_one_terms/pallas_call | solution.py:26
  34.0 4.7 %collective-permute-start.6 = (bf16[8,32,896]{2,1,0:T(8,128)(2,1)S(1)}, bf16[8,32,896]{2,1,0:T(8,128)(2,1)S(1)}, u32[]{:S(2)}, u32[]{:S(2)}) collective-permute-start(bf16[8,32,896]{2,1,0:T(8,128)(2,1)S(1)} %get-tuple-element.58), channel_id=1, source_target_pairs={{0,1},{1,0},{2,3},{3,2},{4,5},{5,4},{6,7},{7,6},{8,9},{9,8},{10,11... | collective-permute-start | bytes 1376264 | tf_op jit(solution)/shard_map/ppermute | solution.py:483
  38.6 1.4 %collective-permute-done.6.arrived = bf16[8,32,896]{2,1,0:T(8,128)(2,1)S(1)} collective-permute-done((bf16[8,32,896]{2,1,0:T(8,128)(2,1)S(1)}, bf16[8,32,896]{2,1,0:T(8,128)(2,1)S(1)}, u32[]{:S(2)}, u32[]{:S(2)}) %collective-permute-start.6) | collective-permute-done | bytes 458784 | tf_op jit(solution)/shard_map/ppermute | solution.py:483
  40.1 0.1 sum_pair.1
  40.2 0.8 %copy-done.13 = bf16[8,32,896]{2,1,0:T(8,128)(2,1)} copy-done((bf16[8,32,896]{2,1,0:T(8,128)(2,1)}, bf16[8,32,896]{2,1,0:T(8,128)(2,1)S(1)}, u32[]{:S(2)}) %copy-start.13) | copy-done | bytes 458776
  41.0 0.6 %copy-done.17 = f32[24,896]{1,0:T(8,128)} copy-done((f32[24,896]{1,0:T(8,128)}, f32[24,896]{1,0:T(8,128)S(1)}, u32[]{:S(2)}) %copy-start.17) | copy-done | bytes 86040
  41.6 6.0 %all-to-all-start = ((bf16[8,32,896]{2,1,0:T(8,128)(2,1)}), bf16[8,32,896]{2,1,0:T(8,128)(2,1)}, u32[]{:S(2)}, u32[]{:S(2)}) async-start(bf16[8,32,896]{2,1,0:T(8,128)(2,1)} %copy-done.13), calls=%async_computation | async-start | bytes 917504 | tf_op jit(solution)/shard_map/all_to_all | solution.py:489
  47.7 1.3 %copy-done.5 = bf16[2304,256]{1,0:T(8,128)(2,1)S(1)} copy-done((bf16[2304,256]{1,0:T(8,128)(2,1)S(1)}, bf16[2304,256]{1,0:T(8,128)(2,1)}, u32[]{:S(2)}) %copy-start.5) | copy-done | bytes 1179672
  49.0 3.9 %output.1 = f32[2,2048,128]{2,1,0:T(8,128)} custom-call(bf16[2112,768]{1,0:T(8,128)(2,1)S(1)} %get-tuple-element.60.act_windows, bf16[2304,256]{1,0:T(8,128)(2,1)S(1)} %copy-done.5), custom_call_target="tpu_custom_call" | custom-call | flops 1 | bytes 1 | tf_op jit(solution)/shard_map/output/pallas_call | solution.py:26
  52.9 4.8 %grad_volume.1 = f32[2,2048,64]{2,1,0:T(8,128)} custom-call(s32[1]{0:T(128)} %bitcast.me, bf16[2048,128]{1,0:T(8,128)(2,1)S(1)} %copy-done.2, bf16[1024,128]{1,0:T(8,128)(2,1)S(1)} %collective-permute-done.4.inner, bf16[1024,128]{1,0:T(8,128)(2,1)S(1)} %copy-done.16, bf16[128,2304]{1,0:T(8,128)(2,1)S(1)} %copy-done.8), custom_call_target="tpu_custom_call" | custom-call | flops 1 | bytes 1 | tf_op jit(solution)/shard_map/grad_volume/pallas_call | solution.py:26
  57.7 3.7 %all-to-all-done.arrived = bf16[8,32,896]{2,1,0:T(8,128)(2,1)} async-done(((bf16[8,32,896]{2,1,0:T(8,128)(2,1)}), bf16[8,32,896]{2,1,0:T(8,128)(2,1)}, u32[]{:S(2)}, u32[]{:S(2)}) %all-to-all-start) | async-done | bytes 458784 | tf_op jit(solution)/shard_map/all_to_all | solution.py:489
  61.4 1.8 %finish.1 = (f32[27,4,64]{2,1,0:T(4,128)}, f32[27,8,64]{2,1,0:T(8,128)}) custom-call(s32[1]{0:T(128)} %bitcast.me, f32[24,896]{1,0:T(8,128)S(1)} %copy-done.18, bf16[8,32,896]{2,1,0:T(8,128)(2,1)} %all-to-all-done.arrived), custom_call_target="tpu_custom_call" | custom-call | flops 1 | bytes 1 | tf_op jit(solution)/shard_map/finish/pallas_call | solution.py:26
  (33 shorter events, 0.1 us)
Async XLA Ops:
  0.6 6.9 %copy-start = (bf16[2,64,32,128]{3,2,1,0:T(8,128)(2,1)S(1)}, bf16[2,64,32,128]{3,2,1,0:T(8,128)(2,1)}, u32[]{:S(2)}) copy-start(bf16[2,64,32,128]{3,2,1,0:T(8,128)(2,1)} %param.7) | copy-start | bytes 3145732
  0.6 1.3 %copy-start.6 = (bf16[2,64,32,64]{3,2,1,0:T(8,128)(2,1)S(1)}, bf16[2,64,32,64]{3,2,1,0:T(8,128)(2,1)}, u32[]{:S(2)}) copy-start(bf16[2,64,32,64]{3,2,1,0:T(8,128)(2,1)} %param.4) | copy-start | bytes 1572868
  2.0 10.6 %copy-start.14 = (bf16[3,3,3,64,64]{4,3,2,1,0:T(8,128)(2,1)S(1)}, bf16[3,3,3,64,64]{4,3,2,1,0:T(8,128)(2,1)}, u32[]{:S(2)}) copy-start(bf16[3,3,3,64,64]{4,3,2,1,0:T(8,128)(2,1)} %param.5) | copy-start | bytes 663556
  2.5 14.6 %collective-permute-start.1 = (bf16[2048,128]{1,0:T(8,128)(2,1)S(1)}, bf16[2048,128]{1,0:T(8,128)(2,1)S(1)}, u32[]{:S(2)}, u32[]{:S(2)}) collective-permute-start(bf16[2048,128]{1,0:T(8,128)(2,1)S(1)} %pack_volume.1.own), channel_id=1, source_target_pairs={{1,2},{3,4},{5,6},{7,8},{9,10},{11,12},{13,14},{2,1},{4,3},{6,5},{... | collective-permute-start | bytes 1572872 | tf_op jit(solution)/shard_map/ppermute | solution.py:416
  3.2 14.7 %collective-permute-start = (bf16[2048,128]{1,0:T(8,128)(2,1)S(1)}, bf16[2048,128]{1,0:T(8,128)(2,1)S(1)}, u32[]{:S(2)}, u32[]{:S(2)}) collective-permute-start(bf16[2048,128]{1,0:T(8,128)(2,1)S(1)} %pack_volume.1.own), channel_id=1, source_target_pairs={{0,1},{1,0},{2,3},{3,2},{4,5},{5,4},{6,7},{7,6},{8,9},{9,8},{10,11... | collective-permute-start | bytes 1572872 | tf_op jit(solution)/shard_map/ppermute | solution.py:417
  7.6 1.0 %copy-start.3 = (bf16[3,3,3,64,128]{4,3,2,1,0:T(8,128)(2,1)S(1)}, bf16[3,3,3,64,128]{4,3,2,1,0:T(8,128)(2,1)}, u32[]{:S(2)}) copy-start(bf16[3,3,3,64,128]{4,3,2,1,0:T(8,128)(2,1)} %param.6) | copy-start | bytes 1327108
  15.4 1.0 %copy-start.4 = (bf16[2304,256]{1,0:T(8,128)(2,1)}, bf16[2304,256]{1,0:T(8,128)(2,1)S(1)}, u32[]{:S(2)}) copy-start(bf16[2304,256]{1,0:T(8,128)(2,1)S(1)} %get-tuple-element.61.taps) | copy-start | bytes 3538948
  16.4 8.7 %copy-start.7 = (bf16[128,2304]{1,0:T(8,128)(2,1)}, bf16[128,2304]{1,0:T(8,128)(2,1)S(1)}, u32[]{:S(2)}) copy-start(bf16[128,2304]{1,0:T(8,128)(2,1)S(1)} %get-tuple-element.65.taps) | copy-start | bytes 1769476
  16.4 8.7 %collective-permute-start.2 = (bf16[1024,128]{1,0:T(8,128)(2,1)S(1)}, bf16[1024,128]{1,0:T(8,128)(2,1)S(1)}, u32[]{:S(2)}, u32[]{:S(2)}) collective-permute-start(bf16[1024,128]{1,0:T(8,128)(2,1)S(1)} %get-tuple-element.45), channel_id=1, source_target_pairs={{0,1},{1,0},{2,3},{3,2},{4,5},{5,4},{6,7},{7,6},{8,9},{9,8},{10,11... | collective-permute-start | bytes 786440 | tf_op jit(solution)/shard_map/ppermute | solution.py:417
  16.4 8.7 %collective-permute-start.3 = (bf16[1024,128]{1,0:T(8,128)(2,1)S(1)}, bf16[1024,128]{1,0:T(8,128)(2,1)S(1)}, u32[]{:S(2)}, u32[]{:S(2)}) collective-permute-start(bf16[1024,128]{1,0:T(8,128)(2,1)S(1)} %get-tuple-element.46), channel_id=1, source_target_pairs={{1,2},{3,4},{5,6},{7,8},{9,10},{11,12},{13,14},{2,1},{4,3},{6,5},{... | collective-permute-start | bytes 786440 | tf_op jit(solution)/shard_map/ppermute | solution.py:416
  17.1 0.8 %copy-start.9 = (bf16[2048,128]{1,0:T(8,128)(2,1)}, bf16[2048,128]{1,0:T(8,128)(2,1)S(1)}, u32[]{:S(2)}) copy-start(bf16[2048,128]{1,0:T(8,128)(2,1)S(1)} %collective-permute-done.1.outer) | copy-start | bytes 1572868
  17.9 0.8 %copy-start.11 = (bf16[2048,128]{1,0:T(8,128)(2,1)}, bf16[2048,128]{1,0:T(8,128)(2,1)S(1)}, u32[]{:S(2)}) copy-start(bf16[2048,128]{1,0:T(8,128)(2,1)S(1)} %collective-permute-done.inner) | copy-start | bytes 1572868
  18.7 1.0 %copy-start.10 = (bf16[2048,128]{1,0:T(8,128)(2,1)S(1)}, bf16[2048,128]{1,0:T(8,128)(2,1)}, u32[]{:S(2)}) copy-start(bf16[2048,128]{1,0:T(8,128)(2,1)} %copy-done.9) | copy-start | bytes 1572868
  19.8 1.0 %copy-start.12 = (bf16[2048,128]{1,0:T(8,128)(2,1)S(1)}, bf16[2048,128]{1,0:T(8,128)(2,1)}, u32[]{:S(2)}) copy-start(bf16[2048,128]{1,0:T(8,128)(2,1)} %copy-done.11) | copy-start | bytes 1572868
  26.0 6.3 %copy-start.1 = (bf16[2048,128]{1,0:T(8,128)(2,1)}, bf16[2048,128]{1,0:T(8,128)(2,1)S(1)}, u32[]{:S(2)}) copy-start(bf16[2048,128]{1,0:T(8,128)(2,1)S(1)} %get-tuple-element.62.grad.own) | copy-start | bytes 1572868
  26.0 8.0 %collective-permute-start.4 = (bf16[1024,128]{1,0:T(8,128)(2,1)S(1)}, bf16[1024,128]{1,0:T(8,128)(2,1)S(1)}, u32[]{:S(2)}, u32[]{:S(2)}) collective-permute-start(bf16[1024,128]{1,0:T(8,128)(2,1)S(1)} %get-tuple-element.56), channel_id=1, source_target_pairs={{0,1},{1,0},{2,3},{3,2},{4,5},{5,4},{6,7},{7,6},{8,9},{9,8},{10,11... | collective-permute-start | bytes 786440 | tf_op jit(solution)/shard_map/ppermute | solution.py:417
  28.9 5.1 %collective-permute-start.5 = (bf16[1024,128]{1,0:T(8,128)(2,1)S(1)}, bf16[1024,128]{1,0:T(8,128)(2,1)S(1)}, u32[]{:S(2)}, u32[]{:S(2)}) collective-permute-start(bf16[1024,128]{1,0:T(8,128)(2,1)S(1)} %get-tuple-element.57), channel_id=1, source_target_pairs={{1,2},{3,4},{5,6},{7,8},{9,10},{11,12},{13,14},{2,1},{4,3},{6,5},{... | collective-permute-start | bytes 786440 | tf_op jit(solution)/shard_map/ppermute | solution.py:416
  34.0 6.3 %copy-start.15 = (bf16[1024,128]{1,0:T(8,128)(2,1)}, bf16[1024,128]{1,0:T(8,128)(2,1)S(1)}, u32[]{:S(2)}) copy-start(bf16[1024,128]{1,0:T(8,128)(2,1)S(1)} %collective-permute-done.5.outer) | copy-start | bytes 786436
  34.0 6.1 %collective-permute-start.6 = (bf16[8,32,896]{2,1,0:T(8,128)(2,1)S(1)}, bf16[8,32,896]{2,1,0:T(8,128)(2,1)S(1)}, u32[]{:S(2)}, u32[]{:S(2)}) collective-permute-start(bf16[8,32,896]{2,1,0:T(8,128)(2,1)S(1)} %get-tuple-element.58), channel_id=1, source_target_pairs={{0,1},{1,0},{2,3},{3,2},{4,5},{5,4},{6,7},{7,6},{8,9},{9,8},{10,11... | collective-permute-start | bytes 1376264 | tf_op jit(solution)/shard_map/ppermute | solution.py:483
  40.2 0.8 %copy-start.13 = (bf16[8,32,896]{2,1,0:T(8,128)(2,1)}, bf16[8,32,896]{2,1,0:T(8,128)(2,1)S(1)}, u32[]{:S(2)}) copy-start(bf16[8,32,896]{2,1,0:T(8,128)(2,1)S(1)} %get-tuple-element.67) | copy-start | bytes 1376260
  41.0 0.6 %copy-start.17 = (f32[24,896]{1,0:T(8,128)}, f32[24,896]{1,0:T(8,128)S(1)}, u32[]{:S(2)}) copy-start(f32[24,896]{1,0:T(8,128)S(1)} %get-tuple-element.66.mine) | copy-start | bytes 258052
  41.6 19.7 %all-to-all-start = ((bf16[8,32,896]{2,1,0:T(8,128)(2,1)}), bf16[8,32,896]{2,1,0:T(8,128)(2,1)}, u32[]{:S(2)}, u32[]{:S(2)}) async-start(bf16[8,32,896]{2,1,0:T(8,128)(2,1)} %copy-done.13), calls=%async_computation | async-start | bytes 917504 | tf_op jit(solution)/shard_map/all_to_all | solution.py:489
  47.7 1.3 %copy-start.5 = (bf16[2304,256]{1,0:T(8,128)(2,1)S(1)}, bf16[2304,256]{1,0:T(8,128)(2,1)}, u32[]{:S(2)}) copy-start(bf16[2304,256]{1,0:T(8,128)(2,1)} %copy-done.4) | copy-start | bytes 3538948
  48.9 3.9 %copy-start.2 = (bf16[2048,128]{1,0:T(8,128)(2,1)S(1)}, bf16[2048,128]{1,0:T(8,128)(2,1)}, u32[]{:S(2)}) copy-start(bf16[2048,128]{1,0:T(8,128)(2,1)} %copy-done.1) | copy-start | bytes 1572868
  49.0 3.9 %copy-start.8 = (bf16[128,2304]{1,0:T(8,128)(2,1)S(1)}, bf16[128,2304]{1,0:T(8,128)(2,1)}, u32[]{:S(2)}) copy-start(bf16[128,2304]{1,0:T(8,128)(2,1)} %copy-done.7) | copy-start | bytes 1769476
  49.0 3.9 %copy-start.16 = (bf16[1024,128]{1,0:T(8,128)(2,1)S(1)}, bf16[1024,128]{1,0:T(8,128)(2,1)}, u32[]{:S(2)}) copy-start(bf16[1024,128]{1,0:T(8,128)(2,1)} %copy-done.15) | copy-start | bytes 786436
  52.9 8.5 %copy-start.18 = (f32[24,896]{1,0:T(8,128)S(1)}, f32[24,896]{1,0:T(8,128)}, u32[]{:S(2)}) copy-start(f32[24,896]{1,0:T(8,128)} %copy-done.17) | copy-start | bytes 258052

commit v3 on v2

--- a/solution.py
+++ b/solution.py
@@ -10,7 +10,7 @@
 
 F32, BF16 = jnp.float32, jnp.bfloat16
 STEP, BLOCK = 256, 512
-VMEM_LIMIT = 24 * 2**20
+VMEM_LIMIT = 16 * 2**20
 NN = (((1,), (0,)), ((), ()))
 NT = (((1,), (1,)), ((), ()))
 
@@ -23,6 +23,7 @@
 
 
 def call(body, outs, ins, scratch=(), flops=0, name=None, smem=(), apart=()):
+    moved = sum(math.prod(s.shape) * s.dtype.itemsize for s in (*outs, *ins))
     return pl.pallas_call(
         body,
         out_shape=list(outs),
@@ -35,7 +36,7 @@
         out_specs=[pl.BlockSpec(memory_space=pltpu.VMEM)] * len(outs),
         scratch_shapes=list(scratch),
         compiler_params=pltpu.CompilerParams(vmem_limit_bytes=VMEM_LIMIT),
-        cost_estimate=pl.CostEstimate(flops=1, bytes_accessed=1, transcendentals=0),
+        cost_estimate=pl.CostEstimate(flops=flops, bytes_accessed=moved, transcendentals=0),
         name=name,
     )(*ins)
 
@@ -114,16 +115,22 @@
 
 
 def leave_body(
-    columns, me, cotangent, weight, own, inner, outer, windows, taps, held, kernel, sems, sem
+    columns, me, cotangent, weight_far, own, inner, outer, windows, taps, weight, sem
 ):
-    half = held.shape[1] // 2
+    half = cotangent.shape[1] // 2
     odd = me[0] % 2 == 1
-    fetch = pltpu.make_async_copy(weight, kernel, sem)
+    fetch = pltpu.make_async_copy(weight_far, weight, sem)
     fetch.start()
-    copies = pieces_of(cotangent, held, sems, sems.shape[0])
-    for copy in copies:
-        copy.start()
     clear_edges(windows, columns)
+
+    def fill(i, carry):
+        start = pl.multiple_of(i * STEP, STEP)
+        for plane in range(2):
+            chunk = cotangent[plane, pl.ds(start, STEP), :].astype(F32)
+            fill_windows(windows, start, plane * 128, chunk, columns, 256)
+        return carry
+
+    lax.fori_loop(0, 2 * half // STEP, fill, 0)
     fetch.wait()
     for row in range(3):
         for column in range(3):
@@ -134,20 +141,8 @@
                     taps[at * 64 : at * 64 + 64, first : first + 128] = (
                         jnp.zeros((64, 128), BF16)
                         if depth is None
-                        else kernel[(2 - depth) * 9 + (2 - row) * 3 + 2 - column]
+                        else weight[(2 - depth) * 9 + (2 - row) * 3 + 2 - column]
                     )
-    size = 2 * half // len(copies)
-    for i, copy in enumerate(copies):
-        copy.wait()
-
-        def fill(j, carry):
-            start = pl.multiple_of(i * size + j * STEP, STEP)
-            for plane in range(2):
-                chunk = held[plane, pl.ds(start, STEP), :].astype(F32)
-                fill_windows(windows, start, plane * 128, chunk, columns, 256)
-            return carry
-
-        lax.fori_loop(0, size // STEP, fill, 0)
     for start in range(0, half, BLOCK):
         sides = []
         for first in (start, start + half):
@@ -160,11 +155,29 @@
 
 
 def prepare_body(
-    columns, own, weight_one, weight_two, cotangent,
+    columns, own, far_one, far_two, cotangent,
     own_windows, hidden, side_taps, out_taps, back_taps, turned, own_taps,
+    weight_one, weight_two, sems,
 ):
+    fetches = [
+        pltpu.make_async_copy(far_one, weight_one, sems.at[0]),
+        pltpu.make_async_copy(far_two, weight_two, sems.at[1]),
+    ]
+    for fetch in fetches:
+        fetch.start()
+
+    def fill(i, carry):
+        start = pl.multiple_of(i * STEP, STEP)
+        chunk = own[pl.ds(start, STEP), :].astype(F32)
+        fill_windows(own_windows, start, 0, chunk, columns, 128)
+        return carry
+
+    clear_edges(own_windows, columns)
+    lax.fori_loop(0, own.shape[0] // STEP, fill, 0)
     turn(cotangent.at[0], turned, 0)
     turn(cotangent.at[1], turned, 128)
+    for fetch in fetches:
+        fetch.wait()
     zero, wide_zero = jnp.zeros((64, 64), BF16), jnp.zeros((64, 128), BF16)
     for row in range(3):
         for column in range(3):
@@ -196,14 +209,6 @@
                         jnp.concatenate(parts[2 * pair : 2 * pair + 2], axis=1)
                     )
 
-    def fill(i, carry):
-        start = pl.multiple_of(i * STEP, STEP)
-        chunk = own[pl.ds(start, STEP), :].astype(F32)
-        fill_windows(own_windows, start, 0, chunk, columns, 128)
-        return carry
-
-    clear_edges(own_windows, columns)
-    lax.fori_loop(0, own.shape[0] // STEP, fill, 0)
     for start in range(0, own.shape[0], BLOCK):
         hidden[start : start + BLOCK, :] = window_dot(own_windows, own_taps, start, columns, NN)
 
@@ -427,8 +432,11 @@
     two_flops = 2 * planes * cells * 27 * mid * wide
 
     dma = pltpu.SemaphoreType.DMA
+    far_one, far_two, far_volume = (
+        pltpu.with_memory_space_constraint(x, pltpu.HBM) for x in (weight_one, weight_two, volume)
+    )
     own, = call(
-        pack_body, (flat,), (volume,),
+        pack_body, (flat,), (far_volume,),
         (pltpu.VMEM((planes, cells, channels), BF16), dma((4,))),
         name="pack_volume", apart=(0,),
     )
@@ -436,22 +444,23 @@
     terms, inner, outer = call(
         functools.partial(leave_body, columns),
         (shape((cells, 128), F32), pack, pack),
-        (me, cotangent, weight_two),
-        (
-            windows, pltpu.VMEM((256, 3 * 768), BF16), pltpu.VMEM(cotangent.shape, BF16),
-            pltpu.VMEM(weight_two.shape, BF16), dma((4,)), dma,
-        ),
-        two_flops, "grad_act_terms", (0,), (1, 2),
-    )
+        (me, cotangent, far_two),
+        (windows, pltpu.VMEM((256, 3 * 768), BF16), pltpu.VMEM(weight_two.shape, BF16), dma),
+        two_flops, "grad_act_terms", (0,), (2,),
+    )
+    own, terms = lax.optimization_barrier((own, terms))
     own_windows, part, side_taps, out_taps, back_taps, turned = call(
         functools.partial(prepare_body, columns),
         (
             shape((slab[0], 384), BF16), shape((cells, 256), F32), shape((9 * 256, 256), BF16),
             shape((9 * 256, 256), BF16), shape((128, 9 * 256), BF16), shape((256, cells), BF16),
         ),
-        (own, weight_one, weight_two, cotangent),
-        (pltpu.VMEM((9 * 128, 256), BF16),),
-        one_flops, "prepare",
+        (own, far_one, far_two, cotangent),
+        (
+            pltpu.VMEM((9 * 128, 256), BF16), pltpu.VMEM(weight_one.shape, BF16),
+            pltpu.VMEM(weight_two.shape, BF16), dma((2,)),
+        ),
+        one_flops, "prepare", (), (1, 2),
     )
     inner, outer, part = lax.optimization_barrier((inner, outer, part))
     act_terms_halo = exchange(inner, outer)

time: 63.7 us -> 60.8 us (0.954)
  local copies, waits for them, and re-layouts: 9.69 us -> 2.24 us
  starting transfers between devices: 20 us -> 22.8 us
  waiting for transfers between devices: 5.12 us -> 6.3 us
  Pallas kernels: 27.5 us -> 28.3 us
    unnamed x38 -> x10, local copies, waits for them, and re-layouts: 9.69 us -> 2.24 us
    ppermute x3, starting transfers between devices: 7.31 us -> 9.05 us  [exchange(): return (lax.ppermute(inner, 'space', within), outer)]
    all_to_all x1, waiting for transfers between devices: 3.66 us -> 4.84 us  [shards(): lax.all_to_all(sent, 'space', 0, 0, tiled=True, axis_index_groups=[list(r...]
    pallas_call x11, Pallas kernels: 27.5 us -> 28.3 us  [call(): pl.pallas_call(body, out_shape=list(outs), in_specs=[pl.BlockSpec(memory_...]
    ppermute x1, starting transfers between devices: 4.65 us -> 5.38 us  [shards(): arrived = lax.ppermute(sent, 'space', within)]
  transfers between devices with their start and end apart: 8 -> 8, of which waited for: 2 -> 2; matrix products, arithmetic and copies ran while one was open for 0% -> 0% of each run, Pallas kernels for 38% -> 40%
where the time goes in v3:
time: 60.8 us; the launch traced here: 60.4 us
  Pallas kernels  28.3 us (47%)
  starting transfers between devices  22.8 us (38%)
  waiting for transfers between devices  6.3 us (10%)
  local copies, waits for them, and re-layouts  2.24 us (4%)
  between operations  0.79 us (1%)
    pallas_call x11, Pallas kernels, call(): pl.pallas_call(body, out_shape=list(outs), in_specs=[pl.BlockSpec(memory_...  28.3 us
    ppermute x3, starting transfers between devices, exchange(): return (lax.ppermute(inner, 'space', within), outer)  9.05 us
    all_to_all x1, starting transfers between devices, shards(): lax.all_to_all(sent, 'space', 0, 0, tiled=True, axis_index_groups=[list(r...  6.35 us
    ppermute x1, starting transfers between devices, shards(): arrived = lax.ppermute(sent, 'space', within)  5.38 us
    all_to_all x1, waiting for transfers between devices, shards(): lax.all_to_all(sent, 'space', 0, 0, tiled=True, axis_index_groups=[list(r...  4.84 us
    unnamed x10, local copies, waits for them, and re-layouts  2.24 us
    ppermute x3, starting transfers between devices, exchange(): outer = lax.ppermute(outer, 'space', across)  2.02 us
    ppermute x1, waiting for transfers between devices, shards(): arrived = lax.ppermute(sent, 'space', within)  1.44 us
  transfers between devices with their start and end apart: 8, of which 2 were waited for; matrix products, arithmetic and copies ran while one was open for 0% of the time, Pallas kernels for 40%

profile of v3, /device:TPU:0, one launch (start us, length us, event | category | flops | bytes accessed | tf_op | source)
XLA Modules:
  0.0 60.4 jit_solution(8286499109709345677)
XLA Ops:
  0.6 1.4 %pack_volume.1.own = bf16[2048,128]{1,0:T(8,128)(2,1)S(1)} custom-call(bf16[2,2048,64]{2,1,0:T(8,128)(2,1)} %bitcast.16), custom_call_target="tpu_custom_call" | custom-call | bytes 1048576 | tf_op jit(solution)/shard_map/pack_volume/pallas_call | solution.py:27
  2.0 0.7 %collective-permute-start.1 = (bf16[2048,128]{1,0:T(8,128)(2,1)S(1)}, bf16[2048,128]{1,0:T(8,128)(2,1)S(1)}, u32[]{:S(2)}, u32[]{:S(2)}) collective-permute-start(bf16[2048,128]{1,0:T(8,128)(2,1)S(1)} %pack_volume.1.own), channel_id=1, source_target_pairs={{1,2},{3,4},{5,6},{7,8},{9,10},{11,12},{13,14},{2,1},{4,3},{6,5},{... | collective-permute-start | bytes 1572872 | tf_op jit(solution)/shard_map/ppermute | solution.py:421
  2.7 4.4 %collective-permute-start = (bf16[2048,128]{1,0:T(8,128)(2,1)S(1)}, bf16[2048,128]{1,0:T(8,128)(2,1)S(1)}, u32[]{:S(2)}, u32[]{:S(2)}) collective-permute-start(bf16[2048,128]{1,0:T(8,128)(2,1)S(1)} %pack_volume.1.own), channel_id=1, source_target_pairs={{0,1},{1,0},{2,3},{3,2},{4,5},{5,4},{6,7},{7,6},{8,9},{9,8},{10,11... | collective-permute-start | bytes 1572872 | tf_op jit(solution)/shard_map/ppermute | solution.py:422
  7.1 1.2 %copy-done = bf16[2,64,32,128]{3,2,1,0:T(8,128)(2,1)S(1)} copy-done((bf16[2,64,32,128]{3,2,1,0:T(8,128)(2,1)S(1)}, bf16[2,64,32,128]{3,2,1,0:T(8,128)(2,1)}, u32[]{:S(2)}) %copy-start) | copy-done | bytes 1048600
  8.3 3.8 %grad_act_terms.1 = (f32[2048,128]{1,0:T(8,128)S(1)}, bf16[1024,128]{1,0:T(8,128)(2,1)S(1)}, bf16[1024,128]{1,0:T(8,128)(2,1)S(1)}) custom-call(s32[1]{0:T(128)} %bitcast.me, bf16[2,2048,128]{2,1,0:T(8,128)(2,1)S(1)} %bitcast.13, bf16[27,64,128]{2,1,0:T(8,128)(2,1)} %bitcast.18), custom_call_target="tpu_custom_call" | custom-call | flops 1811939328 | bytes 3063812 | tf_op jit(solution)/shard_map/grad_act_terms/pallas_call | solution.py:27
  12.1 3.1 %prepare.1 = (bf16[2112,384]{1,0:T(8,128)(2,1)S(1)}, f32[2048,256]{1,0:T(8,128)S(1)}, bf16[2304,256]{1,0:T(8,128)(2,1)S(1)}, bf16[2304,256]{1,0:T(8,128)(2,1)S(1...) custom-call(bf16[2048,128]{1,0:T(8,128)(2,1)S(1)} %pack_volume.1.own, bf16[27,64,64]{2,1,0:T(8,128)(2,1)} %bitcast.17, ...), custom_call_target="tpu_custom_call" | custom-call | flops 905969664 | bytes 9953280 | tf_op jit(solution)/shard_map/prepare/pallas_call | solution.py:27
  15.2 0.0 copy-start.3
  15.2 1.0 %copy-done.3 = bf16[2304,256]{1,0:T(8,128)(2,1)} copy-done((bf16[2304,256]{1,0:T(8,128)(2,1)}, bf16[2304,256]{1,0:T(8,128)(2,1)S(1)}, u32[]{:S(2)}) %copy-start.3) | copy-done | bytes 1179672
  16.2 0.0 collective-permute-start.2
  16.2 0.7 %collective-permute-start.3 = (bf16[1024,128]{1,0:T(8,128)(2,1)S(1)}, bf16[1024,128]{1,0:T(8,128)(2,1)S(1)}, u32[]{:S(2)}, u32[]{:S(2)}) collective-permute-start(bf16[1024,128]{1,0:T(8,128)(2,1)S(1)} %get-tuple-element.50), channel_id=1, source_target_pairs={{1,2},{3,4},{5,6},{7,8},{9,10},{11,12},{13,14},{2,1},{4,3},{6,5},{... | collective-permute-start | bytes 786440 | tf_op jit(solution)/shard_map/ppermute | solution.py:421
  16.9 0.0 collective-permute-done.1.outer
  16.9 0.0 collective-permute-done.inner
  16.9 4.3 %hidden.1 = (bf16[2112,768]{1,0:T(8,128)(2,1)S(1)}, bf16[2112,768]{1,0:T(8,128)(2,1)S(1)}, f32[2048,128]{1,0:T(8,128)S(1)}) custom-call(s32[1]{0:T(128)} %bitcast.me, bf16[2048,128]{1,0:T(8,128)(2,1)S(1)} %collective-permute-done.inner, bf16[2048,128]{1,0:T(8,128)(2,1)S(1)} %collective-permute-done.1.outer, f32[2048,256]{1,0:T(8,128)S(1)} %get-tuple-element.45.part, ...), custom_call_target="tpu_custom_call" | custom-call | flops 1811939328 | bytes 11862020 | tf_op jit(solution)/shard_map/hidden/pallas_call | solution.py:27
  21.2 0.0 copy-start.1
  21.2 0.0 collective-permute-done.2.inner
  21.3 0.0 collective-permute-done.3.outer
  21.3 0.9 %grad_hidden.1 = (bf16[2048,128]{1,0:T(8,128)(2,1)S(1)}, bf16[1024,128]{1,0:T(8,128)(2,1)S(1)}, bf16[1024,128]{1,0:T(8,128)(2,1)S(1)}) custom-call(s32[1]{0:T(128)} %bitcast.me, f32[2048,128]{1,0:T(8,128)S(1)} %get-tuple-element.48.terms, bf16[1024,128]{1,0:T(8,128)(2,1)S(1)} %collective-permute-done.2.inner, ...), custom_call_target="tpu_custom_call" | custom-call | bytes 3670020 | tf_op jit(solution)/shard_map/grad_hidden/pallas_call | solution.py:27
  22.1 4.7 %collective-permute-start.4 = (bf16[1024,128]{1,0:T(8,128)(2,1)S(1)}, bf16[1024,128]{1,0:T(8,128)(2,1)S(1)}, u32[]{:S(2)}, u32[]{:S(2)}) collective-permute-start(bf16[1024,128]{1,0:T(8,128)(2,1)S(1)} %get-tuple-element.60), channel_id=1, source_target_pairs={{0,1},{1,0},{2,3},{3,2},{4,5},{5,4},{6,7},{7,6},{8,9},{9,8},{10,11... | collective-permute-start | bytes 786440 | tf_op jit(solution)/shard_map/ppermute | solution.py:422
  26.8 0.7 %collective-permute-start.5 = (bf16[1024,128]{1,0:T(8,128)(2,1)S(1)}, bf16[1024,128]{1,0:T(8,128)(2,1)S(1)}, u32[]{:S(2)}, u32[]{:S(2)}) collective-permute-start(bf16[1024,128]{1,0:T(8,128)(2,1)S(1)} %get-tuple-element.61), channel_id=1, source_target_pairs={{1,2},{3,4},{5,6},{7,8},{9,10},{11,12},{13,14},{2,1},{4,3},{6,5},{... | collective-permute-start | bytes 786440 | tf_op jit(solution)/shard_map/ppermute | solution.py:421
  27.5 2.7 %grad_two_terms.1.other = f32[128,1792]{1,0:T(8,128)S(1)} custom-call(bf16[2112,768]{1,0:T(8,128)(2,1)S(1)} %get-tuple-element.64.act_windows, bf16[256,2048]{1,0:T(8,128)(2,1)S(1)} %get-tuple-element.57.turned), custom_call_target="tpu_custom_call" | custom-call | flops 1811939328 | bytes 5210112 | tf_op jit(solution)/shard_map/grad_two_terms/pallas_call | solution.py:27
  30.2 0.0 copy-done.1
  30.2 1.7 %grad_one_terms.1 = (bf16[8,32,896]{2,1,0:T(8,128)(2,1)S(1)}, f32[8,24,896]{2,1,0:T(8,128)S(1)}) custom-call(s32[1]{0:T(128)} %bitcast.me, bf16[2112,384]{1,0:T(8,128)(2,1)S(1)} %get-tuple-element.41.own_windows, bf16[2112,768]{1,0:T(8,128)(2,1)S(1)} %get-tuple-element.47.side_windows, bf16[2048,128]{1,0:T(8,128)(2,1)S(1)} %get-tuple-element.66.grad.own, ...), custom_call_target="tpu_custom_call" | custom-call | flops 905969664 | bytes 7454724 | tf_op jit(solution)/shard_map/grad_one_terms/pallas_call | solution.py:27
  31.9 0.0 collective-permute-done.4.inner
  31.9 0.0 collective-permute-done.5.outer
  31.9 5.4 %collective-permute-start.6 = (bf16[8,32,896]{2,1,0:T(8,128)(2,1)S(1)}, bf16[8,32,896]{2,1,0:T(8,128)(2,1)S(1)}, u32[]{:S(2)}, u32[]{:S(2)}) collective-permute-start(bf16[8,32,896]{2,1,0:T(8,128)(2,1)S(1)} %get-tuple-element.62), channel_id=1, source_target_pairs={{0,1},{1,0},{2,3},{3,2},{4,5},{5,4},{6,7},{7,6},{8,9},{9,8},{10,11... | collective-permute-start | bytes 1376264 | tf_op jit(solution)/shard_map/ppermute | solution.py:492
  37.3 1.4 %collective-permute-done.6.arrived = bf16[8,32,896]{2,1,0:T(8,128)(2,1)S(1)} collective-permute-done((bf16[8,32,896]{2,1,0:T(8,128)(2,1)S(1)}, bf16[8,32,896]{2,1,0:T(8,128)(2,1)S(1)}, u32[]{:S(2)}, u32[]{:S(2)}) %collective-permute-start.6) | collective-permute-done | bytes 458784 | tf_op jit(solution)/shard_map/ppermute | solution.py:492
  38.8 0.9 %sum_pair.1 = (bf16[8,32,896]{2,1,0:T(8,128)(2,1)}, f32[24,896]{1,0:T(8,128)S(1)}) custom-call(s32[1]{0:T(128)} %bitcast.me, f32[8,24,896]{2,1,0:T(8,128)S(1)} %get-tuple-element.58.mine, bf16[8,32,896]{2,1,0:T(8,128)(2,1)S(1)} %collective-permute-done.6.arrived), custom_call_target="tpu_custom_call" | custom-call | bytes 1691652 | tf_op jit(solution)/shard_map/sum_pair/pallas_call | solution.py:27
  39.7 6.4 %all-to-all-start = ((bf16[8,32,896]{2,1,0:T(8,128)(2,1)}), bf16[8,32,896]{2,1,0:T(8,128)(2,1)S(1)}, u32[]{:S(2)}, u32[]{:S(2)}) async-start(bf16[8,32,896]{2,1,0:T(8,128)(2,1)} %get-tuple-element.71), calls=%async_computation | async-start | bytes 917504 | tf_op jit(solution)/shard_map/all_to_all | solution.py:498
  46.0 4.8 %grad_volume.1 = f32[2,2048,64]{2,1,0:T(8,128)} custom-call(s32[1]{0:T(128)} %bitcast.me, bf16[2048,128]{1,0:T(8,128)(2,1)S(1)} %get-tuple-element.66.grad.own, bf16[1024,128]{1,0:T(8,128)(2,1)S(1)} %collective-permute-done.4.inner, bf16[1024,128]{1,0:T(8,128)(2,1)S(1)} %collective-permute-done.5.outer, bf16[128,2304]{1,0:T(8,128)(2,1)S(1)} %get-tuple-element.69.taps), custom_call_target="tpu_custom_call" | custom-call | flops 905969664 | bytes 2686980 | tf_op jit(solution)/shard_map/grad_volume/pallas_call | solution.py:27
  50.9 3.9 %output.1 = f32[2,2048,128]{2,1,0:T(8,128)} custom-call(bf16[2112,768]{1,0:T(8,128)(2,1)S(1)} %copy-done.2, bf16[2304,256]{1,0:T(8,128)(2,1)S(1)} %copy-done.4), custom_call_target="tpu_custom_call" | custom-call | flops 1811939328 | bytes 6520832 | tf_op jit(solution)/shard_map/output/pallas_call | solution.py:27
  54.8 4.8 %all-to-all-done.arrived = bf16[8,32,896]{2,1,0:T(8,128)(2,1)S(1)} async-done(((bf16[8,32,896]{2,1,0:T(8,128)(2,1)}), bf16[8,32,896]{2,1,0:T(8,128)(2,1)S(1)}, u32[]{:S(2)}, u32[]{:S(2)}) %all-to-all-start) | async-done | bytes 458784 | tf_op jit(solution)/shard_map/all_to_all | solution.py:498
  59.6 0.8 %finish.1 = (f32[27,4,64]{2,1,0:T(4,128)}, f32[27,8,64]{2,1,0:T(8,128)}) custom-call(s32[1]{0:T(128)} %bitcast.me, f32[24,896]{1,0:T(8,128)S(1)} %get-tuple-element.70.mine, bf16[8,32,896]{2,1,0:T(8,128)(2,1)S(1)} %all-to-all-done.arrived), custom_call_target="tpu_custom_call" | custom-call | bytes 627716 | tf_op jit(solution)/shard_map/finish/pallas_call | solution.py:27
  (5 shorter events, 0.0 us)
Async XLA Ops:
  2.0 14.9 %collective-permute-start.1 = (bf16[2048,128]{1,0:T(8,128)(2,1)S(1)}, bf16[2048,128]{1,0:T(8,128)(2,1)S(1)}, u32[]{:S(2)}, u32[]{:S(2)}) collective-permute-start(bf16[2048,128]{1,0:T(8,128)(2,1)S(1)} %pack_volume.1.own), channel_id=1, source_target_pairs={{1,2},{3,4},{5,6},{7,8},{9,10},{11,12},{13,14},{2,1},{4,3},{6,5},{... | collective-permute-start | bytes 1572872 | tf_op jit(solution)/shard_map/ppermute | solution.py:421
  2.7 14.2 %collective-permute-start = (bf16[2048,128]{1,0:T(8,128)(2,1)S(1)}, bf16[2048,128]{1,0:T(8,128)(2,1)S(1)}, u32[]{:S(2)}, u32[]{:S(2)}) collective-permute-start(bf16[2048,128]{1,0:T(8,128)(2,1)S(1)} %pack_volume.1.own), channel_id=1, source_target_pairs={{0,1},{1,0},{2,3},{3,2},{4,5},{5,4},{6,7},{7,6},{8,9},{9,8},{10,11... | collective-permute-start | bytes 1572872 | tf_op jit(solution)/shard_map/ppermute | solution.py:422
  7.1 1.2 %copy-start = (bf16[2,64,32,128]{3,2,1,0:T(8,128)(2,1)S(1)}, bf16[2,64,32,128]{3,2,1,0:T(8,128)(2,1)}, u32[]{:S(2)}) copy-start(bf16[2,64,32,128]{3,2,1,0:T(8,128)(2,1)} %param.7) | copy-start | bytes 3145732
  15.2 1.0 %copy-start.3 = (bf16[2304,256]{1,0:T(8,128)(2,1)}, bf16[2304,256]{1,0:T(8,128)(2,1)S(1)}, u32[]{:S(2)}) copy-start(bf16[2304,256]{1,0:T(8,128)(2,1)S(1)} %get-tuple-element.65.taps) | copy-start | bytes 3538948
  16.2 5.0 %collective-permute-start.2 = (bf16[1024,128]{1,0:T(8,128)(2,1)S(1)}, bf16[1024,128]{1,0:T(8,128)(2,1)S(1)}, u32[]{:S(2)}, u32[]{:S(2)}) collective-permute-start(bf16[1024,128]{1,0:T(8,128)(2,1)S(1)} %get-tuple-element.49), channel_id=1, source_target_pairs={{0,1},{1,0},{2,3},{3,2},{4,5},{5,4},{6,7},{7,6},{8,9},{9,8},{10,11... | collective-permute-start | bytes 786440 | tf_op jit(solution)/shard_map/ppermute | solution.py:422
  16.2 5.0 %collective-permute-start.3 = (bf16[1024,128]{1,0:T(8,128)(2,1)S(1)}, bf16[1024,128]{1,0:T(8,128)(2,1)S(1)}, u32[]{:S(2)}, u32[]{:S(2)}) collective-permute-start(bf16[1024,128]{1,0:T(8,128)(2,1)S(1)} %get-tuple-element.50), channel_id=1, source_target_pairs={{1,2},{3,4},{5,6},{7,8},{9,10},{11,12},{13,14},{2,1},{4,3},{6,5},{... | collective-permute-start | bytes 786440 | tf_op jit(solution)/shard_map/ppermute | solution.py:421
  21.2 8.9 %copy-start.1 = (bf16[2112,768]{1,0:T(8,128)(2,1)}, bf16[2112,768]{1,0:T(8,128)(2,1)S(1)}, u32[]{:S(2)}) copy-start(bf16[2112,768]{1,0:T(8,128)(2,1)S(1)} %get-tuple-element.64.act_windows) | copy-start | bytes 9732100
  22.1 9.8 %collective-permute-start.4 = (bf16[1024,128]{1,0:T(8,128)(2,1)S(1)}, bf16[1024,128]{1,0:T(8,128)(2,1)S(1)}, u32[]{:S(2)}, u32[]{:S(2)}) collective-permute-start(bf16[1024,128]{1,0:T(8,128)(2,1)S(1)} %get-tuple-element.60), channel_id=1, source_target_pairs={{0,1},{1,0},{2,3},{3,2},{4,5},{5,4},{6,7},{7,6},{8,9},{9,8},{10,11... | collective-permute-start | bytes 786440 | tf_op jit(solution)/shard_map/ppermute | solution.py:422
  26.8 5.1 %collective-permute-start.5 = (bf16[1024,128]{1,0:T(8,128)(2,1)S(1)}, bf16[1024,128]{1,0:T(8,128)(2,1)S(1)}, u32[]{:S(2)}, u32[]{:S(2)}) collective-permute-start(bf16[1024,128]{1,0:T(8,128)(2,1)S(1)} %get-tuple-element.61), channel_id=1, source_target_pairs={{1,2},{3,4},{5,6},{7,8},{9,10},{11,12},{13,14},{2,1},{4,3},{6,5},{... | collective-permute-start | bytes 786440 | tf_op jit(solution)/shard_map/ppermute | solution.py:421
  31.9 6.8 %collective-permute-start.6 = (bf16[8,32,896]{2,1,0:T(8,128)(2,1)S(1)}, bf16[8,32,896]{2,1,0:T(8,128)(2,1)S(1)}, u32[]{:S(2)}, u32[]{:S(2)}) collective-permute-start(bf16[8,32,896]{2,1,0:T(8,128)(2,1)S(1)} %get-tuple-element.62), channel_id=1, source_target_pairs={{0,1},{1,0},{2,3},{3,2},{4,5},{5,4},{6,7},{7,6},{8,9},{9,8},{10,11... | collective-permute-start | bytes 1376264 | tf_op jit(solution)/shard_map/ppermute | solution.py:492
  39.7 11.2 %copy-start.4 = (bf16[2304,256]{1,0:T(8,128)(2,1)S(1)}, bf16[2304,256]{1,0:T(8,128)(2,1)}, u32[]{:S(2)}) copy-start(bf16[2304,256]{1,0:T(8,128)(2,1)} %copy-done.3) | copy-start | bytes 3538948
  39.7 20.0 %all-to-all-start = ((bf16[8,32,896]{2,1,0:T(8,128)(2,1)}), bf16[8,32,896]{2,1,0:T(8,128)(2,1)S(1)}, u32[]{:S(2)}, u32[]{:S(2)}) async-start(bf16[8,32,896]{2,1,0:T(8,128)(2,1)} %get-tuple-element.71), calls=%async_computation | async-start | bytes 917504 | tf_op jit(solution)/shard_map/all_to_all | solution.py:498
  46.0 4.8 %copy-start.2 = (bf16[2112,768]{1,0:T(8,128)(2,1)S(1)}, bf16[2112,768]{1,0:T(8,128)(2,1)}, u32[]{:S(2)}) copy-start(bf16[2112,768]{1,0:T(8,128)(2,1)} %copy-done.1) | copy-start | bytes 9732100

commit v4 on v3

--- a/solution.py
+++ b/solution.py
@@ -22,7 +22,7 @@
     return tap if 0 <= tap <= 2 else None
 
 
-def call(body, outs, ins, scratch=(), flops=0, name=None, smem=(), apart=()):
+def call(body, outs, ins, scratch=(), flops=0, name=None, smem=(), apart=(), far=False):
     moved = sum(math.prod(s.shape) * s.dtype.itemsize for s in (*outs, *ins))
     return pl.pallas_call(
         body,
@@ -33,7 +33,7 @@
             )
             for i in range(len(ins))
         ],
-        out_specs=[pl.BlockSpec(memory_space=pltpu.VMEM)] * len(outs),
+        out_specs=[pl.BlockSpec(memory_space=pl.ANY if far else pltpu.VMEM)] * len(outs),
         scratch_shapes=list(scratch),
         compiler_params=pltpu.CompilerParams(vmem_limit_bytes=VMEM_LIMIT),
         cost_estimate=pl.CostEstimate(flops=flops, bytes_accessed=moved, transcendentals=0),
@@ -115,22 +115,30 @@
 
 
 def leave_body(
-    columns, me, cotangent, weight_far, own, inner, outer, windows, taps, weight, sem
+    columns, me, far_cotangent, far_weight, own, inner, outer, turned,
+    windows, taps, cotangent, weight, sems, sem,
 ):
-    half = cotangent.shape[1] // 2
+    cells = own.shape[0]
+    half = cells // 2
     odd = me[0] % 2 == 1
-    fetch = pltpu.make_async_copy(weight_far, weight, sem)
+    fetch = pltpu.make_async_copy(far_weight, weight, sem)
+    copies = pieces_of(far_cotangent, cotangent, sems, sems.shape[0])
+    for copy in copies:
+        copy.start()
     fetch.start()
     clear_edges(windows, columns)
-
-    def fill(i, carry):
-        start = pl.multiple_of(i * STEP, STEP)
-        for plane in range(2):
-            chunk = cotangent[plane, pl.ds(start, STEP), :].astype(F32)
-            fill_windows(windows, start, plane * 128, chunk, columns, 256)
-        return carry
-
-    lax.fori_loop(0, 2 * half // STEP, fill, 0)
+    size = cells // len(copies)
+    for at, copy in enumerate(copies):
+        copy.wait()
+
+        def fill(i, carry):
+            start = pl.multiple_of(at * size + i * STEP, STEP)
+            for plane in range(2):
+                chunk = cotangent[plane, pl.ds(start, STEP), :].astype(F32)
+                fill_windows(windows, start, plane * 128, chunk, columns, 256)
+            return carry
+
+        lax.fori_loop(0, size // STEP, fill, 0)
     fetch.wait()
     for row in range(3):
         for column in range(3):
@@ -152,19 +160,15 @@
         upper, lower = packed(*sides)
         inner[start : start + BLOCK, :] = jnp.where(odd, lower, upper).astype(BF16)
         outer[start : start + BLOCK, :] = jnp.where(odd, upper, lower).astype(BF16)
+    for plane in range(2):
+        turn(cotangent.at[plane], turned, plane * 128)
 
 
 def prepare_body(
-    columns, own, far_one, far_two, cotangent,
-    own_windows, hidden, side_taps, out_taps, back_taps, turned, own_taps,
-    weight_one, weight_two, sems,
+    columns, own, far_weight, own_windows, hidden, side_taps, back_taps, own_taps, weight, sem
 ):
-    fetches = [
-        pltpu.make_async_copy(far_one, weight_one, sems.at[0]),
-        pltpu.make_async_copy(far_two, weight_two, sems.at[1]),
-    ]
-    for fetch in fetches:
-        fetch.start()
+    fetch = pltpu.make_async_copy(far_weight, weight, sem)
+    fetch.start()
 
     def fill(i, carry):
         start = pl.multiple_of(i * STEP, STEP)
@@ -174,41 +178,29 @@
 
     clear_edges(own_windows, columns)
     lax.fori_loop(0, own.shape[0] // STEP, fill, 0)
-    turn(cotangent.at[0], turned, 0)
-    turn(cotangent.at[1], turned, 128)
-    for fetch in fetches:
-        fetch.wait()
-    zero, wide_zero = jnp.zeros((64, 64), BF16), jnp.zeros((64, 128), BF16)
+    fetch.wait()
+    zero = jnp.zeros((64, 64), BF16)
     for row in range(3):
         for column in range(3):
             tap = row * 3 + column
             for at, source in enumerate(PLANES):
                 depths = [depth_tap(source, target) for target in PLANES[:4]]
-                parts = [zero if d is None else weight_one[d * 9 + tap] for d in depths]
+                parts = [zero if d is None else weight[d * 9 + tap] for d in depths]
                 if at < 2:
                     target, first = own_taps, tap * 128 + at * 64
                 else:
                     target, first = side_taps, tap * 256 + (at - 2) * 64
                 target[first : first + 64, :128] = jnp.concatenate(parts[:2], axis=1)
                 target[first : first + 64, 128:] = jnp.concatenate(parts[2:], axis=1)
-            for at, source in enumerate(PLANES[:4]):
-                first = tap * 256 + at * 64
-                for plane in range(2):
-                    depth = depth_tap(source, plane)
-                    out_taps[first : first + 64, plane * 128 : plane * 128 + 128] = (
-                        wide_zero if depth is None else weight_two[depth * 9 + tap]
-                    )
             for plane in range(2):
                 depths = [depth_tap(source, plane) for source in PLANES[:4]]
-                parts = [
-                    zero if d is None else weight_one[(2 - d) * 9 + 8 - tap] for d in depths
-                ]
+                parts = [zero if d is None else weight[(2 - d) * 9 + 8 - tap] for d in depths]
+                at = row * 128 + plane * 64
                 for pair in range(2):
-                    first = tap * 256 + pair * 128
-                    back_taps[plane * 64 : plane * 64 + 64, first : first + 128] = (
-                        jnp.concatenate(parts[2 * pair : 2 * pair + 2], axis=1)
+                    first = column * 256 + pair * 128
+                    back_taps[at : at + 64, first : first + 128] = jnp.concatenate(
+                        parts[2 * pair : 2 * pair + 2], axis=1
                     )
-
     for start in range(0, own.shape[0], BLOCK):
         hidden[start : start + BLOCK, :] = window_dot(own_windows, own_taps, start, columns, NN)
 
@@ -216,7 +208,7 @@
 def hidden_body(
     columns, count, me, inner, outer, part, side_taps, side_windows, act_windows, slope
 ):
-    cells = inner.shape[0]
+    cells = outer.shape[0]
     odd = me[0] % 2 == 1
 
     def fill(i, carry):
@@ -251,9 +243,8 @@
     def step(i, carry):
         start = pl.multiple_of(i * STEP, STEP)
         low, high = pl.ds(start, STEP), pl.ds(start + half, STEP)
-        arrived = unpacked(
-            *by_side(odd, inner[low, :].astype(F32), outer[low, :].astype(F32))
-        )
+        near = inner[low, :].astype(F32)
+        arrived = unpacked(*by_side(odd, near, outer[low, :].astype(F32)))
         sides = []
         for rows, extra in zip((low, high), arrived):
             value = ((terms[rows, :] + extra) * slope[rows, :]).astype(BF16)
@@ -302,17 +293,23 @@
 
 def coded(value, split):
     head = value[:split].astype(BF16)
-    rest = (value[:split] - head.astype(F32)).astype(BF16)
-    return jnp.concatenate([head, rest, value[split:].astype(BF16)], axis=0)
+    parts = [head, (value[:split] - head.astype(F32)).astype(BF16)]
+    if split < value.shape[0]:
+        parts.append(value[split:].astype(BF16))
+    return jnp.concatenate(parts, axis=0)
 
 
 def decoded(value, split):
     value = value.astype(F32)
-    return jnp.concatenate([value[:split] + value[split : 2 * split], value[2 * split :]], axis=0)
+    parts = [value[:split] + value[split : 2 * split]]
+    if 2 * split < value.shape[0]:
+        parts.append(value[2 * split :])
+    return jnp.concatenate(parts, axis=0)
 
 
 def grad_one_body(
-    columns, count, me, own_windows, side_windows, grad, other, sent, kept, turned, terms
+    columns, count, me, own_windows, side_windows, grad, other, to_inner,
+    message, kept, turned, terms,
 ):
     cells = grad.shape[0]
 
@@ -339,18 +336,33 @@
             parts += [block[:, :half], block[:, half:]]
         return jnp.concatenate(parts, axis=0)
 
-    split = 2 * terms.shape[0] // count
+    groups = half // 128
     for pair in range(count // 2):
         even_share, odd_share = share(2 * pair), share(2 * pair + 1)
-        sent[pair] = coded(jnp.where(odd, even_share, odd_share), split)
         kept[pair] = jnp.where(odd, odd_share, even_share)
-
-
-def sum_body(split, me, mine, arrived, sent, kept):
+        given = coded(jnp.where(odd, even_share, odd_share), kept.shape[1])
+        size = given.shape[0]
+        for group in range(groups):
+            first = (pair * groups + group) * size
+            message[first : first + size, :] = given[:, group * 128 : group * 128 + 128]
+    message[message.shape[0] - to_inner.shape[0] :, :] = to_inner[...]
+
+
+def sum_body(split, me, mine, message, sent, kept):
     place = me[0] // 2
+    size, lanes = mine.shape[1:]
+    groups = lanes // 128
+
+    def arrived(at):
+        parts = []
+        for group in range(groups):
+            first = pl.multiple_of((at * groups + group) * 2 * size, 8)
+            parts.append(decoded(message[pl.ds(first, 2 * size), :], size))
+        return jnp.concatenate(parts, axis=1)
+
     for at in range(mine.shape[0]):
-        sent[at] = coded(mine[at] + decoded(arrived[at], split), split)
-    kept[...] = mine[place] + decoded(arrived[place], split)
+        sent[at] = coded(mine[at] + arrived(at), split)
+    kept[...] = mine[place] + arrived(place)
 
 
 def finish_body(scale, split, sizes, me, mine, arrived, grad_one, grad_two):
@@ -370,21 +382,44 @@
                 out[depth * 9 + tap] = block[:, lane : lane + 64]
 
 
-def output_body(columns, act_windows, taps, output):
-    for start in range(0, output.shape[1], BLOCK):
-        value = window_dot(act_windows, taps, start, columns, NN)
+def output_body(columns, act_windows, far_weight, far, taps, weight, output, sem, sems):
+    fetch = pltpu.make_async_copy(far_weight, weight, sem)
+    fetch.start()
+    fetch.wait()
+    for row in range(3):
+        for column in range(3):
+            for at, source in enumerate(PLANES[:4]):
+                first = row * 768 + column * 256 + at * 64
+                for plane in range(2):
+                    depth = depth_tap(source, plane)
+                    taps[first : first + 64, plane * 128 : plane * 128 + 128] = (
+                        jnp.zeros((64, 128), BF16)
+                        if depth is None
+                        else weight[depth * 9 + row * 3 + column]
+                    )
+    copies = pieces_of(output, far, sems, output.shape[1] // BLOCK)
+    for at, copy in enumerate(copies):
+        start = at * BLOCK
+        value = None
+        for row, rows in enumerate(row_windows(act_windows, start, columns)):
+            term = jnp.dot(rows, taps[row * 768 : row * 768 + 768, :], preferred_element_type=F32)
+            value = term if value is None else value + term
         output[0, start : start + BLOCK, :] = value[:, :128]
         output[1, start : start + BLOCK, :] = value[:, 128:]
-
-
-def grad_volume_body(columns, me, own, inner, outer, taps, output, windows):
+        copy.start()
+    for copy in copies:
+        copy.wait()
+
+
+def grad_volume_body(columns, me, own, message, outer, taps, far, windows, output, sems):
     half = own.shape[0] // 2
     odd = me[0] % 2 == 1
+    before = message.shape[0] - half
 
     def fill(i, carry):
         start = pl.multiple_of(i * STEP, STEP)
-        rows = pl.ds(start, STEP)
-        below, above = by_side(odd, inner[rows, :].astype(F32), outer[rows, :].astype(F32))
+        near = message[pl.ds(before + start, STEP), :].astype(F32)
+        below, above = by_side(odd, near, outer[pl.ds(start, STEP), :].astype(F32))
         for first, side in zip((start, start + half), unpacked(above, below)):
             fill_windows(windows, first, 0, own[pl.ds(first, STEP), :].astype(F32), columns, 256)
             fill_windows(windows, first, 128, side, columns, 256)
@@ -392,10 +427,19 @@
 
     clear_edges(windows, columns)
     lax.fori_loop(0, half // STEP, fill, 0)
-    for start in range(0, 2 * half, BLOCK):
-        value = window_dot(windows, taps, start, columns, NT)
+    copies = pieces_of(output, far, sems, output.shape[1] // BLOCK)
+    for at, copy in enumerate(copies):
+        start = at * BLOCK
+        rows = windows[start : start + BLOCK + 2 * columns, :]
+        terms = lax.dot_general(rows, taps[...], NT, preferred_element_type=F32)
+        value = terms[:BLOCK, :128]
+        value = value + terms[columns : columns + BLOCK, 128:256]
+        value = value + terms[2 * columns : 2 * columns + BLOCK, 256:]
         output[0, start : start + BLOCK, :] = value[:, :64]
         output[1, start : start + BLOCK, :] = value[:, 64:]
+        copy.start()
+    for copy in copies:
+        copy.wait()
 
 
 def shards(volume, weight_one, weight_two, cotangent):
@@ -417,10 +461,6 @@
     across = [(i, i + 1) for i in range(1, count - 1, 2)]
     across += [(j, i) for i, j in across]
 
-    def exchange(inner, outer):
-        outer = lax.ppermute(outer, "space", across)
-        return lax.ppermute(inner, "space", within), outer
-
     def shares(*lead):
         return shape((*lead, chunk + split, lanes), BF16), shape((*lead, chunk, lanes), F32)
 
@@ -432,69 +472,79 @@
     two_flops = 2 * planes * cells * 27 * mid * wide
 
     dma = pltpu.SemaphoreType.DMA
-    far_one, far_two, far_volume = (
-        pltpu.with_memory_space_constraint(x, pltpu.HBM) for x in (weight_one, weight_two, volume)
+    far_one, far_two, far_volume, far_cotangent = (
+        pltpu.with_memory_space_constraint(x, pltpu.HBM)
+        for x in (weight_one, weight_two, volume, cotangent)
     )
     own, = call(
         pack_body, (flat,), (far_volume,),
         (pltpu.VMEM((planes, cells, channels), BF16), dma((4,))),
         name="pack_volume", apart=(0,),
     )
-    vol_halo = exchange(own, own)
-    terms, inner, outer = call(
+    vol_outer = lax.ppermute(own, "space", across)
+    vol_inner = lax.ppermute(own, "space", within)
+    terms, inner, outer, turned = call(
         functools.partial(leave_body, columns),
-        (shape((cells, 128), F32), pack, pack),
-        (me, cotangent, far_two),
-        (windows, pltpu.VMEM((256, 3 * 768), BF16), pltpu.VMEM(weight_two.shape, BF16), dma),
-        two_flops, "grad_act_terms", (0,), (2,),
+        (
+            shape((cells, 128), F32), pack, pack, shape((256, cells), BF16),
+        ),
+        (me, far_cotangent, far_two),
+        (
+            windows, pltpu.VMEM((256, 3 * 768), BF16), pltpu.VMEM(cotangent.shape, BF16),
+            pltpu.VMEM(weight_two.shape, BF16), dma((4,)), dma,
+        ),
+        two_flops, "grad_act_terms", (0,), (1, 2),
     )
     own, terms = lax.optimization_barrier((own, terms))
-    own_windows, part, side_taps, out_taps, back_taps, turned = call(
+    own_windows, part, side_taps, back_taps = call(
         functools.partial(prepare_body, columns),
         (
             shape((slab[0], 384), BF16), shape((cells, 256), F32), shape((9 * 256, 256), BF16),
-            shape((9 * 256, 256), BF16), shape((128, 9 * 256), BF16), shape((256, cells), BF16),
+            shape((3 * 128, 768), BF16),
         ),
-        (own, far_one, far_two, cotangent),
-        (
-            pltpu.VMEM((9 * 128, 256), BF16), pltpu.VMEM(weight_one.shape, BF16),
-            pltpu.VMEM(weight_two.shape, BF16), dma((2,)),
-        ),
-        one_flops, "prepare", (), (1, 2),
+        (own, far_one),
+        (pltpu.VMEM((9 * 128, 256), BF16), pltpu.VMEM(weight_one.shape, BF16), dma),
+        one_flops, "prepare", (), (1,),
     )
     inner, outer, part = lax.optimization_barrier((inner, outer, part))
-    act_terms_halo = exchange(inner, outer)
+    terms_outer = lax.ppermute(outer, "space", across)
+    terms_inner = lax.ppermute(inner, "space", within)
     side_windows, act_windows, slope = call(
         functools.partial(hidden_body, columns, count),
         (shape(slab, BF16), shape(slab, BF16), shape((cells, 128), F32)),
-        (me, *vol_halo, part, side_taps),
+        (me, vol_inner, vol_outer, part, side_taps),
         (), 2 * one_flops, "hidden", (0,),
     )
-    grad_hidden, inner, outer = call(
-        slope_body, (flat, pack, pack), (me, terms, *act_terms_halo, slope),
-        name="grad_hidden", smem=(0,),
-    )
-    inner, outer, act_windows = lax.optimization_barrier((inner, outer, act_windows))
-    grad_halo = exchange(inner, outer)
     terms_two, = call(
         functools.partial(grad_two_body, columns),
         (shape((wide, 2 * lanes), F32),),
         (act_windows, turned), (), two_flops, "grad_two_terms",
     )
-    sent, kept = call(
+    terms_two, terms_outer = lax.optimization_barrier((terms_two, terms_outer))
+    grad_hidden, to_inner, outer = call(
+        slope_body, (flat, pack, pack), (me, terms, terms_inner, terms_outer, slope),
+        name="grad_hidden", smem=(0,),
+    )
+    grad_outer = lax.ppermute(outer, "space", across)
+    groups = lanes // 128
+    message, kept = call(
         functools.partial(grad_one_body, columns, count),
-        shares(count // 2),
-        (me, own_windows, side_windows, grad_hidden, terms_two),
+        (
+            shape((count // 2 * groups * 2 * chunk + cells // 2, 128), BF16),
+            shares(count // 2)[1],
+        ),
+        (me, own_windows, side_windows, grad_hidden, terms_two, to_inner),
         (pltpu.VMEM((128, cells), BF16), pltpu.VMEM((mid, 2 * lanes), F32)),
         one_flops, "grad_one_terms", (0,),
     )
-    sent, grad_halo = lax.optimization_barrier((sent, grad_halo))
-    arrived = lax.ppermute(sent, "space", within)
+    message = lax.ppermute(message, "space", within)
     sent, mine = call(
         functools.partial(sum_body, split), (shares(count // 2)[0], shares()[1]),
-        (me, kept, arrived), name="sum_pair", smem=(0,),
-    )
-    sent, act_windows, grad_hidden = lax.optimization_barrier((sent, act_windows, grad_hidden))
+        (me, kept, message), name="sum_pair", smem=(0,),
+    )
+    sent, act_windows, grad_hidden, grad_outer = lax.optimization_barrier(
+        (sent, act_windows, grad_hidden, grad_outer)
+    )
     arrived = lax.all_to_all(
         sent, "space", 0, 0, tiled=True,
         axis_index_groups=[list(range(core, count, 2)) for core in range(2)],
@@ -502,13 +552,19 @@
     output, = call(
         functools.partial(output_body, columns),
         (shape((planes, cells, wide), F32),),
-        (act_windows, out_taps), (), two_flops, "output",
+        (act_windows, far_two),
+        (
+            pltpu.VMEM((3 * 768, 256), BF16), pltpu.VMEM(weight_two.shape, BF16),
+            pltpu.VMEM((planes, cells, wide), F32), dma, dma((cells // BLOCK,)),
+        ),
+        two_flops, "output", (), (1,), True,
     )
     grad_volume, = call(
         functools.partial(grad_volume_body, columns),
         (shape((planes, cells, channels), F32),),
-        (me, grad_hidden, *grad_halo, back_taps),
-        (windows,), one_flops, "grad_volume", (0,),
+        (me, grad_hidden, message, grad_outer, back_taps),
+        (windows, pltpu.VMEM((planes, cells, channels), F32), dma((cells // BLOCK,))),
+        one_flops, "grad_volume", (0,), (), True,
     )
     grad_one, grad_two = call(
         functools.partial(finish_body, scale, split, (mid // count, wide // count)),

time: 60.8 us -> 59.2 us (0.974)
  local copies, waits for them, and re-layouts: 2.24 us -> 0.01 us
    all_to_all x1, starting transfers between devices: 6.35 us -> 13.1 us  [shards(): lax.all_to_all(sent, 'space', 0, 0, tiled=True, axis_index_groups=[list(r...]
    ppermute x7 -> x6, starting transfers between devices: 16.5 us -> 10.1 us  [the longest x1 4.36 us: shards(): vol_inner = lax.ppermute(own, 'space', within)]
    unnamed x10 -> x4, local copies, waits for them, and re-layouts: 2.24 us -> 0.01 us
    ppermute x7 -> x6, waiting for transfers between devices: 1.46 us -> 1.49 us  [the longest x1 1.47 us: shards(): message = lax.ppermute(message, 'space', within)]
  transfers between devices with their start and end apart: 8 -> 7, of which waited for: 2 -> 2; matrix products, arithmetic and copies ran while one was open for 0% -> 0% of each run, Pallas kernels for 40% -> 40%
where the time goes in v4:
time: 59.2 us; the launch traced here: 58.8 us
  Pallas kernels  28.6 us (48%)
  starting transfers between devices  23.2 us (39%)
  waiting for transfers between devices  6.19 us (10%)
  between operations  0.79 us (1%)
    pallas_call x11, Pallas kernels, call(): pl.pallas_call(body, out_shape=list(outs), in_specs=[pl.BlockSpec(memory_...  28.6 us
    all_to_all x1, starting transfers between devices, shards(): lax.all_to_all(sent, 'space', 0, 0, tiled=True, axis_index_groups=[list(r...  13.1 us
    all_to_all x1, waiting for transfers between devices, shards(): lax.all_to_all(sent, 'space', 0, 0, tiled=True, axis_index_groups=[list(r...  4.71 us
    ppermute x1, starting transfers between devices, shards(): vol_inner = lax.ppermute(own, 'space', within)  4.36 us
    ppermute x1, starting transfers between devices, shards(): message = lax.ppermute(message, 'space', within)  3.61 us
    ppermute x1, waiting for transfers between devices, shards(): message = lax.ppermute(message, 'space', within)  1.47 us
  transfers between devices with their start and end apart: 7, of which 2 were waited for; matrix products, arithmetic and copies ran while one was open for 0% of the time, Pallas kernels for 40%

profile of v4, /device:TPU:0, one launch (start us, length us, event | category | flops | bytes accessed | tf_op | source)
XLA Modules:
  0.0 58.8 jit_solution(6317553754314222524)
XLA Ops:
  0.6 1.4 %pack_volume.1.own = bf16[2048,128]{1,0:T(8,128)(2,1)S(1)} custom-call(bf16[2,2048,64]{2,1,0:T(8,128)(2,1)} %bitcast.14), custom_call_target="tpu_custom_call" | custom-call | bytes 1048576 | tf_op jit(solution)/shard_map/pack_volume/pallas_call | solution.py:27
  2.0 0.7 %collective-permute-start.1 = (bf16[2048,128]{1,0:T(8,128)(2,1)S(1)}, bf16[2048,128]{1,0:T(8,128)(2,1)S(1)}, u32[]{:S(2)}, u32[]{:S(2)}) collective-permute-start(bf16[2048,128]{1,0:T(8,128)(2,1)S(1)} %pack_volume.1.own), channel_id=1, source_target_pairs={{1,2},{3,4},{5,6},{7,8},{9,10},{11,12},{13,14},{2,1},{4,3},{6,5},{... | collective-permute-start | bytes 1572872 | tf_op jit(solution)/shard_map/ppermute | solution.py:484
  2.7 4.4 %collective-permute-start = (bf16[2048,128]{1,0:T(8,128)(2,1)S(1)}, bf16[2048,128]{1,0:T(8,128)(2,1)S(1)}, u32[]{:S(2)}, u32[]{:S(2)}) collective-permute-start(bf16[2048,128]{1,0:T(8,128)(2,1)S(1)} %pack_volume.1.own), channel_id=1, source_target_pairs={{0,1},{1,0},{2,3},{3,2},{4,5},{5,4},{6,7},{7,6},{8,9},{9,8},{10,11... | collective-permute-start | bytes 1572872 | tf_op jit(solution)/shard_map/ppermute | solution.py:485
  7.1 4.5 %grad_act_terms.1 = (f32[2048,128]{1,0:T(8,128)S(1)}, bf16[1024,128]{1,0:T(8,128)(2,1)S(1)}, bf16[1024,128]{1,0:T(8,128)(2,1)S(1)}, bf16[256,2048]{1,0:T(8,128)(2,1)S(1)}) custom-call(s32[1]{0:T(128)} %bitcast.me, bf16[2,2048,128]{2,1,0:T(8,128)(2,1)} %bitcast.15, bf16[27,64,128]{2,1,0:T(8,128)(2,1)} %bitcast.17), custom_call_target="tpu_custom_call" | custom-call | flops 1811939328 | bytes 4112388 | tf_op jit(solution)/shard_map/grad_act_terms/pallas_call | solution.py:27
  11.6 2.8 %prepare.1 = (bf16[2112,384]{1,0:T(8,128)(2,1)S(1)}, f32[2048,256]{1,0:T(8,128)S(1)}, bf16[2304,256]{1,0:T(8,128)(2,1)S(1)}, bf16[384,768]{1,0:T(8,128)(2,1)S(1)}) custom-call(bf16[2048,128]{1,0:T(8,128)(2,1)S(1)} %pack_volume.1.own, bf16[27,64,64]{2,1,0:T(8,128)(2,1)} %bitcast.16), custom_call_target="tpu_custom_call" | custom-call | flops 905969664 | bytes 6234112 | tf_op jit(solution)/shard_map/prepare/pallas_call | solution.py:27
  14.4 0.1 collective-permute-start.2
  14.5 0.7 %collective-permute-start.3 = (bf16[1024,128]{1,0:T(8,128)(2,1)S(1)}, bf16[1024,128]{1,0:T(8,128)(2,1)S(1)}, u32[]{:S(2)}, u32[]{:S(2)}) collective-permute-start(bf16[1024,128]{1,0:T(8,128)(2,1)S(1)} %get-tuple-element.48), channel_id=1, source_target_pairs={{1,2},{3,4},{5,6},{7,8},{9,10},{11,12},{13,14},{2,1},{4,3},{6,5},{... | collective-permute-start | bytes 786440 | tf_op jit(solution)/shard_map/ppermute | solution.py:510
  15.2 0.0 collective-permute-done.1.outer
  15.2 0.0 collective-permute-done.inner
  15.2 4.3 %hidden.1 = (bf16[2112,768]{1,0:T(8,128)(2,1)S(1)}, bf16[2112,768]{1,0:T(8,128)(2,1)S(1)}, f32[2048,128]{1,0:T(8,128)S(1)}) custom-call(s32[1]{0:T(128)} %bitcast.me, bf16[2048,128]{1,0:T(8,128)(2,1)S(1)} %collective-permute-done.inner, bf16[2048,128]{1,0:T(8,128)(2,1)S(1)} %collective-permute-done.1.outer, f32[2048,256]{1,0:T(8,128)S(1)} %get-tuple-element.41.part, ...), custom_call_target="tpu_custom_call" | custom-call | flops 1811939328 | bytes 11862020 | tf_op jit(solution)/shard_map/hidden/pallas_call | solution.py:27
  19.5 0.0 copy-start
  19.5 2.8 %grad_two_terms.1.other = f32[128,1792]{1,0:T(8,128)S(1)} custom-call(bf16[2112,768]{1,0:T(8,128)(2,1)S(1)} %get-tuple-element.58.act_windows, bf16[256,2048]{1,0:T(8,128)(2,1)S(1)} %get-tuple-element.47.turned), custom_call_target="tpu_custom_call" | custom-call | flops 1811939328 | bytes 5210112 | tf_op jit(solution)/shard_map/grad_two_terms/pallas_call | solution.py:27
  22.3 0.0 copy-done
  22.3 0.0 collective-permute-done.3.outer
  22.3 0.0 collective-permute-done.2.inner
  22.3 0.9 %grad_hidden.1 = (bf16[2048,128]{1,0:T(8,128)(2,1)S(1)}, bf16[1024,128]{1,0:T(8,128)(2,1)S(1)}, bf16[1024,128]{1,0:T(8,128)(2,1)S(1)}) custom-call(s32[1]{0:T(128)} %bitcast.me, f32[2048,128]{1,0:T(8,128)S(1)} %get-tuple-element.44.terms, bf16[1024,128]{1,0:T(8,128)(2,1)S(1)} %collective-permute-done.2.inner, ...), custom_call_target="tpu_custom_call" | custom-call | bytes 3670020 | tf_op jit(solution)/shard_map/grad_hidden/pallas_call | solution.py:27
  23.2 1.8 %grad_one_terms.1 = (bf16[3712,128]{1,0:T(8,128)(2,1)S(1)}, f32[8,24,896]{2,1,0:T(8,128)S(1)}) custom-call(s32[1]{0:T(128)} %bitcast.me, bf16[2112,384]{1,0:T(8,128)(2,1)S(1)} %get-tuple-element.37.own_windows, bf16[2112,768]{1,0:T(8,128)(2,1)S(1)} %get-tuple-element.43.side_windows, bf16[2048,128]{1,0:T(8,128)(2,1)S(1)} %get-tuple-element.59.grad.own, ...), custom_call_target="tpu_custom_call" | custom-call | flops 905969664 | bytes 8208388 | tf_op jit(solution)/shard_map/grad_one_terms/pallas_call | solution.py:27
  25.0 3.6 %collective-permute-start.4 = (bf16[3712,128]{1,0:T(8,128)(2,1)S(1)}, bf16[3712,128]{1,0:T(8,128)(2,1)S(1)}, u32[]{:S(2)}, u32[]{:S(2)}) collective-permute-start(bf16[3712,128]{1,0:T(8,128)(2,1)S(1)} %get-tuple-element.55), channel_id=1, source_target_pairs={{0,1},{1,0},{2,3},{3,2},{4,5},{5,4},{6,7},{7,6},{8,9},{9,8},{10,11... | collective-permute-start | bytes 2850824 | tf_op jit(solution)/shard_map/ppermute | solution.py:540
  28.6 0.7 %collective-permute-start.5 = (bf16[1024,128]{1,0:T(8,128)(2,1)S(1)}, bf16[1024,128]{1,0:T(8,128)(2,1)S(1)}, u32[]{:S(2)}, u32[]{:S(2)}) collective-permute-start(bf16[1024,128]{1,0:T(8,128)(2,1)S(1)} %get-tuple-element.57), channel_id=1, source_target_pairs={{1,2},{3,4},{5,6},{7,8},{9,10},{11,12},{13,14},{2,1},{4,3},{6,5},{... | collective-permute-start | bytes 786440 | tf_op jit(solution)/shard_map/ppermute | solution.py:528
  29.3 1.5 %collective-permute-done.4.message = bf16[3712,128]{1,0:T(8,128)(2,1)S(1)} collective-permute-done((bf16[3712,128]{1,0:T(8,128)(2,1)S(1)}, bf16[3712,128]{1,0:T(8,128)(2,1)S(1)}, u32[]{:S(2)}, u32[]{:S(2)}) %collective-permute-start.4) | collective-permute-done | bytes 950304 | tf_op jit(solution)/shard_map/ppermute | solution.py:540
  30.7 0.9 %sum_pair.1 = (bf16[8,32,896]{2,1,0:T(8,128)(2,1)}, f32[24,896]{1,0:T(8,128)S(1)}) custom-call(s32[1]{0:T(128)} %bitcast.me, f32[8,24,896]{2,1,0:T(8,128)S(1)} %get-tuple-element.54.mine, bf16[3712,128]{1,0:T(8,128)(2,1)S(1)} %collective-permute-done.4.message), custom_call_target="tpu_custom_call" | custom-call | bytes 2183172 | tf_op jit(solution)/shard_map/sum_pair/pallas_call | solution.py:27
  31.7 0.0 collective-permute-done.5.outer
  31.7 13.1 %all-to-all-start = ((bf16[8,32,896]{2,1,0:T(8,128)(2,1)}), bf16[8,32,896]{2,1,0:T(8,128)(2,1)S(1)}, u32[]{:S(2)}, u32[]{:S(2)}) async-start(bf16[8,32,896]{2,1,0:T(8,128)(2,1)} %get-tuple-element.63), calls=%async_computation | async-start | bytes 917504 | tf_op jit(solution)/shard_map/all_to_all | solution.py:548
  44.8 0.0 copy-start.1
  44.8 3.8 %grad_volume.1 = f32[2,2048,64]{2,1,0:T(8,128)} custom-call(s32[1]{0:T(128)} %bitcast.me, bf16[2048,128]{1,0:T(8,128)(2,1)S(1)} %get-tuple-element.59.grad.own, bf16[3712,128]{1,0:T(8,128)(2,1)S(1)} %collective-permute-done.4.message, bf16[1024,128]{1,0:T(8,128)(2,1)S(1)} %collective-permute-done.5.outer, bf16[384,768]{1,0:T(8,128)(2,1)S(1)} %get-tuple-element.61.taps), custom_call_target="tpu_custom_call" | custom-call | flops 905969664 | bytes 3375108 | tf_op jit(solution)/shard_map/grad_volume/pallas_call | solution.py:27
  48.5 0.0 copy-done.1
  48.5 4.7 %output.1 = f32[2,2048,128]{2,1,0:T(8,128)} custom-call(bf16[2112,768]{1,0:T(8,128)(2,1)S(1)} %copy-done.1, bf16[27,64,128]{2,1,0:T(8,128)(2,1)} %bitcast.18), custom_call_target="tpu_custom_call" | custom-call | flops 1811939328 | bytes 5783552 | tf_op jit(solution)/shard_map/output/pallas_call | solution.py:27
  53.3 4.7 %all-to-all-done.arrived = bf16[8,32,896]{2,1,0:T(8,128)(2,1)S(1)} async-done(((bf16[8,32,896]{2,1,0:T(8,128)(2,1)}), bf16[8,32,896]{2,1,0:T(8,128)(2,1)S(1)}, u32[]{:S(2)}, u32[]{:S(2)}) %all-to-all-start) | async-done | bytes 458784 | tf_op jit(solution)/shard_map/all_to_all | solution.py:548
  58.0 0.8 %finish.1 = (f32[27,4,64]{2,1,0:T(4,128)}, f32[27,8,64]{2,1,0:T(8,128)}) custom-call(s32[1]{0:T(128)} %bitcast.me, f32[24,896]{1,0:T(8,128)S(1)} %get-tuple-element.62.mine, bf16[8,32,896]{2,1,0:T(8,128)(2,1)S(1)} %all-to-all-done.arrived), custom_call_target="tpu_custom_call" | custom-call | bytes 627716 | tf_op jit(solution)/shard_map/finish/pallas_call | solution.py:27
Async XLA Ops:
  2.0 13.2 %collective-permute-start.1 = (bf16[2048,128]{1,0:T(8,128)(2,1)S(1)}, bf16[2048,128]{1,0:T(8,128)(2,1)S(1)}, u32[]{:S(2)}, u32[]{:S(2)}) collective-permute-start(bf16[2048,128]{1,0:T(8,128)(2,1)S(1)} %pack_volume.1.own), channel_id=1, source_target_pairs={{1,2},{3,4},{5,6},{7,8},{9,10},{11,12},{13,14},{2,1},{4,3},{6,5},{... | collective-permute-start | bytes 1572872 | tf_op jit(solution)/shard_map/ppermute | solution.py:484
  2.7 12.5 %collective-permute-start = (bf16[2048,128]{1,0:T(8,128)(2,1)S(1)}, bf16[2048,128]{1,0:T(8,128)(2,1)S(1)}, u32[]{:S(2)}, u32[]{:S(2)}) collective-permute-start(bf16[2048,128]{1,0:T(8,128)(2,1)S(1)} %pack_volume.1.own), channel_id=1, source_target_pairs={{0,1},{1,0},{2,3},{3,2},{4,5},{5,4},{6,7},{7,6},{8,9},{9,8},{10,11... | collective-permute-start | bytes 1572872 | tf_op jit(solution)/shard_map/ppermute | solution.py:485
  14.4 7.9 %collective-permute-start.2 = (bf16[1024,128]{1,0:T(8,128)(2,1)S(1)}, bf16[1024,128]{1,0:T(8,128)(2,1)S(1)}, u32[]{:S(2)}, u32[]{:S(2)}) collective-permute-start(bf16[1024,128]{1,0:T(8,128)(2,1)S(1)} %get-tuple-element.45), channel_id=1, source_target_pairs={{0,1},{1,0},{2,3},{3,2},{4,5},{5,4},{6,7},{7,6},{8,9},{9,8},{10,11... | collective-permute-start | bytes 786440 | tf_op jit(solution)/shard_map/ppermute | solution.py:511
  14.5 7.8 %collective-permute-start.3 = (bf16[1024,128]{1,0:T(8,128)(2,1)S(1)}, bf16[1024,128]{1,0:T(8,128)(2,1)S(1)}, u32[]{:S(2)}, u32[]{:S(2)}) collective-permute-start(bf16[1024,128]{1,0:T(8,128)(2,1)S(1)} %get-tuple-element.48), channel_id=1, source_target_pairs={{1,2},{3,4},{5,6},{7,8},{9,10},{11,12},{13,14},{2,1},{4,3},{6,5},{... | collective-permute-start | bytes 786440 | tf_op jit(solution)/shard_map/ppermute | solution.py:510
  19.5 2.8 %copy-start = (bf16[2112,768]{1,0:T(8,128)(2,1)}, bf16[2112,768]{1,0:T(8,128)(2,1)S(1)}, u32[]{:S(2)}) copy-start(bf16[2112,768]{1,0:T(8,128)(2,1)S(1)} %get-tuple-element.58.act_windows) | copy-start | bytes 9732100
  25.0 5.8 %collective-permute-start.4 = (bf16[3712,128]{1,0:T(8,128)(2,1)S(1)}, bf16[3712,128]{1,0:T(8,128)(2,1)S(1)}, u32[]{:S(2)}, u32[]{:S(2)}) collective-permute-start(bf16[3712,128]{1,0:T(8,128)(2,1)S(1)} %get-tuple-element.55), channel_id=1, source_target_pairs={{0,1},{1,0},{2,3},{3,2},{4,5},{5,4},{6,7},{7,6},{8,9},{9,8},{10,11... | collective-permute-start | bytes 2850824 | tf_op jit(solution)/shard_map/ppermute | solution.py:540
  28.6 3.1 %collective-permute-start.5 = (bf16[1024,128]{1,0:T(8,128)(2,1)S(1)}, bf16[1024,128]{1,0:T(8,128)(2,1)S(1)}, u32[]{:S(2)}, u32[]{:S(2)}) collective-permute-start(bf16[1024,128]{1,0:T(8,128)(2,1)S(1)} %get-tuple-element.57), channel_id=1, source_target_pairs={{1,2},{3,4},{5,6},{7,8},{9,10},{11,12},{13,14},{2,1},{4,3},{6,5},{... | collective-permute-start | bytes 786440 | tf_op jit(solution)/shard_map/ppermute | solution.py:528
  31.7 26.3 %all-to-all-start = ((bf16[8,32,896]{2,1,0:T(8,128)(2,1)}), bf16[8,32,896]{2,1,0:T(8,128)(2,1)S(1)}, u32[]{:S(2)}, u32[]{:S(2)}) async-start(bf16[8,32,896]{2,1,0:T(8,128)(2,1)} %get-tuple-element.63), calls=%async_computation | async-start | bytes 917504 | tf_op jit(solution)/shard_map/all_to_all | solution.py:548
  44.8 3.8 %copy-start.1 = (bf16[2112,768]{1,0:T(8,128)(2,1)S(1)}, bf16[2112,768]{1,0:T(8,128)(2,1)}, u32[]{:S(2)}) copy-start(bf16[2112,768]{1,0:T(8,128)(2,1)} %copy-done) | copy-start | bytes 9732100

commit v5 on v4

--- a/solution.py
+++ b/solution.py
@@ -308,8 +308,7 @@
 
 
 def grad_one_body(
-    columns, count, me, own_windows, side_windows, grad, other, to_inner,
-    message, kept, turned, terms,
+    columns, count, me, own_windows, side_windows, grad, other, message, kept, turned, terms
 ):
     cells = grad.shape[0]
 
@@ -345,30 +344,39 @@
         for group in range(groups):
             first = (pair * groups + group) * size
             message[first : first + size, :] = given[:, group * 128 : group * 128 + 128]
-    message[message.shape[0] - to_inner.shape[0] :, :] = to_inner[...]
-
-
-def sum_body(split, me, mine, message, sent, kept):
-    place = me[0] // 2
+
+
+def halve_body(split, me, mine, message, sent, kept):
+    odd = (me[0] // 2) % 2
     size, lanes = mine.shape[1:]
     groups = lanes // 128
 
-    def arrived(at):
+    def total(at):
         parts = []
         for group in range(groups):
             first = pl.multiple_of((at * groups + group) * 2 * size, 8)
             parts.append(decoded(message[pl.ds(first, 2 * size), :], size))
-        return jnp.concatenate(parts, axis=1)
-
-    for at in range(mine.shape[0]):
-        sent[at] = coded(mine[at] + arrived(at), split)
-    kept[...] = mine[place] + arrived(place)
-
-
-def finish_body(scale, split, sizes, me, mine, arrived, grad_one, grad_two):
+        return mine[at] + jnp.concatenate(parts, axis=1)
+
+    for pair in range(sent.shape[0]):
+        sent[pair] = coded(total(2 * pair + 1 - odd), split)
+        kept[pair] = total(2 * pair + odd)
+
+
+def spread_body(split, me, mine, arrived, kept, *sent):
+    ring = mine.shape[0]
+    place = me[0] // 4
+    kept[...] = mine[place] + decoded(arrived[place], split)
+    for hop, out in enumerate(sent):
+        there = (place + hop + 1) % ring
+        out[...] = (mine[there] + decoded(arrived[there], split)).astype(BF16)
+
+
+def finish_body(scale, sizes, mine, *refs):
+    arrived, (grad_one, grad_two) = refs[:-2], refs[-2:]
     total = mine[...]
-    for at in range(arrived.shape[0]):
-        total = total + jnp.where(at == me[0] // 2, 0.0, decoded(arrived[at], split))
+    for part in arrived:
+        total = total + part[...].astype(F32)
     total = total * scale
     half = total.shape[1]
     first = 0
@@ -382,10 +390,7 @@
                 out[depth * 9 + tap] = block[:, lane : lane + 64]
 
 
-def output_body(columns, act_windows, far_weight, far, taps, weight, output, sem, sems):
-    fetch = pltpu.make_async_copy(far_weight, weight, sem)
-    fetch.start()
-    fetch.wait()
+def output_body(columns, act_windows, weight, far, taps, output, sems):
     for row in range(3):
         for column in range(3):
             for at, source in enumerate(PLANES[:4]):
@@ -400,10 +405,7 @@
     copies = pieces_of(output, far, sems, output.shape[1] // BLOCK)
     for at, copy in enumerate(copies):
         start = at * BLOCK
-        value = None
-        for row, rows in enumerate(row_windows(act_windows, start, columns)):
-            term = jnp.dot(rows, taps[row * 768 : row * 768 + 768, :], preferred_element_type=F32)
-            value = term if value is None else value + term
+        value = window_dot(act_windows, taps, start, columns, NN)
         output[0, start : start + BLOCK, :] = value[:, :128]
         output[1, start : start + BLOCK, :] = value[:, 128:]
         copy.start()
@@ -411,15 +413,14 @@
         copy.wait()
 
 
-def grad_volume_body(columns, me, own, message, outer, taps, far, windows, output, sems):
+def grad_windows_body(columns, me, own, inner, outer, windows):
     half = own.shape[0] // 2
     odd = me[0] % 2 == 1
-    before = message.shape[0] - half
 
     def fill(i, carry):
         start = pl.multiple_of(i * STEP, STEP)
-        near = message[pl.ds(before + start, STEP), :].astype(F32)
-        below, above = by_side(odd, near, outer[pl.ds(start, STEP), :].astype(F32))
+        rows = pl.ds(start, STEP)
+        below, above = by_side(odd, inner[rows, :].astype(F32), outer[rows, :].astype(F32))
         for first, side in zip((start, start + half), unpacked(above, below)):
             fill_windows(windows, first, 0, own[pl.ds(first, STEP), :].astype(F32), columns, 256)
             fill_windows(windows, first, 128, side, columns, 256)
@@ -427,6 +428,9 @@
 
     clear_edges(windows, columns)
     lax.fori_loop(0, half // STEP, fill, 0)
+
+
+def grad_volume_body(columns, windows, taps, far, output, sems):
     copies = pieces_of(output, far, sems, output.shape[1] // BLOCK)
     for at, copy in enumerate(copies):
         start = at * BLOCK
@@ -526,50 +530,63 @@
         name="grad_hidden", smem=(0,),
     )
     grad_outer = lax.ppermute(outer, "space", across)
+    grad_inner = lax.ppermute(to_inner, "space", within)
     groups = lanes // 128
     message, kept = call(
         functools.partial(grad_one_body, columns, count),
         (
-            shape((count // 2 * groups * 2 * chunk + cells // 2, 128), BF16),
+            shape((count // 2 * groups * 2 * chunk, 128), BF16),
             shares(count // 2)[1],
         ),
-        (me, own_windows, side_windows, grad_hidden, terms_two, to_inner),
+        (me, own_windows, side_windows, grad_hidden, terms_two),
         (pltpu.VMEM((128, cells), BF16), pltpu.VMEM((mid, 2 * lanes), F32)),
         one_flops, "grad_one_terms", (0,),
     )
     message = lax.ppermute(message, "space", within)
-    sent, mine = call(
-        functools.partial(sum_body, split), (shares(count // 2)[0], shares()[1]),
-        (me, kept, message), name="sum_pair", smem=(0,),
-    )
-    sent, act_windows, grad_hidden, grad_outer = lax.optimization_barrier(
-        (sent, act_windows, grad_hidden, grad_outer)
-    )
-    arrived = lax.all_to_all(
-        sent, "space", 0, 0, tiled=True,
-        axis_index_groups=[list(range(core, count, 2)) for core in range(2)],
-    )
+    grad_windows, = call(
+        functools.partial(grad_windows_body, columns), (shape(slab, BF16),),
+        (me, grad_hidden, grad_inner, grad_outer),
+        (), 16 * two_flops, "grad_windows", (0,),
+    )
+    message, grad_windows = lax.optimization_barrier((message, grad_windows))
+    sent, kept = call(
+        functools.partial(halve_body, split), shares(count // 4),
+        (me, kept, message), name="halve", smem=(0,),
+    )
+    sent, act_windows = lax.optimization_barrier((sent, act_windows))
+    arrived = lax.ppermute(sent, "space", [(i, i ^ 2) for i in range(count)])
     output, = call(
         functools.partial(output_body, columns),
         (shape((planes, cells, wide), F32),),
-        (act_windows, far_two),
+        (act_windows, weight_two),
         (
-            pltpu.VMEM((3 * 768, 256), BF16), pltpu.VMEM(weight_two.shape, BF16),
-            pltpu.VMEM((planes, cells, wide), F32), dma, dma((cells // BLOCK,)),
+            pltpu.VMEM((3 * 768, 256), BF16), pltpu.VMEM((planes, cells, wide), F32),
+            dma((cells // BLOCK,)),
         ),
-        two_flops, "output", (), (1,), True,
-    )
+        two_flops, "output", (), (), True,
+    )
+    ring = count // 4
+    mine, *sent = call(
+        functools.partial(spread_body, split),
+        (shares()[1], *[shape((chunk, lanes), BF16)] * (ring - 1)),
+        (me, kept, arrived), name="spread", smem=(0,),
+    )
+    sent, grad_windows = lax.optimization_barrier((sent, grad_windows))
+    rest = [
+        lax.ppermute(x, "space", [(i, (i + 4 * hop + 4) % count) for i in range(count)])
+        for hop, x in enumerate(sent)
+    ]
     grad_volume, = call(
         functools.partial(grad_volume_body, columns),
         (shape((planes, cells, channels), F32),),
-        (me, grad_hidden, message, grad_outer, back_taps),
-        (windows, pltpu.VMEM((planes, cells, channels), F32), dma((cells // BLOCK,))),
-        one_flops, "grad_volume", (0,), (), True,
+        (grad_windows, back_taps),
+        (pltpu.VMEM((planes, cells, channels), F32), dma((cells // BLOCK,))),
+        one_flops, "grad_volume", (), (), True,
     )
     grad_one, grad_two = call(
-        functools.partial(finish_body, scale, split, (mid // count, wide // count)),
+        functools.partial(finish_body, scale, (mid // count, wide // count)),
         (shape((27, mid // count, channels), F32), shape((27, wide // count, mid), F32)),
-        (me, mine, arrived), name="finish", smem=(0,),
+        (mine, *rest), name="finish",
     )
     return (
         output.reshape(planes, rows, columns, wide),

time: 59.2 us -> 56.1 us (0.948)
  waiting for transfers between devices: 6.19 us -> 2.36 us
  starting transfers between devices: 23.2 us -> 26 us
  Pallas kernels: 28.6 us -> 26.7 us
    ppermute x0 -> x5, starting transfers between devices: none -> 15.5 us  [the longest x3 6.32 us: shards(): lax.ppermute(x, 'space', [(i, (i + 4 * hop + 4) % count) for i in range(c...]
    all_to_all x1 -> x0, starting transfers between devices: 13.1 us -> none  [shards(): lax.all_to_all(sent, 'space', 0, 0, tiled=True, axis_index_groups=[list(r...]
    all_to_all x1 -> x0, waiting for transfers between devices: 4.71 us -> none  [shards(): lax.all_to_all(sent, 'space', 0, 0, tiled=True, axis_index_groups=[list(r...]
    pallas_call x11 -> x13, Pallas kernels: 28.6 us -> 26.7 us  [call(): pl.pallas_call(body, out_shape=list(outs), in_specs=[pl.BlockSpec(memory_...]
    ppermute x0 -> x5, waiting for transfers between devices: none -> 1.44 us  [the longest x1 1.43 us: shards(): arrived = lax.ppermute(sent, 'space', [(i, i ^ 2) for i in range(count)])]
  transfers between devices with their start and end apart: 7 -> 11, of which waited for: 2 -> 2; matrix products, arithmetic and copies ran while one was open for 0% -> 0% of each run, Pallas kernels for 40% -> 42%
where the time goes in v5:
time: 56.1 us; the launch traced here: 55.9 us
  Pallas kernels  26.7 us (48%)
  starting transfers between devices  26 us (46%)
  waiting for transfers between devices  2.36 us (4%)
  between operations  0.81 us (1%)
    pallas_call x13, Pallas kernels, call(): pl.pallas_call(body, out_shape=list(outs), in_specs=[pl.BlockSpec(memory_...  26.7 us
    ppermute x3, starting transfers between devices, shards(): lax.ppermute(x, 'space', [(i, (i + 4 * hop + 4) % count) for i in range(c...  6.32 us
    ppermute x1, starting transfers between devices, shards(): arrived = lax.ppermute(sent, 'space', [(i, i ^ 2) for i in range(count)])  5.61 us
    ppermute x1, starting transfers between devices, shards(): vol_inner = lax.ppermute(own, 'space', within)  4.36 us
    ppermute x1, starting transfers between devices, shards(): message = lax.ppermute(message, 'space', within)  3.8 us
    ppermute x1, starting transfers between devices, shards(): grad_inner = lax.ppermute(to_inner, 'space', within)  3.6 us
    ppermute x1, waiting for transfers between devices, shards(): arrived = lax.ppermute(sent, 'space', [(i, i ^ 2) for i in range(count)])  1.43 us
  transfers between devices with their start and end apart: 11, of which 2 were waited for; matrix products, arithmetic and copies ran while one was open for 0% of the time, Pallas kernels for 42%

profile of v5, /device:TPU:0, one launch (start us, length us, event | category | flops | bytes accessed | tf_op | source)
XLA Modules:
  0.0 55.9 jit_solution(8276392580450677812)
XLA Ops:
  0.6 1.4 %pack_volume.1.own = bf16[2048,128]{1,0:T(8,128)(2,1)S(1)} custom-call(bf16[2,2048,64]{2,1,0:T(8,128)(2,1)} %bitcast.16), custom_call_target="tpu_custom_call" | custom-call | bytes 1048576 | tf_op jit(solution)/shard_map/pack_volume/pallas_call | solution.py:27
  2.0 0.7 %collective-permute-start.1 = (bf16[2048,128]{1,0:T(8,128)(2,1)S(1)}, bf16[2048,128]{1,0:T(8,128)(2,1)S(1)}, u32[]{:S(2)}, u32[]{:S(2)}) collective-permute-start(bf16[2048,128]{1,0:T(8,128)(2,1)S(1)} %pack_volume.1.own), channel_id=1, source_target_pairs={{1,2},{3,4},{5,6},{7,8},{9,10},{11,12},{13,14},{2,1},{4,3},{6,5},{... | collective-permute-start | bytes 1572872 | tf_op jit(solution)/shard_map/ppermute | solution.py:488
  2.7 4.4 %collective-permute-start = (bf16[2048,128]{1,0:T(8,128)(2,1)S(1)}, bf16[2048,128]{1,0:T(8,128)(2,1)S(1)}, u32[]{:S(2)}, u32[]{:S(2)}) collective-permute-start(bf16[2048,128]{1,0:T(8,128)(2,1)S(1)} %pack_volume.1.own), channel_id=1, source_target_pairs={{0,1},{1,0},{2,3},{3,2},{4,5},{5,4},{6,7},{7,6},{8,9},{9,8},{10,11... | collective-permute-start | bytes 1572872 | tf_op jit(solution)/shard_map/ppermute | solution.py:489
  7.1 4.5 %grad_act_terms.1 = (f32[2048,128]{1,0:T(8,128)S(1)}, bf16[1024,128]{1,0:T(8,128)(2,1)S(1)}, bf16[1024,128]{1,0:T(8,128)(2,1)S(1)}, bf16[256,2048]{1,0:T(8,128)(2,1)S(1)}) custom-call(s32[1]{0:T(128)} %bitcast.me, bf16[2,2048,128]{2,1,0:T(8,128)(2,1)} %bitcast.17, bf16[27,64,128]{2,1,0:T(8,128)(2,1)} %bitcast.13), custom_call_target="tpu_custom_call" | custom-call | flops 1811939328 | bytes 4112388 | tf_op jit(solution)/shard_map/grad_act_terms/pallas_call | solution.py:27
  11.6 2.8 %prepare.1 = (bf16[2112,384]{1,0:T(8,128)(2,1)S(1)}, f32[2048,256]{1,0:T(8,128)S(1)}, bf16[2304,256]{1,0:T(8,128)(2,1)S(1)}, bf16[384,768]{1,0:T(8,128)(2,1)S(1)}) custom-call(bf16[2048,128]{1,0:T(8,128)(2,1)S(1)} %pack_volume.1.own, bf16[27,64,64]{2,1,0:T(8,128)(2,1)} %bitcast.18), custom_call_target="tpu_custom_call" | custom-call | flops 905969664 | bytes 6234112 | tf_op jit(solution)/shard_map/prepare/pallas_call | solution.py:27
  14.4 0.1 collective-permute-start.2
  14.5 0.7 %collective-permute-start.3 = (bf16[1024,128]{1,0:T(8,128)(2,1)S(1)}, bf16[1024,128]{1,0:T(8,128)(2,1)S(1)}, u32[]{:S(2)}, u32[]{:S(2)}) collective-permute-start(bf16[1024,128]{1,0:T(8,128)(2,1)S(1)} %get-tuple-element.56), channel_id=1, source_target_pairs={{1,2},{3,4},{5,6},{7,8},{9,10},{11,12},{13,14},{2,1},{4,3},{6,5},{... | collective-permute-start | bytes 786440 | tf_op jit(solution)/shard_map/ppermute | solution.py:514
  15.2 0.0 collective-permute-done.1.outer
  15.2 0.0 collective-permute-done.inner
  15.2 4.3 %hidden.1 = (bf16[2112,768]{1,0:T(8,128)(2,1)S(1)}, bf16[2112,768]{1,0:T(8,128)(2,1)S(1)}, f32[2048,128]{1,0:T(8,128)S(1)}) custom-call(s32[1]{0:T(128)} %bitcast.me, bf16[2048,128]{1,0:T(8,128)(2,1)S(1)} %collective-permute-done.inner, bf16[2048,128]{1,0:T(8,128)(2,1)S(1)} %collective-permute-done.1.outer, f32[2048,256]{1,0:T(8,128)S(1)} %get-tuple-element.49.part, ...), custom_call_target="tpu_custom_call" | custom-call | flops 1811939328 | bytes 11862020 | tf_op jit(solution)/shard_map/hidden/pallas_call | solution.py:27
  19.5 2.7 %grad_two_terms.1.other = f32[128,1792]{1,0:T(8,128)S(1)} custom-call(bf16[2112,768]{1,0:T(8,128)(2,1)S(1)} %get-tuple-element.67.act_windows, bf16[256,2048]{1,0:T(8,128)(2,1)S(1)} %get-tuple-element.55.turned), custom_call_target="tpu_custom_call" | custom-call | flops 1811939328 | bytes 5210112 | tf_op jit(solution)/shard_map/grad_two_terms/pallas_call | solution.py:27
  22.2 0.0 collective-permute-done.2.inner
  22.2 0.9 %grad_hidden.1 = (bf16[2048,128]{1,0:T(8,128)(2,1)S(1)}, bf16[1024,128]{1,0:T(8,128)(2,1)S(1)}, bf16[1024,128]{1,0:T(8,128)(2,1)S(1)}) custom-call(s32[1]{0:T(128)} %bitcast.me, f32[2048,128]{1,0:T(8,128)S(1)} %get-tuple-element.52.terms, bf16[1024,128]{1,0:T(8,128)(2,1)S(1)} %collective-permute-done.2.inner, ...), custom_call_target="tpu_custom_call" | custom-call | bytes 3670020 | tf_op jit(solution)/shard_map/grad_hidden/pallas_call | solution.py:27
  23.1 3.6 %collective-permute-start.5 = (bf16[1024,128]{1,0:T(8,128)(2,1)S(1)}, bf16[1024,128]{1,0:T(8,128)(2,1)S(1)}, u32[]{:S(2)}, u32[]{:S(2)}) collective-permute-start(bf16[1024,128]{1,0:T(8,128)(2,1)S(1)} %get-tuple-element.63), channel_id=1, source_target_pairs={{0,1},{1,0},{2,3},{3,2},{4,5},{5,4},{6,7},{7,6},{8,9},{9,8},{10,11... | collective-permute-start | bytes 786440 | tf_op jit(solution)/shard_map/ppermute | solution.py:533
  26.7 0.8 %collective-permute-start.6 = (bf16[1024,128]{1,0:T(8,128)(2,1)S(1)}, bf16[1024,128]{1,0:T(8,128)(2,1)S(1)}, u32[]{:S(2)}, u32[]{:S(2)}) collective-permute-start(bf16[1024,128]{1,0:T(8,128)(2,1)S(1)} %get-tuple-element.64), channel_id=1, source_target_pairs={{1,2},{3,4},{5,6},{7,8},{9,10},{11,12},{13,14},{2,1},{4,3},{6,5},{... | collective-permute-start | bytes 786440 | tf_op jit(solution)/shard_map/ppermute | solution.py:532
  27.6 1.8 %grad_one_terms.1 = (bf16[2688,128]{1,0:T(8,128)(2,1)S(1)}, f32[8,24,896]{2,1,0:T(8,128)S(1)}) custom-call(s32[1]{0:T(128)} %bitcast.me, bf16[2112,384]{1,0:T(8,128)(2,1)S(1)} %get-tuple-element.45.own_windows, bf16[2112,768]{1,0:T(8,128)(2,1)S(1)} %get-tuple-element.51.side_windows, bf16[2048,128]{1,0:T(8,128)(2,1)S(1)} %get-tuple-element.59.grad.own, ...), custom_call_target="tpu_custom_call" | custom-call | flops 905969664 | bytes 7684100 | tf_op jit(solution)/shard_map/grad_one_terms/pallas_call | solution.py:27
  29.3 0.0 copy-start
  29.3 3.8 %collective-permute-start.4 = (bf16[2688,128]{1,0:T(8,128)(2,1)S(1)}, bf16[2688,128]{1,0:T(8,128)(2,1)S(1)}, u32[]{:S(2)}, u32[]{:S(2)}) collective-permute-start(bf16[2688,128]{1,0:T(8,128)(2,1)S(1)} %get-tuple-element.62), channel_id=1, source_target_pairs={{0,1},{1,0},{2,3},{3,2},{4,5},{5,4},{6,7},{7,6},{8,9},{9,8},{10,11... | collective-permute-start | bytes 2064392 | tf_op jit(solution)/shard_map/ppermute | solution.py:545
  33.1 0.0 collective-permute-done.5.inner
  33.2 0.0 collective-permute-done.6.outer
  33.2 0.8 %grad_windows.1.windows = bf16[2112,768]{1,0:T(8,128)(2,1)S(1)} custom-call(s32[1]{0:T(128)} %bitcast.me, bf16[2048,128]{1,0:T(8,128)(2,1)S(1)} %get-tuple-element.59.grad.own, bf16[1024,128]{1,0:T(8,128)(2,1)S(1)} %collective-permute-done.5.inner, bf16[1024,128]{1,0:T(8,128)(2,1)S(1)} %collective-permute-done.6.outer), custom_call_target="tpu_custom_call" | custom-call | flops 28991029248 | bytes 4292612 | tf_op jit(solution)/shard_map/grad_windows/pallas_call | solution.py:27
  34.0 0.9 %collective-permute-done.4.message = bf16[2688,128]{1,0:T(8,128)(2,1)S(1)} collective-permute-done((bf16[2688,128]{1,0:T(8,128)(2,1)S(1)}, bf16[2688,128]{1,0:T(8,128)(2,1)S(1)}, u32[]{:S(2)}, u32[]{:S(2)}) %collective-permute-start.4) | collective-permute-done | bytes 688160 | tf_op jit(solution)/shard_map/ppermute | solution.py:545
  34.9 0.1 halve.1
  35.1 5.6 %collective-permute-start.7 = (bf16[4,32,896]{2,1,0:T(8,128)(2,1)S(1)}, bf16[4,32,896]{2,1,0:T(8,128)(2,1)S(1)}, u32[]{:S(2)}, u32[]{:S(2)}) collective-permute-start(bf16[4,32,896]{2,1,0:T(8,128)(2,1)S(1)} %get-tuple-element.69), channel_id=1, source_target_pairs={{0,2},{1,3},{2,0},{3,1},{4,6},{5,7},{6,4},{7,5},{8,10},{9,11},{10,... | collective-permute-start | bytes 688136 | tf_op jit(solution)/shard_map/ppermute | solution.py:557
  40.7 3.7 %output.1 = f32[2,2048,128]{2,1,0:T(8,128)} custom-call(bf16[2112,768]{1,0:T(8,128)(2,1)S(1)} %get-tuple-element.67.act_windows, bf16[27,64,128]{2,1,0:T(8,128)(2,1)S(1)} %bitcast.14), custom_call_target="tpu_custom_call" | custom-call | flops 1811939328 | bytes 5783552 | tf_op jit(solution)/shard_map/output/pallas_call | solution.py:27
  44.4 1.4 %collective-permute-done.7.arrived = bf16[4,32,896]{2,1,0:T(8,128)(2,1)S(1)} collective-permute-done((bf16[4,32,896]{2,1,0:T(8,128)(2,1)S(1)}, bf16[4,32,896]{2,1,0:T(8,128)(2,1)S(1)}, u32[]{:S(2)}, u32[]{:S(2)}) %collective-permute-start.7) | collective-permute-done | bytes 229408 | tf_op jit(solution)/shard_map/ppermute | solution.py:557
  45.9 2.4 %collective-permute-start.8 = (bf16[24,896]{1,0:T(8,128)(2,1)S(1)}, bf16[24,896]{1,0:T(8,128)(2,1)S(1)}, u32[]{:S(2)}, u32[]{:S(2)}) collective-permute-start(bf16[24,896]{1,0:T(8,128)(2,1)S(1)} %get-tuple-element.77), channel_id=1, source_target_pairs={{0,4},{1,5},{2,6},{3,7},{4,8},{5,9},{6,10},{7,11},{8,12},{9,13},{1... | collective-permute-start | bytes 129032 | tf_op jit(solution)/shard_map/ppermute | solution.py:576
  48.2 1.1 %collective-permute-start.9 = (bf16[24,896]{1,0:T(8,128)(2,1)S(1)}, bf16[24,896]{1,0:T(8,128)(2,1)S(1)}, u32[]{:S(2)}, u32[]{:S(2)}) collective-permute-start(bf16[24,896]{1,0:T(8,128)(2,1)S(1)} %get-tuple-element.78), channel_id=1, source_target_pairs={{0,8},{1,9},{2,10},{3,11},{4,12},{5,13},{6,14},{7,15},{8,0},{9,1},... | collective-permute-start | bytes 129032 | tf_op jit(solution)/shard_map/ppermute | solution.py:576
  49.3 2.8 %collective-permute-start.10 = (bf16[24,896]{1,0:T(8,128)(2,1)S(1)}, bf16[24,896]{1,0:T(8,128)(2,1)S(1)}, u32[]{:S(2)}, u32[]{:S(2)}) collective-permute-start(bf16[24,896]{1,0:T(8,128)(2,1)S(1)} %get-tuple-element.79), channel_id=1, source_target_pairs={{0,12},{1,13},{2,14},{3,15},{4,0},{5,1},{6,2},{7,3},{8,4},{9,5},{1... | collective-permute-start | bytes 129032 | tf_op jit(solution)/shard_map/ppermute | solution.py:576
  52.2 2.9 %grad_volume.1 = f32[2,2048,64]{2,1,0:T(8,128)} custom-call(bf16[2112,768]{1,0:T(8,128)(2,1)S(1)} %grad_windows.1.windows, bf16[384,768]{1,0:T(8,128)(2,1)S(1)} %get-tuple-element.75.taps), custom_call_target="tpu_custom_call" | custom-call | flops 905969664 | bytes 4882432 | tf_op jit(solution)/shard_map/grad_volume/pallas_call | solution.py:27
  55.1 0.0 collective-permute-done.9.refs_1_
  55.1 0.7 %finish.1 = (f32[27,4,64]{2,1,0:T(4,128)}, f32[27,8,64]{2,1,0:T(8,128)}) custom-call(f32[24,896]{1,0:T(8,128)S(1)} %get-tuple-element.76.mine, bf16[24,896]{1,0:T(8,128)(2,1)S(1)} %collective-permute-done.8.refs_0_, bf16[24,896]{1,0:T(8,128)(2,1)S(1)} %collective-permute-done.9.refs_1_, bf16[24,896]{1,0:T(8,128)(2,1)S(1)} %collective-permute-done.10.refs_2_), custom_call_target="tpu_custom_call" | custom-call | bytes 297984 | tf_op jit(solution)/shard_map/finish/pallas_call | solution.py:27
  (5 shorter events, 0.1 us)
Async XLA Ops:
  2.0 13.2 %collective-permute-start.1 = (bf16[2048,128]{1,0:T(8,128)(2,1)S(1)}, bf16[2048,128]{1,0:T(8,128)(2,1)S(1)}, u32[]{:S(2)}, u32[]{:S(2)}) collective-permute-start(bf16[2048,128]{1,0:T(8,128)(2,1)S(1)} %pack_volume.1.own), channel_id=1, source_target_pairs={{1,2},{3,4},{5,6},{7,8},{9,10},{11,12},{13,14},{2,1},{4,3},{6,5},{... | collective-permute-start | bytes 1572872 | tf_op jit(solution)/shard_map/ppermute | solution.py:488
  2.7 12.5 %collective-permute-start = (bf16[2048,128]{1,0:T(8,128)(2,1)S(1)}, bf16[2048,128]{1,0:T(8,128)(2,1)S(1)}, u32[]{:S(2)}, u32[]{:S(2)}) collective-permute-start(bf16[2048,128]{1,0:T(8,128)(2,1)S(1)} %pack_volume.1.own), channel_id=1, source_target_pairs={{0,1},{1,0},{2,3},{3,2},{4,5},{5,4},{6,7},{7,6},{8,9},{9,8},{10,11... | collective-permute-start | bytes 1572872 | tf_op jit(solution)/shard_map/ppermute | solution.py:489
  14.4 7.8 %collective-permute-start.2 = (bf16[1024,128]{1,0:T(8,128)(2,1)S(1)}, bf16[1024,128]{1,0:T(8,128)(2,1)S(1)}, u32[]{:S(2)}, u32[]{:S(2)}) collective-permute-start(bf16[1024,128]{1,0:T(8,128)(2,1)S(1)} %get-tuple-element.53), channel_id=1, source_target_pairs={{0,1},{1,0},{2,3},{3,2},{4,5},{5,4},{6,7},{7,6},{8,9},{9,8},{10,11... | collective-permute-start | bytes 786440 | tf_op jit(solution)/shard_map/ppermute | solution.py:515
  14.5 7.7 %collective-permute-start.3 = (bf16[1024,128]{1,0:T(8,128)(2,1)S(1)}, bf16[1024,128]{1,0:T(8,128)(2,1)S(1)}, u32[]{:S(2)}, u32[]{:S(2)}) collective-permute-start(bf16[1024,128]{1,0:T(8,128)(2,1)S(1)} %get-tuple-element.56), channel_id=1, source_target_pairs={{1,2},{3,4},{5,6},{7,8},{9,10},{11,12},{13,14},{2,1},{4,3},{6,5},{... | collective-permute-start | bytes 786440 | tf_op jit(solution)/shard_map/ppermute | solution.py:514
  23.1 10.0 %collective-permute-start.5 = (bf16[1024,128]{1,0:T(8,128)(2,1)S(1)}, bf16[1024,128]{1,0:T(8,128)(2,1)S(1)}, u32[]{:S(2)}, u32[]{:S(2)}) collective-permute-start(bf16[1024,128]{1,0:T(8,128)(2,1)S(1)} %get-tuple-element.63), channel_id=1, source_target_pairs={{0,1},{1,0},{2,3},{3,2},{4,5},{5,4},{6,7},{7,6},{8,9},{9,8},{10,11... | collective-permute-start | bytes 786440 | tf_op jit(solution)/shard_map/ppermute | solution.py:533
  26.7 6.4 %collective-permute-start.6 = (bf16[1024,128]{1,0:T(8,128)(2,1)S(1)}, bf16[1024,128]{1,0:T(8,128)(2,1)S(1)}, u32[]{:S(2)}, u32[]{:S(2)}) collective-permute-start(bf16[1024,128]{1,0:T(8,128)(2,1)S(1)} %get-tuple-element.64), channel_id=1, source_target_pairs={{1,2},{3,4},{5,6},{7,8},{9,10},{11,12},{13,14},{2,1},{4,3},{6,5},{... | collective-permute-start | bytes 786440 | tf_op jit(solution)/shard_map/ppermute | solution.py:532
  29.3 11.3 %copy-start = (bf16[3,3,3,64,128]{4,3,2,1,0:T(8,128)(2,1)S(1)}, bf16[3,3,3,64,128]{4,3,2,1,0:T(8,128)(2,1)}, u32[]{:S(2)}) copy-start(bf16[3,3,3,64,128]{4,3,2,1,0:T(8,128)(2,1)} %param.6) | copy-start | bytes 1327108
  29.3 5.6 %collective-permute-start.4 = (bf16[2688,128]{1,0:T(8,128)(2,1)S(1)}, bf16[2688,128]{1,0:T(8,128)(2,1)S(1)}, u32[]{:S(2)}, u32[]{:S(2)}) collective-permute-start(bf16[2688,128]{1,0:T(8,128)(2,1)S(1)} %get-tuple-element.62), channel_id=1, source_target_pairs={{0,1},{1,0},{2,3},{3,2},{4,5},{5,4},{6,7},{7,6},{8,9},{9,8},{10,11... | collective-permute-start | bytes 2064392 | tf_op jit(solution)/shard_map/ppermute | solution.py:545
  35.1 10.8 %collective-permute-start.7 = (bf16[4,32,896]{2,1,0:T(8,128)(2,1)S(1)}, bf16[4,32,896]{2,1,0:T(8,128)(2,1)S(1)}, u32[]{:S(2)}, u32[]{:S(2)}) collective-permute-start(bf16[4,32,896]{2,1,0:T(8,128)(2,1)S(1)} %get-tuple-element.69), channel_id=1, source_target_pairs={{0,2},{1,3},{2,0},{3,1},{4,6},{5,7},{6,4},{7,5},{8,10},{9,11},{10,... | collective-permute-start | bytes 688136 | tf_op jit(solution)/shard_map/ppermute | solution.py:557
  45.9 9.2 %collective-permute-start.8 = (bf16[24,896]{1,0:T(8,128)(2,1)S(1)}, bf16[24,896]{1,0:T(8,128)(2,1)S(1)}, u32[]{:S(2)}, u32[]{:S(2)}) collective-permute-start(bf16[24,896]{1,0:T(8,128)(2,1)S(1)} %get-tuple-element.77), channel_id=1, source_target_pairs={{0,4},{1,5},{2,6},{3,7},{4,8},{5,9},{6,10},{7,11},{8,12},{9,13},{1... | collective-permute-start | bytes 129032 | tf_op jit(solution)/shard_map/ppermute | solution.py:576
  48.2 6.9 %collective-permute-start.9 = (bf16[24,896]{1,0:T(8,128)(2,1)S(1)}, bf16[24,896]{1,0:T(8,128)(2,1)S(1)}, u32[]{:S(2)}, u32[]{:S(2)}) collective-permute-start(bf16[24,896]{1,0:T(8,128)(2,1)S(1)} %get-tuple-element.78), channel_id=1, source_target_pairs={{0,8},{1,9},{2,10},{3,11},{4,12},{5,13},{6,14},{7,15},{8,0},{9,1},... | collective-permute-start | bytes 129032 | tf_op jit(solution)/shard_map/ppermute | solution.py:576
  49.3 5.8 %collective-permute-start.10 = (bf16[24,896]{1,0:T(8,128)(2,1)S(1)}, bf16[24,896]{1,0:T(8,128)(2,1)S(1)}, u32[]{:S(2)}, u32[]{:S(2)}) collective-permute-start(bf16[24,896]{1,0:T(8,128)(2,1)S(1)} %get-tuple-element.79), channel_id=1, source_target_pairs={{0,12},{1,13},{2,14},{3,15},{4,0},{5,1},{6,2},{7,3},{8,4},{9,5},{1... | collective-permute-start | bytes 129032 | tf_op jit(solution)/shard_map/ppermute | solution.py:576

commit v6 on v5

--- a/solution.py
+++ b/solution.py
@@ -363,20 +363,17 @@
         kept[pair] = total(2 * pair + odd)
 
 
-def spread_body(split, me, mine, arrived, kept, *sent):
-    ring = mine.shape[0]
+def spread_body(split, me, mine, arrived, sent, kept):
     place = me[0] // 4
+    for at in range(mine.shape[0]):
+        sent[at] = (mine[at] + decoded(arrived[at], split)).astype(BF16)
     kept[...] = mine[place] + decoded(arrived[place], split)
-    for hop, out in enumerate(sent):
-        there = (place + hop + 1) % ring
-        out[...] = (mine[there] + decoded(arrived[there], split)).astype(BF16)
-
-
-def finish_body(scale, sizes, mine, *refs):
-    arrived, (grad_one, grad_two) = refs[:-2], refs[-2:]
+
+
+def finish_body(scale, sizes, me, mine, arrived, grad_one, grad_two):
     total = mine[...]
-    for part in arrived:
-        total = total + part[...].astype(F32)
+    for at in range(arrived.shape[0]):
+        total = total + jnp.where(at == me[0] // 4, 0.0, arrived[at].astype(F32))
     total = total * scale
     half = total.shape[1]
     first = 0
@@ -519,18 +516,18 @@
         (me, vol_inner, vol_outer, part, side_taps),
         (), 2 * one_flops, "hidden", (0,),
     )
+    grad_hidden, to_inner, outer = call(
+        slope_body, (flat, pack, pack), (me, terms, terms_inner, terms_outer, slope),
+        name="grad_hidden", smem=(0,),
+    )
+    grad_outer = lax.ppermute(outer, "space", across)
+    grad_inner = lax.ppermute(to_inner, "space", within)
+    act_windows, grad_hidden = lax.optimization_barrier((act_windows, grad_hidden))
     terms_two, = call(
         functools.partial(grad_two_body, columns),
         (shape((wide, 2 * lanes), F32),),
         (act_windows, turned), (), two_flops, "grad_two_terms",
     )
-    terms_two, terms_outer = lax.optimization_barrier((terms_two, terms_outer))
-    grad_hidden, to_inner, outer = call(
-        slope_body, (flat, pack, pack), (me, terms, terms_inner, terms_outer, slope),
-        name="grad_hidden", smem=(0,),
-    )
-    grad_outer = lax.ppermute(outer, "space", across)
-    grad_inner = lax.ppermute(to_inner, "space", within)
     groups = lanes // 128
     message, kept = call(
         functools.partial(grad_one_body, columns, count),
@@ -565,17 +562,16 @@
         ),
         two_flops, "output", (), (), True,
     )
-    ring = count // 4
-    mine, *sent = call(
+    sent, mine = call(
         functools.partial(spread_body, split),
-        (shares()[1], *[shape((chunk, lanes), BF16)] * (ring - 1)),
+        (shape((count // 4, chunk, lanes), BF16), shares()[1]),
         (me, kept, arrived), name="spread", smem=(0,),
     )
     sent, grad_windows = lax.optimization_barrier((sent, grad_windows))
-    rest = [
-        lax.ppermute(x, "space", [(i, (i + 4 * hop + 4) % count) for i in range(count)])
-        for hop, x in enumerate(sent)
-    ]
+    arrived = lax.all_to_all(
+        sent, "space", 0, 0, tiled=True,
+        axis_index_groups=[list(range(i, count, 4)) for i in range(4)],
+    )
     grad_volume, = call(
         functools.partial(grad_volume_body, columns),
         (shape((planes, cells, channels), F32),),
@@ -586,7 +582,7 @@
     grad_one, grad_two = call(
         functools.partial(finish_body, scale, (mid // count, wide // count)),
         (shape((27, mid // count, channels), F32), shape((27, wide // count, mid), F32)),
-        (mine, *rest), name="finish",
+        (me, mine, arrived), name="finish", smem=(0,),
     )
     return (
         output.reshape(planes, rows, columns, wide),

time: 56.1 us -> 60.9 us (1.086)
  waiting for transfers between devices: 2.36 us -> 6.07 us
  local copies, waits for them, and re-layouts: 0.01 us -> 3.6 us
  starting transfers between devices: 26 us -> 23.2 us
    ppermute x3 -> x0, starting transfers between devices: 6.32 us -> none  [shards(): lax.ppermute(x, 'space', [(i, (i + 4 * hop + 4) % count) for i in range(c...]
    all_to_all x0 -> x1, starting transfers between devices: none -> 4.98 us  [shards(): lax.all_to_all(sent, 'space', 0, 0, tiled=True, axis_index_groups=[list(r...]
    ppermute x1, waiting for transfers between devices: 1.43 us -> 5.14 us  [shards(): arrived = lax.ppermute(sent, 'space', [(i, i ^ 2) for i in range(count)])]
    unnamed x2 -> x12, local copies, waits for them, and re-layouts: 0.01 us -> 3.6 us
    ppermute x1, starting transfers between devices: 5.61 us -> 3.07 us  [shards(): arrived = lax.ppermute(sent, 'space', [(i, i ^ 2) for i in range(count)])]
    ppermute x1, starting transfers between devices: 3.6 us -> 4.9 us  [shards(): grad_inner = lax.ppermute(to_inner, 'space', within)]
  transfers between devices with their start and end apart: 11 -> 9, of which waited for: 2 -> 2; matrix products, arithmetic and copies ran while one was open for 0% -> 0% of each run, Pallas kernels for 42% -> 39%
where the time goes in v6:
time: 60.9 us; the launch traced here: 60.4 us
  Pallas kernels  26.7 us (44%)
  starting transfers between devices  23.2 us (38%)
  waiting for transfers between devices  6.07 us (10%)
  local copies, waits for them, and re-layouts  3.6 us (6%)
  between operations  0.83 us (1%)
    pallas_call x13, Pallas kernels, call(): pl.pallas_call(body, out_shape=list(outs), in_specs=[pl.BlockSpec(memory_...  26.7 us
    ppermute x1, waiting for transfers between devices, shards(): arrived = lax.ppermute(sent, 'space', [(i, i ^ 2) for i in range(count)])  5.14 us
    all_to_all x1, starting transfers between devices, shards(): lax.all_to_all(sent, 'space', 0, 0, tiled=True, axis_index_groups=[list(r...  4.98 us
    ppermute x1, starting transfers between devices, shards(): grad_inner = lax.ppermute(to_inner, 'space', within)  4.9 us
    ppermute x1, starting transfers between devices, shards(): vol_inner = lax.ppermute(own, 'space', within)  4.36 us
    ppermute x1, starting transfers between devices, shards(): message = lax.ppermute(message, 'space', within)  3.8 us
    unnamed x12, local copies, waits for them, and re-layouts  3.6 us
    ppermute x1, starting transfers between devices, shards(): arrived = lax.ppermute(sent, 'space', [(i, i ^ 2) for i in range(count)])  3.07 us
  transfers between devices with their start and end apart: 9, of which 2 were waited for; matrix products, arithmetic and copies ran while one was open for 0% of the time, Pallas kernels for 39%

profile of v6, /device:TPU:0, one launch (start us, length us, event | category | flops | bytes accessed | tf_op | source)
XLA Modules:
  0.0 60.4 jit_solution(722193975539829409)
XLA Ops:
  0.6 1.4 %pack_volume.1.own = bf16[2048,128]{1,0:T(8,128)(2,1)S(1)} custom-call(bf16[2,2048,64]{2,1,0:T(8,128)(2,1)} %bitcast.16), custom_call_target="tpu_custom_call" | custom-call | bytes 1048576 | tf_op jit(solution)/shard_map/pack_volume/pallas_call | solution.py:27
  2.0 0.7 %collective-permute-start.1 = (bf16[2048,128]{1,0:T(8,128)(2,1)S(1)}, bf16[2048,128]{1,0:T(8,128)(2,1)S(1)}, u32[]{:S(2)}, u32[]{:S(2)}) collective-permute-start(bf16[2048,128]{1,0:T(8,128)(2,1)S(1)} %pack_volume.1.own), channel_id=1, source_target_pairs={{1,2},{3,4},{5,6},{7,8},{9,10},{11,12},{13,14},{2,1},{4,3},{6,5},{... | collective-permute-start | bytes 1572872 | tf_op jit(solution)/shard_map/ppermute | solution.py:485
  2.7 4.4 %collective-permute-start = (bf16[2048,128]{1,0:T(8,128)(2,1)S(1)}, bf16[2048,128]{1,0:T(8,128)(2,1)S(1)}, u32[]{:S(2)}, u32[]{:S(2)}) collective-permute-start(bf16[2048,128]{1,0:T(8,128)(2,1)S(1)} %pack_volume.1.own), channel_id=1, source_target_pairs={{0,1},{1,0},{2,3},{3,2},{4,5},{5,4},{6,7},{7,6},{8,9},{9,8},{10,11... | collective-permute-start | bytes 1572872 | tf_op jit(solution)/shard_map/ppermute | solution.py:486
  7.1 4.5 %grad_act_terms.1 = (f32[2048,128]{1,0:T(8,128)S(1)}, bf16[1024,128]{1,0:T(8,128)(2,1)S(1)}, bf16[1024,128]{1,0:T(8,128)(2,1)S(1)}, bf16[256,2048]{1,0:T(8,128)(2,1)S(1)}) custom-call(s32[1]{0:T(128)} %bitcast.me, bf16[2,2048,128]{2,1,0:T(8,128)(2,1)} %bitcast.17, bf16[27,64,128]{2,1,0:T(8,128)(2,1)} %bitcast.13), custom_call_target="tpu_custom_call" | custom-call | flops 1811939328 | bytes 4112388 | tf_op jit(solution)/shard_map/grad_act_terms/pallas_call | solution.py:27
  11.6 2.8 %prepare.1 = (bf16[2112,384]{1,0:T(8,128)(2,1)S(1)}, f32[2048,256]{1,0:T(8,128)S(1)}, bf16[2304,256]{1,0:T(8,128)(2,1)S(1)}, bf16[384,768]{1,0:T(8,128)(2,1)S(1)}) custom-call(bf16[2048,128]{1,0:T(8,128)(2,1)S(1)} %pack_volume.1.own, bf16[27,64,64]{2,1,0:T(8,128)(2,1)} %bitcast.18), custom_call_target="tpu_custom_call" | custom-call | flops 905969664 | bytes 6234112 | tf_op jit(solution)/shard_map/prepare/pallas_call | solution.py:27
  14.4 0.0 copy-start
  14.4 0.1 collective-permute-start.2
  14.5 0.7 %collective-permute-start.3 = (bf16[1024,128]{1,0:T(8,128)(2,1)S(1)}, bf16[1024,128]{1,0:T(8,128)(2,1)S(1)}, u32[]{:S(2)}, u32[]{:S(2)}) collective-permute-start(bf16[1024,128]{1,0:T(8,128)(2,1)S(1)} %get-tuple-element.51), channel_id=1, source_target_pairs={{1,2},{3,4},{5,6},{7,8},{9,10},{11,12},{13,14},{2,1},{4,3},{6,5},{... | collective-permute-start | bytes 786440 | tf_op jit(solution)/shard_map/ppermute | solution.py:511
  15.2 0.0 collective-permute-done.1.outer
  15.2 0.0 collective-permute-done.inner
  15.2 4.3 %hidden.1 = (bf16[2112,768]{1,0:T(8,128)(2,1)S(1)}, bf16[2112,768]{1,0:T(8,128)(2,1)S(1)}, f32[2048,128]{1,0:T(8,128)S(1)}) custom-call(s32[1]{0:T(128)} %bitcast.me, bf16[2048,128]{1,0:T(8,128)(2,1)S(1)} %collective-permute-done.inner, bf16[2048,128]{1,0:T(8,128)(2,1)S(1)} %collective-permute-done.1.outer, f32[2048,256]{1,0:T(8,128)S(1)} %get-tuple-element.45.part, ...), custom_call_target="tpu_custom_call" | custom-call | flops 1811939328 | bytes 11862020 | tf_op jit(solution)/shard_map/hidden/pallas_call | solution.py:27
  19.5 0.0 collective-permute-done.2.inner
  19.5 0.0 collective-permute-done.3.outer
  19.5 0.8 %grad_hidden.1 = (bf16[2048,128]{1,0:T(8,128)(2,1)S(1)}, bf16[1024,128]{1,0:T(8,128)(2,1)S(1)}, bf16[1024,128]{1,0:T(8,128)(2,1)S(1)}) custom-call(s32[1]{0:T(128)} %bitcast.me, f32[2048,128]{1,0:T(8,128)S(1)} %get-tuple-element.49.terms, bf16[1024,128]{1,0:T(8,128)(2,1)S(1)} %collective-permute-done.2.inner, ...), custom_call_target="tpu_custom_call" | custom-call | bytes 3670020 | tf_op jit(solution)/shard_map/grad_hidden/pallas_call | solution.py:27
  20.4 4.9 %collective-permute-start.5 = (bf16[1024,128]{1,0:T(8,128)(2,1)S(1)}, bf16[1024,128]{1,0:T(8,128)(2,1)S(1)}, u32[]{:S(2)}, u32[]{:S(2)}) collective-permute-start(bf16[1024,128]{1,0:T(8,128)(2,1)S(1)} %get-tuple-element.59), channel_id=1, source_target_pairs={{0,1},{1,0},{2,3},{3,2},{4,5},{5,4},{6,7},{7,6},{8,9},{9,8},{10,11... | collective-permute-start | bytes 786440 | tf_op jit(solution)/shard_map/ppermute | solution.py:524
  25.3 0.7 %collective-permute-start.6 = (bf16[1024,128]{1,0:T(8,128)(2,1)S(1)}, bf16[1024,128]{1,0:T(8,128)(2,1)S(1)}, u32[]{:S(2)}, u32[]{:S(2)}) collective-permute-start(bf16[1024,128]{1,0:T(8,128)(2,1)S(1)} %get-tuple-element.60), channel_id=1, source_target_pairs={{1,2},{3,4},{5,6},{7,8},{9,10},{11,12},{13,14},{2,1},{4,3},{6,5},{... | collective-permute-start | bytes 786440 | tf_op jit(solution)/shard_map/ppermute | solution.py:523
  26.0 2.8 %grad_two_terms.1.other = f32[128,1792]{1,0:T(8,128)S(1)} custom-call(bf16[2112,768]{1,0:T(8,128)(2,1)S(1)} %get-tuple-element.63.act_windows, bf16[256,2048]{1,0:T(8,128)(2,1)S(1)} %get-tuple-element.56.turned), custom_call_target="tpu_custom_call" | custom-call | flops 1811939328 | bytes 5210112 | tf_op jit(solution)/shard_map/grad_two_terms/pallas_call | solution.py:27
  28.7 1.7 %grad_one_terms.1 = (bf16[2688,128]{1,0:T(8,128)(2,1)S(1)}, f32[8,24,896]{2,1,0:T(8,128)S(1)}) custom-call(s32[1]{0:T(128)} %bitcast.me, bf16[2112,384]{1,0:T(8,128)(2,1)S(1)} %get-tuple-element.41.own_windows, bf16[2112,768]{1,0:T(8,128)(2,1)S(1)} %get-tuple-element.47.side_windows, bf16[2048,128]{1,0:T(8,128)(2,1)S(1)} %get-tuple-element.54.grad.own, ...), custom_call_target="tpu_custom_call" | custom-call | flops 905969664 | bytes 7684100 | tf_op jit(solution)/shard_map/grad_one_terms/pallas_call | solution.py:27
  30.5 3.8 %collective-permute-start.4 = (bf16[2688,128]{1,0:T(8,128)(2,1)S(1)}, bf16[2688,128]{1,0:T(8,128)(2,1)S(1)}, u32[]{:S(2)}, u32[]{:S(2)}) collective-permute-start(bf16[2688,128]{1,0:T(8,128)(2,1)S(1)} %get-tuple-element.58), channel_id=1, source_target_pairs={{0,1},{1,0},{2,3},{3,2},{4,5},{5,4},{6,7},{7,6},{8,9},{9,8},{10,11... | collective-permute-start | bytes 2064392 | tf_op jit(solution)/shard_map/ppermute | solution.py:542
  34.3 0.8 %grad_windows.1.windows = bf16[2112,768]{1,0:T(8,128)(2,1)S(1)} custom-call(s32[1]{0:T(128)} %bitcast.me, bf16[2048,128]{1,0:T(8,128)(2,1)S(1)} %get-tuple-element.54.grad.own, bf16[1024,128]{1,0:T(8,128)(2,1)S(1)} %collective-permute-done.5.inner, bf16[1024,128]{1,0:T(8,128)(2,1)S(1)} %collective-permute-done.6.outer), custom_call_target="tpu_custom_call" | custom-call | flops 28991029248 | bytes 4292612 | tf_op jit(solution)/shard_map/grad_windows/pallas_call | solution.py:27
  35.1 0.9 %collective-permute-done.4.message = bf16[2688,128]{1,0:T(8,128)(2,1)S(1)} collective-permute-done((bf16[2688,128]{1,0:T(8,128)(2,1)S(1)}, bf16[2688,128]{1,0:T(8,128)(2,1)S(1)}, u32[]{:S(2)}, u32[]{:S(2)}) %collective-permute-start.4) | collective-permute-done | bytes 688160 | tf_op jit(solution)/shard_map/ppermute | solution.py:542
  36.0 0.1 halve.1
  36.2 3.1 %collective-permute-start.7 = (bf16[4,32,896]{2,1,0:T(8,128)(2,1)S(1)}, bf16[4,32,896]{2,1,0:T(8,128)(2,1)S(1)}, u32[]{:S(2)}, u32[]{:S(2)}) collective-permute-start(bf16[4,32,896]{2,1,0:T(8,128)(2,1)S(1)} %get-tuple-element.65), channel_id=1, source_target_pairs={{0,2},{1,3},{2,0},{3,1},{4,6},{5,7},{6,4},{7,5},{8,10},{9,11},{10,... | collective-permute-start | bytes 688136 | tf_op jit(solution)/shard_map/ppermute | solution.py:554
  39.3 5.1 %collective-permute-done.7.arrived = bf16[4,32,896]{2,1,0:T(8,128)(2,1)S(1)} collective-permute-done((bf16[4,32,896]{2,1,0:T(8,128)(2,1)S(1)}, bf16[4,32,896]{2,1,0:T(8,128)(2,1)S(1)}, u32[]{:S(2)}, u32[]{:S(2)}) %collective-permute-start.7) | collective-permute-done | bytes 229408 | tf_op jit(solution)/shard_map/ppermute | solution.py:554
  44.5 0.7 %copy-done.2 = bf16[4,24,896]{2,1,0:T(8,128)(2,1)} copy-done((bf16[4,24,896]{2,1,0:T(8,128)(2,1)}, bf16[4,24,896]{2,1,0:T(8,128)(2,1)S(1)}, u32[]{:S(2)}) %copy-start.2) | copy-done | bytes 172056
  45.1 5.0 %all-to-all-start = ((bf16[4,24,896]{2,1,0:T(8,128)(2,1)}), bf16[4,24,896]{2,1,0:T(8,128)(2,1)S(1)}, u32[]{:S(2)}, u32[]{:S(2)}) async-start(bf16[4,24,896]{2,1,0:T(8,128)(2,1)} %copy-done.2), calls=%async_computation | async-start | bytes 344064 | tf_op jit(solution)/shard_map/all_to_all | solution.py:571
  50.1 1.0 %copy-done.3 = bf16[3,3,3,64,128]{4,3,2,1,0:T(8,128)(2,1)S(1)} copy-done((bf16[3,3,3,64,128]{4,3,2,1,0:T(8,128)(2,1)S(1)}, bf16[3,3,3,64,128]{4,3,2,1,0:T(8,128)(2,1)}, u32[]{:S(2)}) %copy-start.3) | copy-done | bytes 442392
  51.1 1.9 %copy-done.5 = bf16[2112,768]{1,0:T(8,128)(2,1)S(1)} copy-done((bf16[2112,768]{1,0:T(8,128)(2,1)S(1)}, bf16[2112,768]{1,0:T(8,128)(2,1)}, u32[]{:S(2)}) %copy-start.5) | copy-done | bytes 3244056
  53.0 3.7 %output.1 = f32[2,2048,128]{2,1,0:T(8,128)} custom-call(bf16[2112,768]{1,0:T(8,128)(2,1)S(1)} %copy-done.5, bf16[27,64,128]{2,1,0:T(8,128)(2,1)S(1)} %bitcast.14), custom_call_target="tpu_custom_call" | custom-call | flops 1811939328 | bytes 5783552 | tf_op jit(solution)/shard_map/output/pallas_call | solution.py:27
  56.7 2.9 %grad_volume.1 = f32[2,2048,64]{2,1,0:T(8,128)} custom-call(bf16[2112,768]{1,0:T(8,128)(2,1)S(1)} %grad_windows.1.windows, bf16[384,768]{1,0:T(8,128)(2,1)S(1)} %copy-done.1), custom_call_target="tpu_custom_call" | custom-call | flops 905969664 | bytes 4882432 | tf_op jit(solution)/shard_map/grad_volume/pallas_call | solution.py:27
  59.7 0.0 all-to-all-done.arrived
  59.7 0.8 %finish.1 = (f32[27,4,64]{2,1,0:T(4,128)}, f32[27,8,64]{2,1,0:T(8,128)}) custom-call(s32[1]{0:T(128)} %bitcast.me, f32[24,896]{1,0:T(8,128)S(1)} %get-tuple-element.70.mine, bf16[4,24,896]{2,1,0:T(8,128)(2,1)S(1)} %all-to-all-done.arrived), custom_call_target="tpu_custom_call" | custom-call | bytes 340996 | tf_op jit(solution)/shard_map/finish/pallas_call | solution.py:27
  (11 shorter events, 0.1 us)
Async XLA Ops:
  2.0 13.2 %collective-permute-start.1 = (bf16[2048,128]{1,0:T(8,128)(2,1)S(1)}, bf16[2048,128]{1,0:T(8,128)(2,1)S(1)}, u32[]{:S(2)}, u32[]{:S(2)}) collective-permute-start(bf16[2048,128]{1,0:T(8,128)(2,1)S(1)} %pack_volume.1.own), channel_id=1, source_target_pairs={{1,2},{3,4},{5,6},{7,8},{9,10},{11,12},{13,14},{2,1},{4,3},{6,5},{... | collective-permute-start | bytes 1572872 | tf_op jit(solution)/shard_map/ppermute | solution.py:485
  2.7 12.5 %collective-permute-start = (bf16[2048,128]{1,0:T(8,128)(2,1)S(1)}, bf16[2048,128]{1,0:T(8,128)(2,1)S(1)}, u32[]{:S(2)}, u32[]{:S(2)}) collective-permute-start(bf16[2048,128]{1,0:T(8,128)(2,1)S(1)} %pack_volume.1.own), channel_id=1, source_target_pairs={{0,1},{1,0},{2,3},{3,2},{4,5},{5,4},{6,7},{7,6},{8,9},{9,8},{10,11... | collective-permute-start | bytes 1572872 | tf_op jit(solution)/shard_map/ppermute | solution.py:486
  14.4 5.1 %copy-start = (bf16[384,768]{1,0:T(8,128)(2,1)}, bf16[384,768]{1,0:T(8,128)(2,1)S(1)}, u32[]{:S(2)}) copy-start(bf16[384,768]{1,0:T(8,128)(2,1)S(1)} %get-tuple-element.69.taps) | copy-start | bytes 1769476
  14.4 5.1 %collective-permute-start.2 = (bf16[1024,128]{1,0:T(8,128)(2,1)S(1)}, bf16[1024,128]{1,0:T(8,128)(2,1)S(1)}, u32[]{:S(2)}, u32[]{:S(2)}) collective-permute-start(bf16[1024,128]{1,0:T(8,128)(2,1)S(1)} %get-tuple-element.50), channel_id=1, source_target_pairs={{0,1},{1,0},{2,3},{3,2},{4,5},{5,4},{6,7},{7,6},{8,9},{9,8},{10,11... | collective-permute-start | bytes 786440 | tf_op jit(solution)/shard_map/ppermute | solution.py:512
  14.5 5.0 %collective-permute-start.3 = (bf16[1024,128]{1,0:T(8,128)(2,1)S(1)}, bf16[1024,128]{1,0:T(8,128)(2,1)S(1)}, u32[]{:S(2)}, u32[]{:S(2)}) collective-permute-start(bf16[1024,128]{1,0:T(8,128)(2,1)S(1)} %get-tuple-element.51), channel_id=1, source_target_pairs={{1,2},{3,4},{5,6},{7,8},{9,10},{11,12},{13,14},{2,1},{4,3},{6,5},{... | collective-permute-start | bytes 786440 | tf_op jit(solution)/shard_map/ppermute | solution.py:511
  19.5 9.2 %copy-start.4 = (bf16[2112,768]{1,0:T(8,128)(2,1)}, bf16[2112,768]{1,0:T(8,128)(2,1)S(1)}, u32[]{:S(2)}) copy-start(bf16[2112,768]{1,0:T(8,128)(2,1)S(1)} %get-tuple-element.63.act_windows) | copy-start | bytes 9732100
  20.4 13.9 %collective-permute-start.5 = (bf16[1024,128]{1,0:T(8,128)(2,1)S(1)}, bf16[1024,128]{1,0:T(8,128)(2,1)S(1)}, u32[]{:S(2)}, u32[]{:S(2)}) collective-permute-start(bf16[1024,128]{1,0:T(8,128)(2,1)S(1)} %get-tuple-element.59), channel_id=1, source_target_pairs={{0,1},{1,0},{2,3},{3,2},{4,5},{5,4},{6,7},{7,6},{8,9},{9,8},{10,11... | collective-permute-start | bytes 786440 | tf_op jit(solution)/shard_map/ppermute | solution.py:524
  25.3 9.0 %collective-permute-start.6 = (bf16[1024,128]{1,0:T(8,128)(2,1)S(1)}, bf16[1024,128]{1,0:T(8,128)(2,1)S(1)}, u32[]{:S(2)}, u32[]{:S(2)}) collective-permute-start(bf16[1024,128]{1,0:T(8,128)(2,1)S(1)} %get-tuple-element.60), channel_id=1, source_target_pairs={{1,2},{3,4},{5,6},{7,8},{9,10},{11,12},{13,14},{2,1},{4,3},{6,5},{... | collective-permute-start | bytes 786440 | tf_op jit(solution)/shard_map/ppermute | solution.py:523
  30.5 5.6 %collective-permute-start.4 = (bf16[2688,128]{1,0:T(8,128)(2,1)S(1)}, bf16[2688,128]{1,0:T(8,128)(2,1)S(1)}, u32[]{:S(2)}, u32[]{:S(2)}) collective-permute-start(bf16[2688,128]{1,0:T(8,128)(2,1)S(1)} %get-tuple-element.58), channel_id=1, source_target_pairs={{0,1},{1,0},{2,3},{3,2},{4,5},{5,4},{6,7},{7,6},{8,9},{9,8},{10,11... | collective-permute-start | bytes 2064392 | tf_op jit(solution)/shard_map/ppermute | solution.py:542
  36.2 8.2 %collective-permute-start.7 = (bf16[4,32,896]{2,1,0:T(8,128)(2,1)S(1)}, bf16[4,32,896]{2,1,0:T(8,128)(2,1)S(1)}, u32[]{:S(2)}, u32[]{:S(2)}) collective-permute-start(bf16[4,32,896]{2,1,0:T(8,128)(2,1)S(1)} %get-tuple-element.65), channel_id=1, source_target_pairs={{0,2},{1,3},{2,0},{3,1},{4,6},{5,7},{6,4},{7,5},{8,10},{9,11},{10,... | collective-permute-start | bytes 688136 | tf_op jit(solution)/shard_map/ppermute | solution.py:554
  44.4 0.7 %copy-start.2 = (bf16[4,24,896]{2,1,0:T(8,128)(2,1)}, bf16[4,24,896]{2,1,0:T(8,128)(2,1)S(1)}, u32[]{:S(2)}) copy-start(bf16[4,24,896]{2,1,0:T(8,128)(2,1)S(1)} %get-tuple-element.71) | copy-start | bytes 516100
  45.1 14.6 %all-to-all-start = ((bf16[4,24,896]{2,1,0:T(8,128)(2,1)}), bf16[4,24,896]{2,1,0:T(8,128)(2,1)S(1)}, u32[]{:S(2)}, u32[]{:S(2)}) async-start(bf16[4,24,896]{2,1,0:T(8,128)(2,1)} %copy-done.2), calls=%async_computation | async-start | bytes 344064 | tf_op jit(solution)/shard_map/all_to_all | solution.py:571
  50.1 1.0 %copy-start.3 = (bf16[3,3,3,64,128]{4,3,2,1,0:T(8,128)(2,1)S(1)}, bf16[3,3,3,64,128]{4,3,2,1,0:T(8,128)(2,1)}, u32[]{:S(2)}) copy-start(bf16[3,3,3,64,128]{4,3,2,1,0:T(8,128)(2,1)} %param.6) | copy-start | bytes 1327108
  51.1 1.9 %copy-start.5 = (bf16[2112,768]{1,0:T(8,128)(2,1)S(1)}, bf16[2112,768]{1,0:T(8,128)(2,1)}, u32[]{:S(2)}) copy-start(bf16[2112,768]{1,0:T(8,128)(2,1)} %copy-done.4) | copy-start | bytes 9732100
  53.0 3.7 %copy-start.1 = (bf16[384,768]{1,0:T(8,128)(2,1)S(1)}, bf16[384,768]{1,0:T(8,128)(2,1)}, u32[]{:S(2)}) copy-start(bf16[384,768]{1,0:T(8,128)(2,1)} %copy-done) | copy-start | bytes 1769476

commit v7 on v5

--- a/solution.py
+++ b/solution.py
@@ -165,7 +165,7 @@
 
 
 def prepare_body(
-    columns, own, far_weight, own_windows, hidden, side_taps, back_taps, own_taps, weight, sem
+    columns, own, far_weight, own_windows, hidden, side_taps, own_taps, weight, sem
 ):
     fetch = pltpu.make_async_copy(far_weight, weight, sem)
     fetch.start()
@@ -192,6 +192,15 @@
                     target, first = side_taps, tap * 256 + (at - 2) * 64
                 target[first : first + 64, :128] = jnp.concatenate(parts[:2], axis=1)
                 target[first : first + 64, 128:] = jnp.concatenate(parts[2:], axis=1)
+    for start in range(0, own.shape[0], BLOCK):
+        hidden[start : start + BLOCK, :] = window_dot(own_windows, own_taps, start, columns, NN)
+
+
+def back_taps_body(weight, back_taps):
+    zero = jnp.zeros((64, 64), BF16)
+    for row in range(3):
+        for column in range(3):
+            tap = row * 3 + column
             for plane in range(2):
                 depths = [depth_tap(source, plane) for source in PLANES[:4]]
                 parts = [zero if d is None else weight[(2 - d) * 9 + 8 - tap] for d in depths]
@@ -201,8 +210,6 @@
                     back_taps[at : at + 64, first : first + 128] = jnp.concatenate(
                         parts[2 * pair : 2 * pair + 2], axis=1
                     )
-    for start in range(0, own.shape[0], BLOCK):
-        hidden[start : start + BLOCK, :] = window_dot(own_windows, own_taps, start, columns, NN)
 
 
 def hidden_body(
@@ -308,7 +315,8 @@
 
 
 def grad_one_body(
-    columns, count, me, own_windows, side_windows, grad, other, message, kept, turned, terms
+    columns, count, me, own_windows, side_windows, grad, other, to_inner,
+    message, kept, turned, terms,
 ):
     cells = grad.shape[0]
 
@@ -344,6 +352,7 @@
         for group in range(groups):
             first = (pair * groups + group) * size
             message[first : first + size, :] = given[:, group * 128 : group * 128 + 128]
+    message[message.shape[0] - to_inner.shape[0] :, :] = to_inner[...]
 
 
 def halve_body(split, me, mine, message, sent, kept):
@@ -364,11 +373,10 @@
 
 
 def spread_body(split, me, mine, arrived, kept, *sent):
-    ring = mine.shape[0]
     place = me[0] // 4
     kept[...] = mine[place] + decoded(arrived[place], split)
     for hop, out in enumerate(sent):
-        there = (place + hop + 1) % ring
+        there = place ^ (hop + 1)
         out[...] = (mine[there] + decoded(arrived[there], split)).astype(BF16)
 
 
@@ -413,17 +421,23 @@
         copy.wait()
 
 
-def grad_windows_body(columns, me, own, inner, outer, windows):
+def grad_windows_body(columns, count, me, own, message, outer, windows):
     half = own.shape[0] // 2
-    odd = me[0] % 2 == 1
+    side = me[0] % 2
+    near, across = message.shape[0] - half, side * half
+    edge = jnp.logical_or(me[0] == 0, me[0] == count - 1)
+    inside = jnp.where(edge, 0.0, 1.0).astype(F32)
 
     def fill(i, carry):
         start = pl.multiple_of(i * STEP, STEP)
-        rows = pl.ds(start, STEP)
-        below, above = by_side(odd, inner[rows, :].astype(F32), outer[rows, :].astype(F32))
-        for first, side in zip((start, start + half), unpacked(above, below)):
+        below, above = by_side(
+            side == 1,
+            message[pl.ds(near + start, STEP), :].astype(F32),
+            outer[pl.ds(pl.multiple_of(across + start, STEP), STEP), :].astype(F32) * inside,
+        )
+        for first, side_planes in zip((start, start + half), unpacked(above, below)):
             fill_windows(windows, first, 0, own[pl.ds(first, STEP), :].astype(F32), columns, 256)
-            fill_windows(windows, first, 128, side, columns, 256)
+            fill_windows(windows, first, 128, side_planes, columns, 256)
         return carry
 
     clear_edges(windows, columns)
@@ -500,11 +514,10 @@
         two_flops, "grad_act_terms", (0,), (1, 2),
     )
     own, terms = lax.optimization_barrier((own, terms))
-    own_windows, part, side_taps, back_taps = call(
+    own_windows, part, side_taps = call(
         functools.partial(prepare_body, columns),
         (
             shape((slab[0], 384), BF16), shape((cells, 256), F32), shape((9 * 256, 256), BF16),
-            shape((3 * 128, 768), BF16),
         ),
         (own, far_one),
         (pltpu.VMEM((9 * 128, 256), BF16), pltpu.VMEM(weight_one.shape, BF16), dma),
@@ -519,36 +532,34 @@
         (me, vol_inner, vol_outer, part, side_taps),
         (), 2 * one_flops, "hidden", (0,),
     )
+    grad_hidden, to_inner, outer = call(
+        slope_body, (flat, pack, pack), (me, terms, terms_inner, terms_outer, slope),
+        name="grad_hidden", smem=(0,),
+    )
+    pairs = [[i, (i + 1) % count] for i in range(1, count, 2)]
+    grad_outer = lax.all_gather(outer, "space", axis_index_groups=pairs, tiled=True)
+    act_windows, grad_hidden = lax.optimization_barrier((act_windows, grad_hidden))
     terms_two, = call(
         functools.partial(grad_two_body, columns),
         (shape((wide, 2 * lanes), F32),),
         (act_windows, turned), (), two_flops, "grad_two_terms",
     )
-    terms_two, terms_outer = lax.optimization_barrier((terms_two, terms_outer))
-    grad_hidden, to_inner, outer = call(
-        slope_body, (flat, pack, pack), (me, terms, terms_inner, terms_outer, slope),
-        name="grad_hidden", smem=(0,),
-    )
-    grad_outer = lax.ppermute(outer, "space", across)
-    grad_inner = lax.ppermute(to_inner, "space", within)
     groups = lanes // 128
     message, kept = call(
         functools.partial(grad_one_body, columns, count),
         (
-            shape((count // 2 * groups * 2 * chunk, 128), BF16),
+            shape((count // 2 * groups * 2 * chunk + cells // 2, 128), BF16),
             shares(count // 2)[1],
         ),
-        (me, own_windows, side_windows, grad_hidden, terms_two),
+        (me, own_windows, side_windows, grad_hidden, terms_two, to_inner),
         (pltpu.VMEM((128, cells), BF16), pltpu.VMEM((mid, 2 * lanes), F32)),
         one_flops, "grad_one_terms", (0,),
     )
     message = lax.ppermute(message, "space", within)
-    grad_windows, = call(
-        functools.partial(grad_windows_body, columns), (shape(slab, BF16),),
-        (me, grad_hidden, grad_inner, grad_outer),
-        (), 16 * two_flops, "grad_windows", (0,),
-    )
-    message, grad_windows = lax.optimization_barrier((message, grad_windows))
+    back_taps, = call(
+        back_taps_body, (shape((3 * 128, 768), BF16),), (weight_one,), (), 2 * one_flops, "back_taps"
+    )
+    message, back_taps = lax.optimization_barrier((message, back_taps))
     sent, kept = call(
         functools.partial(halve_body, split), shares(count // 4),
         (me, kept, message), name="halve", smem=(0,),
@@ -571,11 +582,16 @@
         (shares()[1], *[shape((chunk, lanes), BF16)] * (ring - 1)),
         (me, kept, arrived), name="spread", smem=(0,),
     )
-    sent, grad_windows = lax.optimization_barrier((sent, grad_windows))
+    sent, grad_hidden = lax.optimization_barrier((sent, grad_hidden))
     rest = [
-        lax.ppermute(x, "space", [(i, (i + 4 * hop + 4) % count) for i in range(count)])
+        lax.ppermute(x, "space", [(i, i ^ (4 * hop + 4)) for i in range(count)])
         for hop, x in enumerate(sent)
     ]
+    grad_windows, = call(
+        functools.partial(grad_windows_body, columns, count), (shape(slab, BF16),),
+        (me, grad_hidden, message, grad_outer),
+        (), one_flops // 4, "grad_windows", (0,),
+    )
     grad_volume, = call(
         functools.partial(grad_volume_body, columns),
         (shape((planes, cells, channels), F32),),

time: 56.1 us -> 59.6 us (1.062)
  the two profiles are of different devices: /device:TPU:0 before, /device:TPU:1 now
where the time goes in v7:
time: 59.6 us; the launch traced here: 59.4 us
  Pallas kernels  27 us (45%)
  starting transfers between devices  14.8 us (25%)
  blocking collectives  11.5 us (19%)
  waiting for transfers between devices  5.3 us (9%)
  between operations  0.82 us (1%)
    pallas_call x14, Pallas kernels, call(): pl.pallas_call(body, out_shape=list(outs), in_specs=[pl.BlockSpec(memory_...  27 us
    all_gather x1, blocking collectives, shards(): lax.all_gather(outer, 'space', axis_index_groups=pairs, tiled=True)  11.5 us
    ppermute x1, starting transfers between devices, shards(): vol_outer = lax.ppermute(own, 'space', across)  4.49 us
    ppermute x3, starting transfers between devices, shards(): lax.ppermute(x, 'space', [(i, i ^ 4 * hop + 4) for i in range(count)])  4.25 us
    ppermute x1, starting transfers between devices, shards(): terms_outer = lax.ppermute(outer, 'space', across)  3.5 us
    ppermute x1, waiting for transfers between devices, shards(): message = lax.ppermute(message, 'space', within)  2.3 us
    ppermute x1, starting transfers between devices, shards(): arrived = lax.ppermute(sent, 'space', [(i, i ^ 2) for i in range(count)])  2.28 us
    ppermute x1, waiting for transfers between devices, shards(): terms_outer = lax.ppermute(outer, 'space', across)  1.33 us
  transfers between devices with their start and end apart: 9, of which 4 were waited for; matrix products, arithmetic and copies ran while one was open for 0% of the time, Pallas kernels for 32%

profile of v7, /device:TPU:1, one launch (start us, length us, event | category | flops | bytes accessed | tf_op | source)
XLA Modules:
  0.0 59.4 jit_solution(17897375197817541725)
XLA Ops:
  0.6 1.4 %pack_volume.1.own = bf16[2048,128]{1,0:T(8,128)(2,1)S(1)} custom-call(bf16[2,2048,64]{2,1,0:T(8,128)(2,1)} %bitcast.18), custom_call_target="tpu_custom_call" | custom-call | bytes 1048576 | tf_op jit(solution)/shard_map/pack_volume/pallas_call | solution.py:27
  2.0 0.1 collective-permute-start
  2.2 4.5 %collective-permute-start.1 = (bf16[2048,128]{1,0:T(8,128)(2,1)S(1)}, bf16[2048,128]{1,0:T(8,128)(2,1)S(1)}, u32[]{:S(2)}, u32[]{:S(2)}) collective-permute-start(bf16[2048,128]{1,0:T(8,128)(2,1)S(1)} %pack_volume.1.own), channel_id=1, source_target_pairs={{1,2},{3,4},{5,6},{7,8},{9,10},{11,12},{13,14},{2,1},{4,3},{6,5},{... | collective-permute-start | bytes 1572872 | tf_op jit(solution)/shard_map/ppermute | solution.py:502
  6.7 4.5 %grad_act_terms.1 = (f32[2048,128]{1,0:T(8,128)S(1)}, bf16[1024,128]{1,0:T(8,128)(2,1)S(1)}, bf16[1024,128]{1,0:T(8,128)(2,1)S(1)}, bf16[256,2048]{1,0:T(8,128)(2,1)S(1)}) custom-call(s32[1]{0:T(128)} %bitcast.me, bf16[2,2048,128]{2,1,0:T(8,128)(2,1)} %bitcast.19, bf16[27,64,128]{2,1,0:T(8,128)(2,1)} %bitcast.15), custom_call_target="tpu_custom_call" | custom-call | flops 1811939328 | bytes 4112388 | tf_op jit(solution)/shard_map/grad_act_terms/pallas_call | solution.py:27
  11.2 2.8 %prepare.1 = (bf16[2112,384]{1,0:T(8,128)(2,1)S(1)}, f32[2048,256]{1,0:T(8,128)S(1)}, bf16[2304,256]{1,0:T(8,128)(2,1)S(1)}) custom-call(bf16[2048,128]{1,0:T(8,128)(2,1)S(1)} %pack_volume.1.own, bf16[27,64,64]{2,1,0:T(8,128)(2,1)} %bitcast.13), custom_call_target="tpu_custom_call" | custom-call | flops 905969664 | bytes 5644288 | tf_op jit(solution)/shard_map/prepare/pallas_call | solution.py:27
  14.0 0.1 collective-permute-start.2
  14.1 3.5 %collective-permute-start.3 = (bf16[1024,128]{1,0:T(8,128)(2,1)S(1)}, bf16[1024,128]{1,0:T(8,128)(2,1)S(1)}, u32[]{:S(2)}, u32[]{:S(2)}) collective-permute-start(bf16[1024,128]{1,0:T(8,128)(2,1)S(1)} %get-tuple-element.54), channel_id=1, source_target_pairs={{1,2},{3,4},{5,6},{7,8},{9,10},{11,12},{13,14},{2,1},{4,3},{6,5},{... | collective-permute-start | bytes 786440 | tf_op jit(solution)/shard_map/ppermute | solution.py:527
  17.6 0.8 %collective-permute-done.1.outer = bf16[2048,128]{1,0:T(8,128)(2,1)S(1)} collective-permute-done((bf16[2048,128]{1,0:T(8,128)(2,1)S(1)}, bf16[2048,128]{1,0:T(8,128)(2,1)S(1)}, u32[]{:S(2)}, u32[]{:S(2)}) %collective-permute-start.1) | collective-permute-done | bytes 524320 | tf_op jit(solution)/shard_map/ppermute | solution.py:502
  18.4 4.3 %hidden.1 = (bf16[2112,768]{1,0:T(8,128)(2,1)S(1)}, bf16[2112,768]{1,0:T(8,128)(2,1)S(1)}, f32[2048,128]{1,0:T(8,128)S(1)}) custom-call(s32[1]{0:T(128)} %bitcast.me, bf16[2048,128]{1,0:T(8,128)(2,1)S(1)} %collective-permute-done.inner, bf16[2048,128]{1,0:T(8,128)(2,1)S(1)} %collective-permute-done.1.outer, f32[2048,256]{1,0:T(8,128)S(1)} %get-tuple-element.48.part, ...), custom_call_target="tpu_custom_call" | custom-call | flops 1811939328 | bytes 11862020 | tf_op jit(solution)/shard_map/hidden/pallas_call | solution.py:27
  22.7 0.0 collective-permute-done.2.inner
  22.7 1.3 %collective-permute-done.3.outer = bf16[1024,128]{1,0:T(8,128)(2,1)S(1)} collective-permute-done((bf16[1024,128]{1,0:T(8,128)(2,1)S(1)}, bf16[1024,128]{1,0:T(8,128)(2,1)S(1)}, u32[]{:S(2)}, u32[]{:S(2)}) %collective-permute-start.3) | collective-permute-done | bytes 262176 | tf_op jit(solution)/shard_map/ppermute | solution.py:527
  24.0 0.9 %grad_hidden.1 = (bf16[2048,128]{1,0:T(8,128)(2,1)S(1)}, bf16[1024,128]{1,0:T(8,128)(2,1)S(1)}, bf16[1024,128]{1,0:T(8,128)(2,1)S(1)}) custom-call(s32[1]{0:T(128)} %bitcast.me, f32[2048,128]{1,0:T(8,128)S(1)} %get-tuple-element.52.terms, bf16[1024,128]{1,0:T(8,128)(2,1)S(1)} %collective-permute-done.2.inner, ...), custom_call_target="tpu_custom_call" | custom-call | bytes 3670020 | tf_op jit(solution)/shard_map/grad_hidden/pallas_call | solution.py:27
  24.9 2.8 %grad_two_terms.1.other = f32[128,1792]{1,0:T(8,128)S(1)} custom-call(bf16[2112,768]{1,0:T(8,128)(2,1)S(1)} %get-tuple-element.65.act_windows, bf16[256,2048]{1,0:T(8,128)(2,1)S(1)} %get-tuple-element.59.turned), custom_call_target="tpu_custom_call" | custom-call | flops 1811939328 | bytes 5210112 | tf_op jit(solution)/shard_map/grad_two_terms/pallas_call | solution.py:27
  27.6 0.0 copy-start
  27.7 1.8 %grad_one_terms.1 = (bf16[3712,128]{1,0:T(8,128)(2,1)S(1)}, f32[8,24,896]{2,1,0:T(8,128)S(1)}) custom-call(s32[1]{0:T(128)} %bitcast.me, bf16[2112,384]{1,0:T(8,128)(2,1)S(1)} %get-tuple-element.44.own_windows, bf16[2112,768]{1,0:T(8,128)(2,1)S(1)} %get-tuple-element.50.side_windows, bf16[2048,128]{1,0:T(8,128)(2,1)S(1)} %get-tuple-element.71.grad.own, ...), custom_call_target="tpu_custom_call" | custom-call | flops 905969664 | bytes 8208388 | tf_op jit(solution)/shard_map/grad_one_terms/pallas_call | solution.py:27
  29.5 0.1 collective-permute-start.4
  29.5 0.2 back_taps.1.taps
  29.7 0.0 copy-start.1
  29.7 2.3 %collective-permute-done.4.message = bf16[3712,128]{1,0:T(8,128)(2,1)S(1)} collective-permute-done((bf16[3712,128]{1,0:T(8,128)(2,1)S(1)}, bf16[3712,128]{1,0:T(8,128)(2,1)S(1)}, u32[]{:S(2)}, u32[]{:S(2)}) %collective-permute-start.4) | collective-permute-done | bytes 950304 | tf_op jit(solution)/shard_map/ppermute | solution.py:558
  32.0 0.1 halve.1
  32.2 2.3 %collective-permute-start.5 = (bf16[4,32,896]{2,1,0:T(8,128)(2,1)S(1)}, bf16[4,32,896]{2,1,0:T(8,128)(2,1)S(1)}, u32[]{:S(2)}, u32[]{:S(2)}) collective-permute-start(bf16[4,32,896]{2,1,0:T(8,128)(2,1)S(1)} %get-tuple-element.67), channel_id=1, source_target_pairs={{0,2},{1,3},{2,0},{3,1},{4,6},{5,7},{6,4},{7,5},{8,10},{9,11},{10,... | collective-permute-start | bytes 688136 | tf_op jit(solution)/shard_map/ppermute | solution.py:568
  34.5 11.5 %all_gather.3.outer = bf16[2048,128]{1,0:T(8,128)(2,1)S(1)} all-gather(bf16[1024,128]{1,0:T(8,128)(2,1)S(1)} %get-tuple-element.72), channel_id=1, replica_groups={{1,2},{3,4},{5,6},{7,8},{9,10},{11,12},{13,14},{15,0},{17,18},{19,20},{..., dimensions={0}, use_global_device_ids=true | all-gather | bytes 786432 | tf_op jit(solution)/shard_map/all_gather | solution.py:540
  46.0 3.7 %output.1 = f32[2,2048,128]{2,1,0:T(8,128)} custom-call(bf16[2112,768]{1,0:T(8,128)(2,1)S(1)} %get-tuple-element.65.act_windows, bf16[27,64,128]{2,1,0:T(8,128)(2,1)S(1)} %bitcast.16), custom_call_target="tpu_custom_call" | custom-call | flops 1811939328 | bytes 5783552 | tf_op jit(solution)/shard_map/output/pallas_call | solution.py:27
  49.7 0.0 collective-permute-done.5.arrived
  49.7 0.1 spread.1
  49.7 1.9 %collective-permute-start.6 = (bf16[24,896]{1,0:T(8,128)(2,1)S(1)}, bf16[24,896]{1,0:T(8,128)(2,1)S(1)}, u32[]{:S(2)}, u32[]{:S(2)}) collective-permute-start(bf16[24,896]{1,0:T(8,128)(2,1)S(1)} %get-tuple-element.75), channel_id=1, source_target_pairs={{0,4},{1,5},{2,6},{3,7},{4,0},{5,1},{6,2},{7,3},{8,12},{9,13},{10,... | collective-permute-start | bytes 129032 | tf_op jit(solution)/shard_map/ppermute | solution.py:587
  51.7 2.3 %collective-permute-start.7 = (bf16[24,896]{1,0:T(8,128)(2,1)S(1)}, bf16[24,896]{1,0:T(8,128)(2,1)S(1)}, u32[]{:S(2)}, u32[]{:S(2)}) collective-permute-start(bf16[24,896]{1,0:T(8,128)(2,1)S(1)} %get-tuple-element.76), channel_id=1, source_target_pairs={{0,8},{1,9},{2,10},{3,11},{4,12},{5,13},{6,14},{7,15},{8,0},{9,1},... | collective-permute-start | bytes 129032 | tf_op jit(solution)/shard_map/ppermute | solution.py:587
  54.0 0.0 collective-permute-start.8
  54.0 0.8 %grad_windows.1.windows = bf16[2112,768]{1,0:T(8,128)(2,1)S(1)} custom-call(s32[1]{0:T(128)} %bitcast.me, bf16[2048,128]{1,0:T(8,128)(2,1)S(1)} %get-tuple-element.71.grad.own, bf16[3712,128]{1,0:T(8,128)(2,1)S(1)} %collective-permute-done.4.message, bf16[2048,128]{1,0:T(8,128)(2,1)S(1)} %all_gather.3.outer), custom_call_target="tpu_custom_call" | custom-call | flops 226492416 | bytes 5242884 | tf_op jit(solution)/shard_map/grad_windows/pallas_call | solution.py:27
  54.8 2.9 %grad_volume.1 = f32[2,2048,64]{2,1,0:T(8,128)} custom-call(bf16[2112,768]{1,0:T(8,128)(2,1)S(1)} %grad_windows.1.windows, bf16[384,768]{1,0:T(8,128)(2,1)S(1)} %back_taps.1.taps), custom_call_target="tpu_custom_call" | custom-call | flops 905969664 | bytes 4882432 | tf_op jit(solution)/shard_map/grad_volume/pallas_call | solution.py:27
  57.8 0.9 %collective-permute-done.8.refs_2_ = bf16[24,896]{1,0:T(8,128)(2,1)S(1)} collective-permute-done((bf16[24,896]{1,0:T(8,128)(2,1)S(1)}, bf16[24,896]{1,0:T(8,128)(2,1)S(1)}, u32[]{:S(2)}, u32[]{:S(2)}) %collective-permute-start.8) | collective-permute-done | bytes 43040 | tf_op jit(solution)/shard_map/ppermute | solution.py:587
  58.7 0.8 %finish.1 = (f32[27,4,64]{2,1,0:T(4,128)}, f32[27,8,64]{2,1,0:T(8,128)}) custom-call(f32[24,896]{1,0:T(8,128)S(1)} %get-tuple-element.74.mine, bf16[24,896]{1,0:T(8,128)(2,1)S(1)} %collective-permute-done.6.refs_0_, bf16[24,896]{1,0:T(8,128)(2,1)S(1)} %collective-permute-done.7.refs_1_, bf16[24,896]{1,0:T(8,128)(2,1)S(1)} %collective-permute-done.8.refs_2_), custom_call_target="tpu_custom_call" | custom-call | bytes 297984 | tf_op jit(solution)/shard_map/finish/pallas_call | solution.py:27
  (5 shorter events, 0.0 us)
Async XLA Ops:
  2.0 15.6 %collective-permute-start = (bf16[2048,128]{1,0:T(8,128)(2,1)S(1)}, bf16[2048,128]{1,0:T(8,128)(2,1)S(1)}, u32[]{:S(2)}, u32[]{:S(2)}) collective-permute-start(bf16[2048,128]{1,0:T(8,128)(2,1)S(1)} %pack_volume.1.own), channel_id=1, source_target_pairs={{0,1},{1,0},{2,3},{3,2},{4,5},{5,4},{6,7},{7,6},{8,9},{9,8},{10,11... | collective-permute-start | bytes 1572872 | tf_op jit(solution)/shard_map/ppermute | solution.py:503
  2.2 16.2 %collective-permute-start.1 = (bf16[2048,128]{1,0:T(8,128)(2,1)S(1)}, bf16[2048,128]{1,0:T(8,128)(2,1)S(1)}, u32[]{:S(2)}, u32[]{:S(2)}) collective-permute-start(bf16[2048,128]{1,0:T(8,128)(2,1)S(1)} %pack_volume.1.own), channel_id=1, source_target_pairs={{1,2},{3,4},{5,6},{7,8},{9,10},{11,12},{13,14},{2,1},{4,3},{6,5},{... | collective-permute-start | bytes 1572872 | tf_op jit(solution)/shard_map/ppermute | solution.py:502
  14.0 8.7 %collective-permute-start.2 = (bf16[1024,128]{1,0:T(8,128)(2,1)S(1)}, bf16[1024,128]{1,0:T(8,128)(2,1)S(1)}, u32[]{:S(2)}, u32[]{:S(2)}) collective-permute-start(bf16[1024,128]{1,0:T(8,128)(2,1)S(1)} %get-tuple-element.53), channel_id=1, source_target_pairs={{0,1},{1,0},{2,3},{3,2},{4,5},{5,4},{6,7},{7,6},{8,9},{9,8},{10,11... | collective-permute-start | bytes 786440 | tf_op jit(solution)/shard_map/ppermute | solution.py:528
  14.1 9.9 %collective-permute-start.3 = (bf16[1024,128]{1,0:T(8,128)(2,1)S(1)}, bf16[1024,128]{1,0:T(8,128)(2,1)S(1)}, u32[]{:S(2)}, u32[]{:S(2)}) collective-permute-start(bf16[1024,128]{1,0:T(8,128)(2,1)S(1)} %get-tuple-element.54), channel_id=1, source_target_pairs={{1,2},{3,4},{5,6},{7,8},{9,10},{11,12},{13,14},{2,1},{4,3},{6,5},{... | collective-permute-start | bytes 786440 | tf_op jit(solution)/shard_map/ppermute | solution.py:527
  27.6 1.9 %copy-start = (bf16[3,3,3,64,64]{4,3,2,1,0:T(8,128)(2,1)S(1)}, bf16[3,3,3,64,64]{4,3,2,1,0:T(8,128)(2,1)}, u32[]{:S(2)}) copy-start(bf16[3,3,3,64,64]{4,3,2,1,0:T(8,128)(2,1)} %param.5) | copy-start | bytes 663556
  29.5 2.6 %collective-permute-start.4 = (bf16[3712,128]{1,0:T(8,128)(2,1)S(1)}, bf16[3712,128]{1,0:T(8,128)(2,1)S(1)}, u32[]{:S(2)}, u32[]{:S(2)}) collective-permute-start(bf16[3712,128]{1,0:T(8,128)(2,1)S(1)} %get-tuple-element.62), channel_id=1, source_target_pairs={{0,1},{1,0},{2,3},{3,2},{4,5},{5,4},{6,7},{7,6},{8,9},{9,8},{10,11... | collective-permute-start | bytes 2850824 | tf_op jit(solution)/shard_map/ppermute | solution.py:558
  29.7 16.2 %copy-start.1 = (bf16[3,3,3,64,128]{4,3,2,1,0:T(8,128)(2,1)S(1)}, bf16[3,3,3,64,128]{4,3,2,1,0:T(8,128)(2,1)}, u32[]{:S(2)}) copy-start(bf16[3,3,3,64,128]{4,3,2,1,0:T(8,128)(2,1)} %param.6) | copy-start | bytes 1327108
  32.2 17.5 %collective-permute-start.5 = (bf16[4,32,896]{2,1,0:T(8,128)(2,1)S(1)}, bf16[4,32,896]{2,1,0:T(8,128)(2,1)S(1)}, u32[]{:S(2)}, u32[]{:S(2)}) collective-permute-start(bf16[4,32,896]{2,1,0:T(8,128)(2,1)S(1)} %get-tuple-element.67), channel_id=1, source_target_pairs={{0,2},{1,3},{2,0},{3,1},{4,6},{5,7},{6,4},{7,5},{8,10},{9,11},{10,... | collective-permute-start | bytes 688136 | tf_op jit(solution)/shard_map/ppermute | solution.py:568
  49.7 8.0 %collective-permute-start.6 = (bf16[24,896]{1,0:T(8,128)(2,1)S(1)}, bf16[24,896]{1,0:T(8,128)(2,1)S(1)}, u32[]{:S(2)}, u32[]{:S(2)}) collective-permute-start(bf16[24,896]{1,0:T(8,128)(2,1)S(1)} %get-tuple-element.75), channel_id=1, source_target_pairs={{0,4},{1,5},{2,6},{3,7},{4,0},{5,1},{6,2},{7,3},{8,12},{9,13},{10,... | collective-permute-start | bytes 129032 | tf_op jit(solution)/shard_map/ppermute | solution.py:587
  51.7 6.1 %collective-permute-start.7 = (bf16[24,896]{1,0:T(8,128)(2,1)S(1)}, bf16[24,896]{1,0:T(8,128)(2,1)S(1)}, u32[]{:S(2)}, u32[]{:S(2)}) collective-permute-start(bf16[24,896]{1,0:T(8,128)(2,1)S(1)} %get-tuple-element.76), channel_id=1, source_target_pairs={{0,8},{1,9},{2,10},{3,11},{4,12},{5,13},{6,14},{7,15},{8,0},{9,1},... | collective-permute-start | bytes 129032 | tf_op jit(solution)/shard_map/ppermute | solution.py:587
  54.0 4.7 %collective-permute-start.8 = (bf16[24,896]{1,0:T(8,128)(2,1)S(1)}, bf16[24,896]{1,0:T(8,128)(2,1)S(1)}, u32[]{:S(2)}, u32[]{:S(2)}) collective-permute-start(bf16[24,896]{1,0:T(8,128)(2,1)S(1)} %get-tuple-element.77), channel_id=1, source_target_pairs={{0,12},{1,13},{2,14},{3,15},{4,8},{5,9},{6,10},{7,11},{8,4},{9,5},... | collective-permute-start | bytes 129032 | tf_op jit(solution)/shard_map/ppermute | solution.py:587

commit v8 on v4

--- a/solution.py
+++ b/solution.py
@@ -165,7 +165,7 @@
 
 
 def prepare_body(
-    columns, own, far_weight, own_windows, hidden, side_taps, back_taps, own_taps, weight, sem
+    columns, own, far_weight, own_windows, hidden, side_taps, own_taps, weight, sem
 ):
     fetch = pltpu.make_async_copy(far_weight, weight, sem)
     fetch.start()
@@ -192,6 +192,15 @@
                     target, first = side_taps, tap * 256 + (at - 2) * 64
                 target[first : first + 64, :128] = jnp.concatenate(parts[:2], axis=1)
                 target[first : first + 64, 128:] = jnp.concatenate(parts[2:], axis=1)
+    for start in range(0, own.shape[0], BLOCK):
+        hidden[start : start + BLOCK, :] = window_dot(own_windows, own_taps, start, columns, NN)
+
+
+def back_taps_body(weight, back_taps):
+    zero = jnp.zeros((64, 64), BF16)
+    for row in range(3):
+        for column in range(3):
+            tap = row * 3 + column
             for plane in range(2):
                 depths = [depth_tap(source, plane) for source in PLANES[:4]]
                 parts = [zero if d is None else weight[(2 - d) * 9 + 8 - tap] for d in depths]
@@ -201,8 +210,6 @@
                     back_taps[at : at + 64, first : first + 128] = jnp.concatenate(
                         parts[2 * pair : 2 * pair + 2], axis=1
                     )
-    for start in range(0, own.shape[0], BLOCK):
-        hidden[start : start + BLOCK, :] = window_dot(own_windows, own_taps, start, columns, NN)
 
 
 def hidden_body(
@@ -292,18 +299,21 @@
 
 
 def coded(value, split):
-    head = value[:split].astype(BF16)
-    parts = [head, (value[:split] - head.astype(F32)).astype(BF16)]
-    if split < value.shape[0]:
-        parts.append(value[split:].astype(BF16))
-    return jnp.concatenate(parts, axis=0)
+    head = value.astype(BF16)
+    if split == 0:
+        return head
+    rest = (value[:split] - head[:split].astype(F32)).astype(BF16)
+    return jnp.concatenate([head, rest], axis=0)
 
 
 def decoded(value, split):
     value = value.astype(F32)
-    parts = [value[:split] + value[split : 2 * split]]
-    if 2 * split < value.shape[0]:
-        parts.append(value[2 * split :])
+    if split == 0:
+        return value
+    size = value.shape[0] - split
+    parts = [value[:split] + value[size:]]
+    if split < size:
+        parts.append(value[split:size])
     return jnp.concatenate(parts, axis=0)
 
 
@@ -348,28 +358,30 @@
     message[message.shape[0] - to_inner.shape[0] :, :] = to_inner[...]
 
 
-def sum_body(split, me, mine, message, sent, kept):
-    place = me[0] // 2
+def halve_body(split_in, split_out, owner_bit, at_bit, me, mine, arrived, sent, kept):
+    side = (me[0] >> owner_bit) % 2
     size, lanes = mine.shape[1:]
     groups = lanes // 128
 
-    def arrived(at):
+    def total(at):
+        if len(arrived.shape) == 3:
+            return mine[at] + decoded(arrived[at], split_in)
         parts = []
         for group in range(groups):
             first = pl.multiple_of((at * groups + group) * 2 * size, 8)
-            parts.append(decoded(message[pl.ds(first, 2 * size), :], size))
-        return jnp.concatenate(parts, axis=1)
-
-    for at in range(mine.shape[0]):
-        sent[at] = coded(mine[at] + arrived(at), split)
-    kept[...] = mine[place] + arrived(place)
-
-
-def finish_body(scale, split, sizes, me, mine, arrived, grad_one, grad_two):
-    total = mine[...]
-    for at in range(arrived.shape[0]):
-        total = total + jnp.where(at == me[0] // 2, 0.0, decoded(arrived[at], split))
-    total = total * scale
+            parts.append(decoded(arrived[pl.ds(first, 2 * size), :], split_in))
+        return mine[at] + jnp.concatenate(parts, axis=1)
+
+    for at in range(sent.shape[0]):
+        high, low = at >> at_bit, at & ((1 << at_bit) - 1)
+        keep = ((2 * high + side) << at_bit) + low
+        give = ((2 * high + 1 - side) << at_bit) + low
+        sent[at] = coded(total(give), split_out)
+        kept[at] = total(keep)
+
+
+def finish_body(scale, split, sizes, mine, arrived, grad_one, grad_two):
+    total = (mine[0] + decoded(arrived[0], split)) * scale
     half = total.shape[1]
     first = 0
     for size, out in zip(sizes, (grad_one, grad_two)):
@@ -382,10 +394,7 @@
                 out[depth * 9 + tap] = block[:, lane : lane + 64]
 
 
-def output_body(columns, act_windows, far_weight, far, taps, weight, output, sem, sems):
-    fetch = pltpu.make_async_copy(far_weight, weight, sem)
-    fetch.start()
-    fetch.wait()
+def output_body(columns, act_windows, weight, far, taps, output, sems):
     for row in range(3):
         for column in range(3):
             for at, source in enumerate(PLANES[:4]):
@@ -400,10 +409,7 @@
     copies = pieces_of(output, far, sems, output.shape[1] // BLOCK)
     for at, copy in enumerate(copies):
         start = at * BLOCK
-        value = None
-        for row, rows in enumerate(row_windows(act_windows, start, columns)):
-            term = jnp.dot(rows, taps[row * 768 : row * 768 + 768, :], preferred_element_type=F32)
-            value = term if value is None else value + term
+        value = window_dot(act_windows, taps, start, columns, NN)
         output[0, start : start + BLOCK, :] = value[:, :128]
         output[1, start : start + BLOCK, :] = value[:, 128:]
         copy.start()
@@ -411,7 +417,7 @@
         copy.wait()
 
 
-def grad_volume_body(columns, me, own, message, outer, taps, far, windows, output, sems):
+def grad_windows_body(columns, me, own, message, outer, windows):
     half = own.shape[0] // 2
     odd = me[0] % 2 == 1
     before = message.shape[0] - half
@@ -427,6 +433,9 @@
 
     clear_edges(windows, columns)
     lax.fori_loop(0, half // STEP, fill, 0)
+
+
+def grad_volume_body(columns, windows, taps, far, output, sems):
     copies = pieces_of(output, far, sems, output.shape[1] // BLOCK)
     for at, copy in enumerate(copies):
         start = at * BLOCK
@@ -461,9 +470,6 @@
     across = [(i, i + 1) for i in range(1, count - 1, 2)]
     across += [(j, i) for i, j in across]
 
-    def shares(*lead):
-        return shape((*lead, chunk + split, lanes), BF16), shape((*lead, chunk, lanes), F32)
-
     volume = volume.reshape(planes, cells, channels)
     cotangent = cotangent.reshape(planes, cells, wide)
     weight_one = weight_one.reshape(27, channels, mid)
@@ -496,17 +502,19 @@
         two_flops, "grad_act_terms", (0,), (1, 2),
     )
     own, terms = lax.optimization_barrier((own, terms))
-    own_windows, part, side_taps, back_taps = call(
+    own_windows, part, side_taps = call(
         functools.partial(prepare_body, columns),
         (
             shape((slab[0], 384), BF16), shape((cells, 256), F32), shape((9 * 256, 256), BF16),
-            shape((3 * 128, 768), BF16),
         ),
         (own, far_one),
         (pltpu.VMEM((9 * 128, 256), BF16), pltpu.VMEM(weight_one.shape, BF16), dma),
         one_flops, "prepare", (), (1,),
     )
-    inner, outer, part = lax.optimization_barrier((inner, outer, part))
+    back_taps, = call(
+        back_taps_body, (shape((3 * 128, 768), BF16),), (weight_one,), (), one_flops // 8, "back_taps"
+    )
+    inner, outer, part, back_taps = lax.optimization_barrier((inner, outer, part, back_taps))
     terms_outer = lax.ppermute(outer, "space", across)
     terms_inner = lax.ppermute(inner, "space", within)
     side_windows, act_windows, slope = call(
@@ -531,45 +539,63 @@
         functools.partial(grad_one_body, columns, count),
         (
             shape((count // 2 * groups * 2 * chunk + cells // 2, 128), BF16),
-            shares(count // 2)[1],
+            shape((count // 2, chunk, lanes), F32),
         ),
         (me, own_windows, side_windows, grad_hidden, terms_two, to_inner),
         (pltpu.VMEM((128, cells), BF16), pltpu.VMEM((mid, 2 * lanes), F32)),
         one_flops, "grad_one_terms", (0,),
     )
     message = lax.ppermute(message, "space", within)
-    sent, mine = call(
-        functools.partial(sum_body, split), (shares(count // 2)[0], shares()[1]),
-        (me, kept, message), name="sum_pair", smem=(0,),
-    )
-    sent, act_windows, grad_hidden, grad_outer = lax.optimization_barrier(
-        (sent, act_windows, grad_hidden, grad_outer)
-    )
-    arrived = lax.all_to_all(
-        sent, "space", 0, 0, tiled=True,
-        axis_index_groups=[list(range(core, count, 2)) for core in range(2)],
-    )
+    def halve(bits, bit, split_in, split_out, kept, arrived):
+        left = 2 ** (len(bits) - 1)
+        sent, kept = call(
+            functools.partial(halve_body, split_in, split_out, bit, bits[::-1].index(bit)),
+            (shape((left, chunk + split_out, lanes), BF16), shape((left, chunk, lanes), F32)),
+            (me, kept, arrived), name="halve", smem=(0,),
+        )
+        return [b for b in bits if b != bit], sent, kept
+
+    bits = list(range(count.bit_length() - 2, 0, -1))
+    order = [*range(2, count.bit_length() - 1), 1]
+    bits, sent, kept = halve(bits, order[0], chunk, split, kept, message)
+    sent, act_windows = lax.optimization_barrier((sent, act_windows))
+    arrived = lax.ppermute(sent, "space", [(i, i ^ (1 << order[0])) for i in range(count)])
     output, = call(
         functools.partial(output_body, columns),
         (shape((planes, cells, wide), F32),),
-        (act_windows, far_two),
+        (act_windows, weight_two),
         (
-            pltpu.VMEM((3 * 768, 256), BF16), pltpu.VMEM(weight_two.shape, BF16),
-            pltpu.VMEM((planes, cells, wide), F32), dma, dma((cells // BLOCK,)),
+            pltpu.VMEM((3 * 768, 256), BF16), pltpu.VMEM((planes, cells, wide), F32),
+            dma((cells // BLOCK,)),
         ),
-        two_flops, "output", (), (1,), True,
-    )
-    grad_volume, = call(
-        functools.partial(grad_volume_body, columns),
-        (shape((planes, cells, channels), F32),),
-        (me, grad_hidden, message, grad_outer, back_taps),
-        (windows, pltpu.VMEM((planes, cells, channels), F32), dma((cells // BLOCK,))),
-        one_flops, "grad_volume", (0,), (), True,
-    )
+        two_flops, "output", (), (), True,
+    )
+    grad_windows, = call(
+        functools.partial(grad_windows_body, columns), (shape(slab, BF16),),
+        (me, grad_hidden, message, grad_outer),
+        (), one_flops // 4, "grad_windows", (0,),
+    )
+    came = split
+    for step, bit in enumerate(order[1:]):
+        goes = split if bit == 1 else 0
+        bits, sent, kept = halve(bits, bit, came, goes, kept, arrived)
+        if step == 0:
+            sent, grad_windows, output = lax.optimization_barrier((sent, grad_windows, output))
+            grad_volume, = call(
+                functools.partial(grad_volume_body, columns),
+                (shape((planes, cells, channels), F32),),
+                (grad_windows, back_taps),
+                (pltpu.VMEM((planes, cells, channels), F32), dma((cells // BLOCK,))),
+                one_flops, "grad_volume", (), (), True,
+            )
+        if step == 1:
+            sent, grad_volume = lax.optimization_barrier((sent, grad_volume))
+        arrived = lax.ppermute(sent, "space", [(i, i ^ (1 << bit)) for i in range(count)])
+        came = goes
     grad_one, grad_two = call(
-        functools.partial(finish_body, scale, split, (mid // count, wide // count)),
+        functools.partial(finish_body, scale, came, (mid // count, wide // count)),
         (shape((27, mid // count, channels), F32), shape((27, wide // count, mid), F32)),
-        (me, mine, arrived), name="finish", smem=(0,),
+        (kept, arrived), name="finish",
     )
     return (
         output.reshape(planes, rows, columns, wide),

time: 59.2 us -> 56.9 us (0.961)
  starting transfers between devices: 23.2 us -> 16.7 us
  waiting for transfers between devices: 6.19 us -> 12.1 us
  Pallas kernels: 28.6 us -> 27 us
    all_to_all x1 -> x0, starting transfers between devices: 13.1 us -> none  [shards(): lax.all_to_all(sent, 'space', 0, 0, tiled=True, axis_index_groups=[list(r...]
    ppermute x0 -> x3, waiting for transfers between devices: none -> 10.8 us  [the longest x2 6.55 us: shards(): lax.ppermute(sent, 'space', [(i, i ^ 1 << bit) for i in range(count)])]
    ppermute x0 -> x3, starting transfers between devices: none -> 6.69 us  [the longest x1 3.97 us: shards(): lax.ppermute(sent, 'space', [(i, i ^ 1 << order[0]) for i in range(count)])]
    all_to_all x1 -> x0, waiting for transfers between devices: 4.71 us -> none  [shards(): lax.all_to_all(sent, 'space', 0, 0, tiled=True, axis_index_groups=[list(r...]
    pallas_call x11 -> x15, Pallas kernels: 28.6 us -> 27 us  [call(): pl.pallas_call(body, out_shape=list(outs), in_specs=[pl.BlockSpec(memory_...]
  transfers between devices with their start and end apart: 7 -> 9, of which waited for: 2 -> 4; matrix products, arithmetic and copies ran while one was open for 0% -> 0% of each run, Pallas kernels for 40% -> 39%
where the time goes in v8:
time: 56.9 us; the launch traced here: 56.7 us
  Pallas kernels  27 us (47%)
  starting transfers between devices  16.7 us (29%)
  waiting for transfers between devices  12.1 us (21%)
  between operations  0.82 us (1%)
    pallas_call x15, Pallas kernels, call(): pl.pallas_call(body, out_shape=list(outs), in_specs=[pl.BlockSpec(memory_...  27 us
    ppermute x2, waiting for transfers between devices, shards(): lax.ppermute(sent, 'space', [(i, i ^ 1 << bit) for i in range(count)])  6.55 us
    ppermute x1, starting transfers between devices, shards(): vol_inner = lax.ppermute(own, 'space', within)  4.36 us
    ppermute x1, waiting for transfers between devices, shards(): lax.ppermute(sent, 'space', [(i, i ^ 1 << order[0]) for i in range(count)])  4.24 us
    ppermute x1, starting transfers between devices, shards(): lax.ppermute(sent, 'space', [(i, i ^ 1 << order[0]) for i in range(count)])  3.97 us
    ppermute x1, starting transfers between devices, shards(): message = lax.ppermute(message, 'space', within)  3.35 us
    ppermute x2, starting transfers between devices, shards(): lax.ppermute(sent, 'space', [(i, i ^ 1 << bit) for i in range(count)])  2.73 us
    ppermute x1, waiting for transfers between devices, shards(): message = lax.ppermute(message, 'space', within)  1.29 us
  transfers between devices with their start and end apart: 9, of which 4 were waited for; matrix products, arithmetic and copies ran while one was open for 0% of the time, Pallas kernels for 39%

profile of v8, /device:TPU:0, one launch (start us, length us, event | category | flops | bytes accessed | tf_op | source)
XLA Modules:
  0.0 56.7 jit_solution(11984269833399407818)
XLA Ops:
  0.6 1.4 %pack_volume.1.own = bf16[2048,128]{1,0:T(8,128)(2,1)S(1)} custom-call(bf16[2,2048,64]{2,1,0:T(8,128)(2,1)} %bitcast.18), custom_call_target="tpu_custom_call" | custom-call | bytes 1048576 | tf_op jit(solution)/shard_map/pack_volume/pallas_call | solution.py:27
  2.0 0.7 %collective-permute-start.1 = (bf16[2048,128]{1,0:T(8,128)(2,1)S(1)}, bf16[2048,128]{1,0:T(8,128)(2,1)S(1)}, u32[]{:S(2)}, u32[]{:S(2)}) collective-permute-start(bf16[2048,128]{1,0:T(8,128)(2,1)S(1)} %pack_volume.1.own), channel_id=1, source_target_pairs={{1,2},{3,4},{5,6},{7,8},{9,10},{11,12},{13,14},{2,1},{4,3},{6,5},{... | collective-permute-start | bytes 1572872 | tf_op jit(solution)/shard_map/ppermute | solution.py:490
  2.7 4.4 %collective-permute-start = (bf16[2048,128]{1,0:T(8,128)(2,1)S(1)}, bf16[2048,128]{1,0:T(8,128)(2,1)S(1)}, u32[]{:S(2)}, u32[]{:S(2)}) collective-permute-start(bf16[2048,128]{1,0:T(8,128)(2,1)S(1)} %pack_volume.1.own), channel_id=1, source_target_pairs={{0,1},{1,0},{2,3},{3,2},{4,5},{5,4},{6,7},{7,6},{8,9},{9,8},{10,11... | collective-permute-start | bytes 1572872 | tf_op jit(solution)/shard_map/ppermute | solution.py:491
  7.1 4.6 %grad_act_terms.1 = (f32[2048,128]{1,0:T(8,128)S(1)}, bf16[1024,128]{1,0:T(8,128)(2,1)S(1)}, bf16[1024,128]{1,0:T(8,128)(2,1)S(1)}, bf16[256,2048]{1,0:T(8,128)(2,1)S(1)}) custom-call(s32[1]{0:T(128)} %bitcast.me, bf16[2,2048,128]{2,1,0:T(8,128)(2,1)} %bitcast.19, bf16[27,64,128]{2,1,0:T(8,128)(2,1)} %bitcast.15), custom_call_target="tpu_custom_call" | custom-call | flops 1811939328 | bytes 4112388 | tf_op jit(solution)/shard_map/grad_act_terms/pallas_call | solution.py:27
  11.7 0.2 back_taps.1.taps
  11.9 2.8 %prepare.1 = (bf16[2112,384]{1,0:T(8,128)(2,1)S(1)}, f32[2048,256]{1,0:T(8,128)S(1)}, bf16[2304,256]{1,0:T(8,128)(2,1)S(1)}) custom-call(bf16[2048,128]{1,0:T(8,128)(2,1)S(1)} %pack_volume.1.own, bf16[27,64,64]{2,1,0:T(8,128)(2,1)} %bitcast.13), custom_call_target="tpu_custom_call" | custom-call | flops 905969664 | bytes 5644288 | tf_op jit(solution)/shard_map/prepare/pallas_call | solution.py:27
  14.7 0.1 collective-permute-start.2
  14.8 0.7 %collective-permute-start.3 = (bf16[1024,128]{1,0:T(8,128)(2,1)S(1)}, bf16[1024,128]{1,0:T(8,128)(2,1)S(1)}, u32[]{:S(2)}, u32[]{:S(2)}) collective-permute-start(bf16[1024,128]{1,0:T(8,128)(2,1)S(1)} %get-tuple-element.55), channel_id=1, source_target_pairs={{1,2},{3,4},{5,6},{7,8},{9,10},{11,12},{13,14},{2,1},{4,3},{6,5},{... | collective-permute-start | bytes 786440 | tf_op jit(solution)/shard_map/ppermute | solution.py:518
  15.4 0.0 collective-permute-done.1.outer
  15.5 0.0 collective-permute-done.inner
  15.5 4.3 %hidden.1 = (bf16[2112,768]{1,0:T(8,128)(2,1)S(1)}, bf16[2112,768]{1,0:T(8,128)(2,1)S(1)}, f32[2048,128]{1,0:T(8,128)S(1)}) custom-call(s32[1]{0:T(128)} %bitcast.me, bf16[2048,128]{1,0:T(8,128)(2,1)S(1)} %collective-permute-done.inner, bf16[2048,128]{1,0:T(8,128)(2,1)S(1)} %collective-permute-done.1.outer, f32[2048,256]{1,0:T(8,128)S(1)} %get-tuple-element.48.part, ...), custom_call_target="tpu_custom_call" | custom-call | flops 1811939328 | bytes 11862020 | tf_op jit(solution)/shard_map/hidden/pallas_call | solution.py:27
  19.8 2.8 %grad_two_terms.1.other = f32[128,1792]{1,0:T(8,128)S(1)} custom-call(bf16[2112,768]{1,0:T(8,128)(2,1)S(1)} %get-tuple-element.68.act_windows, bf16[256,2048]{1,0:T(8,128)(2,1)S(1)} %get-tuple-element.54.turned), custom_call_target="tpu_custom_call" | custom-call | flops 1811939328 | bytes 5210112 | tf_op jit(solution)/shard_map/grad_two_terms/pallas_call | solution.py:27
  22.5 0.0 collective-permute-done.3.outer
  22.5 0.0 collective-permute-done.2.inner
  22.5 0.9 %grad_hidden.1 = (bf16[2048,128]{1,0:T(8,128)(2,1)S(1)}, bf16[1024,128]{1,0:T(8,128)(2,1)S(1)}, bf16[1024,128]{1,0:T(8,128)(2,1)S(1)}) custom-call(s32[1]{0:T(128)} %bitcast.me, f32[2048,128]{1,0:T(8,128)S(1)} %get-tuple-element.51.terms, bf16[1024,128]{1,0:T(8,128)(2,1)S(1)} %collective-permute-done.2.inner, ...), custom_call_target="tpu_custom_call" | custom-call | bytes 3670020 | tf_op jit(solution)/shard_map/grad_hidden/pallas_call | solution.py:27
  23.4 1.8 %grad_one_terms.1 = (bf16[3712,128]{1,0:T(8,128)(2,1)S(1)}, f32[8,24,896]{2,1,0:T(8,128)S(1)}) custom-call(s32[1]{0:T(128)} %bitcast.me, bf16[2112,384]{1,0:T(8,128)(2,1)S(1)} %get-tuple-element.44.own_windows, bf16[2112,768]{1,0:T(8,128)(2,1)S(1)} %get-tuple-element.50.side_windows, bf16[2048,128]{1,0:T(8,128)(2,1)S(1)} %get-tuple-element.58.grad.own, ...), custom_call_target="tpu_custom_call" | custom-call | flops 905969664 | bytes 8208388 | tf_op jit(solution)/shard_map/grad_one_terms/pallas_call | solution.py:27
  25.2 3.4 %collective-permute-start.4 = (bf16[3712,128]{1,0:T(8,128)(2,1)S(1)}, bf16[3712,128]{1,0:T(8,128)(2,1)S(1)}, u32[]{:S(2)}, u32[]{:S(2)}) collective-permute-start(bf16[3712,128]{1,0:T(8,128)(2,1)S(1)} %get-tuple-element.62), channel_id=1, source_target_pairs={{0,1},{1,0},{2,3},{3,2},{4,5},{5,4},{6,7},{7,6},{8,9},{9,8},{10,11... | collective-permute-start | bytes 2850824 | tf_op jit(solution)/shard_map/ppermute | solution.py:548
  28.6 0.8 %collective-permute-start.6 = (bf16[1024,128]{1,0:T(8,128)(2,1)S(1)}, bf16[1024,128]{1,0:T(8,128)(2,1)S(1)}, u32[]{:S(2)}, u32[]{:S(2)}) collective-permute-start(bf16[1024,128]{1,0:T(8,128)(2,1)S(1)} %get-tuple-element.67), channel_id=1, source_target_pairs={{1,2},{3,4},{5,6},{7,8},{9,10},{11,12},{13,14},{2,1},{4,3},{6,5},{... | collective-permute-start | bytes 786440 | tf_op jit(solution)/shard_map/ppermute | solution.py:536
  29.4 1.3 %collective-permute-done.4.arrived.message = bf16[3712,128]{1,0:T(8,128)(2,1)S(1)} collective-permute-done((bf16[3712,128]{1,0:T(8,128)(2,1)S(1)}, bf16[3712,128]{1,0:T(8,128)(2,1)S(1)}, u32[]{:S(2)}, u32[]{:S(2)}) %collective-permute-start.4) | collective-permute-done | bytes 950304 | tf_op jit(solution)/shard_map/ppermute | solution.py:548
  30.7 0.1 halve.3
  30.9 0.0 copy-start.1
  30.9 4.0 %collective-permute-start.5 = (bf16[4,32,896]{2,1,0:T(8,128)(2,1)S(1)}, bf16[4,32,896]{2,1,0:T(8,128)(2,1)S(1)}, u32[]{:S(2)}, u32[]{:S(2)}) collective-permute-start(bf16[4,32,896]{2,1,0:T(8,128)(2,1)S(1)} %get-tuple-element.65), channel_id=1, source_target_pairs={{0,4},{1,5},{2,6},{3,7},{4,0},{5,1},{6,2},{7,3},{8,12},{9,13},{10,... | collective-permute-start | bytes 688136 | tf_op jit(solution)/shard_map/ppermute | solution.py:562
  34.8 0.0 collective-permute-done.6.outer
  34.8 0.8 %grad_windows.1.windows = bf16[2112,768]{1,0:T(8,128)(2,1)S(1)} custom-call(s32[1]{0:T(128)} %bitcast.me, bf16[2048,128]{1,0:T(8,128)(2,1)S(1)} %get-tuple-element.58.grad.own, bf16[3712,128]{1,0:T(8,128)(2,1)S(1)} %collective-permute-done.4.arrived.message, bf16[1024,128]{1,0:T(8,128)(2,1)S(1)} %collective-permute-done.6.outer), custom_call_target="tpu_custom_call" | custom-call | flops 226492416 | bytes 4980740 | tf_op jit(solution)/shard_map/grad_windows/pallas_call | solution.py:27
  35.7 3.7 %output.1 = f32[2,2048,128]{2,1,0:T(8,128)} custom-call(bf16[2112,768]{1,0:T(8,128)(2,1)S(1)} %get-tuple-element.68.act_windows, bf16[27,64,128]{2,1,0:T(8,128)(2,1)S(1)} %bitcast.16), custom_call_target="tpu_custom_call" | custom-call | flops 1811939328 | bytes 5783552 | tf_op jit(solution)/shard_map/output/pallas_call | solution.py:27
  39.4 4.2 %collective-permute-done.5.arrived = bf16[4,32,896]{2,1,0:T(8,128)(2,1)S(1)} collective-permute-done((bf16[4,32,896]{2,1,0:T(8,128)(2,1)S(1)}, bf16[4,32,896]{2,1,0:T(8,128)(2,1)S(1)}, u32[]{:S(2)}, u32[]{:S(2)}) %collective-permute-start.5) | collective-permute-done | bytes 229408 | tf_op jit(solution)/shard_map/ppermute | solution.py:562
  43.7 2.7 %collective-permute-start.7 = (bf16[2,24,896]{2,1,0:T(8,128)(2,1)S(1)}, bf16[2,24,896]{2,1,0:T(8,128)(2,1)S(1)}, u32[]{:S(2)}, u32[]{:S(2)}) collective-permute-start(bf16[2,24,896]{2,1,0:T(8,128)(2,1)S(1)} %get-tuple-element.71), channel_id=1, source_target_pairs={{0,8},{1,9},{2,10},{3,11},{4,12},{5,13},{6,14},{7,15},{8,0},{9,1},... | collective-permute-start | bytes 258056 | tf_op jit(solution)/shard_map/ppermute | solution.py:593
  46.3 2.9 %grad_volume.1 = f32[2,2048,64]{2,1,0:T(8,128)} custom-call(bf16[2112,768]{1,0:T(8,128)(2,1)S(1)} %grad_windows.1.windows, bf16[384,768]{1,0:T(8,128)(2,1)S(1)} %back_taps.1.taps), custom_call_target="tpu_custom_call" | custom-call | flops 905969664 | bytes 4882432 | tf_op jit(solution)/shard_map/grad_volume/pallas_call | solution.py:27
  49.3 2.4 %collective-permute-done.7.arrived = bf16[2,24,896]{2,1,0:T(8,128)(2,1)S(1)} collective-permute-done((bf16[2,24,896]{2,1,0:T(8,128)(2,1)S(1)}, bf16[2,24,896]{2,1,0:T(8,128)(2,1)S(1)}, u32[]{:S(2)}, u32[]{:S(2)}) %collective-permute-start.7) | collective-permute-done | bytes 86048 | tf_op jit(solution)/shard_map/ppermute | solution.py:593
  51.7 0.1 collective-permute-start.8
  51.8 4.2 %collective-permute-done.8.arrived = bf16[1,32,896]{2,1,0:T(8,128)(2,1)S(1)} collective-permute-done((bf16[1,32,896]{2,1,0:T(8,128)(2,1)S(1)}, bf16[1,32,896]{2,1,0:T(8,128)(2,1)S(1)}, u32[]{:S(2)}, u32[]{:S(2)}) %collective-permute-start.8) | collective-permute-done | bytes 57376 | tf_op jit(solution)/shard_map/ppermute | solution.py:593
  55.9 0.7 %finish.1 = (f32[27,4,64]{2,1,0:T(4,128)}, f32[27,8,64]{2,1,0:T(8,128)}) custom-call(f32[1,24,896]{2,1,0:T(8,128)S(1)} %get-tuple-element.76.mine, bf16[1,32,896]{2,1,0:T(8,128)(2,1)S(1)} %collective-permute-done.8.arrived), custom_call_target="tpu_custom_call" | custom-call | bytes 226304 | tf_op jit(solution)/shard_map/finish/pallas_call | solution.py:27
  (5 shorter events, 0.1 us)
Async XLA Ops:
  2.0 13.4 %collective-permute-start.1 = (bf16[2048,128]{1,0:T(8,128)(2,1)S(1)}, bf16[2048,128]{1,0:T(8,128)(2,1)S(1)}, u32[]{:S(2)}, u32[]{:S(2)}) collective-permute-start(bf16[2048,128]{1,0:T(8,128)(2,1)S(1)} %pack_volume.1.own), channel_id=1, source_target_pairs={{1,2},{3,4},{5,6},{7,8},{9,10},{11,12},{13,14},{2,1},{4,3},{6,5},{... | collective-permute-start | bytes 1572872 | tf_op jit(solution)/shard_map/ppermute | solution.py:490
  2.7 12.7 %collective-permute-start = (bf16[2048,128]{1,0:T(8,128)(2,1)S(1)}, bf16[2048,128]{1,0:T(8,128)(2,1)S(1)}, u32[]{:S(2)}, u32[]{:S(2)}) collective-permute-start(bf16[2048,128]{1,0:T(8,128)(2,1)S(1)} %pack_volume.1.own), channel_id=1, source_target_pairs={{0,1},{1,0},{2,3},{3,2},{4,5},{5,4},{6,7},{7,6},{8,9},{9,8},{10,11... | collective-permute-start | bytes 1572872 | tf_op jit(solution)/shard_map/ppermute | solution.py:491
  7.1 4.6 %copy-start = (bf16[3,3,3,64,64]{4,3,2,1,0:T(8,128)(2,1)S(1)}, bf16[3,3,3,64,64]{4,3,2,1,0:T(8,128)(2,1)}, u32[]{:S(2)}) copy-start(bf16[3,3,3,64,64]{4,3,2,1,0:T(8,128)(2,1)} %param.5) | copy-start | bytes 663556
  14.7 7.9 %collective-permute-start.2 = (bf16[1024,128]{1,0:T(8,128)(2,1)S(1)}, bf16[1024,128]{1,0:T(8,128)(2,1)S(1)}, u32[]{:S(2)}, u32[]{:S(2)}) collective-permute-start(bf16[1024,128]{1,0:T(8,128)(2,1)S(1)} %get-tuple-element.52), channel_id=1, source_target_pairs={{0,1},{1,0},{2,3},{3,2},{4,5},{5,4},{6,7},{7,6},{8,9},{9,8},{10,11... | collective-permute-start | bytes 786440 | tf_op jit(solution)/shard_map/ppermute | solution.py:519
  14.8 7.8 %collective-permute-start.3 = (bf16[1024,128]{1,0:T(8,128)(2,1)S(1)}, bf16[1024,128]{1,0:T(8,128)(2,1)S(1)}, u32[]{:S(2)}, u32[]{:S(2)}) collective-permute-start(bf16[1024,128]{1,0:T(8,128)(2,1)S(1)} %get-tuple-element.55), channel_id=1, source_target_pairs={{1,2},{3,4},{5,6},{7,8},{9,10},{11,12},{13,14},{2,1},{4,3},{6,5},{... | collective-permute-start | bytes 786440 | tf_op jit(solution)/shard_map/ppermute | solution.py:518
  25.2 5.5 %collective-permute-start.4 = (bf16[3712,128]{1,0:T(8,128)(2,1)S(1)}, bf16[3712,128]{1,0:T(8,128)(2,1)S(1)}, u32[]{:S(2)}, u32[]{:S(2)}) collective-permute-start(bf16[3712,128]{1,0:T(8,128)(2,1)S(1)} %get-tuple-element.62), channel_id=1, source_target_pairs={{0,1},{1,0},{2,3},{3,2},{4,5},{5,4},{6,7},{7,6},{8,9},{9,8},{10,11... | collective-permute-start | bytes 2850824 | tf_op jit(solution)/shard_map/ppermute | solution.py:548
  28.6 6.3 %collective-permute-start.6 = (bf16[1024,128]{1,0:T(8,128)(2,1)S(1)}, bf16[1024,128]{1,0:T(8,128)(2,1)S(1)}, u32[]{:S(2)}, u32[]{:S(2)}) collective-permute-start(bf16[1024,128]{1,0:T(8,128)(2,1)S(1)} %get-tuple-element.67), channel_id=1, source_target_pairs={{1,2},{3,4},{5,6},{7,8},{9,10},{11,12},{13,14},{2,1},{4,3},{6,5},{... | collective-permute-start | bytes 786440 | tf_op jit(solution)/shard_map/ppermute | solution.py:536
  30.9 4.8 %copy-start.1 = (bf16[3,3,3,64,128]{4,3,2,1,0:T(8,128)(2,1)S(1)}, bf16[3,3,3,64,128]{4,3,2,1,0:T(8,128)(2,1)}, u32[]{:S(2)}) copy-start(bf16[3,3,3,64,128]{4,3,2,1,0:T(8,128)(2,1)} %param.6) | copy-start | bytes 1327108
  30.9 12.8 %collective-permute-start.5 = (bf16[4,32,896]{2,1,0:T(8,128)(2,1)S(1)}, bf16[4,32,896]{2,1,0:T(8,128)(2,1)S(1)}, u32[]{:S(2)}, u32[]{:S(2)}) collective-permute-start(bf16[4,32,896]{2,1,0:T(8,128)(2,1)S(1)} %get-tuple-element.65), channel_id=1, source_target_pairs={{0,4},{1,5},{2,6},{3,7},{4,0},{5,1},{6,2},{7,3},{8,12},{9,13},{10,... | collective-permute-start | bytes 688136 | tf_op jit(solution)/shard_map/ppermute | solution.py:562
  43.7 8.0 %collective-permute-start.7 = (bf16[2,24,896]{2,1,0:T(8,128)(2,1)S(1)}, bf16[2,24,896]{2,1,0:T(8,128)(2,1)S(1)}, u32[]{:S(2)}, u32[]{:S(2)}) collective-permute-start(bf16[2,24,896]{2,1,0:T(8,128)(2,1)S(1)} %get-tuple-element.71), channel_id=1, source_target_pairs={{0,8},{1,9},{2,10},{3,11},{4,12},{5,13},{6,14},{7,15},{8,0},{9,1},... | collective-permute-start | bytes 258056 | tf_op jit(solution)/shard_map/ppermute | solution.py:593
  51.7 4.2 %collective-permute-start.8 = (bf16[1,32,896]{2,1,0:T(8,128)(2,1)S(1)}, bf16[1,32,896]{2,1,0:T(8,128)(2,1)S(1)}, u32[]{:S(2)}, u32[]{:S(2)}) collective-permute-start(bf16[1,32,896]{2,1,0:T(8,128)(2,1)S(1)} %get-tuple-element.77), channel_id=1, source_target_pairs={{0,2},{1,3},{2,0},{3,1},{4,6},{5,7},{6,4},{7,5},{8,10},{9,11},{10,... | collective-permute-start | bytes 172040 | tf_op jit(solution)/shard_map/ppermute | solution.py:593

commit v9 on v8

--- a/solution.py
+++ b/solution.py
@@ -570,6 +570,7 @@
         ),
         two_flops, "output", (), (), True,
     )
+    output, grad_outer = lax.optimization_barrier((output, grad_outer))
     grad_windows, = call(
         functools.partial(grad_windows_body, columns), (shape(slab, BF16),),
         (me, grad_hidden, message, grad_outer),

time: 56.9 us -> 54.6 us (0.960)
  waiting for transfers between devices: 12.1 us -> 9.09 us
  starting transfers between devices: 16.7 us -> 17.4 us
    ppermute x2, waiting for transfers between devices: 6.55 us -> 3.53 us  [shards(): lax.ppermute(sent, 'space', [(i, i ^ 1 << bit) for i in range(count)])]
    ppermute x2, starting transfers between devices: 2.73 us -> 3.36 us  [shards(): lax.ppermute(sent, 'space', [(i, i ^ 1 << bit) for i in range(count)])]
  transfers between devices with their start and end apart: 9 -> 9, of which waited for: 4 -> 3; matrix products, arithmetic and copies ran while one was open for 0% -> 0% of each run, Pallas kernels for 39% -> 41%
where the time goes in v9:
time: 54.6 us; the launch traced here: 54.3 us
  Pallas kernels  27.1 us (50%)
  starting transfers between devices  17.4 us (32%)
  waiting for transfers between devices  9.09 us (17%)
  between operations  0.82 us (2%)
    pallas_call x15, Pallas kernels, call(): pl.pallas_call(body, out_shape=list(outs), in_specs=[pl.BlockSpec(memory_...  27.1 us
    ppermute x1, starting transfers between devices, shards(): vol_inner = lax.ppermute(own, 'space', within)  4.36 us
    ppermute x1, waiting for transfers between devices, shards(): lax.ppermute(sent, 'space', [(i, i ^ 1 << order[0]) for i in range(count)])  4.25 us
    ppermute x1, starting transfers between devices, shards(): lax.ppermute(sent, 'space', [(i, i ^ 1 << order[0]) for i in range(count)])  3.97 us
    ppermute x2, waiting for transfers between devices, shards(): lax.ppermute(sent, 'space', [(i, i ^ 1 << bit) for i in range(count)])  3.53 us
    ppermute x2, starting transfers between devices, shards(): lax.ppermute(sent, 'space', [(i, i ^ 1 << bit) for i in range(count)])  3.36 us
    ppermute x1, starting transfers between devices, shards(): message = lax.ppermute(message, 'space', within)  3.35 us
    ppermute x1, waiting for transfers between devices, shards(): message = lax.ppermute(message, 'space', within)  1.29 us
  transfers between devices with their start and end apart: 9, of which 3 were waited for; matrix products, arithmetic and copies ran while one was open for 0% of the time, Pallas kernels for 41%

profile of v9, /device:TPU:0, one launch (start us, length us, event | category | flops | bytes accessed | tf_op | source)
XLA Modules:
  0.0 54.3 jit_solution(1213600730602758721)
XLA Ops:
  0.6 1.4 %pack_volume.1.own = bf16[2048,128]{1,0:T(8,128)(2,1)S(1)} custom-call(bf16[2,2048,64]{2,1,0:T(8,128)(2,1)} %bitcast.18), custom_call_target="tpu_custom_call" | custom-call | bytes 1048576 | tf_op jit(solution)/shard_map/pack_volume/pallas_call | solution.py:27
  2.0 0.7 %collective-permute-start.1 = (bf16[2048,128]{1,0:T(8,128)(2,1)S(1)}, bf16[2048,128]{1,0:T(8,128)(2,1)S(1)}, u32[]{:S(2)}, u32[]{:S(2)}) collective-permute-start(bf16[2048,128]{1,0:T(8,128)(2,1)S(1)} %pack_volume.1.own), channel_id=1, source_target_pairs={{1,2},{3,4},{5,6},{7,8},{9,10},{11,12},{13,14},{2,1},{4,3},{6,5},{... | collective-permute-start | bytes 1572872 | tf_op jit(solution)/shard_map/ppermute | solution.py:490
  2.7 4.4 %collective-permute-start = (bf16[2048,128]{1,0:T(8,128)(2,1)S(1)}, bf16[2048,128]{1,0:T(8,128)(2,1)S(1)}, u32[]{:S(2)}, u32[]{:S(2)}) collective-permute-start(bf16[2048,128]{1,0:T(8,128)(2,1)S(1)} %pack_volume.1.own), channel_id=1, source_target_pairs={{0,1},{1,0},{2,3},{3,2},{4,5},{5,4},{6,7},{7,6},{8,9},{9,8},{10,11... | collective-permute-start | bytes 1572872 | tf_op jit(solution)/shard_map/ppermute | solution.py:491
  7.1 4.6 %grad_act_terms.1 = (f32[2048,128]{1,0:T(8,128)S(1)}, bf16[1024,128]{1,0:T(8,128)(2,1)S(1)}, bf16[1024,128]{1,0:T(8,128)(2,1)S(1)}, bf16[256,2048]{1,0:T(8,128)(2,1)S(1)}) custom-call(s32[1]{0:T(128)} %bitcast.me, bf16[2,2048,128]{2,1,0:T(8,128)(2,1)} %bitcast.19, bf16[27,64,128]{2,1,0:T(8,128)(2,1)} %bitcast.15), custom_call_target="tpu_custom_call" | custom-call | flops 1811939328 | bytes 4112388 | tf_op jit(solution)/shard_map/grad_act_terms/pallas_call | solution.py:27
  11.7 0.2 back_taps.1.taps
  11.9 2.8 %prepare.1 = (bf16[2112,384]{1,0:T(8,128)(2,1)S(1)}, f32[2048,256]{1,0:T(8,128)S(1)}, bf16[2304,256]{1,0:T(8,128)(2,1)S(1)}) custom-call(bf16[2048,128]{1,0:T(8,128)(2,1)S(1)} %pack_volume.1.own, bf16[27,64,64]{2,1,0:T(8,128)(2,1)} %bitcast.13), custom_call_target="tpu_custom_call" | custom-call | flops 905969664 | bytes 5644288 | tf_op jit(solution)/shard_map/prepare/pallas_call | solution.py:27
  14.7 0.1 collective-permute-start.2
  14.8 0.7 %collective-permute-start.3 = (bf16[1024,128]{1,0:T(8,128)(2,1)S(1)}, bf16[1024,128]{1,0:T(8,128)(2,1)S(1)}, u32[]{:S(2)}, u32[]{:S(2)}) collective-permute-start(bf16[1024,128]{1,0:T(8,128)(2,1)S(1)} %get-tuple-element.57), channel_id=1, source_target_pairs={{1,2},{3,4},{5,6},{7,8},{9,10},{11,12},{13,14},{2,1},{4,3},{6,5},{... | collective-permute-start | bytes 786440 | tf_op jit(solution)/shard_map/ppermute | solution.py:518
  15.4 0.0 collective-permute-done.1.outer
  15.5 0.0 collective-permute-done.inner
  15.5 4.3 %hidden.1 = (bf16[2112,768]{1,0:T(8,128)(2,1)S(1)}, bf16[2112,768]{1,0:T(8,128)(2,1)S(1)}, f32[2048,128]{1,0:T(8,128)S(1)}) custom-call(s32[1]{0:T(128)} %bitcast.me, bf16[2048,128]{1,0:T(8,128)(2,1)S(1)} %collective-permute-done.inner, bf16[2048,128]{1,0:T(8,128)(2,1)S(1)} %collective-permute-done.1.outer, f32[2048,256]{1,0:T(8,128)S(1)} %get-tuple-element.50.part, ...), custom_call_target="tpu_custom_call" | custom-call | flops 1811939328 | bytes 11862020 | tf_op jit(solution)/shard_map/hidden/pallas_call | solution.py:27
  19.8 2.8 %grad_two_terms.1.other = f32[128,1792]{1,0:T(8,128)S(1)} custom-call(bf16[2112,768]{1,0:T(8,128)(2,1)S(1)} %get-tuple-element.69.act_windows, bf16[256,2048]{1,0:T(8,128)(2,1)S(1)} %get-tuple-element.56.turned), custom_call_target="tpu_custom_call" | custom-call | flops 1811939328 | bytes 5210112 | tf_op jit(solution)/shard_map/grad_two_terms/pallas_call | solution.py:27
  22.5 0.0 collective-permute-done.3.outer
  22.5 0.0 collective-permute-done.2.inner
  22.5 0.9 %grad_hidden.1 = (bf16[2048,128]{1,0:T(8,128)(2,1)S(1)}, bf16[1024,128]{1,0:T(8,128)(2,1)S(1)}, bf16[1024,128]{1,0:T(8,128)(2,1)S(1)}) custom-call(s32[1]{0:T(128)} %bitcast.me, f32[2048,128]{1,0:T(8,128)S(1)} %get-tuple-element.53.terms, bf16[1024,128]{1,0:T(8,128)(2,1)S(1)} %collective-permute-done.2.inner, ...), custom_call_target="tpu_custom_call" | custom-call | bytes 3670020 | tf_op jit(solution)/shard_map/grad_hidden/pallas_call | solution.py:27
  23.4 0.0 copy-start.1
  23.4 1.8 %grad_one_terms.1 = (bf16[3712,128]{1,0:T(8,128)(2,1)S(1)}, f32[8,24,896]{2,1,0:T(8,128)S(1)}) custom-call(s32[1]{0:T(128)} %bitcast.me, bf16[2112,384]{1,0:T(8,128)(2,1)S(1)} %get-tuple-element.46.own_windows, bf16[2112,768]{1,0:T(8,128)(2,1)S(1)} %get-tuple-element.52.side_windows, bf16[2048,128]{1,0:T(8,128)(2,1)S(1)} %get-tuple-element.60.grad.own, ...), custom_call_target="tpu_custom_call" | custom-call | flops 905969664 | bytes 8208388 | tf_op jit(solution)/shard_map/grad_one_terms/pallas_call | solution.py:27
  25.2 3.4 %collective-permute-start.4 = (bf16[3712,128]{1,0:T(8,128)(2,1)S(1)}, bf16[3712,128]{1,0:T(8,128)(2,1)S(1)}, u32[]{:S(2)}, u32[]{:S(2)}) collective-permute-start(bf16[3712,128]{1,0:T(8,128)(2,1)S(1)} %get-tuple-element.64), channel_id=1, source_target_pairs={{0,1},{1,0},{2,3},{3,2},{4,5},{5,4},{6,7},{7,6},{8,9},{9,8},{10,11... | collective-permute-start | bytes 2850824 | tf_op jit(solution)/shard_map/ppermute | solution.py:548
  28.6 0.8 %collective-permute-start.6 = (bf16[1024,128]{1,0:T(8,128)(2,1)S(1)}, bf16[1024,128]{1,0:T(8,128)(2,1)S(1)}, u32[]{:S(2)}, u32[]{:S(2)}) collective-permute-start(bf16[1024,128]{1,0:T(8,128)(2,1)S(1)} %get-tuple-element.70), channel_id=1, source_target_pairs={{1,2},{3,4},{5,6},{7,8},{9,10},{11,12},{13,14},{2,1},{4,3},{6,5},{... | collective-permute-start | bytes 786440 | tf_op jit(solution)/shard_map/ppermute | solution.py:536
  29.4 1.3 %collective-permute-done.4.arrived.message = bf16[3712,128]{1,0:T(8,128)(2,1)S(1)} collective-permute-done((bf16[3712,128]{1,0:T(8,128)(2,1)S(1)}, bf16[3712,128]{1,0:T(8,128)(2,1)S(1)}, u32[]{:S(2)}, u32[]{:S(2)}) %collective-permute-start.4) | collective-permute-done | bytes 950304 | tf_op jit(solution)/shard_map/ppermute | solution.py:548
  30.7 0.1 halve.3
  30.9 4.0 %collective-permute-start.5 = (bf16[4,32,896]{2,1,0:T(8,128)(2,1)S(1)}, bf16[4,32,896]{2,1,0:T(8,128)(2,1)S(1)}, u32[]{:S(2)}, u32[]{:S(2)}) collective-permute-start(bf16[4,32,896]{2,1,0:T(8,128)(2,1)S(1)} %get-tuple-element.67), channel_id=1, source_target_pairs={{0,4},{1,5},{2,6},{3,7},{4,0},{5,1},{6,2},{7,3},{8,12},{9,13},{10,... | collective-permute-start | bytes 688136 | tf_op jit(solution)/shard_map/ppermute | solution.py:562
  34.8 3.7 %output.1 = f32[2,2048,128]{2,1,0:T(8,128)} custom-call(bf16[2112,768]{1,0:T(8,128)(2,1)S(1)} %get-tuple-element.69.act_windows, bf16[27,64,128]{2,1,0:T(8,128)(2,1)S(1)} %bitcast.16), custom_call_target="tpu_custom_call" | custom-call | flops 1811939328 | bytes 5783552 | tf_op jit(solution)/shard_map/output/pallas_call | solution.py:27
  38.5 0.0 collective-permute-done.6.outer
  38.6 0.8 %grad_windows.1.windows = bf16[2112,768]{1,0:T(8,128)(2,1)S(1)} custom-call(s32[1]{0:T(128)} %bitcast.me, bf16[2048,128]{1,0:T(8,128)(2,1)S(1)} %get-tuple-element.60.grad.own, bf16[3712,128]{1,0:T(8,128)(2,1)S(1)} %collective-permute-done.4.arrived.message, bf16[1024,128]{1,0:T(8,128)(2,1)S(1)} %collective-permute-done.6.outer), custom_call_target="tpu_custom_call" | custom-call | flops 226492416 | bytes 4980740 | tf_op jit(solution)/shard_map/grad_windows/pallas_call | solution.py:27
  39.4 4.3 %collective-permute-done.5.arrived = bf16[4,32,896]{2,1,0:T(8,128)(2,1)S(1)} collective-permute-done((bf16[4,32,896]{2,1,0:T(8,128)(2,1)S(1)}, bf16[4,32,896]{2,1,0:T(8,128)(2,1)S(1)}, u32[]{:S(2)}, u32[]{:S(2)}) %collective-permute-start.5) | collective-permute-done | bytes 229408 | tf_op jit(solution)/shard_map/ppermute | solution.py:562
  43.7 2.6 %collective-permute-start.7 = (bf16[2,24,896]{2,1,0:T(8,128)(2,1)S(1)}, bf16[2,24,896]{2,1,0:T(8,128)(2,1)S(1)}, u32[]{:S(2)}, u32[]{:S(2)}) collective-permute-start(bf16[2,24,896]{2,1,0:T(8,128)(2,1)S(1)} %get-tuple-element.75), channel_id=1, source_target_pairs={{0,8},{1,9},{2,10},{3,11},{4,12},{5,13},{6,14},{7,15},{8,0},{9,1},... | collective-permute-start | bytes 258056 | tf_op jit(solution)/shard_map/ppermute | solution.py:594
  46.4 2.9 %grad_volume.1 = f32[2,2048,64]{2,1,0:T(8,128)} custom-call(bf16[2112,768]{1,0:T(8,128)(2,1)S(1)} %grad_windows.1.windows, bf16[384,768]{1,0:T(8,128)(2,1)S(1)} %back_taps.1.taps), custom_call_target="tpu_custom_call" | custom-call | flops 905969664 | bytes 4882432 | tf_op jit(solution)/shard_map/grad_volume/pallas_call | solution.py:27
  49.3 0.0 collective-permute-done.7.arrived
  49.3 0.7 %collective-permute-start.8 = (bf16[1,32,896]{2,1,0:T(8,128)(2,1)S(1)}, bf16[1,32,896]{2,1,0:T(8,128)(2,1)S(1)}, u32[]{:S(2)}, u32[]{:S(2)}) collective-permute-start(bf16[1,32,896]{2,1,0:T(8,128)(2,1)S(1)} %get-tuple-element.81), channel_id=1, source_target_pairs={{0,2},{1,3},{2,0},{3,1},{4,6},{5,7},{6,4},{7,5},{8,10},{9,11},{10,... | collective-permute-start | bytes 172040 | tf_op jit(solution)/shard_map/ppermute | solution.py:594
  50.0 3.5 %collective-permute-done.8.arrived = bf16[1,32,896]{2,1,0:T(8,128)(2,1)S(1)} collective-permute-done((bf16[1,32,896]{2,1,0:T(8,128)(2,1)S(1)}, bf16[1,32,896]{2,1,0:T(8,128)(2,1)S(1)}, u32[]{:S(2)}, u32[]{:S(2)}) %collective-permute-start.8) | collective-permute-done | bytes 57376 | tf_op jit(solution)/shard_map/ppermute | solution.py:594
  53.6 0.7 %finish.1 = (f32[27,4,64]{2,1,0:T(4,128)}, f32[27,8,64]{2,1,0:T(8,128)}) custom-call(f32[1,24,896]{2,1,0:T(8,128)S(1)} %get-tuple-element.80.mine, bf16[1,32,896]{2,1,0:T(8,128)(2,1)S(1)} %collective-permute-done.8.arrived), custom_call_target="tpu_custom_call" | custom-call | bytes 226304 | tf_op jit(solution)/shard_map/finish/pallas_call | solution.py:27
  (5 shorter events, 0.1 us)
Async XLA Ops:
  2.0 13.4 %collective-permute-start.1 = (bf16[2048,128]{1,0:T(8,128)(2,1)S(1)}, bf16[2048,128]{1,0:T(8,128)(2,1)S(1)}, u32[]{:S(2)}, u32[]{:S(2)}) collective-permute-start(bf16[2048,128]{1,0:T(8,128)(2,1)S(1)} %pack_volume.1.own), channel_id=1, source_target_pairs={{1,2},{3,4},{5,6},{7,8},{9,10},{11,12},{13,14},{2,1},{4,3},{6,5},{... | collective-permute-start | bytes 1572872 | tf_op jit(solution)/shard_map/ppermute | solution.py:490
  2.7 12.7 %collective-permute-start = (bf16[2048,128]{1,0:T(8,128)(2,1)S(1)}, bf16[2048,128]{1,0:T(8,128)(2,1)S(1)}, u32[]{:S(2)}, u32[]{:S(2)}) collective-permute-start(bf16[2048,128]{1,0:T(8,128)(2,1)S(1)} %pack_volume.1.own), channel_id=1, source_target_pairs={{0,1},{1,0},{2,3},{3,2},{4,5},{5,4},{6,7},{7,6},{8,9},{9,8},{10,11... | collective-permute-start | bytes 1572872 | tf_op jit(solution)/shard_map/ppermute | solution.py:491
  7.1 4.6 %copy-start = (bf16[3,3,3,64,64]{4,3,2,1,0:T(8,128)(2,1)S(1)}, bf16[3,3,3,64,64]{4,3,2,1,0:T(8,128)(2,1)}, u32[]{:S(2)}) copy-start(bf16[3,3,3,64,64]{4,3,2,1,0:T(8,128)(2,1)} %param.5) | copy-start | bytes 663556
  14.7 7.9 %collective-permute-start.2 = (bf16[1024,128]{1,0:T(8,128)(2,1)S(1)}, bf16[1024,128]{1,0:T(8,128)(2,1)S(1)}, u32[]{:S(2)}, u32[]{:S(2)}) collective-permute-start(bf16[1024,128]{1,0:T(8,128)(2,1)S(1)} %get-tuple-element.54), channel_id=1, source_target_pairs={{0,1},{1,0},{2,3},{3,2},{4,5},{5,4},{6,7},{7,6},{8,9},{9,8},{10,11... | collective-permute-start | bytes 786440 | tf_op jit(solution)/shard_map/ppermute | solution.py:519
  14.8 7.8 %collective-permute-start.3 = (bf16[1024,128]{1,0:T(8,128)(2,1)S(1)}, bf16[1024,128]{1,0:T(8,128)(2,1)S(1)}, u32[]{:S(2)}, u32[]{:S(2)}) collective-permute-start(bf16[1024,128]{1,0:T(8,128)(2,1)S(1)} %get-tuple-element.57), channel_id=1, source_target_pairs={{1,2},{3,4},{5,6},{7,8},{9,10},{11,12},{13,14},{2,1},{4,3},{6,5},{... | collective-permute-start | bytes 786440 | tf_op jit(solution)/shard_map/ppermute | solution.py:518
  23.4 11.4 %copy-start.1 = (bf16[3,3,3,64,128]{4,3,2,1,0:T(8,128)(2,1)S(1)}, bf16[3,3,3,64,128]{4,3,2,1,0:T(8,128)(2,1)}, u32[]{:S(2)}) copy-start(bf16[3,3,3,64,128]{4,3,2,1,0:T(8,128)(2,1)} %param.6) | copy-start | bytes 1327108
  25.2 5.5 %collective-permute-start.4 = (bf16[3712,128]{1,0:T(8,128)(2,1)S(1)}, bf16[3712,128]{1,0:T(8,128)(2,1)S(1)}, u32[]{:S(2)}, u32[]{:S(2)}) collective-permute-start(bf16[3712,128]{1,0:T(8,128)(2,1)S(1)} %get-tuple-element.64), channel_id=1, source_target_pairs={{0,1},{1,0},{2,3},{3,2},{4,5},{5,4},{6,7},{7,6},{8,9},{9,8},{10,11... | collective-permute-start | bytes 2850824 | tf_op jit(solution)/shard_map/ppermute | solution.py:548
  28.6 10.0 %collective-permute-start.6 = (bf16[1024,128]{1,0:T(8,128)(2,1)S(1)}, bf16[1024,128]{1,0:T(8,128)(2,1)S(1)}, u32[]{:S(2)}, u32[]{:S(2)}) collective-permute-start(bf16[1024,128]{1,0:T(8,128)(2,1)S(1)} %get-tuple-element.70), channel_id=1, source_target_pairs={{1,2},{3,4},{5,6},{7,8},{9,10},{11,12},{13,14},{2,1},{4,3},{6,5},{... | collective-permute-start | bytes 786440 | tf_op jit(solution)/shard_map/ppermute | solution.py:536
  30.9 12.8 %collective-permute-start.5 = (bf16[4,32,896]{2,1,0:T(8,128)(2,1)S(1)}, bf16[4,32,896]{2,1,0:T(8,128)(2,1)S(1)}, u32[]{:S(2)}, u32[]{:S(2)}) collective-permute-start(bf16[4,32,896]{2,1,0:T(8,128)(2,1)S(1)} %get-tuple-element.67), channel_id=1, source_target_pairs={{0,4},{1,5},{2,6},{3,7},{4,0},{5,1},{6,2},{7,3},{8,12},{9,13},{10,... | collective-permute-start | bytes 688136 | tf_op jit(solution)/shard_map/ppermute | solution.py:562
  43.7 5.6 %collective-permute-start.7 = (bf16[2,24,896]{2,1,0:T(8,128)(2,1)S(1)}, bf16[2,24,896]{2,1,0:T(8,128)(2,1)S(1)}, u32[]{:S(2)}, u32[]{:S(2)}) collective-permute-start(bf16[2,24,896]{2,1,0:T(8,128)(2,1)S(1)} %get-tuple-element.75), channel_id=1, source_target_pairs={{0,8},{1,9},{2,10},{3,11},{4,12},{5,13},{6,14},{7,15},{8,0},{9,1},... | collective-permute-start | bytes 258056 | tf_op jit(solution)/shard_map/ppermute | solution.py:594
  49.3 4.2 %collective-permute-start.8 = (bf16[1,32,896]{2,1,0:T(8,128)(2,1)S(1)}, bf16[1,32,896]{2,1,0:T(8,128)(2,1)S(1)}, u32[]{:S(2)}, u32[]{:S(2)}) collective-permute-start(bf16[1,32,896]{2,1,0:T(8,128)(2,1)S(1)} %get-tuple-element.81), channel_id=1, source_target_pairs={{0,2},{1,3},{2,0},{3,1},{4,6},{5,7},{6,4},{7,5},{8,10},{9,11},{10,... | collective-permute-start | bytes 172040 | tf_op jit(solution)/shard_map/ppermute | solution.py:594

commit v10 on v8

--- a/solution.py
+++ b/solution.py
@@ -380,8 +380,22 @@
         kept[at] = total(keep)
 
 
-def finish_body(scale, split, sizes, mine, arrived, grad_one, grad_two):
-    total = (mine[0] + decoded(arrived[0], split)) * scale
+def spread_body(split_in, owner_bits, me, mine, arrived, kept, *sent):
+    place = 0
+    for bit in owner_bits:
+        place = 2 * place + (me[0] >> bit) % 2
+    kept[...] = mine[place] + decoded(arrived[place], split_in)
+    for at, out in enumerate(sent):
+        there = place ^ (at + 1)
+        out[...] = (mine[there] + decoded(arrived[there], split_in)).astype(BF16)
+
+
+def finish_body(scale, sizes, mine, *refs):
+    arrived, (grad_one, grad_two) = refs[:-2], refs[-2:]
+    total = mine[...]
+    for part in arrived:
+        total = total + part[...].astype(F32)
+    total = total * scale
     half = total.shape[1]
     first = 0
     for size, out in zip(sizes, (grad_one, grad_two)):
@@ -533,7 +547,6 @@
         slope_body, (flat, pack, pack), (me, terms, terms_inner, terms_outer, slope),
         name="grad_hidden", smem=(0,),
     )
-    grad_outer = lax.ppermute(outer, "space", across)
     groups = lanes // 128
     message, kept = call(
         functools.partial(grad_one_body, columns, count),
@@ -556,10 +569,10 @@
         return [b for b in bits if b != bit], sent, kept
 
     bits = list(range(count.bit_length() - 2, 0, -1))
-    order = [*range(2, count.bit_length() - 1), 1]
-    bits, sent, kept = halve(bits, order[0], chunk, split, kept, message)
-    sent, act_windows = lax.optimization_barrier((sent, act_windows))
-    arrived = lax.ppermute(sent, "space", [(i, i ^ (1 << order[0])) for i in range(count)])
+    bits, sent, kept = halve(bits, 2, chunk, split, kept, message)
+    sent, act_windows, outer = lax.optimization_barrier((sent, act_windows, outer))
+    arrived = lax.ppermute(sent, "space", [(i, i ^ 4) for i in range(count)])
+    grad_outer = lax.ppermute(outer, "space", across)
     output, = call(
         functools.partial(output_body, columns),
         (shape((planes, cells, wide), F32),),
@@ -570,32 +583,33 @@
         ),
         two_flops, "output", (), (), True,
     )
+    others = 2 ** len(bits) - 1
+    mine, *sent = call(
+        functools.partial(spread_body, split, bits),
+        (shape((chunk, lanes), F32), *[shape((chunk, lanes), BF16)] * others),
+        (me, kept, arrived), flops=one_flops, name="spread", smem=(0,),
+    )
+    sent, output, grad_hidden = lax.optimization_barrier((sent, output, grad_hidden))
+    arrived = []
+    for at, part in enumerate(sent):
+        away = sum(((at + 1) >> i & 1) << bit for i, bit in enumerate(bits[::-1]))
+        arrived.append(lax.ppermute(part, "space", [(i, i ^ away) for i in range(count)]))
     grad_windows, = call(
         functools.partial(grad_windows_body, columns), (shape(slab, BF16),),
         (me, grad_hidden, message, grad_outer),
         (), one_flops // 4, "grad_windows", (0,),
     )
-    came = split
-    for step, bit in enumerate(order[1:]):
-        goes = split if bit == 1 else 0
-        bits, sent, kept = halve(bits, bit, came, goes, kept, arrived)
-        if step == 0:
-            sent, grad_windows, output = lax.optimization_barrier((sent, grad_windows, output))
-            grad_volume, = call(
-                functools.partial(grad_volume_body, columns),
-                (shape((planes, cells, channels), F32),),
-                (grad_windows, back_taps),
-                (pltpu.VMEM((planes, cells, channels), F32), dma((cells // BLOCK,))),
-                one_flops, "grad_volume", (), (), True,
-            )
-        if step == 1:
-            sent, grad_volume = lax.optimization_barrier((sent, grad_volume))
-        arrived = lax.ppermute(sent, "space", [(i, i ^ (1 << bit)) for i in range(count)])
-        came = goes
+    grad_volume, = call(
+        functools.partial(grad_volume_body, columns),
+        (shape((planes, cells, channels), F32),),
+        (grad_windows, back_taps),
+        (pltpu.VMEM((planes, cells, channels), F32), dma((cells // BLOCK,))),
+        one_flops, "grad_volume", (), (), True,
+    )
     grad_one, grad_two = call(
-        functools.partial(finish_body, scale, came, (mid // count, wide // count)),
+        functools.partial(finish_body, scale, (mid // count, wide // count)),
         (shape((27, mid // count, channels), F32), shape((27, wide // count, mid), F32)),
-        (kept, arrived), name="finish",
+        (mine, *arrived), name="finish",
     )
     return (
         output.reshape(planes, rows, columns, wide),

time: 56.9 us -> 51.3 us (0.902)
  waiting for transfers between devices: 12.1 us -> 6.2 us
    ppermute x3 -> x4, waiting for transfers between devices: 10.8 us -> 4.04 us  [the longest x3 2.49 us: shards(): lax.ppermute(part, 'space', [(i, i ^ away) for i in range(count)])]
    ppermute x1, waiting for transfers between devices: 1.29 us -> 2.15 us  [shards(): message = lax.ppermute(message, 'space', within)]
    ppermute x3 -> x4, starting transfers between devices: 6.69 us -> 6.97 us  [the longest x3 4.57 us: shards(): lax.ppermute(part, 'space', [(i, i ^ away) for i in range(count)])]
    pallas_call x15 -> x14, Pallas kernels: 27 us -> 27 us  [call(): pl.pallas_call(body, out_shape=list(outs), in_specs=[pl.BlockSpec(memory_...]
  transfers between devices with their start and end apart: 9 -> 10, of which waited for: 4 -> 3; matrix products, arithmetic and copies ran while one was open for 0% -> 0% of each run, Pallas kernels for 39% -> 43%
where the time goes in v10:
time: 51.3 us; the launch traced here: 51 us
  Pallas kernels  27 us (53%)
  starting transfers between devices  17 us (33%)
  waiting for transfers between devices  6.2 us (12%)
  between operations  0.82 us (2%)
    pallas_call x14, Pallas kernels, call(): pl.pallas_call(body, out_shape=list(outs), in_specs=[pl.BlockSpec(memory_...  27 us
    ppermute x3, starting transfers between devices, shards(): lax.ppermute(part, 'space', [(i, i ^ away) for i in range(count)])  4.57 us
    ppermute x1, starting transfers between devices, shards(): vol_inner = lax.ppermute(own, 'space', within)  4.36 us
    ppermute x1, starting transfers between devices, shards(): message = lax.ppermute(message, 'space', within)  3.35 us
    ppermute x3, waiting for transfers between devices, shards(): lax.ppermute(part, 'space', [(i, i ^ away) for i in range(count)])  2.49 us
    ppermute x1, starting transfers between devices, shards(): arrived = lax.ppermute(sent, 'space', [(i, i ^ 4) for i in range(count)])  2.4 us
    ppermute x1, waiting for transfers between devices, shards(): message = lax.ppermute(message, 'space', within)  2.15 us
    ppermute x1, waiting for transfers between devices, shards(): arrived = lax.ppermute(sent, 'space', [(i, i ^ 4) for i in range(count)])  1.56 us
  transfers between devices with their start and end apart: 10, of which 3 were waited for; matrix products, arithmetic and copies ran while one was open for 0% of the time, Pallas kernels for 43%

profile of v10, /device:TPU:0, one launch (start us, length us, event | category | flops | bytes accessed | tf_op | source)
XLA Modules:
  0.0 51.0 jit_solution(8266485383727222891)
XLA Ops:
  0.6 1.4 %pack_volume.1.own = bf16[2048,128]{1,0:T(8,128)(2,1)S(1)} custom-call(bf16[2,2048,64]{2,1,0:T(8,128)(2,1)} %bitcast.18), custom_call_target="tpu_custom_call" | custom-call | bytes 1048576 | tf_op jit(solution)/shard_map/pack_volume/pallas_call | solution.py:27
  2.0 0.7 %collective-permute-start.1 = (bf16[2048,128]{1,0:T(8,128)(2,1)S(1)}, bf16[2048,128]{1,0:T(8,128)(2,1)S(1)}, u32[]{:S(2)}, u32[]{:S(2)}) collective-permute-start(bf16[2048,128]{1,0:T(8,128)(2,1)S(1)} %pack_volume.1.own), channel_id=1, source_target_pairs={{1,2},{3,4},{5,6},{7,8},{9,10},{11,12},{13,14},{2,1},{4,3},{6,5},{... | collective-permute-start | bytes 1572872 | tf_op jit(solution)/shard_map/ppermute | solution.py:504
  2.7 4.4 %collective-permute-start = (bf16[2048,128]{1,0:T(8,128)(2,1)S(1)}, bf16[2048,128]{1,0:T(8,128)(2,1)S(1)}, u32[]{:S(2)}, u32[]{:S(2)}) collective-permute-start(bf16[2048,128]{1,0:T(8,128)(2,1)S(1)} %pack_volume.1.own), channel_id=1, source_target_pairs={{0,1},{1,0},{2,3},{3,2},{4,5},{5,4},{6,7},{7,6},{8,9},{9,8},{10,11... | collective-permute-start | bytes 1572872 | tf_op jit(solution)/shard_map/ppermute | solution.py:505
  7.1 4.6 %grad_act_terms.1 = (f32[2048,128]{1,0:T(8,128)S(1)}, bf16[1024,128]{1,0:T(8,128)(2,1)S(1)}, bf16[1024,128]{1,0:T(8,128)(2,1)S(1)}, bf16[256,2048]{1,0:T(8,128)(2,1)S(1)}) custom-call(s32[1]{0:T(128)} %bitcast.me, bf16[2,2048,128]{2,1,0:T(8,128)(2,1)} %bitcast.19, bf16[27,64,128]{2,1,0:T(8,128)(2,1)} %bitcast.15), custom_call_target="tpu_custom_call" | custom-call | flops 1811939328 | bytes 4112388 | tf_op jit(solution)/shard_map/grad_act_terms/pallas_call | solution.py:27
  11.7 0.2 back_taps.1.taps
  11.9 2.8 %prepare.1 = (bf16[2112,384]{1,0:T(8,128)(2,1)S(1)}, f32[2048,256]{1,0:T(8,128)S(1)}, bf16[2304,256]{1,0:T(8,128)(2,1)S(1)}) custom-call(bf16[2048,128]{1,0:T(8,128)(2,1)S(1)} %pack_volume.1.own, bf16[27,64,64]{2,1,0:T(8,128)(2,1)} %bitcast.13), custom_call_target="tpu_custom_call" | custom-call | flops 905969664 | bytes 5644288 | tf_op jit(solution)/shard_map/prepare/pallas_call | solution.py:27
  14.7 0.1 collective-permute-start.2
  14.8 0.7 %collective-permute-start.3 = (bf16[1024,128]{1,0:T(8,128)(2,1)S(1)}, bf16[1024,128]{1,0:T(8,128)(2,1)S(1)}, u32[]{:S(2)}, u32[]{:S(2)}) collective-permute-start(bf16[1024,128]{1,0:T(8,128)(2,1)S(1)} %get-tuple-element.56), channel_id=1, source_target_pairs={{1,2},{3,4},{5,6},{7,8},{9,10},{11,12},{13,14},{2,1},{4,3},{6,5},{... | collective-permute-start | bytes 786440 | tf_op jit(solution)/shard_map/ppermute | solution.py:532
  15.4 0.0 collective-permute-done.1.outer
  15.5 0.0 collective-permute-done.inner
  15.5 4.3 %hidden.1 = (bf16[2112,768]{1,0:T(8,128)(2,1)S(1)}, bf16[2112,768]{1,0:T(8,128)(2,1)S(1)}, f32[2048,128]{1,0:T(8,128)S(1)}) custom-call(s32[1]{0:T(128)} %bitcast.me, bf16[2048,128]{1,0:T(8,128)(2,1)S(1)} %collective-permute-done.inner, bf16[2048,128]{1,0:T(8,128)(2,1)S(1)} %collective-permute-done.1.outer, f32[2048,256]{1,0:T(8,128)S(1)} %get-tuple-element.49.part, ...), custom_call_target="tpu_custom_call" | custom-call | flops 1811939328 | bytes 11862020 | tf_op jit(solution)/shard_map/hidden/pallas_call | solution.py:27
  19.8 2.8 %grad_two_terms.1.other = f32[128,1792]{1,0:T(8,128)S(1)} custom-call(bf16[2112,768]{1,0:T(8,128)(2,1)S(1)} %get-tuple-element.71.act_windows, bf16[256,2048]{1,0:T(8,128)(2,1)S(1)} %get-tuple-element.55.turned), custom_call_target="tpu_custom_call" | custom-call | flops 1811939328 | bytes 5210112 | tf_op jit(solution)/shard_map/grad_two_terms/pallas_call | solution.py:27
  22.5 0.0 collective-permute-done.3.outer
  22.5 0.0 collective-permute-done.2.inner
  22.5 0.9 %grad_hidden.1 = (bf16[2048,128]{1,0:T(8,128)(2,1)S(1)}, bf16[1024,128]{1,0:T(8,128)(2,1)S(1)}, bf16[1024,128]{1,0:T(8,128)(2,1)S(1)}) custom-call(s32[1]{0:T(128)} %bitcast.me, f32[2048,128]{1,0:T(8,128)S(1)} %get-tuple-element.52.terms, bf16[1024,128]{1,0:T(8,128)(2,1)S(1)} %collective-permute-done.2.inner, ...), custom_call_target="tpu_custom_call" | custom-call | bytes 3670020 | tf_op jit(solution)/shard_map/grad_hidden/pallas_call | solution.py:27
  23.4 0.0 copy-start.1
  23.4 1.8 %grad_one_terms.1 = (bf16[3712,128]{1,0:T(8,128)(2,1)S(1)}, f32[8,24,896]{2,1,0:T(8,128)S(1)}) custom-call(s32[1]{0:T(128)} %bitcast.me, bf16[2112,384]{1,0:T(8,128)(2,1)S(1)} %get-tuple-element.45.own_windows, bf16[2112,768]{1,0:T(8,128)(2,1)S(1)} %get-tuple-element.51.side_windows, bf16[2048,128]{1,0:T(8,128)(2,1)S(1)} %get-tuple-element.73.grad.own, ...), custom_call_target="tpu_custom_call" | custom-call | flops 905969664 | bytes 8208388 | tf_op jit(solution)/shard_map/grad_one_terms/pallas_call | solution.py:27
  25.2 3.4 %collective-permute-start.4 = (bf16[3712,128]{1,0:T(8,128)(2,1)S(1)}, bf16[3712,128]{1,0:T(8,128)(2,1)S(1)}, u32[]{:S(2)}, u32[]{:S(2)}) collective-permute-start(bf16[3712,128]{1,0:T(8,128)(2,1)S(1)} %get-tuple-element.63), channel_id=1, source_target_pairs={{0,1},{1,0},{2,3},{3,2},{4,5},{5,4},{6,7},{7,6},{8,9},{9,8},{10,11... | collective-permute-start | bytes 2850824 | tf_op jit(solution)/shard_map/ppermute | solution.py:561
  28.6 2.1 %collective-permute-done.4.arrived.message = bf16[3712,128]{1,0:T(8,128)(2,1)S(1)} collective-permute-done((bf16[3712,128]{1,0:T(8,128)(2,1)S(1)}, bf16[3712,128]{1,0:T(8,128)(2,1)S(1)}, u32[]{:S(2)}, u32[]{:S(2)}) %collective-permute-start.4) | collective-permute-done | bytes 950304 | tf_op jit(solution)/shard_map/ppermute | solution.py:561
  30.7 0.1 halve.1
  30.9 2.4 %collective-permute-start.5 = (bf16[4,32,896]{2,1,0:T(8,128)(2,1)S(1)}, bf16[4,32,896]{2,1,0:T(8,128)(2,1)S(1)}, u32[]{:S(2)}, u32[]{:S(2)}) collective-permute-start(bf16[4,32,896]{2,1,0:T(8,128)(2,1)S(1)} %get-tuple-element.67), channel_id=1, source_target_pairs={{0,4},{1,5},{2,6},{3,7},{4,0},{5,1},{6,2},{7,3},{8,12},{9,13},{10,... | collective-permute-start | bytes 688136 | tf_op jit(solution)/shard_map/ppermute | solution.py:574
  33.3 0.8 %collective-permute-start.6 = (bf16[1024,128]{1,0:T(8,128)(2,1)S(1)}, bf16[1024,128]{1,0:T(8,128)(2,1)S(1)}, u32[]{:S(2)}, u32[]{:S(2)}) collective-permute-start(bf16[1024,128]{1,0:T(8,128)(2,1)S(1)} %get-tuple-element.74), channel_id=1, source_target_pairs={{1,2},{3,4},{5,6},{7,8},{9,10},{11,12},{13,14},{2,1},{4,3},{6,5},{... | collective-permute-start | bytes 786440 | tf_op jit(solution)/shard_map/ppermute | solution.py:575
  34.1 3.7 %output.1 = f32[2,2048,128]{2,1,0:T(8,128)} custom-call(bf16[2112,768]{1,0:T(8,128)(2,1)S(1)} %get-tuple-element.71.act_windows, bf16[27,64,128]{2,1,0:T(8,128)(2,1)S(1)} %bitcast.16), custom_call_target="tpu_custom_call" | custom-call | flops 1811939328 | bytes 5783552 | tf_op jit(solution)/shard_map/output/pallas_call | solution.py:27
  37.8 1.6 %collective-permute-done.5.arrived = bf16[4,32,896]{2,1,0:T(8,128)(2,1)S(1)} collective-permute-done((bf16[4,32,896]{2,1,0:T(8,128)(2,1)S(1)}, bf16[4,32,896]{2,1,0:T(8,128)(2,1)S(1)}, u32[]{:S(2)}, u32[]{:S(2)}) %collective-permute-start.5) | collective-permute-done | bytes 229408 | tf_op jit(solution)/shard_map/ppermute | solution.py:574
  39.4 2.0 %collective-permute-start.7 = (bf16[24,896]{1,0:T(8,128)(2,1)S(1)}, bf16[24,896]{1,0:T(8,128)(2,1)S(1)}, u32[]{:S(2)}, u32[]{:S(2)}) collective-permute-start(bf16[24,896]{1,0:T(8,128)(2,1)S(1)} %get-tuple-element.77), channel_id=1, source_target_pairs={{0,2},{1,3},{2,0},{3,1},{4,6},{5,7},{6,4},{7,5},{8,10},{9,11},{10,... | collective-permute-start | bytes 129032 | tf_op jit(solution)/shard_map/ppermute | solution.py:596
  41.4 2.6 %collective-permute-start.8 = (bf16[24,896]{1,0:T(8,128)(2,1)S(1)}, bf16[24,896]{1,0:T(8,128)(2,1)S(1)}, u32[]{:S(2)}, u32[]{:S(2)}) collective-permute-start(bf16[24,896]{1,0:T(8,128)(2,1)S(1)} %get-tuple-element.78), channel_id=1, source_target_pairs={{0,8},{1,9},{2,10},{3,11},{4,12},{5,13},{6,14},{7,15},{8,0},{9,1},... | collective-permute-start | bytes 129032 | tf_op jit(solution)/shard_map/ppermute | solution.py:596
  44.0 0.0 collective-permute-done.6.outer
  44.0 0.8 %grad_windows.1.windows = bf16[2112,768]{1,0:T(8,128)(2,1)S(1)} custom-call(s32[1]{0:T(128)} %bitcast.me, bf16[2048,128]{1,0:T(8,128)(2,1)S(1)} %get-tuple-element.73.grad.own, bf16[3712,128]{1,0:T(8,128)(2,1)S(1)} %collective-permute-done.4.arrived.message, bf16[1024,128]{1,0:T(8,128)(2,1)S(1)} %collective-permute-done.6.outer), custom_call_target="tpu_custom_call" | custom-call | flops 226492416 | bytes 4980740 | tf_op jit(solution)/shard_map/grad_windows/pallas_call | solution.py:27
  44.9 2.9 %grad_volume.1 = f32[2,2048,64]{2,1,0:T(8,128)} custom-call(bf16[2112,768]{1,0:T(8,128)(2,1)S(1)} %grad_windows.1.windows, bf16[384,768]{1,0:T(8,128)(2,1)S(1)} %back_taps.1.taps), custom_call_target="tpu_custom_call" | custom-call | flops 905969664 | bytes 4882432 | tf_op jit(solution)/shard_map/grad_volume/pallas_call | solution.py:27
  47.8 0.0 collective-permute-done.7.refs_0_
  47.8 2.5 %collective-permute-done.9.refs_2_ = bf16[24,896]{1,0:T(8,128)(2,1)S(1)} collective-permute-done((bf16[24,896]{1,0:T(8,128)(2,1)S(1)}, bf16[24,896]{1,0:T(8,128)(2,1)S(1)}, u32[]{:S(2)}, u32[]{:S(2)}) %collective-permute-start.9) | collective-permute-done | bytes 43040 | tf_op jit(solution)/shard_map/ppermute | solution.py:596
  50.3 0.7 %finish.1 = (f32[27,4,64]{2,1,0:T(4,128)}, f32[27,8,64]{2,1,0:T(8,128)}) custom-call(f32[24,896]{1,0:T(8,128)S(1)} %get-tuple-element.76.mine, bf16[24,896]{1,0:T(8,128)(2,1)S(1)} %collective-permute-done.7.refs_0_, bf16[24,896]{1,0:T(8,128)(2,1)S(1)} %collective-permute-done.8.refs_1_, bf16[24,896]{1,0:T(8,128)(2,1)S(1)} %collective-permute-done.9.refs_2_), custom_call_target="tpu_custom_call" | custom-call | bytes 297984 | tf_op jit(solution)/shard_map/finish/pallas_call | solution.py:27
  (6 shorter events, 0.1 us)
Async XLA Ops:
  2.0 13.4 %collective-permute-start.1 = (bf16[2048,128]{1,0:T(8,128)(2,1)S(1)}, bf16[2048,128]{1,0:T(8,128)(2,1)S(1)}, u32[]{:S(2)}, u32[]{:S(2)}) collective-permute-start(bf16[2048,128]{1,0:T(8,128)(2,1)S(1)} %pack_volume.1.own), channel_id=1, source_target_pairs={{1,2},{3,4},{5,6},{7,8},{9,10},{11,12},{13,14},{2,1},{4,3},{6,5},{... | collective-permute-start | bytes 1572872 | tf_op jit(solution)/shard_map/ppermute | solution.py:504
  2.7 12.7 %collective-permute-start = (bf16[2048,128]{1,0:T(8,128)(2,1)S(1)}, bf16[2048,128]{1,0:T(8,128)(2,1)S(1)}, u32[]{:S(2)}, u32[]{:S(2)}) collective-permute-start(bf16[2048,128]{1,0:T(8,128)(2,1)S(1)} %pack_volume.1.own), channel_id=1, source_target_pairs={{0,1},{1,0},{2,3},{3,2},{4,5},{5,4},{6,7},{7,6},{8,9},{9,8},{10,11... | collective-permute-start | bytes 1572872 | tf_op jit(solution)/shard_map/ppermute | solution.py:505
  7.1 4.6 %copy-start = (bf16[3,3,3,64,64]{4,3,2,1,0:T(8,128)(2,1)S(1)}, bf16[3,3,3,64,64]{4,3,2,1,0:T(8,128)(2,1)}, u32[]{:S(2)}) copy-start(bf16[3,3,3,64,64]{4,3,2,1,0:T(8,128)(2,1)} %param.5) | copy-start | bytes 663556
  14.7 7.9 %collective-permute-start.2 = (bf16[1024,128]{1,0:T(8,128)(2,1)S(1)}, bf16[1024,128]{1,0:T(8,128)(2,1)S(1)}, u32[]{:S(2)}, u32[]{:S(2)}) collective-permute-start(bf16[1024,128]{1,0:T(8,128)(2,1)S(1)} %get-tuple-element.53), channel_id=1, source_target_pairs={{0,1},{1,0},{2,3},{3,2},{4,5},{5,4},{6,7},{7,6},{8,9},{9,8},{10,11... | collective-permute-start | bytes 786440 | tf_op jit(solution)/shard_map/ppermute | solution.py:533
  14.8 7.8 %collective-permute-start.3 = (bf16[1024,128]{1,0:T(8,128)(2,1)S(1)}, bf16[1024,128]{1,0:T(8,128)(2,1)S(1)}, u32[]{:S(2)}, u32[]{:S(2)}) collective-permute-start(bf16[1024,128]{1,0:T(8,128)(2,1)S(1)} %get-tuple-element.56), channel_id=1, source_target_pairs={{1,2},{3,4},{5,6},{7,8},{9,10},{11,12},{13,14},{2,1},{4,3},{6,5},{... | collective-permute-start | bytes 786440 | tf_op jit(solution)/shard_map/ppermute | solution.py:532
  23.4 10.7 %copy-start.1 = (bf16[3,3,3,64,128]{4,3,2,1,0:T(8,128)(2,1)S(1)}, bf16[3,3,3,64,128]{4,3,2,1,0:T(8,128)(2,1)}, u32[]{:S(2)}) copy-start(bf16[3,3,3,64,128]{4,3,2,1,0:T(8,128)(2,1)} %param.6) | copy-start | bytes 1327108
  25.2 5.5 %collective-permute-start.4 = (bf16[3712,128]{1,0:T(8,128)(2,1)S(1)}, bf16[3712,128]{1,0:T(8,128)(2,1)S(1)}, u32[]{:S(2)}, u32[]{:S(2)}) collective-permute-start(bf16[3712,128]{1,0:T(8,128)(2,1)S(1)} %get-tuple-element.63), channel_id=1, source_target_pairs={{0,1},{1,0},{2,3},{3,2},{4,5},{5,4},{6,7},{7,6},{8,9},{9,8},{10,11... | collective-permute-start | bytes 2850824 | tf_op jit(solution)/shard_map/ppermute | solution.py:561
  30.9 8.5 %collective-permute-start.5 = (bf16[4,32,896]{2,1,0:T(8,128)(2,1)S(1)}, bf16[4,32,896]{2,1,0:T(8,128)(2,1)S(1)}, u32[]{:S(2)}, u32[]{:S(2)}) collective-permute-start(bf16[4,32,896]{2,1,0:T(8,128)(2,1)S(1)} %get-tuple-element.67), channel_id=1, source_target_pairs={{0,4},{1,5},{2,6},{3,7},{4,0},{5,1},{6,2},{7,3},{8,12},{9,13},{10,... | collective-permute-start | bytes 688136 | tf_op jit(solution)/shard_map/ppermute | solution.py:574
  33.3 10.8 %collective-permute-start.6 = (bf16[1024,128]{1,0:T(8,128)(2,1)S(1)}, bf16[1024,128]{1,0:T(8,128)(2,1)S(1)}, u32[]{:S(2)}, u32[]{:S(2)}) collective-permute-start(bf16[1024,128]{1,0:T(8,128)(2,1)S(1)} %get-tuple-element.74), channel_id=1, source_target_pairs={{1,2},{3,4},{5,6},{7,8},{9,10},{11,12},{13,14},{2,1},{4,3},{6,5},{... | collective-permute-start | bytes 786440 | tf_op jit(solution)/shard_map/ppermute | solution.py:575
  39.4 8.4 %collective-permute-start.7 = (bf16[24,896]{1,0:T(8,128)(2,1)S(1)}, bf16[24,896]{1,0:T(8,128)(2,1)S(1)}, u32[]{:S(2)}, u32[]{:S(2)}) collective-permute-start(bf16[24,896]{1,0:T(8,128)(2,1)S(1)} %get-tuple-element.77), channel_id=1, source_target_pairs={{0,2},{1,3},{2,0},{3,1},{4,6},{5,7},{6,4},{7,5},{8,10},{9,11},{10,... | collective-permute-start | bytes 129032 | tf_op jit(solution)/shard_map/ppermute | solution.py:596
  41.4 6.4 %collective-permute-start.8 = (bf16[24,896]{1,0:T(8,128)(2,1)S(1)}, bf16[24,896]{1,0:T(8,128)(2,1)S(1)}, u32[]{:S(2)}, u32[]{:S(2)}) collective-permute-start(bf16[24,896]{1,0:T(8,128)(2,1)S(1)} %get-tuple-element.78), channel_id=1, source_target_pairs={{0,8},{1,9},{2,10},{3,11},{4,12},{5,13},{6,14},{7,15},{8,0},{9,1},... | collective-permute-start | bytes 129032 | tf_op jit(solution)/shard_map/ppermute | solution.py:596
  44.0 6.3 %collective-permute-start.9 = (bf16[24,896]{1,0:T(8,128)(2,1)S(1)}, bf16[24,896]{1,0:T(8,128)(2,1)S(1)}, u32[]{:S(2)}, u32[]{:S(2)}) collective-permute-start(bf16[24,896]{1,0:T(8,128)(2,1)S(1)} %get-tuple-element.79), channel_id=1, source_target_pairs={{0,10},{1,11},{2,8},{3,9},{4,14},{5,15},{6,12},{7,13},{8,2},{9,3},... | collective-permute-start | bytes 129032 | tf_op jit(solution)/shard_map/ppermute | solution.py:596

commit v11 on v10

--- a/solution.py
+++ b/solution.py
@@ -9,12 +9,12 @@
 from jax.sharding import PartitionSpec as P
 
 F32, BF16 = jnp.float32, jnp.bfloat16
-STEP, BLOCK = 256, 512
+STEP, BLOCK = 256, 1024
 VMEM_LIMIT = 16 * 2**20
 NN = (((1,), (0,)), ((), ()))
 NT = (((1,), (1,)), ((), ()))
 
-PLANES = (0, 1, 2, -1, -2, 3)
+PLANES = (0, 1, 2, -1)
 
 
 def depth_tap(source, target):
@@ -144,7 +144,7 @@
         for column in range(3):
             for source in range(2):
                 first = row * 768 + column * 256 + source * 128
-                for at, target in enumerate(PLANES[:4]):
+                for at, target in enumerate(PLANES):
                     depth = depth_tap(source, target)
                     taps[at * 64 : at * 64 + 64, first : first + 128] = (
                         jnp.zeros((64, 128), BF16)
@@ -165,35 +165,44 @@
 
 
 def prepare_body(
-    columns, own, far_weight, own_windows, hidden, side_taps, own_taps, weight, sem
+    columns, me, own, inner, far_weight, own_windows, inner_windows, hidden, outer_taps,
+    taps, weight, sem,
 ):
     fetch = pltpu.make_async_copy(far_weight, weight, sem)
     fetch.start()
+    odd = me[0] % 2 == 1
 
     def fill(i, carry):
         start = pl.multiple_of(i * STEP, STEP)
-        chunk = own[pl.ds(start, STEP), :].astype(F32)
-        fill_windows(own_windows, start, 0, chunk, columns, 128)
+        rows = pl.ds(start, STEP)
+        fill_windows(own_windows, start, 0, own[rows, :].astype(F32), columns, 128)
+        fill_windows(inner_windows, start, 0, inner[rows, :].astype(F32), columns, 128)
         return carry
 
     clear_edges(own_windows, columns)
+    clear_edges(inner_windows, columns)
     lax.fori_loop(0, own.shape[0] // STEP, fill, 0)
     fetch.wait()
     zero = jnp.zeros((64, 64), BF16)
-    for row in range(3):
-        for column in range(3):
-            tap = row * 3 + column
-            for at, source in enumerate(PLANES):
-                depths = [depth_tap(source, target) for target in PLANES[:4]]
-                parts = [zero if d is None else weight[d * 9 + tap] for d in depths]
-                if at < 2:
-                    target, first = own_taps, tap * 128 + at * 64
-                else:
-                    target, first = side_taps, tap * 256 + (at - 2) * 64
-                target[first : first + 64, :128] = jnp.concatenate(parts[:2], axis=1)
-                target[first : first + 64, 128:] = jnp.concatenate(parts[2:], axis=1)
+    for tap in range(9):
+
+        def kernel_rows(source):
+            depths = [depth_tap(source, target) for target in PLANES]
+            parts = [zero if d is None else weight[d * 9 + tap] for d in depths]
+            return jnp.concatenate(parts, axis=1)
+
+        for at in range(2):
+            rows = slice(tap * 128 + at * 64, tap * 128 + at * 64 + 64)
+            taps[rows, :] = kernel_rows(at)
+            upper, lower = kernel_rows(2 + at).astype(F32), kernel_rows(at - 2).astype(F32)
+            first = 9 * 128 + rows.start
+            taps[first : first + 64, :] = jnp.where(odd, lower, upper).astype(BF16)
+            outer_taps[rows, :] = jnp.where(odd, upper, lower).astype(BF16)
     for start in range(0, own.shape[0], BLOCK):
-        hidden[start : start + BLOCK, :] = window_dot(own_windows, own_taps, start, columns, NN)
+        rows = row_windows(own_windows, start, columns) + row_windows(inner_windows, start, columns)
+        hidden[start : start + BLOCK, :] = jnp.dot(
+            jnp.concatenate(rows, axis=1), taps[...], preferred_element_type=F32
+        )
 
 
 def back_taps_body(weight, back_taps):
@@ -202,7 +211,7 @@
         for column in range(3):
             tap = row * 3 + column
             for plane in range(2):
-                depths = [depth_tap(source, plane) for source in PLANES[:4]]
+                depths = [depth_tap(source, plane) for source in PLANES]
                 parts = [zero if d is None else weight[(2 - d) * 9 + 8 - tap] for d in depths]
                 at = row * 128 + plane * 64
                 for pair in range(2):
@@ -213,20 +222,17 @@
 
 
 def hidden_body(
-    columns, count, me, inner, outer, part, side_taps, side_windows, act_windows, slope
+    columns, count, me, outer, part, outer_taps, outer_windows, act_windows, slope
 ):
     cells = outer.shape[0]
-    odd = me[0] % 2 == 1
 
     def fill(i, carry):
         start = pl.multiple_of(i * STEP, STEP)
-        rows = pl.ds(start, STEP)
-        below, above = by_side(odd, inner[rows, :].astype(F32), outer[rows, :].astype(F32))
-        fill_windows(side_windows, start, 0, pick(above, below), columns, 256)
-        fill_windows(side_windows, start, 128, pick(below, above), columns, 256)
+        chunk = outer[pl.ds(start, STEP), :].astype(F32)
+        fill_windows(outer_windows, start, 0, chunk, columns, 128)
         return carry
 
-    clear_edges(side_windows, columns)
+    clear_edges(outer_windows, columns)
     clear_edges(act_windows, columns)
     lax.fori_loop(0, cells // STEP, fill, 0)
     lanes = lax.broadcasted_iota(jnp.int32, (BLOCK, 128), 1)
@@ -234,35 +240,13 @@
     inside = jnp.where(lanes < 64, edges[0], edges[1])
     for start in range(0, cells, BLOCK):
         hidden = part[start : start + BLOCK, :]
-        hidden = hidden + window_dot(side_windows, side_taps, start, columns, NN)
+        hidden = hidden + window_dot(outer_windows, outer_taps, start, columns, NN)
         gate = jax.nn.sigmoid(hidden)
         act = (hidden * gate).astype(BF16).astype(F32)
         fill_windows(act_windows, start, 0, act[:, :128], columns, 256)
         fill_windows(act_windows, start, 128, act[:, 128:] * inside, columns, 256)
         hidden, gate = hidden[:, :128], gate[:, :128]
         slope[start : start + BLOCK, :] = gate * (1.0 + hidden * (1.0 - gate))
-
-
-def slope_body(me, terms, inner, outer, slope, grad, to_inner, to_outer):
-    half = terms.shape[0] // 2
-    odd = me[0] % 2 == 1
-
-    def step(i, carry):
-        start = pl.multiple_of(i * STEP, STEP)
-        low, high = pl.ds(start, STEP), pl.ds(start + half, STEP)
-        near = inner[low, :].astype(F32)
-        arrived = unpacked(*by_side(odd, near, outer[low, :].astype(F32)))
-        sides = []
-        for rows, extra in zip((low, high), arrived):
-            value = ((terms[rows, :] + extra) * slope[rows, :]).astype(BF16)
-            grad[rows, :] = value
-            sides.append(value.astype(F32))
-        lower, upper = packed(*sides)
-        to_inner[low, :] = jnp.where(odd, lower, upper).astype(BF16)
-        to_outer[low, :] = jnp.where(odd, upper, lower).astype(BF16)
-        return carry
-
-    lax.fori_loop(0, half // STEP, step, 0)
 
 
 def kernel_terms(columns, out_channels, slices, turned, terms):
@@ -318,25 +302,40 @@
 
 
 def grad_one_body(
-    columns, count, me, own_windows, side_windows, grad, other, to_inner,
-    message, kept, turned, terms,
+    columns, count, me, own_windows, inner_windows, outer_windows, act_terms, inner, outer, slope,
+    other, grad, to_outer, message, kept, turned, terms,
 ):
     cells = grad.shape[0]
+    odd = me[0] % 2 == 1
+    before = message.shape[0] - cells // 2
+    for start in range(0, cells // 2, STEP):
+        low, high = slice(start, start + STEP), slice(start + cells // 2, start + cells // 2 + STEP)
+        arrived = unpacked(*by_side(odd, inner[low, :].astype(F32), outer[low, :].astype(F32)))
+        sides = []
+        for rows, extra in zip((low, high), arrived):
+            value = ((act_terms[rows, :] + extra) * slope[rows, :]).astype(BF16)
+            grad[rows, :] = value
+            value = value.astype(F32)
+            turned[:, rows] = value.T.astype(BF16)
+            sides.append(value)
+        lower, upper = packed(*sides)
+        message[before + start : before + start + STEP, :] = jnp.where(
+            odd, lower, upper
+        ).astype(BF16)
+        to_outer[low, :] = jnp.where(odd, upper, lower).astype(BF16)
+    from_inner = lax.broadcasted_iota(jnp.int32, (16, 128), 1) // 64 == me[0] % 2
+    from_inner = jnp.where(from_inner, 1.0, 0.0).astype(BF16)[:1]
+    from_outer = 1 - from_inner
 
     def slices(row, column):
         rows = slice(row * columns, row * columns + cells)
-        return jnp.concatenate(
-            [
-                own_windows[rows, column * 128 : column * 128 + 128],
-                side_windows[rows, column * 256 : column * 256 + 128],
-            ],
-            axis=1,
-        )
-
-    turn(grad, turned, 0)
+        lanes = slice(column * 128, column * 128 + 128)
+        sides = inner_windows[rows, lanes] * from_inner + outer_windows[rows, lanes] * from_outer
+        return jnp.concatenate([own_windows[rows, lanes], sides], axis=1)
+
     kernel_terms(columns, 64, slices, turned, terms)
     half = terms.shape[1] // 2
-    odd = me[0] % 2 == 1
+    split = 2 * terms.shape[0] // count
 
     def share(owner):
         parts = []
@@ -350,12 +349,11 @@
     for pair in range(count // 2):
         even_share, odd_share = share(2 * pair), share(2 * pair + 1)
         kept[pair] = jnp.where(odd, odd_share, even_share)
-        given = coded(jnp.where(odd, even_share, odd_share), kept.shape[1])
+        given = coded(jnp.where(odd, even_share, odd_share), split)
         size = given.shape[0]
         for group in range(groups):
             first = (pair * groups + group) * size
             message[first : first + size, :] = given[:, group * 128 : group * 128 + 128]
-    message[message.shape[0] - to_inner.shape[0] :, :] = to_inner[...]
 
 
 def halve_body(split_in, split_out, owner_bit, at_bit, me, mine, arrived, sent, kept):
@@ -368,8 +366,9 @@
             return mine[at] + decoded(arrived[at], split_in)
         parts = []
         for group in range(groups):
-            first = pl.multiple_of((at * groups + group) * 2 * size, 8)
-            parts.append(decoded(arrived[pl.ds(first, 2 * size), :], split_in))
+            rows = size + split_in
+            first = pl.multiple_of((at * groups + group) * rows, 8)
+            parts.append(decoded(arrived[pl.ds(first, rows), :], split_in))
         return mine[at] + jnp.concatenate(parts, axis=1)
 
     for at in range(sent.shape[0]):
@@ -411,7 +410,7 @@
 def output_body(columns, act_windows, weight, far, taps, output, sems):
     for row in range(3):
         for column in range(3):
-            for at, source in enumerate(PLANES[:4]):
+            for at, source in enumerate(PLANES):
                 first = row * 768 + column * 256 + at * 64
                 for plane in range(2):
                     depth = depth_tap(source, plane)
@@ -516,14 +515,13 @@
         two_flops, "grad_act_terms", (0,), (1, 2),
     )
     own, terms = lax.optimization_barrier((own, terms))
-    own_windows, part, side_taps = call(
+    third = shape((slab[0], 384), BF16)
+    own_windows, inner_windows, part, outer_taps = call(
         functools.partial(prepare_body, columns),
-        (
-            shape((slab[0], 384), BF16), shape((cells, 256), F32), shape((9 * 256, 256), BF16),
-        ),
-        (own, far_one),
-        (pltpu.VMEM((9 * 128, 256), BF16), pltpu.VMEM(weight_one.shape, BF16), dma),
-        one_flops, "prepare", (), (1,),
+        (third, third, shape((cells, 256), F32), shape((9 * 128, 256), BF16)),
+        (me, own, vol_inner, far_one),
+        (pltpu.VMEM((2 * 9 * 128, 256), BF16), pltpu.VMEM(weight_one.shape, BF16), dma),
+        one_flops, "prepare", (0,), (3,),
     )
     back_taps, = call(
         back_taps_body, (shape((3 * 128, 768), BF16),), (weight_one,), (), one_flops // 8, "back_taps"
@@ -531,10 +529,10 @@
     inner, outer, part, back_taps = lax.optimization_barrier((inner, outer, part, back_taps))
     terms_outer = lax.ppermute(outer, "space", across)
     terms_inner = lax.ppermute(inner, "space", within)
-    side_windows, act_windows, slope = call(
+    outer_windows, act_windows, slope = call(
         functools.partial(hidden_body, columns, count),
-        (shape(slab, BF16), shape(slab, BF16), shape((cells, 128), F32)),
-        (me, vol_inner, vol_outer, part, side_taps),
+        (third, shape(slab, BF16), shape((cells, 128), F32)),
+        (me, vol_outer, part, outer_taps),
         (), 2 * one_flops, "hidden", (0,),
     )
     terms_two, = call(
@@ -542,19 +540,18 @@
         (shape((wide, 2 * lanes), F32),),
         (act_windows, turned), (), two_flops, "grad_two_terms",
     )
-    terms_two, terms_outer = lax.optimization_barrier((terms_two, terms_outer))
-    grad_hidden, to_inner, outer = call(
-        slope_body, (flat, pack, pack), (me, terms, terms_inner, terms_outer, slope),
-        name="grad_hidden", smem=(0,),
-    )
     groups = lanes // 128
-    message, kept = call(
+    grad_hidden, outer, message, kept = call(
         functools.partial(grad_one_body, columns, count),
         (
-            shape((count // 2 * groups * 2 * chunk + cells // 2, 128), BF16),
+            flat, pack,
+            shape((count // 2 * groups * (chunk + split) + cells // 2, 128), BF16),
             shape((count // 2, chunk, lanes), F32),
         ),
-        (me, own_windows, side_windows, grad_hidden, terms_two, to_inner),
+        (
+            me, own_windows, inner_windows, outer_windows, terms, terms_inner, terms_outer, slope,
+            terms_two,
+        ),
         (pltpu.VMEM((128, cells), BF16), pltpu.VMEM((mid, 2 * lanes), F32)),
         one_flops, "grad_one_terms", (0,),
     )
@@ -569,7 +566,7 @@
         return [b for b in bits if b != bit], sent, kept
 
     bits = list(range(count.bit_length() - 2, 0, -1))
-    bits, sent, kept = halve(bits, 2, chunk, split, kept, message)
+    bits, sent, kept = halve(bits, 2, split, split, kept, message)
     sent, act_windows, outer = lax.optimization_barrier((sent, act_windows, outer))
     arrived = lax.ppermute(sent, "space", [(i, i ^ 4) for i in range(count)])
     grad_outer = lax.ppermute(outer, "space", across)

time: 51.3 us -> 50.6 us (0.986)
  waiting for transfers between devices: 6.2 us -> 5.43 us
    ppermute x1, starting transfers between devices: 4.36 us -> 0.52 us  [shards(): vol_inner = lax.ppermute(own, 'space', within)]
    ppermute x1, starting transfers between devices: 0.1 us -> 3.93 us  [shards(): terms_inner = lax.ppermute(inner, 'space', within)]
    pallas_call x14 -> x13, Pallas kernels: 27 us -> 26.7 us  [call(): pl.pallas_call(body, out_shape=list(outs), in_specs=[pl.BlockSpec(memory_...]
where the time goes in v11:
time: 50.6 us; the launch traced here: 50.4 us
  Pallas kernels  26.7 us (53%)
  starting transfers between devices  17.4 us (34%)
  waiting for transfers between devices  5.43 us (11%)
  between operations  0.83 us (2%)
    pallas_call x13, Pallas kernels, call(): pl.pallas_call(body, out_shape=list(outs), in_specs=[pl.BlockSpec(memory_...  26.7 us
    ppermute x3, starting transfers between devices, shards(): lax.ppermute(part, 'space', [(i, i ^ away) for i in range(count)])  4.45 us
    ppermute x1, starting transfers between devices, shards(): terms_inner = lax.ppermute(inner, 'space', within)  3.93 us
    ppermute x1, starting transfers between devices, shards(): message = lax.ppermute(message, 'space', within)  3.46 us
    ppermute x1, starting transfers between devices, shards(): arrived = lax.ppermute(sent, 'space', [(i, i ^ 4) for i in range(count)])  2.85 us
    ppermute x3, waiting for transfers between devices, shards(): lax.ppermute(part, 'space', [(i, i ^ away) for i in range(count)])  2.34 us
    ppermute x1, waiting for transfers between devices, shards(): message = lax.ppermute(message, 'space', within)  1.82 us
    ppermute x1, waiting for transfers between devices, shards(): arrived = lax.ppermute(sent, 'space', [(i, i ^ 4) for i in range(count)])  1.26 us
  transfers between devices with their start and end apart: 10, of which 3 were waited for; matrix products, arithmetic and copies ran while one was open for 0% of the time, Pallas kernels for 43%

profile of v11, /device:TPU:0, one launch (start us, length us, event | category | flops | bytes accessed | tf_op | source)
XLA Modules:
  0.0 50.4 jit_solution(7338027327734564456)
XLA Ops:
  0.6 1.4 %pack_volume.1.own = bf16[2048,128]{1,0:T(8,128)(2,1)S(1)} custom-call(bf16[2,2048,64]{2,1,0:T(8,128)(2,1)} %bitcast.18), custom_call_target="tpu_custom_call" | custom-call | bytes 1048576 | tf_op jit(solution)/shard_map/pack_volume/pallas_call | solution.py:27
  2.0 0.5 %collective-permute-start = (bf16[2048,128]{1,0:T(8,128)(2,1)S(1)}, bf16[2048,128]{1,0:T(8,128)(2,1)S(1)}, u32[]{:S(2)}, u32[]{:S(2)}) collective-permute-start(bf16[2048,128]{1,0:T(8,128)(2,1)S(1)} %pack_volume.1.own), channel_id=1, source_target_pairs={{0,1},{1,0},{2,3},{3,2},{4,5},{5,4},{6,7},{7,6},{8,9},{9,8},{10,11... | collective-permute-start | bytes 1572872 | tf_op jit(solution)/shard_map/ppermute | solution.py:504
  2.6 0.7 %collective-permute-start.1 = (bf16[2048,128]{1,0:T(8,128)(2,1)S(1)}, bf16[2048,128]{1,0:T(8,128)(2,1)S(1)}, u32[]{:S(2)}, u32[]{:S(2)}) collective-permute-start(bf16[2048,128]{1,0:T(8,128)(2,1)S(1)} %pack_volume.1.own), channel_id=1, source_target_pairs={{1,2},{3,4},{5,6},{7,8},{9,10},{11,12},{13,14},{2,1},{4,3},{6,5},{... | collective-permute-start | bytes 1572872 | tf_op jit(solution)/shard_map/ppermute | solution.py:503
  3.2 0.0 copy-start
  3.3 4.6 %grad_act_terms.1 = (f32[2048,128]{1,0:T(8,128)S(1)}, bf16[1024,128]{1,0:T(8,128)(2,1)S(1)}, bf16[1024,128]{1,0:T(8,128)(2,1)S(1)}, bf16[256,2048]{1,0:T(8,128)(2,1)S(1)}) custom-call(s32[1]{0:T(128)} %bitcast.me, bf16[2,2048,128]{2,1,0:T(8,128)(2,1)} %bitcast.19, bf16[27,64,128]{2,1,0:T(8,128)(2,1)} %bitcast.15), custom_call_target="tpu_custom_call" | custom-call | flops 1811939328 | bytes 4112388 | tf_op jit(solution)/shard_map/grad_act_terms/pallas_call | solution.py:27
  7.9 0.2 back_taps.1.taps
  8.1 0.0 collective-permute-done.inner
  8.1 3.7 %prepare.1 = (bf16[2112,384]{1,0:T(8,128)(2,1)S(1)}, bf16[2112,384]{1,0:T(8,128)(2,1)S(1)}, f32[2048,256]{1,0:T(8,128)S(1)}, bf16[1152,256]{1,0:T(8,128)(2,1)S(1)}) custom-call(s32[1]{0:T(128)} %bitcast.me, bf16[2048,128]{1,0:T(8,128)(2,1)S(1)} %pack_volume.1.own, bf16[2048,128]{1,0:T(8,128)(2,1)S(1)} %collective-permute-done.inner, bf16[27,64,64]{2,1,0:T(8,128)(2,1)} %bitcast.13), custom_call_target="tpu_custom_call" | custom-call | flops 905969664 | bytes 7200772 | tf_op jit(solution)/shard_map/prepare/pallas_call | solution.py:27
  11.8 3.9 %collective-permute-start.2 = (bf16[1024,128]{1,0:T(8,128)(2,1)S(1)}, bf16[1024,128]{1,0:T(8,128)(2,1)S(1)}, u32[]{:S(2)}, u32[]{:S(2)}) collective-permute-start(bf16[1024,128]{1,0:T(8,128)(2,1)S(1)} %get-tuple-element.52), channel_id=1, source_target_pairs={{0,1},{1,0},{2,3},{3,2},{4,5},{5,4},{6,7},{7,6},{8,9},{9,8},{10,11... | collective-permute-start | bytes 786440 | tf_op jit(solution)/shard_map/ppermute | solution.py:531
  15.7 0.7 %collective-permute-start.3 = (bf16[1024,128]{1,0:T(8,128)(2,1)S(1)}, bf16[1024,128]{1,0:T(8,128)(2,1)S(1)}, u32[]{:S(2)}, u32[]{:S(2)}) collective-permute-start(bf16[1024,128]{1,0:T(8,128)(2,1)S(1)} %get-tuple-element.53), channel_id=1, source_target_pairs={{1,2},{3,4},{5,6},{7,8},{9,10},{11,12},{13,14},{2,1},{4,3},{6,5},{... | collective-permute-start | bytes 786440 | tf_op jit(solution)/shard_map/ppermute | solution.py:530
  16.4 0.0 collective-permute-done.1.outer
  16.4 2.8 %hidden.1 = (bf16[2112,384]{1,0:T(8,128)(2,1)S(1)}, bf16[2112,768]{1,0:T(8,128)(2,1)S(1)}, f32[2048,128]{1,0:T(8,128)S(1)}) custom-call(s32[1]{0:T(128)} %bitcast.me, bf16[2048,128]{1,0:T(8,128)(2,1)S(1)} %collective-permute-done.1.outer, f32[2048,256]{1,0:T(8,128)S(1)} %get-tuple-element.48.part, bf16[1152,256]{1,0:T(8,128)(2,1)S(1)} %get-tuple-element.49.outer_taps), custom_call_target="tpu_custom_call" | custom-call | flops 1811939328 | bytes 9125892 | tf_op jit(solution)/shard_map/hidden/pallas_call | solution.py:27
  19.2 2.7 %grad_two_terms.1.other = f32[128,1792]{1,0:T(8,128)S(1)} custom-call(bf16[2112,768]{1,0:T(8,128)(2,1)S(1)} %get-tuple-element.66.act_windows, bf16[256,2048]{1,0:T(8,128)(2,1)S(1)} %get-tuple-element.56.turned), custom_call_target="tpu_custom_call" | custom-call | flops 1811939328 | bytes 5210112 | tf_op jit(solution)/shard_map/grad_two_terms/pallas_call | solution.py:27
  22.0 0.0 collective-permute-done.3.outer
  22.0 0.0 copy-start.1
  22.0 2.6 %grad_one_terms.1 = (bf16[2048,128]{1,0:T(8,128)(2,1)S(1)}, bf16[1024,128]{1,0:T(8,128)(2,1)S(1)}, bf16[2816,128]{1,0:T(8,128)(2,1)S(1)}, f32[8,24,896]{2,1,0:T(8,128)S(1)}) custom-call(s32[1]{0:T(128)} %bitcast.me, bf16[2112,384]{1,0:T(8,128)(2,1)S(1)} %get-tuple-element.43.own_windows, bf16[2112,384]{1,0:T(8,128)(2,1)S(1)} %get-tuple-element.44.inner_windows, ...), custom_call_target="tpu_custom_call" | custom-call | flops 905969664 | bytes 10600452 | tf_op jit(solution)/shard_map/grad_one_terms/pallas_call | solution.py:27
  24.6 3.5 %collective-permute-start.4 = (bf16[2816,128]{1,0:T(8,128)(2,1)S(1)}, bf16[2816,128]{1,0:T(8,128)(2,1)S(1)}, u32[]{:S(2)}, u32[]{:S(2)}) collective-permute-start(bf16[2816,128]{1,0:T(8,128)(2,1)S(1)} %get-tuple-element.58), channel_id=1, source_target_pairs={{0,1},{1,0},{2,3},{3,2},{4,5},{5,4},{6,7},{7,6},{8,9},{9,8},{10,11... | collective-permute-start | bytes 2162696 | tf_op jit(solution)/shard_map/ppermute | solution.py:558
  28.0 1.8 %collective-permute-done.4.arrived.message = bf16[2816,128]{1,0:T(8,128)(2,1)S(1)} collective-permute-done((bf16[2816,128]{1,0:T(8,128)(2,1)S(1)}, bf16[2816,128]{1,0:T(8,128)(2,1)S(1)}, u32[]{:S(2)}, u32[]{:S(2)}) %collective-permute-start.4) | collective-permute-done | bytes 720928 | tf_op jit(solution)/shard_map/ppermute | solution.py:558
  29.8 0.1 halve.1
  29.9 2.9 %collective-permute-start.5 = (bf16[4,32,896]{2,1,0:T(8,128)(2,1)S(1)}, bf16[4,32,896]{2,1,0:T(8,128)(2,1)S(1)}, u32[]{:S(2)}, u32[]{:S(2)}) collective-permute-start(bf16[4,32,896]{2,1,0:T(8,128)(2,1)S(1)} %get-tuple-element.62), channel_id=1, source_target_pairs={{0,4},{1,5},{2,6},{3,7},{4,0},{5,1},{6,2},{7,3},{8,12},{9,13},{10,... | collective-permute-start | bytes 688136 | tf_op jit(solution)/shard_map/ppermute | solution.py:571
  32.8 0.8 %collective-permute-start.6 = (bf16[1024,128]{1,0:T(8,128)(2,1)S(1)}, bf16[1024,128]{1,0:T(8,128)(2,1)S(1)}, u32[]{:S(2)}, u32[]{:S(2)}) collective-permute-start(bf16[1024,128]{1,0:T(8,128)(2,1)S(1)} %get-tuple-element.70), channel_id=1, source_target_pairs={{1,2},{3,4},{5,6},{7,8},{9,10},{11,12},{13,14},{2,1},{4,3},{6,5},{... | collective-permute-start | bytes 786440 | tf_op jit(solution)/shard_map/ppermute | solution.py:572
  33.7 4.0 %output.1 = f32[2,2048,128]{2,1,0:T(8,128)} custom-call(bf16[2112,768]{1,0:T(8,128)(2,1)S(1)} %get-tuple-element.66.act_windows, bf16[27,64,128]{2,1,0:T(8,128)(2,1)S(1)} %bitcast.16), custom_call_target="tpu_custom_call" | custom-call | flops 1811939328 | bytes 5783552 | tf_op jit(solution)/shard_map/output/pallas_call | solution.py:27
  37.7 1.3 %collective-permute-done.5.arrived = bf16[4,32,896]{2,1,0:T(8,128)(2,1)S(1)} collective-permute-done((bf16[4,32,896]{2,1,0:T(8,128)(2,1)S(1)}, bf16[4,32,896]{2,1,0:T(8,128)(2,1)S(1)}, u32[]{:S(2)}, u32[]{:S(2)}) %collective-permute-start.5) | collective-permute-done | bytes 229408 | tf_op jit(solution)/shard_map/ppermute | solution.py:571
  39.0 1.8 %collective-permute-start.7 = (bf16[24,896]{1,0:T(8,128)(2,1)S(1)}, bf16[24,896]{1,0:T(8,128)(2,1)S(1)}, u32[]{:S(2)}, u32[]{:S(2)}) collective-permute-start(bf16[24,896]{1,0:T(8,128)(2,1)S(1)} %get-tuple-element.73), channel_id=1, source_target_pairs={{0,2},{1,3},{2,0},{3,1},{4,6},{5,7},{6,4},{7,5},{8,10},{9,11},{10,... | collective-permute-start | bytes 129032 | tf_op jit(solution)/shard_map/ppermute | solution.py:593
  40.7 2.6 %collective-permute-start.8 = (bf16[24,896]{1,0:T(8,128)(2,1)S(1)}, bf16[24,896]{1,0:T(8,128)(2,1)S(1)}, u32[]{:S(2)}, u32[]{:S(2)}) collective-permute-start(bf16[24,896]{1,0:T(8,128)(2,1)S(1)} %get-tuple-element.74), channel_id=1, source_target_pairs={{0,8},{1,9},{2,10},{3,11},{4,12},{5,13},{6,14},{7,15},{8,0},{9,1},... | collective-permute-start | bytes 129032 | tf_op jit(solution)/shard_map/ppermute | solution.py:593
  43.3 0.1 collective-permute-start.9
  43.4 0.0 collective-permute-done.6.outer
  43.4 0.8 %grad_windows.1.windows = bf16[2112,768]{1,0:T(8,128)(2,1)S(1)} custom-call(s32[1]{0:T(128)} %bitcast.me, bf16[2048,128]{1,0:T(8,128)(2,1)S(1)} %get-tuple-element.69.own, bf16[2816,128]{1,0:T(8,128)(2,1)S(1)} %collective-permute-done.4.arrived.message, bf16[1024,128]{1,0:T(8,128)(2,1)S(1)} %collective-permute-done.6.outer), custom_call_target="tpu_custom_call" | custom-call | flops 226492416 | bytes 4751364 | tf_op jit(solution)/shard_map/grad_windows/pallas_call | solution.py:27
  44.3 3.0 %grad_volume.1 = f32[2,2048,64]{2,1,0:T(8,128)} custom-call(bf16[2112,768]{1,0:T(8,128)(2,1)S(1)} %grad_windows.1.windows, bf16[384,768]{1,0:T(8,128)(2,1)S(1)} %back_taps.1.taps), custom_call_target="tpu_custom_call" | custom-call | flops 905969664 | bytes 4882432 | tf_op jit(solution)/shard_map/grad_volume/pallas_call | solution.py:27
  47.3 0.0 collective-permute-done.8.refs_1_
  47.3 2.3 %collective-permute-done.9.refs_2_ = bf16[24,896]{1,0:T(8,128)(2,1)S(1)} collective-permute-done((bf16[24,896]{1,0:T(8,128)(2,1)S(1)}, bf16[24,896]{1,0:T(8,128)(2,1)S(1)}, u32[]{:S(2)}, u32[]{:S(2)}) %collective-permute-start.9) | collective-permute-done | bytes 43040 | tf_op jit(solution)/shard_map/ppermute | solution.py:593
  49.6 0.7 %finish.1 = (f32[27,4,64]{2,1,0:T(4,128)}, f32[27,8,64]{2,1,0:T(8,128)}) custom-call(f32[24,896]{1,0:T(8,128)S(1)} %get-tuple-element.72.mine, bf16[24,896]{1,0:T(8,128)(2,1)S(1)} %collective-permute-done.7.refs_0_, bf16[24,896]{1,0:T(8,128)(2,1)S(1)} %collective-permute-done.8.refs_1_, bf16[24,896]{1,0:T(8,128)(2,1)S(1)} %collective-permute-done.9.refs_2_), custom_call_target="tpu_custom_call" | custom-call | bytes 297984 | tf_op jit(solution)/shard_map/finish/pallas_call | solution.py:27
  (5 shorter events, 0.1 us)
Async XLA Ops:
  2.0 6.0 %collective-permute-start = (bf16[2048,128]{1,0:T(8,128)(2,1)S(1)}, bf16[2048,128]{1,0:T(8,128)(2,1)S(1)}, u32[]{:S(2)}, u32[]{:S(2)}) collective-permute-start(bf16[2048,128]{1,0:T(8,128)(2,1)S(1)} %pack_volume.1.own), channel_id=1, source_target_pairs={{0,1},{1,0},{2,3},{3,2},{4,5},{5,4},{6,7},{7,6},{8,9},{9,8},{10,11... | collective-permute-start | bytes 1572872 | tf_op jit(solution)/shard_map/ppermute | solution.py:504
  2.6 13.8 %collective-permute-start.1 = (bf16[2048,128]{1,0:T(8,128)(2,1)S(1)}, bf16[2048,128]{1,0:T(8,128)(2,1)S(1)}, u32[]{:S(2)}, u32[]{:S(2)}) collective-permute-start(bf16[2048,128]{1,0:T(8,128)(2,1)S(1)} %pack_volume.1.own), channel_id=1, source_target_pairs={{1,2},{3,4},{5,6},{7,8},{9,10},{11,12},{13,14},{2,1},{4,3},{6,5},{... | collective-permute-start | bytes 1572872 | tf_op jit(solution)/shard_map/ppermute | solution.py:503
  3.2 4.6 %copy-start = (bf16[3,3,3,64,64]{4,3,2,1,0:T(8,128)(2,1)S(1)}, bf16[3,3,3,64,64]{4,3,2,1,0:T(8,128)(2,1)}, u32[]{:S(2)}) copy-start(bf16[3,3,3,64,64]{4,3,2,1,0:T(8,128)(2,1)} %param.5) | copy-start | bytes 663556
  11.8 10.1 %collective-permute-start.2 = (bf16[1024,128]{1,0:T(8,128)(2,1)S(1)}, bf16[1024,128]{1,0:T(8,128)(2,1)S(1)}, u32[]{:S(2)}, u32[]{:S(2)}) collective-permute-start(bf16[1024,128]{1,0:T(8,128)(2,1)S(1)} %get-tuple-element.52), channel_id=1, source_target_pairs={{0,1},{1,0},{2,3},{3,2},{4,5},{5,4},{6,7},{7,6},{8,9},{9,8},{10,11... | collective-permute-start | bytes 786440 | tf_op jit(solution)/shard_map/ppermute | solution.py:531
  15.7 6.2 %collective-permute-start.3 = (bf16[1024,128]{1,0:T(8,128)(2,1)S(1)}, bf16[1024,128]{1,0:T(8,128)(2,1)S(1)}, u32[]{:S(2)}, u32[]{:S(2)}) collective-permute-start(bf16[1024,128]{1,0:T(8,128)(2,1)S(1)} %get-tuple-element.53), channel_id=1, source_target_pairs={{1,2},{3,4},{5,6},{7,8},{9,10},{11,12},{13,14},{2,1},{4,3},{6,5},{... | collective-permute-start | bytes 786440 | tf_op jit(solution)/shard_map/ppermute | solution.py:530
  22.0 11.7 %copy-start.1 = (bf16[3,3,3,64,128]{4,3,2,1,0:T(8,128)(2,1)S(1)}, bf16[3,3,3,64,128]{4,3,2,1,0:T(8,128)(2,1)}, u32[]{:S(2)}) copy-start(bf16[3,3,3,64,128]{4,3,2,1,0:T(8,128)(2,1)} %param.6) | copy-start | bytes 1327108
  24.6 5.3 %collective-permute-start.4 = (bf16[2816,128]{1,0:T(8,128)(2,1)S(1)}, bf16[2816,128]{1,0:T(8,128)(2,1)S(1)}, u32[]{:S(2)}, u32[]{:S(2)}) collective-permute-start(bf16[2816,128]{1,0:T(8,128)(2,1)S(1)} %get-tuple-element.58), channel_id=1, source_target_pairs={{0,1},{1,0},{2,3},{3,2},{4,5},{5,4},{6,7},{7,6},{8,9},{9,8},{10,11... | collective-permute-start | bytes 2162696 | tf_op jit(solution)/shard_map/ppermute | solution.py:558
  29.9 9.0 %collective-permute-start.5 = (bf16[4,32,896]{2,1,0:T(8,128)(2,1)S(1)}, bf16[4,32,896]{2,1,0:T(8,128)(2,1)S(1)}, u32[]{:S(2)}, u32[]{:S(2)}) collective-permute-start(bf16[4,32,896]{2,1,0:T(8,128)(2,1)S(1)} %get-tuple-element.62), channel_id=1, source_target_pairs={{0,4},{1,5},{2,6},{3,7},{4,0},{5,1},{6,2},{7,3},{8,12},{9,13},{10,... | collective-permute-start | bytes 688136 | tf_op jit(solution)/shard_map/ppermute | solution.py:571
  32.8 10.6 %collective-permute-start.6 = (bf16[1024,128]{1,0:T(8,128)(2,1)S(1)}, bf16[1024,128]{1,0:T(8,128)(2,1)S(1)}, u32[]{:S(2)}, u32[]{:S(2)}) collective-permute-start(bf16[1024,128]{1,0:T(8,128)(2,1)S(1)} %get-tuple-element.70), channel_id=1, source_target_pairs={{1,2},{3,4},{5,6},{7,8},{9,10},{11,12},{13,14},{2,1},{4,3},{6,5},{... | collective-permute-start | bytes 786440 | tf_op jit(solution)/shard_map/ppermute | solution.py:572
  39.0 8.3 %collective-permute-start.7 = (bf16[24,896]{1,0:T(8,128)(2,1)S(1)}, bf16[24,896]{1,0:T(8,128)(2,1)S(1)}, u32[]{:S(2)}, u32[]{:S(2)}) collective-permute-start(bf16[24,896]{1,0:T(8,128)(2,1)S(1)} %get-tuple-element.73), channel_id=1, source_target_pairs={{0,2},{1,3},{2,0},{3,1},{4,6},{5,7},{6,4},{7,5},{8,10},{9,11},{10,... | collective-permute-start | bytes 129032 | tf_op jit(solution)/shard_map/ppermute | solution.py:593
  40.7 6.5 %collective-permute-start.8 = (bf16[24,896]{1,0:T(8,128)(2,1)S(1)}, bf16[24,896]{1,0:T(8,128)(2,1)S(1)}, u32[]{:S(2)}, u32[]{:S(2)}) collective-permute-start(bf16[24,896]{1,0:T(8,128)(2,1)S(1)} %get-tuple-element.74), channel_id=1, source_target_pairs={{0,8},{1,9},{2,10},{3,11},{4,12},{5,13},{6,14},{7,15},{8,0},{9,1},... | collective-permute-start | bytes 129032 | tf_op jit(solution)/shard_map/ppermute | solution.py:593
  43.3 6.3 %collective-permute-start.9 = (bf16[24,896]{1,0:T(8,128)(2,1)S(1)}, bf16[24,896]{1,0:T(8,128)(2,1)S(1)}, u32[]{:S(2)}, u32[]{:S(2)}) collective-permute-start(bf16[24,896]{1,0:T(8,128)(2,1)S(1)} %get-tuple-element.75), channel_id=1, source_target_pairs={{0,10},{1,11},{2,8},{3,9},{4,14},{5,15},{6,12},{7,13},{8,2},{9,3},... | collective-permute-start | bytes 129032 | tf_op jit(solution)/shard_map/ppermute | solution.py:593

commit v12 on v11

--- a/solution.py
+++ b/solution.py
@@ -9,7 +9,7 @@
 from jax.sharding import PartitionSpec as P
 
 F32, BF16 = jnp.float32, jnp.bfloat16
-STEP, BLOCK = 256, 1024
+STEP, BLOCK = 256, 512
 VMEM_LIMIT = 16 * 2**20
 NN = (((1,), (0,)), ((), ()))
 NT = (((1,), (1,)), ((), ()))
@@ -22,7 +22,7 @@
     return tap if 0 <= tap <= 2 else None
 
 
-def call(body, outs, ins, scratch=(), flops=0, name=None, smem=(), apart=(), far=False):
+def call(body, outs, ins, scratch=(), flops=0, name=None, smem=(), apart=(), far=(), alias=None):
     moved = sum(math.prod(s.shape) * s.dtype.itemsize for s in (*outs, *ins))
     return pl.pallas_call(
         body,
@@ -33,7 +33,10 @@
             )
             for i in range(len(ins))
         ],
-        out_specs=[pl.BlockSpec(memory_space=pl.ANY if far else pltpu.VMEM)] * len(outs),
+        out_specs=[
+            pl.BlockSpec(memory_space=pl.ANY if i in far else pltpu.VMEM) for i in range(len(outs))
+        ],
+        input_output_aliases=alias or {},
         scratch_shapes=list(scratch),
         compiler_params=pltpu.CompilerParams(vmem_limit_bytes=VMEM_LIMIT),
         cost_estimate=pl.CostEstimate(flops=flops, bytes_accessed=moved, transcendentals=0),
@@ -222,7 +225,8 @@
 
 
 def hidden_body(
-    columns, count, me, outer, part, outer_taps, outer_windows, act_windows, slope
+    columns, count, me, outer, part, outer_taps, inner_windows, act_windows, slope, side_windows,
+    outer_windows,
 ):
     cells = outer.shape[0]
 
@@ -235,6 +239,13 @@
     clear_edges(outer_windows, columns)
     clear_edges(act_windows, columns)
     lax.fori_loop(0, cells // STEP, fill, 0)
+    from_inner = lax.broadcasted_iota(jnp.int32, (16, 128), 1) // 64 == me[0] % 2
+    from_inner = jnp.where(from_inner, 1.0, 0.0).astype(BF16)[:1]
+    for tap in range(3):
+        at = slice(tap * 128, tap * 128 + 128)
+        side_windows[:, at] = (
+            inner_windows[:, at] * from_inner + outer_windows[:, at] * (1 - from_inner)
+        )
     lanes = lax.broadcasted_iota(jnp.int32, (BLOCK, 128), 1)
     edges = [jnp.where(me[0] == end, 0.0, 1.0).astype(F32) for end in (count - 1, 0)]
     inside = jnp.where(lanes < 64, edges[0], edges[1])
@@ -302,8 +313,8 @@
 
 
 def grad_one_body(
-    columns, count, me, own_windows, inner_windows, outer_windows, act_terms, inner, outer, slope,
-    other, grad, to_outer, message, kept, turned, terms,
+    columns, count, me, own_windows, side_windows, act_terms, inner, outer, slope, other,
+    grad, to_outer, message, kept, turned, terms,
 ):
     cells = grad.shape[0]
     odd = me[0] % 2 == 1
@@ -323,15 +334,10 @@
             odd, lower, upper
         ).astype(BF16)
         to_outer[low, :] = jnp.where(odd, upper, lower).astype(BF16)
-    from_inner = lax.broadcasted_iota(jnp.int32, (16, 128), 1) // 64 == me[0] % 2
-    from_inner = jnp.where(from_inner, 1.0, 0.0).astype(BF16)[:1]
-    from_outer = 1 - from_inner
-
     def slices(row, column):
         rows = slice(row * columns, row * columns + cells)
         lanes = slice(column * 128, column * 128 + 128)
-        sides = inner_windows[rows, lanes] * from_inner + outer_windows[rows, lanes] * from_outer
-        return jnp.concatenate([own_windows[rows, lanes], sides], axis=1)
+        return jnp.concatenate([own_windows[rows, lanes], side_windows[rows, lanes]], axis=1)
 
     kernel_terms(columns, 64, slices, turned, terms)
     half = terms.shape[1] // 2
@@ -407,7 +413,7 @@
                 out[depth * 9 + tap] = block[:, lane : lane + 64]
 
 
-def output_body(columns, act_windows, weight, far, taps, output, sems):
+def output_taps(weight, taps):
     for row in range(3):
         for column in range(3):
             for at, source in enumerate(PLANES):
@@ -419,15 +425,33 @@
                         if depth is None
                         else weight[depth * 9 + row * 3 + column]
                     )
-    copies = pieces_of(output, far, sems, output.shape[1] // BLOCK)
-    for at, copy in enumerate(copies):
-        start = at * BLOCK
+
+
+def output_rows(columns, blocks, act_windows, taps, far, output, sems):
+    copies = []
+    for at, block in enumerate(blocks):
+        start = block * BLOCK
         value = window_dot(act_windows, taps, start, columns, NN)
-        output[0, start : start + BLOCK, :] = value[:, :128]
-        output[1, start : start + BLOCK, :] = value[:, 128:]
-        copy.start()
+        here = slice(at * BLOCK, at * BLOCK + BLOCK)
+        output[0, here, :] = value[:, :128]
+        output[1, here, :] = value[:, 128:]
+        copies.append(
+            pltpu.make_async_copy(
+                output.at[:, here, :], far.at[:, start : start + BLOCK, :], sems.at[at]
+            )
+        )
+        copies[-1].start()
     for copy in copies:
         copy.wait()
+
+
+def output_first_body(columns, blocks, act_windows, weight, far, taps, output, sems):
+    output_taps(weight, taps)
+    output_rows(columns, blocks, act_windows, taps, far, output, sems)
+
+
+def output_rest_body(columns, blocks, act_windows, taps, begun, far, output, sems):
+    output_rows(columns, blocks, act_windows, taps, far, output, sems)
 
 
 def grad_windows_body(columns, me, own, message, outer, windows):
@@ -529,17 +553,26 @@
     inner, outer, part, back_taps = lax.optimization_barrier((inner, outer, part, back_taps))
     terms_outer = lax.ppermute(outer, "space", across)
     terms_inner = lax.ppermute(inner, "space", within)
-    outer_windows, act_windows, slope = call(
+    act_windows, slope, side_windows = call(
         functools.partial(hidden_body, columns, count),
-        (third, shape(slab, BF16), shape((cells, 128), F32)),
-        (me, vol_outer, part, outer_taps),
-        (), 2 * one_flops, "hidden", (0,),
+        (shape(slab, BF16), shape((cells, 128), F32), third),
+        (me, vol_outer, part, outer_taps, inner_windows),
+        (pltpu.VMEM((slab[0], 384), BF16),), 2 * one_flops, "hidden", (0,),
     )
     terms_two, = call(
         functools.partial(grad_two_body, columns),
         (shape((wide, 2 * lanes), F32),),
         (act_windows, turned), (), two_flops, "grad_two_terms",
     )
+    blocks = range(cells // BLOCK)
+    output, out_taps = call(
+        functools.partial(output_first_body, columns, blocks[:1]),
+        (shape((planes, cells, wide), F32), shape((9 * 256, 256), BF16)),
+        (act_windows, weight_two),
+        (pltpu.VMEM((planes, BLOCK, wide), F32), dma((1,))),
+        two_flops // 4, "output_first", (), (), (0,),
+    )
+    terms_outer, output, out_taps = lax.optimization_barrier((terms_outer, output, out_taps))
     groups = lanes // 128
     grad_hidden, outer, message, kept = call(
         functools.partial(grad_one_body, columns, count),
@@ -549,8 +582,7 @@
             shape((count // 2, chunk, lanes), F32),
         ),
         (
-            me, own_windows, inner_windows, outer_windows, terms, terms_inner, terms_outer, slope,
-            terms_two,
+            me, own_windows, side_windows, terms, terms_inner, terms_outer, slope, terms_two,
         ),
         (pltpu.VMEM((128, cells), BF16), pltpu.VMEM((mid, 2 * lanes), F32)),
         one_flops, "grad_one_terms", (0,),
@@ -567,24 +599,21 @@
 
     bits = list(range(count.bit_length() - 2, 0, -1))
     bits, sent, kept = halve(bits, 2, split, split, kept, message)
-    sent, act_windows, outer = lax.optimization_barrier((sent, act_windows, outer))
+    sent, act_windows = lax.optimization_barrier((sent, act_windows))
     arrived = lax.ppermute(sent, "space", [(i, i ^ 4) for i in range(count)])
     grad_outer = lax.ppermute(outer, "space", across)
     output, = call(
-        functools.partial(output_body, columns),
+        functools.partial(output_rest_body, columns, blocks[1:]),
         (shape((planes, cells, wide), F32),),
-        (act_windows, weight_two),
-        (
-            pltpu.VMEM((3 * 768, 256), BF16), pltpu.VMEM((planes, cells, wide), F32),
-            dma((cells // BLOCK,)),
-        ),
-        two_flops, "output", (), (), True,
+        (act_windows, out_taps, output),
+        (pltpu.VMEM((planes, cells - BLOCK, wide), F32), dma((len(blocks) - 1,))),
+        two_flops, "output_rest", (), (2,), (0,), {2: 0},
     )
     others = 2 ** len(bits) - 1
     mine, *sent = call(
         functools.partial(spread_body, split, bits),
         (shape((chunk, lanes), F32), *[shape((chunk, lanes), BF16)] * others),
-        (me, kept, arrived), flops=one_flops, name="spread", smem=(0,),
+        (me, kept, arrived), name="spread", smem=(0,),
     )
     sent, output, grad_hidden = lax.optimization_barrier((sent, output, grad_hidden))
     arrived = []
@@ -601,7 +630,7 @@
         (shape((planes, cells, channels), F32),),
         (grad_windows, back_taps),
         (pltpu.VMEM((planes, cells, channels), F32), dma((cells // BLOCK,))),
-        one_flops, "grad_volume", (), (), True,
+        one_flops, "grad_volume", (), (), (0,),
     )
     grad_one, grad_two = call(
         functools.partial(finish_body, scale, (mid // count, wide // count)),

time: 50.6 us -> 54 us (1.067)
  waiting for transfers between devices: 5.43 us -> 7.86 us
  Pallas kernels: 26.7 us -> 27.5 us
    ppermute x1, waiting for transfers between devices: 1.26 us -> 5.89 us  [shards(): arrived = lax.ppermute(sent, 'space', [(i, i ^ 4) for i in range(count)])]
    ppermute x3, waiting for transfers between devices: 2.34 us -> 0.81 us  [shards(): lax.ppermute(part, 'space', [(i, i ^ away) for i in range(count)])]
    pallas_call x13 -> x14, Pallas kernels: 26.7 us -> 27.5 us  [call(): pl.pallas_call(body, out_shape=list(outs), in_specs=[pl.BlockSpec(memory_...]
    ppermute x1, waiting for transfers between devices: 1.82 us -> 1.14 us  [shards(): message = lax.ppermute(message, 'space', within)]
    ppermute x1, starting transfers between devices: 2.85 us -> 3.48 us  [shards(): arrived = lax.ppermute(sent, 'space', [(i, i ^ 4) for i in range(count)])]
where the time goes in v12:
time: 54 us; the launch traced here: 53.7 us
  Pallas kernels  27.5 us (51%)
  starting transfers between devices  17.5 us (32%)
  waiting for transfers between devices  7.86 us (15%)
  between operations  0.84 us (2%)
    pallas_call x14, Pallas kernels, call(): pl.pallas_call(body, out_shape=list(outs), in_specs=[pl.BlockSpec(memory_...  27.5 us
    ppermute x1, waiting for transfers between devices, shards(): arrived = lax.ppermute(sent, 'space', [(i, i ^ 4) for i in range(count)])  5.89 us
    ppermute x3, starting transfers between devices, shards(): lax.ppermute(part, 'space', [(i, i ^ away) for i in range(count)])  4.44 us
    ppermute x1, starting transfers between devices, shards(): terms_inner = lax.ppermute(inner, 'space', within)  3.93 us
    ppermute x1, starting transfers between devices, shards(): arrived = lax.ppermute(sent, 'space', [(i, i ^ 4) for i in range(count)])  3.48 us
    ppermute x1, starting transfers between devices, shards(): message = lax.ppermute(message, 'space', within)  2.93 us
    ppermute x1, waiting for transfers between devices, shards(): message = lax.ppermute(message, 'space', within)  1.14 us
  transfers between devices with their start and end apart: 10, of which 3 were waited for; matrix products, arithmetic and copies ran while one was open for 0% of the time, Pallas kernels for 43%

profile of v12, /device:TPU:0, one launch (start us, length us, event | category | flops | bytes accessed | tf_op | source)
XLA Modules:
  0.0 53.7 jit_solution(6868991643806529205)
XLA Ops:
  0.6 1.4 %pack_volume.1.own = bf16[2048,128]{1,0:T(8,128)(2,1)S(1)} custom-call(bf16[2,2048,64]{2,1,0:T(8,128)(2,1)} %bitcast.19), custom_call_target="tpu_custom_call" | custom-call | bytes 1048576 | tf_op jit(solution)/shard_map/pack_volume/pallas_call | solution.py:27
  2.0 0.5 collective-permute-start
  2.6 0.7 %collective-permute-start.1 = (bf16[2048,128]{1,0:T(8,128)(2,1)S(1)}, bf16[2048,128]{1,0:T(8,128)(2,1)S(1)}, u32[]{:S(2)}, u32[]{:S(2)}) collective-permute-start(bf16[2048,128]{1,0:T(8,128)(2,1)S(1)} %pack_volume.1.own), channel_id=1, source_target_pairs={{1,2},{3,4},{5,6},{7,8},{9,10},{11,12},{13,14},{2,1},{4,3},{6,5},{... | collective-permute-start | bytes 1572872 | tf_op jit(solution)/shard_map/ppermute | solution.py:527
  3.2 0.0 copy-start.1
  3.3 4.6 %grad_act_terms.1 = (f32[2048,128]{1,0:T(8,128)S(1)}, bf16[1024,128]{1,0:T(8,128)(2,1)S(1)}, bf16[1024,128]{1,0:T(8,128)(2,1)S(1)}, bf16[256,2048]{1,0:T(8,128)(2,1)S(1)}) custom-call(s32[1]{0:T(128)} %bitcast.me, bf16[2,2048,128]{2,1,0:T(8,128)(2,1)} %bitcast.20, bf16[27,64,128]{2,1,0:T(8,128)(2,1)} %bitcast.13), custom_call_target="tpu_custom_call" | custom-call | flops 1811939328 | bytes 4112388 | tf_op jit(solution)/shard_map/grad_act_terms/pallas_call | solution.py:27
  7.9 0.2 back_taps.1.taps
  8.1 0.0 collective-permute-done.inner
  8.1 3.7 %prepare.1 = (bf16[2112,384]{1,0:T(8,128)(2,1)S(1)}, bf16[2112,384]{1,0:T(8,128)(2,1)S(1)}, f32[2048,256]{1,0:T(8,128)S(1)}, bf16[1152,256]{1,0:T(8,128)(2,1)S(1)}) custom-call(s32[1]{0:T(128)} %bitcast.me, bf16[2048,128]{1,0:T(8,128)(2,1)S(1)} %pack_volume.1.own, bf16[2048,128]{1,0:T(8,128)(2,1)S(1)} %collective-permute-done.inner, bf16[27,64,64]{2,1,0:T(8,128)(2,1)} %bitcast.15), custom_call_target="tpu_custom_call" | custom-call | flops 905969664 | bytes 7200772 | tf_op jit(solution)/shard_map/prepare/pallas_call | solution.py:27
  11.8 3.9 %collective-permute-start.2 = (bf16[1024,128]{1,0:T(8,128)(2,1)S(1)}, bf16[1024,128]{1,0:T(8,128)(2,1)S(1)}, u32[]{:S(2)}, u32[]{:S(2)}) collective-permute-start(bf16[1024,128]{1,0:T(8,128)(2,1)S(1)} %get-tuple-element.56), channel_id=1, source_target_pairs={{0,1},{1,0},{2,3},{3,2},{4,5},{5,4},{6,7},{7,6},{8,9},{9,8},{10,11... | collective-permute-start | bytes 786440 | tf_op jit(solution)/shard_map/ppermute | solution.py:555
  15.7 0.8 %collective-permute-start.3 = (bf16[1024,128]{1,0:T(8,128)(2,1)S(1)}, bf16[1024,128]{1,0:T(8,128)(2,1)S(1)}, u32[]{:S(2)}, u32[]{:S(2)}) collective-permute-start(bf16[1024,128]{1,0:T(8,128)(2,1)S(1)} %get-tuple-element.57), channel_id=1, source_target_pairs={{1,2},{3,4},{5,6},{7,8},{9,10},{11,12},{13,14},{2,1},{4,3},{6,5},{... | collective-permute-start | bytes 786440 | tf_op jit(solution)/shard_map/ppermute | solution.py:554
  16.6 0.0 copy-start
  16.6 3.5 %hidden.1 = (bf16[2112,768]{1,0:T(8,128)(2,1)S(1)}, f32[2048,128]{1,0:T(8,128)S(1)}, bf16[2112,384]{1,0:T(8,128)(2,1)S(1)}) custom-call(s32[1]{0:T(128)} %bitcast.me, bf16[2048,128]{1,0:T(8,128)(2,1)S(1)} %collective-permute-done.1.outer, f32[2048,256]{1,0:T(8,128)S(1)} %get-tuple-element.51.part, bf16[1152,256]{1,0:T(8,128)(2,1)S(1)} %get-tuple-element.52.outer_taps, ...), custom_call_target="tpu_custom_call" | custom-call | flops 1811939328 | bytes 10747908 | tf_op jit(solution)/shard_map/hidden/pallas_call | solution.py:27
  20.1 1.7 %output_first.1 = (f32[2,2048,128]{2,1,0:T(8,128)}, bf16[2304,256]{1,0:T(8,128)(2,1)S(1)}) custom-call(bf16[2112,768]{1,0:T(8,128)(2,1)S(1)} %get-tuple-element.72.act_windows, bf16[27,64,128]{2,1,0:T(8,128)(2,1)S(1)} %bitcast.14), custom_call_target="tpu_custom_call" | custom-call | flops 452984832 | bytes 6963200 | tf_op jit(solution)/shard_map/output_first/pallas_call | solution.py:27
  21.8 2.7 %grad_two_terms.1.other = f32[128,1792]{1,0:T(8,128)S(1)} custom-call(bf16[2112,768]{1,0:T(8,128)(2,1)S(1)} %get-tuple-element.72.act_windows, bf16[256,2048]{1,0:T(8,128)(2,1)S(1)} %get-tuple-element.63.turned), custom_call_target="tpu_custom_call" | custom-call | flops 1811939328 | bytes 5210112 | tf_op jit(solution)/shard_map/grad_two_terms/pallas_call | solution.py:27
  24.5 0.0 collective-permute-done.3.outer
  24.5 0.0 collective-permute-done.2.inner
  24.5 2.1 %grad_one_terms.1 = (bf16[2048,128]{1,0:T(8,128)(2,1)S(1)}, bf16[1024,128]{1,0:T(8,128)(2,1)S(1)}, bf16[2816,128]{1,0:T(8,128)(2,1)S(1)}, f32[8,24,896]{2,1,0:T(8,128)S(1)}) custom-call(s32[1]{0:T(128)} %bitcast.me, bf16[2112,384]{1,0:T(8,128)(2,1)S(1)} %get-tuple-element.47.own_windows, bf16[2112,384]{1,0:T(8,128)(2,1)S(1)} %get-tuple-element.54.side_windows, ...), custom_call_target="tpu_custom_call" | custom-call | flops 905969664 | bytes 8978436 | tf_op jit(solution)/shard_map/grad_one_terms/pallas_call | solution.py:27
  26.7 2.9 %collective-permute-start.4 = (bf16[2816,128]{1,0:T(8,128)(2,1)S(1)}, bf16[2816,128]{1,0:T(8,128)(2,1)S(1)}, u32[]{:S(2)}, u32[]{:S(2)}) collective-permute-start(bf16[2816,128]{1,0:T(8,128)(2,1)S(1)} %get-tuple-element.65), channel_id=1, source_target_pairs={{0,1},{1,0},{2,3},{3,2},{4,5},{5,4},{6,7},{7,6},{8,9},{9,8},{10,11... | collective-permute-start | bytes 2162696 | tf_op jit(solution)/shard_map/ppermute | solution.py:590
  29.6 0.7 %collective-permute-start.6 = (bf16[1024,128]{1,0:T(8,128)(2,1)S(1)}, bf16[1024,128]{1,0:T(8,128)(2,1)S(1)}, u32[]{:S(2)}, u32[]{:S(2)}) collective-permute-start(bf16[1024,128]{1,0:T(8,128)(2,1)S(1)} %get-tuple-element.78), channel_id=1, source_target_pairs={{1,2},{3,4},{5,6},{7,8},{9,10},{11,12},{13,14},{2,1},{4,3},{6,5},{... | collective-permute-start | bytes 786440 | tf_op jit(solution)/shard_map/ppermute | solution.py:604
  30.3 1.1 %collective-permute-done.4.arrived.message = bf16[2816,128]{1,0:T(8,128)(2,1)S(1)} collective-permute-done((bf16[2816,128]{1,0:T(8,128)(2,1)S(1)}, bf16[2816,128]{1,0:T(8,128)(2,1)S(1)}, u32[]{:S(2)}, u32[]{:S(2)}) %collective-permute-start.4) | collective-permute-done | bytes 720928 | tf_op jit(solution)/shard_map/ppermute | solution.py:590
  31.4 0.1 halve.1
  31.5 3.5 %collective-permute-start.5 = (bf16[4,32,896]{2,1,0:T(8,128)(2,1)S(1)}, bf16[4,32,896]{2,1,0:T(8,128)(2,1)S(1)}, u32[]{:S(2)}, u32[]{:S(2)}) collective-permute-start(bf16[4,32,896]{2,1,0:T(8,128)(2,1)S(1)} %get-tuple-element.68), channel_id=1, source_target_pairs={{0,4},{1,5},{2,6},{3,7},{4,0},{5,1},{6,2},{7,3},{8,12},{9,13},{10,... | collective-permute-start | bytes 688136 | tf_op jit(solution)/shard_map/ppermute | solution.py:603
  35.0 3.0 %output_rest.1 = f32[2,2048,128]{2,1,0:T(8,128)} custom-call(bf16[2112,768]{1,0:T(8,128)(2,1)S(1)} %get-tuple-element.72.act_windows, bf16[2304,256]{1,0:T(8,128)(2,1)S(1)} %get-tuple-element.73.taps, f32[2,2048,128]{2,1,0:T(8,128)} %get-tuple-element.74.begun), custom_call_target="tpu_custom_call", output_to_operand_aliasing={{}: (2, {})} | custom-call | flops 1811939328 | bytes 8617984 | tf_op jit(solution)/shard_map/output_rest/pallas_call | solution.py:27
  38.0 5.9 %collective-permute-done.5.arrived = bf16[4,32,896]{2,1,0:T(8,128)(2,1)S(1)} collective-permute-done((bf16[4,32,896]{2,1,0:T(8,128)(2,1)S(1)}, bf16[4,32,896]{2,1,0:T(8,128)(2,1)S(1)}, u32[]{:S(2)}, u32[]{:S(2)}) %collective-permute-start.5) | collective-permute-done | bytes 229408 | tf_op jit(solution)/shard_map/ppermute | solution.py:603
  43.9 0.1 collective-permute-start.7
  44.0 2.7 %collective-permute-start.8 = (bf16[24,896]{1,0:T(8,128)(2,1)S(1)}, bf16[24,896]{1,0:T(8,128)(2,1)S(1)}, u32[]{:S(2)}, u32[]{:S(2)}) collective-permute-start(bf16[24,896]{1,0:T(8,128)(2,1)S(1)} %get-tuple-element.82), channel_id=1, source_target_pairs={{0,8},{1,9},{2,10},{3,11},{4,12},{5,13},{6,14},{7,15},{8,0},{9,1},... | collective-permute-start | bytes 129032 | tf_op jit(solution)/shard_map/ppermute | solution.py:622
  46.7 1.7 %collective-permute-start.9 = (bf16[24,896]{1,0:T(8,128)(2,1)S(1)}, bf16[24,896]{1,0:T(8,128)(2,1)S(1)}, u32[]{:S(2)}, u32[]{:S(2)}) collective-permute-start(bf16[24,896]{1,0:T(8,128)(2,1)S(1)} %get-tuple-element.83), channel_id=1, source_target_pairs={{0,10},{1,11},{2,8},{3,9},{4,14},{5,15},{6,12},{7,13},{8,2},{9,3},... | collective-permute-start | bytes 129032 | tf_op jit(solution)/shard_map/ppermute | solution.py:622
  48.4 0.0 collective-permute-done.6.outer
  48.4 0.8 %grad_windows.1.windows = bf16[2112,768]{1,0:T(8,128)(2,1)S(1)} custom-call(s32[1]{0:T(128)} %bitcast.me, bf16[2048,128]{1,0:T(8,128)(2,1)S(1)} %get-tuple-element.77.own, bf16[2816,128]{1,0:T(8,128)(2,1)S(1)} %collective-permute-done.4.arrived.message, bf16[1024,128]{1,0:T(8,128)(2,1)S(1)} %collective-permute-done.6.outer), custom_call_target="tpu_custom_call" | custom-call | flops 226492416 | bytes 4751364 | tf_op jit(solution)/shard_map/grad_windows/pallas_call | solution.py:27
  49.2 2.9 %grad_volume.1 = f32[2,2048,64]{2,1,0:T(8,128)} custom-call(bf16[2112,768]{1,0:T(8,128)(2,1)S(1)} %grad_windows.1.windows, bf16[384,768]{1,0:T(8,128)(2,1)S(1)} %back_taps.1.taps), custom_call_target="tpu_custom_call" | custom-call | flops 905969664 | bytes 4882432 | tf_op jit(solution)/shard_map/grad_volume/pallas_call | solution.py:27
  52.2 0.8 %collective-permute-done.9.refs_2_ = bf16[24,896]{1,0:T(8,128)(2,1)S(1)} collective-permute-done((bf16[24,896]{1,0:T(8,128)(2,1)S(1)}, bf16[24,896]{1,0:T(8,128)(2,1)S(1)}, u32[]{:S(2)}, u32[]{:S(2)}) %collective-permute-start.9) | collective-permute-done | bytes 43040 | tf_op jit(solution)/shard_map/ppermute | solution.py:622
  53.0 0.7 %finish.1 = (f32[27,4,64]{2,1,0:T(4,128)}, f32[27,8,64]{2,1,0:T(8,128)}) custom-call(f32[24,896]{1,0:T(8,128)S(1)} %get-tuple-element.80.mine, bf16[24,896]{1,0:T(8,128)(2,1)S(1)} %collective-permute-done.7.refs_0_, bf16[24,896]{1,0:T(8,128)(2,1)S(1)} %collective-permute-done.8.refs_1_, bf16[24,896]{1,0:T(8,128)(2,1)S(1)} %collective-permute-done.9.refs_2_), custom_call_target="tpu_custom_call" | custom-call | bytes 297984 | tf_op jit(solution)/shard_map/finish/pallas_call | solution.py:27
  (6 shorter events, 0.1 us)
Async XLA Ops:
  2.0 6.0 %collective-permute-start = (bf16[2048,128]{1,0:T(8,128)(2,1)S(1)}, bf16[2048,128]{1,0:T(8,128)(2,1)S(1)}, u32[]{:S(2)}, u32[]{:S(2)}) collective-permute-start(bf16[2048,128]{1,0:T(8,128)(2,1)S(1)} %pack_volume.1.own), channel_id=1, source_target_pairs={{0,1},{1,0},{2,3},{3,2},{4,5},{5,4},{6,7},{7,6},{8,9},{9,8},{10,11... | collective-permute-start | bytes 1572872 | tf_op jit(solution)/shard_map/ppermute | solution.py:528
  2.6 14.0 %collective-permute-start.1 = (bf16[2048,128]{1,0:T(8,128)(2,1)S(1)}, bf16[2048,128]{1,0:T(8,128)(2,1)S(1)}, u32[]{:S(2)}, u32[]{:S(2)}) collective-permute-start(bf16[2048,128]{1,0:T(8,128)(2,1)S(1)} %pack_volume.1.own), channel_id=1, source_target_pairs={{1,2},{3,4},{5,6},{7,8},{9,10},{11,12},{13,14},{2,1},{4,3},{6,5},{... | collective-permute-start | bytes 1572872 | tf_op jit(solution)/shard_map/ppermute | solution.py:527
  3.2 4.6 %copy-start.1 = (bf16[3,3,3,64,64]{4,3,2,1,0:T(8,128)(2,1)S(1)}, bf16[3,3,3,64,64]{4,3,2,1,0:T(8,128)(2,1)}, u32[]{:S(2)}) copy-start(bf16[3,3,3,64,64]{4,3,2,1,0:T(8,128)(2,1)} %param.5) | copy-start | bytes 663556
  11.8 12.7 %collective-permute-start.2 = (bf16[1024,128]{1,0:T(8,128)(2,1)S(1)}, bf16[1024,128]{1,0:T(8,128)(2,1)S(1)}, u32[]{:S(2)}, u32[]{:S(2)}) collective-permute-start(bf16[1024,128]{1,0:T(8,128)(2,1)S(1)} %get-tuple-element.56), channel_id=1, source_target_pairs={{0,1},{1,0},{2,3},{3,2},{4,5},{5,4},{6,7},{7,6},{8,9},{9,8},{10,11... | collective-permute-start | bytes 786440 | tf_op jit(solution)/shard_map/ppermute | solution.py:555
  15.7 8.8 %collective-permute-start.3 = (bf16[1024,128]{1,0:T(8,128)(2,1)S(1)}, bf16[1024,128]{1,0:T(8,128)(2,1)S(1)}, u32[]{:S(2)}, u32[]{:S(2)}) collective-permute-start(bf16[1024,128]{1,0:T(8,128)(2,1)S(1)} %get-tuple-element.57), channel_id=1, source_target_pairs={{1,2},{3,4},{5,6},{7,8},{9,10},{11,12},{13,14},{2,1},{4,3},{6,5},{... | collective-permute-start | bytes 786440 | tf_op jit(solution)/shard_map/ppermute | solution.py:554
  16.6 3.5 %copy-start = (bf16[3,3,3,64,128]{4,3,2,1,0:T(8,128)(2,1)S(1)}, bf16[3,3,3,64,128]{4,3,2,1,0:T(8,128)(2,1)}, u32[]{:S(2)}) copy-start(bf16[3,3,3,64,128]{4,3,2,1,0:T(8,128)(2,1)} %param.6) | copy-start | bytes 1327108
  26.7 4.8 %collective-permute-start.4 = (bf16[2816,128]{1,0:T(8,128)(2,1)S(1)}, bf16[2816,128]{1,0:T(8,128)(2,1)S(1)}, u32[]{:S(2)}, u32[]{:S(2)}) collective-permute-start(bf16[2816,128]{1,0:T(8,128)(2,1)S(1)} %get-tuple-element.65), channel_id=1, source_target_pairs={{0,1},{1,0},{2,3},{3,2},{4,5},{5,4},{6,7},{7,6},{8,9},{9,8},{10,11... | collective-permute-start | bytes 2162696 | tf_op jit(solution)/shard_map/ppermute | solution.py:590
  29.6 18.8 %collective-permute-start.6 = (bf16[1024,128]{1,0:T(8,128)(2,1)S(1)}, bf16[1024,128]{1,0:T(8,128)(2,1)S(1)}, u32[]{:S(2)}, u32[]{:S(2)}) collective-permute-start(bf16[1024,128]{1,0:T(8,128)(2,1)S(1)} %get-tuple-element.78), channel_id=1, source_target_pairs={{1,2},{3,4},{5,6},{7,8},{9,10},{11,12},{13,14},{2,1},{4,3},{6,5},{... | collective-permute-start | bytes 786440 | tf_op jit(solution)/shard_map/ppermute | solution.py:604
  31.5 12.4 %collective-permute-start.5 = (bf16[4,32,896]{2,1,0:T(8,128)(2,1)S(1)}, bf16[4,32,896]{2,1,0:T(8,128)(2,1)S(1)}, u32[]{:S(2)}, u32[]{:S(2)}) collective-permute-start(bf16[4,32,896]{2,1,0:T(8,128)(2,1)S(1)} %get-tuple-element.68), channel_id=1, source_target_pairs={{0,4},{1,5},{2,6},{3,7},{4,0},{5,1},{6,2},{7,3},{8,12},{9,13},{10,... | collective-permute-start | bytes 688136 | tf_op jit(solution)/shard_map/ppermute | solution.py:603
  43.9 8.2 %collective-permute-start.7 = (bf16[24,896]{1,0:T(8,128)(2,1)S(1)}, bf16[24,896]{1,0:T(8,128)(2,1)S(1)}, u32[]{:S(2)}, u32[]{:S(2)}) collective-permute-start(bf16[24,896]{1,0:T(8,128)(2,1)S(1)} %get-tuple-element.81), channel_id=1, source_target_pairs={{0,2},{1,3},{2,0},{3,1},{4,6},{5,7},{6,4},{7,5},{8,10},{9,11},{10,... | collective-permute-start | bytes 129032 | tf_op jit(solution)/shard_map/ppermute | solution.py:622
  44.0 8.2 %collective-permute-start.8 = (bf16[24,896]{1,0:T(8,128)(2,1)S(1)}, bf16[24,896]{1,0:T(8,128)(2,1)S(1)}, u32[]{:S(2)}, u32[]{:S(2)}) collective-permute-start(bf16[24,896]{1,0:T(8,128)(2,1)S(1)} %get-tuple-element.82), channel_id=1, source_target_pairs={{0,8},{1,9},{2,10},{3,11},{4,12},{5,13},{6,14},{7,15},{8,0},{9,1},... | collective-permute-start | bytes 129032 | tf_op jit(solution)/shard_map/ppermute | solution.py:622
  46.7 6.3 %collective-permute-start.9 = (bf16[24,896]{1,0:T(8,128)(2,1)S(1)}, bf16[24,896]{1,0:T(8,128)(2,1)S(1)}, u32[]{:S(2)}, u32[]{:S(2)}) collective-permute-start(bf16[24,896]{1,0:T(8,128)(2,1)S(1)} %get-tuple-element.83), channel_id=1, source_target_pairs={{0,10},{1,11},{2,8},{3,9},{4,14},{5,15},{6,12},{7,13},{8,2},{9,3},... | collective-permute-start | bytes 129032 | tf_op jit(solution)/shard_map/ppermute | solution.py:622

commit v13 on v11

--- a/solution.py
+++ b/solution.py
@@ -9,7 +9,7 @@
 from jax.sharding import PartitionSpec as P
 
 F32, BF16 = jnp.float32, jnp.bfloat16
-STEP, BLOCK = 256, 1024
+STEP, BLOCK = 256, 512
 VMEM_LIMIT = 16 * 2**20
 NN = (((1,), (0,)), ((), ()))
 NT = (((1,), (1,)), ((), ()))
@@ -22,7 +22,7 @@
     return tap if 0 <= tap <= 2 else None
 
 
-def call(body, outs, ins, scratch=(), flops=0, name=None, smem=(), apart=(), far=False):
+def call(body, outs, ins, scratch=(), flops=0, name=None, smem=(), apart=(), far=(), alias=None):
     moved = sum(math.prod(s.shape) * s.dtype.itemsize for s in (*outs, *ins))
     return pl.pallas_call(
         body,
@@ -33,7 +33,10 @@
             )
             for i in range(len(ins))
         ],
-        out_specs=[pl.BlockSpec(memory_space=pl.ANY if far else pltpu.VMEM)] * len(outs),
+        out_specs=[
+            pl.BlockSpec(memory_space=pl.ANY if i in far else pltpu.VMEM) for i in range(len(outs))
+        ],
+        input_output_aliases=alias or {},
         scratch_shapes=list(scratch),
         compiler_params=pltpu.CompilerParams(vmem_limit_bytes=VMEM_LIMIT),
         cost_estimate=pl.CostEstimate(flops=flops, bytes_accessed=moved, transcendentals=0),
@@ -215,7 +218,7 @@
                 parts = [zero if d is None else weight[(2 - d) * 9 + 8 - tap] for d in depths]
                 at = row * 128 + plane * 64
                 for pair in range(2):
-                    first = column * 256 + pair * 128
+                    first = pair * 384 + column * 128
                     back_taps[at : at + 64, first : first + 128] = jnp.concatenate(
                         parts[2 * pair : 2 * pair + 2], axis=1
                     )
@@ -407,7 +410,26 @@
                 out[depth * 9 + tap] = block[:, lane : lane + 64]
 
 
-def output_body(columns, act_windows, weight, far, taps, output, sems):
+def output_rows(columns, blocks, act_windows, taps, far, output, sems):
+    copies = []
+    for at, block in enumerate(blocks):
+        start = block * BLOCK
+        value = window_dot(act_windows, taps, start, columns, NN)
+        here = slice(at * BLOCK, at * BLOCK + BLOCK)
+        output[0, here, :] = value[:, :128]
+        output[1, here, :] = value[:, 128:]
+        copies.append(
+            pltpu.make_async_copy(
+                output.at[:, here, :], far.at[:, start : start + BLOCK, :], sems.at[at]
+            )
+        )
+        copies[-1].start()
+    return copies
+
+
+def output_first_body(
+    columns, blocks, act_windows, weight, grad, far, taps, own_windows, output, sems
+):
     for row in range(3):
         for column in range(3):
             for at, source in enumerate(PLANES):
@@ -419,19 +441,27 @@
                         if depth is None
                         else weight[depth * 9 + row * 3 + column]
                     )
-    copies = pieces_of(output, far, sems, output.shape[1] // BLOCK)
-    for at, copy in enumerate(copies):
-        start = at * BLOCK
-        value = window_dot(act_windows, taps, start, columns, NN)
-        output[0, start : start + BLOCK, :] = value[:, :128]
-        output[1, start : start + BLOCK, :] = value[:, 128:]
-        copy.start()
+    copies = output_rows(columns, blocks, act_windows, taps, far, output, sems)
+
+    def fill(i, carry):
+        start = pl.multiple_of(i * STEP, STEP)
+        chunk = grad[pl.ds(start, STEP), :].astype(F32)
+        fill_windows(own_windows, start, 0, chunk, columns, 128)
+        return carry
+
+    clear_edges(own_windows, columns)
+    lax.fori_loop(0, grad.shape[0] // STEP, fill, 0)
     for copy in copies:
         copy.wait()
 
 
-def grad_windows_body(columns, me, own, message, outer, windows):
-    half = own.shape[0] // 2
+def output_rest_body(columns, blocks, act_windows, taps, begun, far, output, sems):
+    for copy in output_rows(columns, blocks, act_windows, taps, far, output, sems):
+        copy.wait()
+
+
+def grad_windows_body(columns, me, message, outer, windows):
+    half = outer.shape[0]
     odd = me[0] % 2 == 1
     before = message.shape[0] - half
 
@@ -440,19 +470,19 @@
         near = message[pl.ds(before + start, STEP), :].astype(F32)
         below, above = by_side(odd, near, outer[pl.ds(start, STEP), :].astype(F32))
         for first, side in zip((start, start + half), unpacked(above, below)):
-            fill_windows(windows, first, 0, own[pl.ds(first, STEP), :].astype(F32), columns, 256)
-            fill_windows(windows, first, 128, side, columns, 256)
+            fill_windows(windows, first, 0, side, columns, 128)
         return carry
 
     clear_edges(windows, columns)
     lax.fori_loop(0, half // STEP, fill, 0)
 
 
-def grad_volume_body(columns, windows, taps, far, output, sems):
+def grad_volume_body(columns, own_windows, side_windows, taps, far, output, sems):
     copies = pieces_of(output, far, sems, output.shape[1] // BLOCK)
     for at, copy in enumerate(copies):
         start = at * BLOCK
-        rows = windows[start : start + BLOCK + 2 * columns, :]
+        rows = slice(start, start + BLOCK + 2 * columns)
+        rows = jnp.concatenate([own_windows[rows, :], side_windows[rows, :]], axis=1)
         terms = lax.dot_general(rows, taps[...], NT, preferred_element_type=F32)
         value = terms[:BLOCK, :128]
         value = value + terms[columns : columns + BLOCK, 128:256]
@@ -556,6 +586,17 @@
         one_flops, "grad_one_terms", (0,),
     )
     message = lax.ppermute(message, "space", within)
+    blocks = range(cells // BLOCK)
+    output, out_taps, back_windows = call(
+        functools.partial(output_first_body, columns, blocks[:1]),
+        (shape((planes, cells, wide), F32), shape((9 * 256, 256), BF16), third),
+        (act_windows, weight_two, grad_hidden),
+        (pltpu.VMEM((planes, BLOCK, wide), F32), dma((1,))),
+        two_flops, "output_first", (), (), (0,),
+    )
+    message, output, out_taps, back_windows = lax.optimization_barrier(
+        (message, output, out_taps, back_windows)
+    )
     def halve(bits, bit, split_in, split_out, kept, arrived):
         left = 2 ** (len(bits) - 1)
         sent, kept = call(
@@ -571,14 +612,11 @@
     arrived = lax.ppermute(sent, "space", [(i, i ^ 4) for i in range(count)])
     grad_outer = lax.ppermute(outer, "space", across)
     output, = call(
-        functools.partial(output_body, columns),
+        functools.partial(output_rest_body, columns, blocks[1:]),
         (shape((planes, cells, wide), F32),),
-        (act_windows, weight_two),
-        (
-            pltpu.VMEM((3 * 768, 256), BF16), pltpu.VMEM((planes, cells, wide), F32),
-            dma((cells // BLOCK,)),
-        ),
-        two_flops, "output", (), (), True,
+        (act_windows, out_taps, output),
+        (pltpu.VMEM((planes, cells - BLOCK, wide), F32), dma((len(blocks) - 1,))),
+        two_flops, "output_rest", (), (2,), (0,), {2: 0},
     )
     others = 2 ** len(bits) - 1
     mine, *sent = call(
@@ -586,22 +624,21 @@
         (shape((chunk, lanes), F32), *[shape((chunk, lanes), BF16)] * others),
         (me, kept, arrived), flops=one_flops, name="spread", smem=(0,),
     )
-    sent, output, grad_hidden = lax.optimization_barrier((sent, output, grad_hidden))
+    sent, output, back_windows = lax.optimization_barrier((sent, output, back_windows))
     arrived = []
     for at, part in enumerate(sent):
         away = sum(((at + 1) >> i & 1) << bit for i, bit in enumerate(bits[::-1]))
         arrived.append(lax.ppermute(part, "space", [(i, i ^ away) for i in range(count)]))
     grad_windows, = call(
-        functools.partial(grad_windows_body, columns), (shape(slab, BF16),),
-        (me, grad_hidden, message, grad_outer),
+        functools.partial(grad_windows_body, columns), (third,), (me, message, grad_outer),
         (), one_flops // 4, "grad_windows", (0,),
     )
     grad_volume, = call(
         functools.partial(grad_volume_body, columns),
         (shape((planes, cells, channels), F32),),
-        (grad_windows, back_taps),
+        (back_windows, grad_windows, back_taps),
         (pltpu.VMEM((planes, cells, channels), F32), dma((cells // BLOCK,))),
-        one_flops, "grad_volume", (), (), True,
+        one_flops, "grad_volume", (), (), (0,),
     )
     grad_one, grad_two = call(
         functools.partial(finish_body, scale, (mid // count, wide // count)),

time: 50.6 us -> 49.9 us (0.986)
  waiting for transfers between devices: 5.43 us -> 4.32 us
    ppermute x1, waiting for transfers between devices: 1.82 us -> 0.13 us  [shards(): message = lax.ppermute(message, 'space', within)]
    ppermute x1, waiting for transfers between devices: 1.26 us -> 2.27 us  [shards(): arrived = lax.ppermute(sent, 'space', [(i, i ^ 4) for i in range(count)])]
    pallas_call x13 -> x14, Pallas kernels: 26.7 us -> 27.1 us  [call(): pl.pallas_call(body, out_shape=list(outs), in_specs=[pl.BlockSpec(memory_...]
  transfers between devices with their start and end apart: 10 -> 10, of which waited for: 3 -> 3; matrix products, arithmetic and copies ran while one was open for 0% -> 0% of each run, Pallas kernels for 43% -> 45%
where the time goes in v13:
time: 49.9 us; the launch traced here: 49.7 us
  Pallas kernels  27.1 us (54%)
  starting transfers between devices  17.4 us (35%)
  waiting for transfers between devices  4.32 us (9%)
  between operations  0.82 us (2%)
    pallas_call x14, Pallas kernels, call(): pl.pallas_call(body, out_shape=list(outs), in_specs=[pl.BlockSpec(memory_...  27.1 us
    ppermute x3, starting transfers between devices, shards(): lax.ppermute(part, 'space', [(i, i ^ away) for i in range(count)])  4.45 us
    ppermute x1, starting transfers between devices, shards(): terms_inner = lax.ppermute(inner, 'space', within)  3.93 us
    ppermute x1, starting transfers between devices, shards(): message = lax.ppermute(message, 'space', within)  3.48 us
    ppermute x1, starting transfers between devices, shards(): arrived = lax.ppermute(sent, 'space', [(i, i ^ 4) for i in range(count)])  2.87 us
    ppermute x1, waiting for transfers between devices, shards(): arrived = lax.ppermute(sent, 'space', [(i, i ^ 4) for i in range(count)])  2.27 us
    ppermute x3, waiting for transfers between devices, shards(): lax.ppermute(part, 'space', [(i, i ^ away) for i in range(count)])  1.9 us
  transfers between devices with their start and end apart: 10, of which 3 were waited for; matrix products, arithmetic and copies ran while one was open for 0% of the time, Pallas kernels for 45%

profile of v13, /device:TPU:0, one launch (start us, length us, event | category | flops | bytes accessed | tf_op | source)
XLA Modules:
  0.0 49.7 jit_solution(15130225506083904677)
XLA Ops:
  0.6 1.4 %pack_volume.1.own = bf16[2048,128]{1,0:T(8,128)(2,1)S(1)} custom-call(bf16[2,2048,64]{2,1,0:T(8,128)(2,1)} %bitcast.19), custom_call_target="tpu_custom_call" | custom-call | bytes 1048576 | tf_op jit(solution)/shard_map/pack_volume/pallas_call | solution.py:27
  2.0 0.5 %collective-permute-start = (bf16[2048,128]{1,0:T(8,128)(2,1)S(1)}, bf16[2048,128]{1,0:T(8,128)(2,1)S(1)}, u32[]{:S(2)}, u32[]{:S(2)}) collective-permute-start(bf16[2048,128]{1,0:T(8,128)(2,1)S(1)} %pack_volume.1.own), channel_id=1, source_target_pairs={{0,1},{1,0},{2,3},{3,2},{4,5},{5,4},{6,7},{7,6},{8,9},{9,8},{10,11... | collective-permute-start | bytes 1572872 | tf_op jit(solution)/shard_map/ppermute | solution.py:534
  2.6 0.7 %collective-permute-start.1 = (bf16[2048,128]{1,0:T(8,128)(2,1)S(1)}, bf16[2048,128]{1,0:T(8,128)(2,1)S(1)}, u32[]{:S(2)}, u32[]{:S(2)}) collective-permute-start(bf16[2048,128]{1,0:T(8,128)(2,1)S(1)} %pack_volume.1.own), channel_id=1, source_target_pairs={{1,2},{3,4},{5,6},{7,8},{9,10},{11,12},{13,14},{2,1},{4,3},{6,5},{... | collective-permute-start | bytes 1572872 | tf_op jit(solution)/shard_map/ppermute | solution.py:533
  3.2 0.0 copy-start
  3.3 4.6 %grad_act_terms.1 = (f32[2048,128]{1,0:T(8,128)S(1)}, bf16[1024,128]{1,0:T(8,128)(2,1)S(1)}, bf16[1024,128]{1,0:T(8,128)(2,1)S(1)}, bf16[256,2048]{1,0:T(8,128)(2,1)S(1)}) custom-call(s32[1]{0:T(128)} %bitcast.me, bf16[2,2048,128]{2,1,0:T(8,128)(2,1)} %bitcast.20, bf16[27,64,128]{2,1,0:T(8,128)(2,1)} %bitcast.15), custom_call_target="tpu_custom_call" | custom-call | flops 1811939328 | bytes 4112388 | tf_op jit(solution)/shard_map/grad_act_terms/pallas_call | solution.py:27
  7.9 0.2 back_taps.1.taps
  8.1 3.7 %prepare.1 = (bf16[2112,384]{1,0:T(8,128)(2,1)S(1)}, bf16[2112,384]{1,0:T(8,128)(2,1)S(1)}, f32[2048,256]{1,0:T(8,128)S(1)}, bf16[1152,256]{1,0:T(8,128)(2,1)S(1)}) custom-call(s32[1]{0:T(128)} %bitcast.me, bf16[2048,128]{1,0:T(8,128)(2,1)S(1)} %pack_volume.1.own, bf16[2048,128]{1,0:T(8,128)(2,1)S(1)} %collective-permute-done.inner, bf16[27,64,64]{2,1,0:T(8,128)(2,1)} %bitcast.13), custom_call_target="tpu_custom_call" | custom-call | flops 905969664 | bytes 7200772 | tf_op jit(solution)/shard_map/prepare/pallas_call | solution.py:27
  11.8 3.9 %collective-permute-start.2 = (bf16[1024,128]{1,0:T(8,128)(2,1)S(1)}, bf16[1024,128]{1,0:T(8,128)(2,1)S(1)}, u32[]{:S(2)}, u32[]{:S(2)}) collective-permute-start(bf16[1024,128]{1,0:T(8,128)(2,1)S(1)} %get-tuple-element.59), channel_id=1, source_target_pairs={{0,1},{1,0},{2,3},{3,2},{4,5},{5,4},{6,7},{7,6},{8,9},{9,8},{10,11... | collective-permute-start | bytes 786440 | tf_op jit(solution)/shard_map/ppermute | solution.py:561
  15.7 0.7 %collective-permute-start.3 = (bf16[1024,128]{1,0:T(8,128)(2,1)S(1)}, bf16[1024,128]{1,0:T(8,128)(2,1)S(1)}, u32[]{:S(2)}, u32[]{:S(2)}) collective-permute-start(bf16[1024,128]{1,0:T(8,128)(2,1)S(1)} %get-tuple-element.60), channel_id=1, source_target_pairs={{1,2},{3,4},{5,6},{7,8},{9,10},{11,12},{13,14},{2,1},{4,3},{6,5},{... | collective-permute-start | bytes 786440 | tf_op jit(solution)/shard_map/ppermute | solution.py:560
  16.4 0.0 collective-permute-done.1.outer
  16.4 2.8 %hidden.1 = (bf16[2112,384]{1,0:T(8,128)(2,1)S(1)}, bf16[2112,768]{1,0:T(8,128)(2,1)S(1)}, f32[2048,128]{1,0:T(8,128)S(1)}) custom-call(s32[1]{0:T(128)} %bitcast.me, bf16[2048,128]{1,0:T(8,128)(2,1)S(1)} %collective-permute-done.1.outer, f32[2048,256]{1,0:T(8,128)S(1)} %get-tuple-element.55.part, bf16[1152,256]{1,0:T(8,128)(2,1)S(1)} %get-tuple-element.56.outer_taps), custom_call_target="tpu_custom_call" | custom-call | flops 1811939328 | bytes 9125892 | tf_op jit(solution)/shard_map/hidden/pallas_call | solution.py:27
  19.2 2.7 %grad_two_terms.1.other = f32[128,1792]{1,0:T(8,128)S(1)} custom-call(bf16[2112,768]{1,0:T(8,128)(2,1)S(1)} %get-tuple-element.78.act_windows, bf16[256,2048]{1,0:T(8,128)(2,1)S(1)} %get-tuple-element.63.turned), custom_call_target="tpu_custom_call" | custom-call | flops 1811939328 | bytes 5210112 | tf_op jit(solution)/shard_map/grad_two_terms/pallas_call | solution.py:27
  21.9 0.0 collective-permute-done.2.inner
  21.9 0.0 copy-start.1
  21.9 2.6 %grad_one_terms.1 = (bf16[2048,128]{1,0:T(8,128)(2,1)S(1)}, bf16[1024,128]{1,0:T(8,128)(2,1)S(1)}, bf16[2816,128]{1,0:T(8,128)(2,1)S(1)}, f32[8,24,896]{2,1,0:T(8,128)S(1)}) custom-call(s32[1]{0:T(128)} %bitcast.me, bf16[2112,384]{1,0:T(8,128)(2,1)S(1)} %get-tuple-element.50.own_windows, bf16[2112,384]{1,0:T(8,128)(2,1)S(1)} %get-tuple-element.51.inner_windows, ...), custom_call_target="tpu_custom_call" | custom-call | flops 905969664 | bytes 10600452 | tf_op jit(solution)/shard_map/grad_one_terms/pallas_call | solution.py:27
  24.5 3.5 %collective-permute-start.4 = (bf16[2816,128]{1,0:T(8,128)(2,1)S(1)}, bf16[2816,128]{1,0:T(8,128)(2,1)S(1)}, u32[]{:S(2)}, u32[]{:S(2)}) collective-permute-start(bf16[2816,128]{1,0:T(8,128)(2,1)S(1)} %get-tuple-element.65), channel_id=1, source_target_pairs={{0,1},{1,0},{2,3},{3,2},{4,5},{5,4},{6,7},{7,6},{8,9},{9,8},{10,11... | collective-permute-start | bytes 2162696 | tf_op jit(solution)/shard_map/ppermute | solution.py:588
  28.0 1.7 %output_first.1 = (f32[2,2048,128]{2,1,0:T(8,128)}, bf16[2304,256]{1,0:T(8,128)(2,1)S(1)}, bf16[2112,384]{1,0:T(8,128)(2,1)S(1)}) custom-call(bf16[2112,768]{1,0:T(8,128)(2,1)S(1)} %get-tuple-element.78.act_windows, bf16[27,64,128]{2,1,0:T(8,128)(2,1)S(1)} %bitcast.16, bf16[2048,128]{1,0:T(8,128)(2,1)S(1)} %get-tuple-element.66.grad), custom_call_target="tpu_custom_call" | custom-call | flops 1811939328 | bytes 9109504 | tf_op jit(solution)/shard_map/output_first/pallas_call | solution.py:27
  29.7 0.1 collective-permute-done.4.arrived.message
  29.8 0.1 halve.1
  29.9 2.9 %collective-permute-start.5 = (bf16[4,32,896]{2,1,0:T(8,128)(2,1)S(1)}, bf16[4,32,896]{2,1,0:T(8,128)(2,1)S(1)}, u32[]{:S(2)}, u32[]{:S(2)}) collective-permute-start(bf16[4,32,896]{2,1,0:T(8,128)(2,1)S(1)} %get-tuple-element.74), channel_id=1, source_target_pairs={{0,4},{1,5},{2,6},{3,7},{4,0},{5,1},{6,2},{7,3},{8,12},{9,13},{10,... | collective-permute-start | bytes 688136 | tf_op jit(solution)/shard_map/ppermute | solution.py:612
  32.8 0.8 %collective-permute-start.6 = (bf16[1024,128]{1,0:T(8,128)(2,1)S(1)}, bf16[1024,128]{1,0:T(8,128)(2,1)S(1)}, u32[]{:S(2)}, u32[]{:S(2)}) collective-permute-start(bf16[1024,128]{1,0:T(8,128)(2,1)S(1)} %get-tuple-element.84), channel_id=1, source_target_pairs={{1,2},{3,4},{5,6},{7,8},{9,10},{11,12},{13,14},{2,1},{4,3},{6,5},{... | collective-permute-start | bytes 786440 | tf_op jit(solution)/shard_map/ppermute | solution.py:613
  33.7 3.0 %output_rest.1 = f32[2,2048,128]{2,1,0:T(8,128)} custom-call(bf16[2112,768]{1,0:T(8,128)(2,1)S(1)} %get-tuple-element.78.act_windows, bf16[2304,256]{1,0:T(8,128)(2,1)S(1)} %get-tuple-element.79.taps, f32[2,2048,128]{2,1,0:T(8,128)} %get-tuple-element.80.begun), custom_call_target="tpu_custom_call", output_to_operand_aliasing={{}: (2, {})} | custom-call | flops 1811939328 | bytes 8617984 | tf_op jit(solution)/shard_map/output_rest/pallas_call | solution.py:27
  36.7 2.3 %collective-permute-done.5.arrived = bf16[4,32,896]{2,1,0:T(8,128)(2,1)S(1)} collective-permute-done((bf16[4,32,896]{2,1,0:T(8,128)(2,1)S(1)}, bf16[4,32,896]{2,1,0:T(8,128)(2,1)S(1)}, u32[]{:S(2)}, u32[]{:S(2)}) %collective-permute-start.5) | collective-permute-done | bytes 229408 | tf_op jit(solution)/shard_map/ppermute | solution.py:612
  39.0 1.5 %collective-permute-start.7 = (bf16[24,896]{1,0:T(8,128)(2,1)S(1)}, bf16[24,896]{1,0:T(8,128)(2,1)S(1)}, u32[]{:S(2)}, u32[]{:S(2)}) collective-permute-start(bf16[24,896]{1,0:T(8,128)(2,1)S(1)} %get-tuple-element.87), channel_id=1, source_target_pairs={{0,2},{1,3},{2,0},{3,1},{4,6},{5,7},{6,4},{7,5},{8,10},{9,11},{10,... | collective-permute-start | bytes 129032 | tf_op jit(solution)/shard_map/ppermute | solution.py:631
  40.5 2.6 %collective-permute-start.8 = (bf16[24,896]{1,0:T(8,128)(2,1)S(1)}, bf16[24,896]{1,0:T(8,128)(2,1)S(1)}, u32[]{:S(2)}, u32[]{:S(2)}) collective-permute-start(bf16[24,896]{1,0:T(8,128)(2,1)S(1)} %get-tuple-element.88), channel_id=1, source_target_pairs={{0,8},{1,9},{2,10},{3,11},{4,12},{5,13},{6,14},{7,15},{8,0},{9,1},... | collective-permute-start | bytes 129032 | tf_op jit(solution)/shard_map/ppermute | solution.py:631
  43.1 0.4 collective-permute-start.9
  43.4 0.0 collective-permute-done.6.outer
  43.4 0.6 %grad_windows.1.side_windows = bf16[2112,384]{1,0:T(8,128)(2,1)S(1)} custom-call(s32[1]{0:T(128)} %bitcast.me, bf16[2816,128]{1,0:T(8,128)(2,1)S(1)} %collective-permute-done.4.arrived.message, bf16[1024,128]{1,0:T(8,128)(2,1)S(1)} %collective-permute-done.6.outer), custom_call_target="tpu_custom_call" | custom-call | flops 226492416 | bytes 2605060 | tf_op jit(solution)/shard_map/grad_windows/pallas_call | solution.py:27
  44.1 2.9 %grad_volume.1 = f32[2,2048,64]{2,1,0:T(8,128)} custom-call(bf16[2112,384]{1,0:T(8,128)(2,1)S(1)} %get-tuple-element.83.own_windows, bf16[2112,384]{1,0:T(8,128)(2,1)S(1)} %grad_windows.1.side_windows, bf16[384,768]{1,0:T(8,128)(2,1)S(1)} %back_taps.1.taps), custom_call_target="tpu_custom_call" | custom-call | flops 905969664 | bytes 4882432 | tf_op jit(solution)/shard_map/grad_volume/pallas_call | solution.py:27
  47.0 0.0 collective-permute-done.8.refs_1_
  47.0 1.9 %collective-permute-done.9.refs_2_ = bf16[24,896]{1,0:T(8,128)(2,1)S(1)} collective-permute-done((bf16[24,896]{1,0:T(8,128)(2,1)S(1)}, bf16[24,896]{1,0:T(8,128)(2,1)S(1)}, u32[]{:S(2)}, u32[]{:S(2)}) %collective-permute-start.9) | collective-permute-done | bytes 43040 | tf_op jit(solution)/shard_map/ppermute | solution.py:631
  48.9 0.7 %finish.1 = (f32[27,4,64]{2,1,0:T(4,128)}, f32[27,8,64]{2,1,0:T(8,128)}) custom-call(f32[24,896]{1,0:T(8,128)S(1)} %get-tuple-element.86.mine, bf16[24,896]{1,0:T(8,128)(2,1)S(1)} %collective-permute-done.7.refs_0_, bf16[24,896]{1,0:T(8,128)(2,1)S(1)} %collective-permute-done.8.refs_1_, bf16[24,896]{1,0:T(8,128)(2,1)S(1)} %collective-permute-done.9.refs_2_), custom_call_target="tpu_custom_call" | custom-call | bytes 297984 | tf_op jit(solution)/shard_map/finish/pallas_call | solution.py:27
  (6 shorter events, 0.1 us)
Async XLA Ops:
  2.0 6.0 %collective-permute-start = (bf16[2048,128]{1,0:T(8,128)(2,1)S(1)}, bf16[2048,128]{1,0:T(8,128)(2,1)S(1)}, u32[]{:S(2)}, u32[]{:S(2)}) collective-permute-start(bf16[2048,128]{1,0:T(8,128)(2,1)S(1)} %pack_volume.1.own), channel_id=1, source_target_pairs={{0,1},{1,0},{2,3},{3,2},{4,5},{5,4},{6,7},{7,6},{8,9},{9,8},{10,11... | collective-permute-start | bytes 1572872 | tf_op jit(solution)/shard_map/ppermute | solution.py:534
  2.6 13.8 %collective-permute-start.1 = (bf16[2048,128]{1,0:T(8,128)(2,1)S(1)}, bf16[2048,128]{1,0:T(8,128)(2,1)S(1)}, u32[]{:S(2)}, u32[]{:S(2)}) collective-permute-start(bf16[2048,128]{1,0:T(8,128)(2,1)S(1)} %pack_volume.1.own), channel_id=1, source_target_pairs={{1,2},{3,4},{5,6},{7,8},{9,10},{11,12},{13,14},{2,1},{4,3},{6,5},{... | collective-permute-start | bytes 1572872 | tf_op jit(solution)/shard_map/ppermute | solution.py:533
  3.2 4.6 %copy-start = (bf16[3,3,3,64,64]{4,3,2,1,0:T(8,128)(2,1)S(1)}, bf16[3,3,3,64,64]{4,3,2,1,0:T(8,128)(2,1)}, u32[]{:S(2)}) copy-start(bf16[3,3,3,64,64]{4,3,2,1,0:T(8,128)(2,1)} %param.5) | copy-start | bytes 663556
  11.8 10.1 %collective-permute-start.2 = (bf16[1024,128]{1,0:T(8,128)(2,1)S(1)}, bf16[1024,128]{1,0:T(8,128)(2,1)S(1)}, u32[]{:S(2)}, u32[]{:S(2)}) collective-permute-start(bf16[1024,128]{1,0:T(8,128)(2,1)S(1)} %get-tuple-element.59), channel_id=1, source_target_pairs={{0,1},{1,0},{2,3},{3,2},{4,5},{5,4},{6,7},{7,6},{8,9},{9,8},{10,11... | collective-permute-start | bytes 786440 | tf_op jit(solution)/shard_map/ppermute | solution.py:561
  15.7 6.2 %collective-permute-start.3 = (bf16[1024,128]{1,0:T(8,128)(2,1)S(1)}, bf16[1024,128]{1,0:T(8,128)(2,1)S(1)}, u32[]{:S(2)}, u32[]{:S(2)}) collective-permute-start(bf16[1024,128]{1,0:T(8,128)(2,1)S(1)} %get-tuple-element.60), channel_id=1, source_target_pairs={{1,2},{3,4},{5,6},{7,8},{9,10},{11,12},{13,14},{2,1},{4,3},{6,5},{... | collective-permute-start | bytes 786440 | tf_op jit(solution)/shard_map/ppermute | solution.py:560
  21.9 6.1 %copy-start.1 = (bf16[3,3,3,64,128]{4,3,2,1,0:T(8,128)(2,1)S(1)}, bf16[3,3,3,64,128]{4,3,2,1,0:T(8,128)(2,1)}, u32[]{:S(2)}) copy-start(bf16[3,3,3,64,128]{4,3,2,1,0:T(8,128)(2,1)} %param.6) | copy-start | bytes 1327108
  24.5 5.3 %collective-permute-start.4 = (bf16[2816,128]{1,0:T(8,128)(2,1)S(1)}, bf16[2816,128]{1,0:T(8,128)(2,1)S(1)}, u32[]{:S(2)}, u32[]{:S(2)}) collective-permute-start(bf16[2816,128]{1,0:T(8,128)(2,1)S(1)} %get-tuple-element.65), channel_id=1, source_target_pairs={{0,1},{1,0},{2,3},{3,2},{4,5},{5,4},{6,7},{7,6},{8,9},{9,8},{10,11... | collective-permute-start | bytes 2162696 | tf_op jit(solution)/shard_map/ppermute | solution.py:588
  29.9 9.0 %collective-permute-start.5 = (bf16[4,32,896]{2,1,0:T(8,128)(2,1)S(1)}, bf16[4,32,896]{2,1,0:T(8,128)(2,1)S(1)}, u32[]{:S(2)}, u32[]{:S(2)}) collective-permute-start(bf16[4,32,896]{2,1,0:T(8,128)(2,1)S(1)} %get-tuple-element.74), channel_id=1, source_target_pairs={{0,4},{1,5},{2,6},{3,7},{4,0},{5,1},{6,2},{7,3},{8,12},{9,13},{10,... | collective-permute-start | bytes 688136 | tf_op jit(solution)/shard_map/ppermute | solution.py:612
  32.8 10.6 %collective-permute-start.6 = (bf16[1024,128]{1,0:T(8,128)(2,1)S(1)}, bf16[1024,128]{1,0:T(8,128)(2,1)S(1)}, u32[]{:S(2)}, u32[]{:S(2)}) collective-permute-start(bf16[1024,128]{1,0:T(8,128)(2,1)S(1)} %get-tuple-element.84), channel_id=1, source_target_pairs={{1,2},{3,4},{5,6},{7,8},{9,10},{11,12},{13,14},{2,1},{4,3},{6,5},{... | collective-permute-start | bytes 786440 | tf_op jit(solution)/shard_map/ppermute | solution.py:613
  39.0 8.0 %collective-permute-start.7 = (bf16[24,896]{1,0:T(8,128)(2,1)S(1)}, bf16[24,896]{1,0:T(8,128)(2,1)S(1)}, u32[]{:S(2)}, u32[]{:S(2)}) collective-permute-start(bf16[24,896]{1,0:T(8,128)(2,1)S(1)} %get-tuple-element.87), channel_id=1, source_target_pairs={{0,2},{1,3},{2,0},{3,1},{4,6},{5,7},{6,4},{7,5},{8,10},{9,11},{10,... | collective-permute-start | bytes 129032 | tf_op jit(solution)/shard_map/ppermute | solution.py:631
  40.5 6.5 %collective-permute-start.8 = (bf16[24,896]{1,0:T(8,128)(2,1)S(1)}, bf16[24,896]{1,0:T(8,128)(2,1)S(1)}, u32[]{:S(2)}, u32[]{:S(2)}) collective-permute-start(bf16[24,896]{1,0:T(8,128)(2,1)S(1)} %get-tuple-element.88), channel_id=1, source_target_pairs={{0,8},{1,9},{2,10},{3,11},{4,12},{5,13},{6,14},{7,15},{8,0},{9,1},... | collective-permute-start | bytes 129032 | tf_op jit(solution)/shard_map/ppermute | solution.py:631
  43.1 5.8 %collective-permute-start.9 = (bf16[24,896]{1,0:T(8,128)(2,1)S(1)}, bf16[24,896]{1,0:T(8,128)(2,1)S(1)}, u32[]{:S(2)}, u32[]{:S(2)}) collective-permute-start(bf16[24,896]{1,0:T(8,128)(2,1)S(1)} %get-tuple-element.89), channel_id=1, source_target_pairs={{0,10},{1,11},{2,8},{3,9},{4,14},{5,15},{6,12},{7,13},{8,2},{9,3},... | collective-permute-start | bytes 129032 | tf_op jit(solution)/shard_map/ppermute | solution.py:631

commit v14 on v13

--- a/solution.py
+++ b/solution.py
@@ -73,15 +73,20 @@
     windows[rows - columns : rows, :] = jnp.zeros((columns, lanes), BF16)
 
 
-def row_windows(windows, start, columns, lanes=slice(None)):
+def row_windows(windows, start, columns, size=BLOCK):
     return [
-        windows[start + tap * columns : start + tap * columns + BLOCK, lanes] for tap in range(3)
+        windows[start + tap * columns : start + tap * columns + size, :] for tap in range(3)
     ]
 
 
-def window_dot(windows, weights, start, columns, dims):
-    rows = jnp.concatenate(row_windows(windows, start, columns), axis=1)
+def window_dot(windows, weights, start, columns, dims, size=BLOCK):
+    rows = jnp.concatenate(row_windows(windows, start, columns, size), axis=1)
     return lax.dot_general(rows, weights[...], dims, preferred_element_type=F32)
+
+
+def row_blocks(first, last):
+    blocks = [(start, BLOCK) for start in range(first, last - BLOCK, BLOCK)]
+    return blocks + [(last - BLOCK, BLOCK // 2), (last - BLOCK // 2, BLOCK // 2)]
 
 
 def packed(low, high):
@@ -161,7 +166,10 @@
             own[first : first + BLOCK, :] = term[:, :128]
             sides.append(term[:, 128:])
         upper, lower = packed(*sides)
-        inner[start : start + BLOCK, :] = jnp.where(odd, lower, upper).astype(BF16)
+        near = jnp.where(odd, lower, upper)
+        head = near.astype(BF16)
+        inner[start : start + BLOCK, :] = head
+        inner[half + start : half + start + BLOCK, :] = (near - head.astype(F32)).astype(BF16)
         outer[start : start + BLOCK, :] = jnp.where(odd, upper, lower).astype(BF16)
     for plane in range(2):
         turn(cotangent.at[plane], turned, plane * 128)
@@ -225,7 +233,8 @@
 
 
 def hidden_body(
-    columns, count, me, outer, part, outer_taps, outer_windows, act_windows, slope
+    columns, count, me, outer, part, outer_taps, inner_windows, act_windows, slope, side_windows,
+    outer_windows,
 ):
     cells = outer.shape[0]
 
@@ -238,6 +247,13 @@
     clear_edges(outer_windows, columns)
     clear_edges(act_windows, columns)
     lax.fori_loop(0, cells // STEP, fill, 0)
+    from_inner = lax.broadcasted_iota(jnp.int32, (16, 128), 1) // 64 == me[0] % 2
+    from_inner = jnp.where(from_inner, 1.0, 0.0).astype(BF16)[:1]
+    for tap in range(3):
+        at = slice(tap * 128, tap * 128 + 128)
+        side_windows[:, at] = (
+            inner_windows[:, at] * from_inner + outer_windows[:, at] * (1 - from_inner)
+        )
     lanes = lax.broadcasted_iota(jnp.int32, (BLOCK, 128), 1)
     edges = [jnp.where(me[0] == end, 0.0, 1.0).astype(F32) for end in (count - 1, 0)]
     inside = jnp.where(lanes < 64, edges[0], edges[1])
@@ -305,15 +321,16 @@
 
 
 def grad_one_body(
-    columns, count, me, own_windows, inner_windows, outer_windows, act_terms, inner, outer, slope,
-    other, grad, to_outer, message, kept, turned, terms,
+    columns, count, me, own_windows, side_windows, act_terms, inner, outer, slope, other,
+    grad, to_outer, message, kept, turned, terms,
 ):
     cells = grad.shape[0]
     odd = me[0] % 2 == 1
     before = message.shape[0] - cells // 2
     for start in range(0, cells // 2, STEP):
         low, high = slice(start, start + STEP), slice(start + cells // 2, start + cells // 2 + STEP)
-        arrived = unpacked(*by_side(odd, inner[low, :].astype(F32), outer[low, :].astype(F32)))
+        near = inner[low, :].astype(F32) + inner[high, :].astype(F32)
+        arrived = unpacked(*by_side(odd, near, outer[low, :].astype(F32)))
         sides = []
         for rows, extra in zip((low, high), arrived):
             value = ((act_terms[rows, :] + extra) * slope[rows, :]).astype(BF16)
@@ -326,15 +343,10 @@
             odd, lower, upper
         ).astype(BF16)
         to_outer[low, :] = jnp.where(odd, upper, lower).astype(BF16)
-    from_inner = lax.broadcasted_iota(jnp.int32, (16, 128), 1) // 64 == me[0] % 2
-    from_inner = jnp.where(from_inner, 1.0, 0.0).astype(BF16)[:1]
-    from_outer = 1 - from_inner
-
     def slices(row, column):
         rows = slice(row * columns, row * columns + cells)
         lanes = slice(column * 128, column * 128 + 128)
-        sides = inner_windows[rows, lanes] * from_inner + outer_windows[rows, lanes] * from_outer
-        return jnp.concatenate([own_windows[rows, lanes], sides], axis=1)
+        return jnp.concatenate([own_windows[rows, lanes], side_windows[rows, lanes]], axis=1)
 
     kernel_terms(columns, 64, slices, turned, terms)
     half = terms.shape[1] // 2
@@ -412,15 +424,14 @@
 
 def output_rows(columns, blocks, act_windows, taps, far, output, sems):
     copies = []
-    for at, block in enumerate(blocks):
-        start = block * BLOCK
-        value = window_dot(act_windows, taps, start, columns, NN)
-        here = slice(at * BLOCK, at * BLOCK + BLOCK)
+    for at, (start, size) in enumerate(blocks):
+        value = window_dot(act_windows, taps, start, columns, NN, size)
+        here = slice(start - blocks[0][0], start - blocks[0][0] + size)
         output[0, here, :] = value[:, :128]
         output[1, here, :] = value[:, 128:]
         copies.append(
             pltpu.make_async_copy(
-                output.at[:, here, :], far.at[:, start : start + BLOCK, :], sems.at[at]
+                output.at[:, here, :], far.at[:, start : start + size, :], sems.at[at]
             )
         )
         copies[-1].start()
@@ -478,18 +489,21 @@
 
 
 def grad_volume_body(columns, own_windows, side_windows, taps, far, output, sems):
-    copies = pieces_of(output, far, sems, output.shape[1] // BLOCK)
-    for at, copy in enumerate(copies):
-        start = at * BLOCK
-        rows = slice(start, start + BLOCK + 2 * columns)
+    copies = []
+    for at, (start, size) in enumerate(row_blocks(0, output.shape[1])):
+        rows = slice(start, start + size + 2 * columns)
         rows = jnp.concatenate([own_windows[rows, :], side_windows[rows, :]], axis=1)
         terms = lax.dot_general(rows, taps[...], NT, preferred_element_type=F32)
-        value = terms[:BLOCK, :128]
-        value = value + terms[columns : columns + BLOCK, 128:256]
-        value = value + terms[2 * columns : 2 * columns + BLOCK, 256:]
-        output[0, start : start + BLOCK, :] = value[:, :64]
-        output[1, start : start + BLOCK, :] = value[:, 64:]
-        copy.start()
+        value = terms[:size, :128]
+        value = value + terms[columns : columns + size, 128:256]
+        value = value + terms[2 * columns : 2 * columns + size, 256:]
+        here = slice(start, start + size)
+        output[0, here, :] = value[:, :64]
+        output[1, here, :] = value[:, 64:]
+        copies.append(
+            pltpu.make_async_copy(output.at[:, here, :], far.at[:, here, :], sems.at[at])
+        )
+        copies[-1].start()
     for copy in copies:
         copy.wait()
 
@@ -535,7 +549,7 @@
     terms, inner, outer, turned = call(
         functools.partial(leave_body, columns),
         (
-            shape((cells, 128), F32), pack, pack, shape((256, cells), BF16),
+            shape((cells, 128), F32), flat, pack, shape((256, cells), BF16),
         ),
         (me, far_cotangent, far_two),
         (
@@ -559,11 +573,11 @@
     inner, outer, part, back_taps = lax.optimization_barrier((inner, outer, part, back_taps))
     terms_outer = lax.ppermute(outer, "space", across)
     terms_inner = lax.ppermute(inner, "space", within)
-    outer_windows, act_windows, slope = call(
+    act_windows, slope, side_windows = call(
         functools.partial(hidden_body, columns, count),
-        (third, shape(slab, BF16), shape((cells, 128), F32)),
-        (me, vol_outer, part, outer_taps),
-        (), 2 * one_flops, "hidden", (0,),
+        (shape(slab, BF16), shape((cells, 128), F32), third),
+        (me, vol_outer, part, outer_taps, inner_windows),
+        (pltpu.VMEM((slab[0], 384), BF16),), 2 * one_flops, "hidden", (0,),
     )
     terms_two, = call(
         functools.partial(grad_two_body, columns),
@@ -579,16 +593,15 @@
             shape((count // 2, chunk, lanes), F32),
         ),
         (
-            me, own_windows, inner_windows, outer_windows, terms, terms_inner, terms_outer, slope,
-            terms_two,
+            me, own_windows, side_windows, terms, terms_inner, terms_outer, slope, terms_two,
         ),
         (pltpu.VMEM((128, cells), BF16), pltpu.VMEM((mid, 2 * lanes), F32)),
         one_flops, "grad_one_terms", (0,),
     )
     message = lax.ppermute(message, "space", within)
-    blocks = range(cells // BLOCK)
+    rest = row_blocks(BLOCK, cells)
     output, out_taps, back_windows = call(
-        functools.partial(output_first_body, columns, blocks[:1]),
+        functools.partial(output_first_body, columns, [(0, BLOCK)]),
         (shape((planes, cells, wide), F32), shape((9 * 256, 256), BF16), third),
         (act_windows, weight_two, grad_hidden),
         (pltpu.VMEM((planes, BLOCK, wide), F32), dma((1,))),
@@ -607,20 +620,20 @@
         return [b for b in bits if b != bit], sent, kept
 
     bits = list(range(count.bit_length() - 2, 0, -1))
-    bits, sent, kept = halve(bits, 2, split, split, kept, message)
+    bits, sent, kept = halve(bits, 2, split, 0, kept, message)
     sent, act_windows, outer = lax.optimization_barrier((sent, act_windows, outer))
     arrived = lax.ppermute(sent, "space", [(i, i ^ 4) for i in range(count)])
     grad_outer = lax.ppermute(outer, "space", across)
     output, = call(
-        functools.partial(output_rest_body, columns, blocks[1:]),
+        functools.partial(output_rest_body, columns, rest),
         (shape((planes, cells, wide), F32),),
         (act_windows, out_taps, output),
-        (pltpu.VMEM((planes, cells - BLOCK, wide), F32), dma((len(blocks) - 1,))),
+        (pltpu.VMEM((planes, cells - BLOCK, wide), F32), dma((len(rest),))),
         two_flops, "output_rest", (), (2,), (0,), {2: 0},
     )
     others = 2 ** len(bits) - 1
     mine, *sent = call(
-        functools.partial(spread_body, split, bits),
+        functools.partial(spread_body, 0, bits),
         (shape((chunk, lanes), F32), *[shape((chunk, lanes), BF16)] * others),
         (me, kept, arrived), flops=one_flops, name="spread", smem=(0,),
     )
@@ -637,9 +650,10 @@
         functools.partial(grad_volume_body, columns),
         (shape((planes, cells, channels), F32),),
         (back_windows, grad_windows, back_taps),
-        (pltpu.VMEM((planes, cells, channels), F32), dma((cells // BLOCK,))),
+        (pltpu.VMEM((planes, cells, channels), F32), dma((cells // BLOCK + 1,))),
         one_flops, "grad_volume", (), (), (0,),
     )
+    mine, grad_volume = lax.optimization_barrier((mine, grad_volume))
     grad_one, grad_two = call(
         functools.partial(finish_body, scale, (mid // count, wide // count)),
         (shape((27, mid // count, channels), F32), shape((27, wide // count, mid), F32)),

time: 49.9 us -> 53.3 us (1.068)
  waiting for transfers between devices: 4.32 us -> 6.16 us
  starting transfers between devices: 17.4 us -> 18.9 us
    ppermute x1, waiting for transfers between devices: 2.27 us -> 5.08 us  [shards(): arrived = lax.ppermute(sent, 'space', [(i, i ^ 4) for i in range(count)])]
    ppermute x1, starting transfers between devices: 2.87 us -> 4.9 us  [shards(): arrived = lax.ppermute(sent, 'space', [(i, i ^ 4) for i in range(count)])]
    ppermute x3, waiting for transfers between devices: 1.9 us -> 0.93 us  [shards(): lax.ppermute(part, 'space', [(i, i ^ away) for i in range(count)])]
    ppermute x1, starting transfers between devices: 3.48 us -> 2.92 us  [shards(): message = lax.ppermute(message, 'space', within)]
  transfers between devices with their start and end apart: 10 -> 10, of which waited for: 3 -> 3; matrix products, arithmetic and copies ran while one was open for 0% -> 0% of each run, Pallas kernels for 45% -> 43%
where the time goes in v14:
time: 53.3 us; the launch traced here: 53.1 us
  Pallas kernels  27.2 us (51%)
  starting transfers between devices  18.9 us (35%)
  waiting for transfers between devices  6.16 us (12%)
  between operations  0.83 us (2%)
    pallas_call x14, Pallas kernels, call(): pl.pallas_call(body, out_shape=list(outs), in_specs=[pl.BlockSpec(memory_...  27.2 us
    ppermute x1, waiting for transfers between devices, shards(): arrived = lax.ppermute(sent, 'space', [(i, i ^ 4) for i in range(count)])  5.08 us
    ppermute x1, starting transfers between devices, shards(): arrived = lax.ppermute(sent, 'space', [(i, i ^ 4) for i in range(count)])  4.9 us
    ppermute x3, starting transfers between devices, shards(): lax.ppermute(part, 'space', [(i, i ^ away) for i in range(count)])  4.44 us
    ppermute x1, starting transfers between devices, shards(): terms_inner = lax.ppermute(inner, 'space', within)  3.95 us
    ppermute x1, starting transfers between devices, shards(): message = lax.ppermute(message, 'space', within)  2.92 us
  transfers between devices with their start and end apart: 10, of which 3 were waited for; matrix products, arithmetic and copies ran while one was open for 0% of the time, Pallas kernels for 43%

profile of v14, /device:TPU:0, one launch (start us, length us, event | category | flops | bytes accessed | tf_op | source)
XLA Modules:
  0.0 53.1 jit_solution(11198108188213367029)
XLA Ops:
  0.6 1.4 %pack_volume.1.own = bf16[2048,128]{1,0:T(8,128)(2,1)S(1)} custom-call(bf16[2,2048,64]{2,1,0:T(8,128)(2,1)} %bitcast.19), custom_call_target="tpu_custom_call" | custom-call | bytes 1048576 | tf_op jit(solution)/shard_map/pack_volume/pallas_call | solution.py:27
  2.0 0.5 collective-permute-start
  2.6 0.7 %collective-permute-start.1 = (bf16[2048,128]{1,0:T(8,128)(2,1)S(1)}, bf16[2048,128]{1,0:T(8,128)(2,1)S(1)}, u32[]{:S(2)}, u32[]{:S(2)}) collective-permute-start(bf16[2048,128]{1,0:T(8,128)(2,1)S(1)} %pack_volume.1.own), channel_id=1, source_target_pairs={{1,2},{3,4},{5,6},{7,8},{9,10},{11,12},{13,14},{2,1},{4,3},{6,5},{... | collective-permute-start | bytes 1572872 | tf_op jit(solution)/shard_map/ppermute | solution.py:547
  3.2 0.0 copy-start
  3.3 4.6 %grad_act_terms.1 = (f32[2048,128]{1,0:T(8,128)S(1)}, bf16[2048,128]{1,0:T(8,128)(2,1)S(1)}, bf16[1024,128]{1,0:T(8,128)(2,1)S(1)}, bf16[256,2048]{1,0:T(8,128)(2,1)S(1)}) custom-call(s32[1]{0:T(128)} %bitcast.me, bf16[2,2048,128]{2,1,0:T(8,128)(2,1)} %bitcast.20, bf16[27,64,128]{2,1,0:T(8,128)(2,1)} %bitcast.15), custom_call_target="tpu_custom_call" | custom-call | flops 1811939328 | bytes 4374532 | tf_op jit(solution)/shard_map/grad_act_terms/pallas_call | solution.py:27
  7.9 0.2 back_taps.1.taps
  8.1 3.7 %prepare.1 = (bf16[2112,384]{1,0:T(8,128)(2,1)S(1)}, bf16[2112,384]{1,0:T(8,128)(2,1)S(1)}, f32[2048,256]{1,0:T(8,128)S(1)}, bf16[1152,256]{1,0:T(8,128)(2,1)S(1)}) custom-call(s32[1]{0:T(128)} %bitcast.me, bf16[2048,128]{1,0:T(8,128)(2,1)S(1)} %pack_volume.1.own, bf16[2048,128]{1,0:T(8,128)(2,1)S(1)} %collective-permute-done.inner, bf16[27,64,64]{2,1,0:T(8,128)(2,1)} %bitcast.13), custom_call_target="tpu_custom_call" | custom-call | flops 905969664 | bytes 7200772 | tf_op jit(solution)/shard_map/prepare/pallas_call | solution.py:27
  11.8 3.9 %collective-permute-start.2 = (bf16[2048,128]{1,0:T(8,128)(2,1)S(1)}, bf16[2048,128]{1,0:T(8,128)(2,1)S(1)}, u32[]{:S(2)}, u32[]{:S(2)}) collective-permute-start(bf16[2048,128]{1,0:T(8,128)(2,1)S(1)} %get-tuple-element.61), channel_id=1, source_target_pairs={{0,1},{1,0},{2,3},{3,2},{4,5},{5,4},{6,7},{7,6},{8,9},{9,8},{10,11... | collective-permute-start | bytes 1572872 | tf_op jit(solution)/shard_map/ppermute | solution.py:575
  15.7 0.8 %collective-permute-start.3 = (bf16[1024,128]{1,0:T(8,128)(2,1)S(1)}, bf16[1024,128]{1,0:T(8,128)(2,1)S(1)}, u32[]{:S(2)}, u32[]{:S(2)}) collective-permute-start(bf16[1024,128]{1,0:T(8,128)(2,1)S(1)} %get-tuple-element.62), channel_id=1, source_target_pairs={{1,2},{3,4},{5,6},{7,8},{9,10},{11,12},{13,14},{2,1},{4,3},{6,5},{... | collective-permute-start | bytes 786440 | tf_op jit(solution)/shard_map/ppermute | solution.py:574
  16.6 3.5 %hidden.1 = (bf16[2112,768]{1,0:T(8,128)(2,1)S(1)}, f32[2048,128]{1,0:T(8,128)S(1)}, bf16[2112,384]{1,0:T(8,128)(2,1)S(1)}) custom-call(s32[1]{0:T(128)} %bitcast.me, bf16[2048,128]{1,0:T(8,128)(2,1)S(1)} %collective-permute-done.1.outer, f32[2048,256]{1,0:T(8,128)S(1)} %get-tuple-element.56.part, bf16[1152,256]{1,0:T(8,128)(2,1)S(1)} %get-tuple-element.57.outer_taps, ...), custom_call_target="tpu_custom_call" | custom-call | flops 1811939328 | bytes 10747908 | tf_op jit(solution)/shard_map/hidden/pallas_call | solution.py:27
  20.1 2.7 %grad_two_terms.1.other = f32[128,1792]{1,0:T(8,128)S(1)} custom-call(bf16[2112,768]{1,0:T(8,128)(2,1)S(1)} %get-tuple-element.80.act_windows, bf16[256,2048]{1,0:T(8,128)(2,1)S(1)} %get-tuple-element.65.turned), custom_call_target="tpu_custom_call" | custom-call | flops 1811939328 | bytes 5210112 | tf_op jit(solution)/shard_map/grad_two_terms/pallas_call | solution.py:27
  22.8 0.0 collective-permute-done.3.outer
  22.8 0.0 collective-permute-done.2.inner
  22.8 0.0 copy-start.1
  22.8 2.1 %grad_one_terms.1 = (bf16[2048,128]{1,0:T(8,128)(2,1)S(1)}, bf16[1024,128]{1,0:T(8,128)(2,1)S(1)}, bf16[2816,128]{1,0:T(8,128)(2,1)S(1)}, f32[8,24,896]{2,1,0:T(8,128)S(1)}) custom-call(s32[1]{0:T(128)} %bitcast.me, bf16[2112,384]{1,0:T(8,128)(2,1)S(1)} %get-tuple-element.52.own_windows, bf16[2112,384]{1,0:T(8,128)(2,1)S(1)} %get-tuple-element.59.side_windows, ...), custom_call_target="tpu_custom_call" | custom-call | flops 905969664 | bytes 9240580 | tf_op jit(solution)/shard_map/grad_one_terms/pallas_call | solution.py:27
  25.0 2.9 %collective-permute-start.4 = (bf16[2816,128]{1,0:T(8,128)(2,1)S(1)}, bf16[2816,128]{1,0:T(8,128)(2,1)S(1)}, u32[]{:S(2)}, u32[]{:S(2)}) collective-permute-start(bf16[2816,128]{1,0:T(8,128)(2,1)S(1)} %get-tuple-element.67), channel_id=1, source_target_pairs={{0,1},{1,0},{2,3},{3,2},{4,5},{5,4},{6,7},{7,6},{8,9},{9,8},{10,11... | collective-permute-start | bytes 2162696 | tf_op jit(solution)/shard_map/ppermute | solution.py:601
  27.9 1.7 %output_first.1 = (f32[2,2048,128]{2,1,0:T(8,128)}, bf16[2304,256]{1,0:T(8,128)(2,1)S(1)}, bf16[2112,384]{1,0:T(8,128)(2,1)S(1)}) custom-call(bf16[2112,768]{1,0:T(8,128)(2,1)S(1)} %get-tuple-element.80.act_windows, bf16[27,64,128]{2,1,0:T(8,128)(2,1)S(1)} %bitcast.16, bf16[2048,128]{1,0:T(8,128)(2,1)S(1)} %get-tuple-element.68.grad), custom_call_target="tpu_custom_call" | custom-call | flops 1811939328 | bytes 9109504 | tf_op jit(solution)/shard_map/output_first/pallas_call | solution.py:27
  29.6 0.1 collective-permute-done.4.arrived.message
  29.7 0.1 halve.1
  29.8 0.7 %collective-permute-start.6 = (bf16[1024,128]{1,0:T(8,128)(2,1)S(1)}, bf16[1024,128]{1,0:T(8,128)(2,1)S(1)}, u32[]{:S(2)}, u32[]{:S(2)}) collective-permute-start(bf16[1024,128]{1,0:T(8,128)(2,1)S(1)} %get-tuple-element.87), channel_id=1, source_target_pairs={{1,2},{3,4},{5,6},{7,8},{9,10},{11,12},{13,14},{2,1},{4,3},{6,5},{... | collective-permute-start | bytes 786440 | tf_op jit(solution)/shard_map/ppermute | solution.py:626
  30.5 4.9 %collective-permute-start.5 = (bf16[4,24,896]{2,1,0:T(8,128)(2,1)S(1)}, bf16[4,24,896]{2,1,0:T(8,128)(2,1)S(1)}, u32[]{:S(2)}, u32[]{:S(2)}) collective-permute-start(bf16[4,24,896]{2,1,0:T(8,128)(2,1)S(1)} %get-tuple-element.76), channel_id=1, source_target_pairs={{0,4},{1,5},{2,6},{3,7},{4,0},{5,1},{6,2},{7,3},{8,12},{9,13},{10,... | collective-permute-start | bytes 516104 | tf_op jit(solution)/shard_map/ppermute | solution.py:625
  35.4 2.9 %output_rest.1 = f32[2,2048,128]{2,1,0:T(8,128)} custom-call(bf16[2112,768]{1,0:T(8,128)(2,1)S(1)} %get-tuple-element.80.act_windows, bf16[2304,256]{1,0:T(8,128)(2,1)S(1)} %get-tuple-element.81.taps, f32[2,2048,128]{2,1,0:T(8,128)} %get-tuple-element.82.begun), custom_call_target="tpu_custom_call", output_to_operand_aliasing={{}: (2, {})} | custom-call | flops 1811939328 | bytes 8617984 | tf_op jit(solution)/shard_map/output_rest/pallas_call | solution.py:27
  38.3 5.1 %collective-permute-done.5.arrived = bf16[4,24,896]{2,1,0:T(8,128)(2,1)S(1)} collective-permute-done((bf16[4,24,896]{2,1,0:T(8,128)(2,1)S(1)}, bf16[4,24,896]{2,1,0:T(8,128)(2,1)S(1)}, u32[]{:S(2)}, u32[]{:S(2)}) %collective-permute-start.5) | collective-permute-done | bytes 172064 | tf_op jit(solution)/shard_map/ppermute | solution.py:625
  43.4 0.1 collective-permute-start.7
  43.5 2.7 %collective-permute-start.8 = (bf16[24,896]{1,0:T(8,128)(2,1)S(1)}, bf16[24,896]{1,0:T(8,128)(2,1)S(1)}, u32[]{:S(2)}, u32[]{:S(2)}) collective-permute-start(bf16[24,896]{1,0:T(8,128)(2,1)S(1)} %get-tuple-element.92), channel_id=1, source_target_pairs={{0,8},{1,9},{2,10},{3,11},{4,12},{5,13},{6,14},{7,15},{8,0},{9,1},... | collective-permute-start | bytes 129032 | tf_op jit(solution)/shard_map/ppermute | solution.py:644
  46.1 1.7 %collective-permute-start.9 = (bf16[24,896]{1,0:T(8,128)(2,1)S(1)}, bf16[24,896]{1,0:T(8,128)(2,1)S(1)}, u32[]{:S(2)}, u32[]{:S(2)}) collective-permute-start(bf16[24,896]{1,0:T(8,128)(2,1)S(1)} %get-tuple-element.93), channel_id=1, source_target_pairs={{0,10},{1,11},{2,8},{3,9},{4,14},{5,15},{6,12},{7,13},{8,2},{9,3},... | collective-permute-start | bytes 129032 | tf_op jit(solution)/shard_map/ppermute | solution.py:644
  47.8 0.0 collective-permute-done.6.outer
  47.8 0.6 %grad_windows.1.side_windows = bf16[2112,384]{1,0:T(8,128)(2,1)S(1)} custom-call(s32[1]{0:T(128)} %bitcast.me, bf16[2816,128]{1,0:T(8,128)(2,1)S(1)} %collective-permute-done.4.arrived.message, bf16[1024,128]{1,0:T(8,128)(2,1)S(1)} %collective-permute-done.6.outer), custom_call_target="tpu_custom_call" | custom-call | flops 226492416 | bytes 2605060 | tf_op jit(solution)/shard_map/grad_windows/pallas_call | solution.py:27
  48.5 2.9 %grad_volume.1 = f32[2,2048,64]{2,1,0:T(8,128)} custom-call(bf16[2112,384]{1,0:T(8,128)(2,1)S(1)} %get-tuple-element.86.own_windows, bf16[2112,384]{1,0:T(8,128)(2,1)S(1)} %grad_windows.1.side_windows, bf16[384,768]{1,0:T(8,128)(2,1)S(1)} %back_taps.1.taps), custom_call_target="tpu_custom_call" | custom-call | flops 905969664 | bytes 4882432 | tf_op jit(solution)/shard_map/grad_volume/pallas_call | solution.py:27
  51.4 0.0 collective-permute-done.7.refs_0_
  51.4 0.9 %collective-permute-done.9.refs_2_ = bf16[24,896]{1,0:T(8,128)(2,1)S(1)} collective-permute-done((bf16[24,896]{1,0:T(8,128)(2,1)S(1)}, bf16[24,896]{1,0:T(8,128)(2,1)S(1)}, u32[]{:S(2)}, u32[]{:S(2)}) %collective-permute-start.9) | collective-permute-done | bytes 43040 | tf_op jit(solution)/shard_map/ppermute | solution.py:644
  52.3 0.7 %finish.1 = (f32[27,4,64]{2,1,0:T(4,128)}, f32[27,8,64]{2,1,0:T(8,128)}) custom-call(f32[24,896]{1,0:T(8,128)S(1)} %get-tuple-element.90.mine, bf16[24,896]{1,0:T(8,128)(2,1)S(1)} %collective-permute-done.7.refs_0_, bf16[24,896]{1,0:T(8,128)(2,1)S(1)} %collective-permute-done.8.refs_1_, bf16[24,896]{1,0:T(8,128)(2,1)S(1)} %collective-permute-done.9.refs_2_), custom_call_target="tpu_custom_call" | custom-call | bytes 297984 | tf_op jit(solution)/shard_map/finish/pallas_call | solution.py:27
  (6 shorter events, 0.1 us)
Async XLA Ops:
  2.0 6.0 %collective-permute-start = (bf16[2048,128]{1,0:T(8,128)(2,1)S(1)}, bf16[2048,128]{1,0:T(8,128)(2,1)S(1)}, u32[]{:S(2)}, u32[]{:S(2)}) collective-permute-start(bf16[2048,128]{1,0:T(8,128)(2,1)S(1)} %pack_volume.1.own), channel_id=1, source_target_pairs={{0,1},{1,0},{2,3},{3,2},{4,5},{5,4},{6,7},{7,6},{8,9},{9,8},{10,11... | collective-permute-start | bytes 1572872 | tf_op jit(solution)/shard_map/ppermute | solution.py:548
  2.6 14.0 %collective-permute-start.1 = (bf16[2048,128]{1,0:T(8,128)(2,1)S(1)}, bf16[2048,128]{1,0:T(8,128)(2,1)S(1)}, u32[]{:S(2)}, u32[]{:S(2)}) collective-permute-start(bf16[2048,128]{1,0:T(8,128)(2,1)S(1)} %pack_volume.1.own), channel_id=1, source_target_pairs={{1,2},{3,4},{5,6},{7,8},{9,10},{11,12},{13,14},{2,1},{4,3},{6,5},{... | collective-permute-start | bytes 1572872 | tf_op jit(solution)/shard_map/ppermute | solution.py:547
  3.2 4.6 %copy-start = (bf16[3,3,3,64,64]{4,3,2,1,0:T(8,128)(2,1)S(1)}, bf16[3,3,3,64,64]{4,3,2,1,0:T(8,128)(2,1)}, u32[]{:S(2)}) copy-start(bf16[3,3,3,64,64]{4,3,2,1,0:T(8,128)(2,1)} %param.5) | copy-start | bytes 663556
  11.8 11.0 %collective-permute-start.2 = (bf16[2048,128]{1,0:T(8,128)(2,1)S(1)}, bf16[2048,128]{1,0:T(8,128)(2,1)S(1)}, u32[]{:S(2)}, u32[]{:S(2)}) collective-permute-start(bf16[2048,128]{1,0:T(8,128)(2,1)S(1)} %get-tuple-element.61), channel_id=1, source_target_pairs={{0,1},{1,0},{2,3},{3,2},{4,5},{5,4},{6,7},{7,6},{8,9},{9,8},{10,11... | collective-permute-start | bytes 1572872 | tf_op jit(solution)/shard_map/ppermute | solution.py:575
  15.7 7.1 %collective-permute-start.3 = (bf16[1024,128]{1,0:T(8,128)(2,1)S(1)}, bf16[1024,128]{1,0:T(8,128)(2,1)S(1)}, u32[]{:S(2)}, u32[]{:S(2)}) collective-permute-start(bf16[1024,128]{1,0:T(8,128)(2,1)S(1)} %get-tuple-element.62), channel_id=1, source_target_pairs={{1,2},{3,4},{5,6},{7,8},{9,10},{11,12},{13,14},{2,1},{4,3},{6,5},{... | collective-permute-start | bytes 786440 | tf_op jit(solution)/shard_map/ppermute | solution.py:574
  22.8 5.1 %copy-start.1 = (bf16[3,3,3,64,128]{4,3,2,1,0:T(8,128)(2,1)S(1)}, bf16[3,3,3,64,128]{4,3,2,1,0:T(8,128)(2,1)}, u32[]{:S(2)}) copy-start(bf16[3,3,3,64,128]{4,3,2,1,0:T(8,128)(2,1)} %param.6) | copy-start | bytes 1327108
  25.0 4.7 %collective-permute-start.4 = (bf16[2816,128]{1,0:T(8,128)(2,1)S(1)}, bf16[2816,128]{1,0:T(8,128)(2,1)S(1)}, u32[]{:S(2)}, u32[]{:S(2)}) collective-permute-start(bf16[2816,128]{1,0:T(8,128)(2,1)S(1)} %get-tuple-element.67), channel_id=1, source_target_pairs={{0,1},{1,0},{2,3},{3,2},{4,5},{5,4},{6,7},{7,6},{8,9},{9,8},{10,11... | collective-permute-start | bytes 2162696 | tf_op jit(solution)/shard_map/ppermute | solution.py:601
  29.8 18.0 %collective-permute-start.6 = (bf16[1024,128]{1,0:T(8,128)(2,1)S(1)}, bf16[1024,128]{1,0:T(8,128)(2,1)S(1)}, u32[]{:S(2)}, u32[]{:S(2)}) collective-permute-start(bf16[1024,128]{1,0:T(8,128)(2,1)S(1)} %get-tuple-element.87), channel_id=1, source_target_pairs={{1,2},{3,4},{5,6},{7,8},{9,10},{11,12},{13,14},{2,1},{4,3},{6,5},{... | collective-permute-start | bytes 786440 | tf_op jit(solution)/shard_map/ppermute | solution.py:626
  30.5 12.8 %collective-permute-start.5 = (bf16[4,24,896]{2,1,0:T(8,128)(2,1)S(1)}, bf16[4,24,896]{2,1,0:T(8,128)(2,1)S(1)}, u32[]{:S(2)}, u32[]{:S(2)}) collective-permute-start(bf16[4,24,896]{2,1,0:T(8,128)(2,1)S(1)} %get-tuple-element.76), channel_id=1, source_target_pairs={{0,4},{1,5},{2,6},{3,7},{4,0},{5,1},{6,2},{7,3},{8,12},{9,13},{10,... | collective-permute-start | bytes 516104 | tf_op jit(solution)/shard_map/ppermute | solution.py:625
  43.4 8.0 %collective-permute-start.7 = (bf16[24,896]{1,0:T(8,128)(2,1)S(1)}, bf16[24,896]{1,0:T(8,128)(2,1)S(1)}, u32[]{:S(2)}, u32[]{:S(2)}) collective-permute-start(bf16[24,896]{1,0:T(8,128)(2,1)S(1)} %get-tuple-element.91), channel_id=1, source_target_pairs={{0,2},{1,3},{2,0},{3,1},{4,6},{5,7},{6,4},{7,5},{8,10},{9,11},{10,... | collective-permute-start | bytes 129032 | tf_op jit(solution)/shard_map/ppermute | solution.py:644
  43.5 7.9 %collective-permute-start.8 = (bf16[24,896]{1,0:T(8,128)(2,1)S(1)}, bf16[24,896]{1,0:T(8,128)(2,1)S(1)}, u32[]{:S(2)}, u32[]{:S(2)}) collective-permute-start(bf16[24,896]{1,0:T(8,128)(2,1)S(1)} %get-tuple-element.92), channel_id=1, source_target_pairs={{0,8},{1,9},{2,10},{3,11},{4,12},{5,13},{6,14},{7,15},{8,0},{9,1},... | collective-permute-start | bytes 129032 | tf_op jit(solution)/shard_map/ppermute | solution.py:644
  46.1 6.2 %collective-permute-start.9 = (bf16[24,896]{1,0:T(8,128)(2,1)S(1)}, bf16[24,896]{1,0:T(8,128)(2,1)S(1)}, u32[]{:S(2)}, u32[]{:S(2)}) collective-permute-start(bf16[24,896]{1,0:T(8,128)(2,1)S(1)} %get-tuple-element.93), channel_id=1, source_target_pairs={{0,10},{1,11},{2,8},{3,9},{4,14},{5,15},{6,12},{7,13},{8,2},{9,3},... | collective-permute-start | bytes 129032 | tf_op jit(solution)/shard_map/ppermute | solution.py:644

commit v15 on v14

--- a/solution.py
+++ b/solution.py
@@ -635,7 +635,7 @@
     mine, *sent = call(
         functools.partial(spread_body, 0, bits),
         (shape((chunk, lanes), F32), *[shape((chunk, lanes), BF16)] * others),
-        (me, kept, arrived), flops=one_flops, name="spread", smem=(0,),
+        (me, kept, arrived), flops=16 * two_flops, name="spread", smem=(0,),
     )
     sent, output, back_windows = lax.optimization_barrier((sent, output, back_windows))
     arrived = []

time: 53.3 us -> 48.7 us (0.914)
  starting transfers between devices: 18.9 us -> 16.6 us
  waiting for transfers between devices: 6.16 us -> 3.92 us
    ppermute x1, waiting for transfers between devices: 5.08 us -> 1.35 us  [shards(): arrived = lax.ppermute(sent, 'space', [(i, i ^ 4) for i in range(count)])]
    ppermute x1, starting transfers between devices: 4.9 us -> 2.53 us  [shards(): arrived = lax.ppermute(sent, 'space', [(i, i ^ 4) for i in range(count)])]
    ppermute x3, waiting for transfers between devices: 0.93 us -> 2.42 us  [shards(): lax.ppermute(part, 'space', [(i, i ^ away) for i in range(count)])]
  transfers between devices with their start and end apart: 10 -> 10, of which waited for: 3 -> 3; matrix products, arithmetic and copies ran while one was open for 0% -> 0% of each run, Pallas kernels for 43% -> 47%
where the time goes in v15:
time: 48.7 us; the launch traced here: 48.5 us
  Pallas kernels  27.2 us (56%)
  starting transfers between devices  16.6 us (34%)
  waiting for transfers between devices  3.92 us (8%)
  between operations  0.82 us (2%)
    pallas_call x14, Pallas kernels, call(): pl.pallas_call(body, out_shape=list(outs), in_specs=[pl.BlockSpec(memory_...  27.2 us
    ppermute x3, starting transfers between devices, shards(): lax.ppermute(part, 'space', [(i, i ^ away) for i in range(count)])  4.45 us
    ppermute x1, starting transfers between devices, shards(): terms_inner = lax.ppermute(inner, 'space', within)  3.95 us
    ppermute x1, starting transfers between devices, shards(): message = lax.ppermute(message, 'space', within)  2.92 us
    ppermute x1, starting transfers between devices, shards(): arrived = lax.ppermute(sent, 'space', [(i, i ^ 4) for i in range(count)])  2.53 us
    ppermute x3, waiting for transfers between devices, shards(): lax.ppermute(part, 'space', [(i, i ^ away) for i in range(count)])  2.42 us
    ppermute x1, waiting for transfers between devices, shards(): arrived = lax.ppermute(sent, 'space', [(i, i ^ 4) for i in range(count)])  1.35 us
  transfers between devices with their start and end apart: 10, of which 3 were waited for; matrix products, arithmetic and copies ran while one was open for 0% of the time, Pallas kernels for 47%

profile of v15, /device:TPU:0, one launch (start us, length us, event | category | flops | bytes accessed | tf_op | source)
XLA Modules:
  0.0 48.5 jit_solution(1294159473197031605)
XLA Ops:
  0.6 1.4 %pack_volume.1.own = bf16[2048,128]{1,0:T(8,128)(2,1)S(1)} custom-call(bf16[2,2048,64]{2,1,0:T(8,128)(2,1)} %bitcast.19), custom_call_target="tpu_custom_call" | custom-call | bytes 1048576 | tf_op jit(solution)/shard_map/pack_volume/pallas_call | solution.py:27
  2.0 0.5 %collective-permute-start = (bf16[2048,128]{1,0:T(8,128)(2,1)S(1)}, bf16[2048,128]{1,0:T(8,128)(2,1)S(1)}, u32[]{:S(2)}, u32[]{:S(2)}) collective-permute-start(bf16[2048,128]{1,0:T(8,128)(2,1)S(1)} %pack_volume.1.own), channel_id=1, source_target_pairs={{0,1},{1,0},{2,3},{3,2},{4,5},{5,4},{6,7},{7,6},{8,9},{9,8},{10,11... | collective-permute-start | bytes 1572872 | tf_op jit(solution)/shard_map/ppermute | solution.py:548
  2.6 0.7 %collective-permute-start.1 = (bf16[2048,128]{1,0:T(8,128)(2,1)S(1)}, bf16[2048,128]{1,0:T(8,128)(2,1)S(1)}, u32[]{:S(2)}, u32[]{:S(2)}) collective-permute-start(bf16[2048,128]{1,0:T(8,128)(2,1)S(1)} %pack_volume.1.own), channel_id=1, source_target_pairs={{1,2},{3,4},{5,6},{7,8},{9,10},{11,12},{13,14},{2,1},{4,3},{6,5},{... | collective-permute-start | bytes 1572872 | tf_op jit(solution)/shard_map/ppermute | solution.py:547
  3.2 0.0 copy-start
  3.3 4.6 %grad_act_terms.1 = (f32[2048,128]{1,0:T(8,128)S(1)}, bf16[2048,128]{1,0:T(8,128)(2,1)S(1)}, bf16[1024,128]{1,0:T(8,128)(2,1)S(1)}, bf16[256,2048]{1,0:T(8,128)(2,1)S(1)}) custom-call(s32[1]{0:T(128)} %bitcast.me, bf16[2,2048,128]{2,1,0:T(8,128)(2,1)} %bitcast.20, bf16[27,64,128]{2,1,0:T(8,128)(2,1)} %bitcast.15), custom_call_target="tpu_custom_call" | custom-call | flops 1811939328 | bytes 4374532 | tf_op jit(solution)/shard_map/grad_act_terms/pallas_call | solution.py:27
  7.9 0.2 back_taps.1.taps
  8.0 0.0 collective-permute-done.inner
  8.1 3.7 %prepare.1 = (bf16[2112,384]{1,0:T(8,128)(2,1)S(1)}, bf16[2112,384]{1,0:T(8,128)(2,1)S(1)}, f32[2048,256]{1,0:T(8,128)S(1)}, bf16[1152,256]{1,0:T(8,128)(2,1)S(1)}) custom-call(s32[1]{0:T(128)} %bitcast.me, bf16[2048,128]{1,0:T(8,128)(2,1)S(1)} %pack_volume.1.own, bf16[2048,128]{1,0:T(8,128)(2,1)S(1)} %collective-permute-done.inner, bf16[27,64,64]{2,1,0:T(8,128)(2,1)} %bitcast.13), custom_call_target="tpu_custom_call" | custom-call | flops 905969664 | bytes 7200772 | tf_op jit(solution)/shard_map/prepare/pallas_call | solution.py:27
  11.8 3.9 %collective-permute-start.2 = (bf16[2048,128]{1,0:T(8,128)(2,1)S(1)}, bf16[2048,128]{1,0:T(8,128)(2,1)S(1)}, u32[]{:S(2)}, u32[]{:S(2)}) collective-permute-start(bf16[2048,128]{1,0:T(8,128)(2,1)S(1)} %get-tuple-element.61), channel_id=1, source_target_pairs={{0,1},{1,0},{2,3},{3,2},{4,5},{5,4},{6,7},{7,6},{8,9},{9,8},{10,11... | collective-permute-start | bytes 1572872 | tf_op jit(solution)/shard_map/ppermute | solution.py:575
  15.7 0.8 %collective-permute-start.3 = (bf16[1024,128]{1,0:T(8,128)(2,1)S(1)}, bf16[1024,128]{1,0:T(8,128)(2,1)S(1)}, u32[]{:S(2)}, u32[]{:S(2)}) collective-permute-start(bf16[1024,128]{1,0:T(8,128)(2,1)S(1)} %get-tuple-element.62), channel_id=1, source_target_pairs={{1,2},{3,4},{5,6},{7,8},{9,10},{11,12},{13,14},{2,1},{4,3},{6,5},{... | collective-permute-start | bytes 786440 | tf_op jit(solution)/shard_map/ppermute | solution.py:574
  16.6 0.0 collective-permute-done.1.outer
  16.6 3.5 %hidden.1 = (bf16[2112,768]{1,0:T(8,128)(2,1)S(1)}, f32[2048,128]{1,0:T(8,128)S(1)}, bf16[2112,384]{1,0:T(8,128)(2,1)S(1)}) custom-call(s32[1]{0:T(128)} %bitcast.me, bf16[2048,128]{1,0:T(8,128)(2,1)S(1)} %collective-permute-done.1.outer, f32[2048,256]{1,0:T(8,128)S(1)} %get-tuple-element.56.part, bf16[1152,256]{1,0:T(8,128)(2,1)S(1)} %get-tuple-element.57.outer_taps, ...), custom_call_target="tpu_custom_call" | custom-call | flops 1811939328 | bytes 10747908 | tf_op jit(solution)/shard_map/hidden/pallas_call | solution.py:27
  20.1 2.7 %grad_two_terms.1.other = f32[128,1792]{1,0:T(8,128)S(1)} custom-call(bf16[2112,768]{1,0:T(8,128)(2,1)S(1)} %get-tuple-element.80.act_windows, bf16[256,2048]{1,0:T(8,128)(2,1)S(1)} %get-tuple-element.65.turned), custom_call_target="tpu_custom_call" | custom-call | flops 1811939328 | bytes 5210112 | tf_op jit(solution)/shard_map/grad_two_terms/pallas_call | solution.py:27
  22.8 0.0 collective-permute-done.2.inner
  22.8 0.0 copy-start.1
  22.8 2.1 %grad_one_terms.1 = (bf16[2048,128]{1,0:T(8,128)(2,1)S(1)}, bf16[1024,128]{1,0:T(8,128)(2,1)S(1)}, bf16[2816,128]{1,0:T(8,128)(2,1)S(1)}, f32[8,24,896]{2,1,0:T(8,128)S(1)}) custom-call(s32[1]{0:T(128)} %bitcast.me, bf16[2112,384]{1,0:T(8,128)(2,1)S(1)} %get-tuple-element.52.own_windows, bf16[2112,384]{1,0:T(8,128)(2,1)S(1)} %get-tuple-element.59.side_windows, ...), custom_call_target="tpu_custom_call" | custom-call | flops 905969664 | bytes 9240580 | tf_op jit(solution)/shard_map/grad_one_terms/pallas_call | solution.py:27
  25.0 2.9 %collective-permute-start.4 = (bf16[2816,128]{1,0:T(8,128)(2,1)S(1)}, bf16[2816,128]{1,0:T(8,128)(2,1)S(1)}, u32[]{:S(2)}, u32[]{:S(2)}) collective-permute-start(bf16[2816,128]{1,0:T(8,128)(2,1)S(1)} %get-tuple-element.67), channel_id=1, source_target_pairs={{0,1},{1,0},{2,3},{3,2},{4,5},{5,4},{6,7},{7,6},{8,9},{9,8},{10,11... | collective-permute-start | bytes 2162696 | tf_op jit(solution)/shard_map/ppermute | solution.py:601
  27.9 1.7 %output_first.1 = (f32[2,2048,128]{2,1,0:T(8,128)}, bf16[2304,256]{1,0:T(8,128)(2,1)S(1)}, bf16[2112,384]{1,0:T(8,128)(2,1)S(1)}) custom-call(bf16[2112,768]{1,0:T(8,128)(2,1)S(1)} %get-tuple-element.80.act_windows, bf16[27,64,128]{2,1,0:T(8,128)(2,1)S(1)} %bitcast.16, bf16[2048,128]{1,0:T(8,128)(2,1)S(1)} %get-tuple-element.68.grad), custom_call_target="tpu_custom_call" | custom-call | flops 1811939328 | bytes 9109504 | tf_op jit(solution)/shard_map/output_first/pallas_call | solution.py:27
  29.6 0.1 collective-permute-done.4.arrived.message
  29.7 0.1 halve.1
  29.8 2.5 %collective-permute-start.5 = (bf16[4,24,896]{2,1,0:T(8,128)(2,1)S(1)}, bf16[4,24,896]{2,1,0:T(8,128)(2,1)S(1)}, u32[]{:S(2)}, u32[]{:S(2)}) collective-permute-start(bf16[4,24,896]{2,1,0:T(8,128)(2,1)S(1)} %get-tuple-element.76), channel_id=1, source_target_pairs={{0,4},{1,5},{2,6},{3,7},{4,0},{5,1},{6,2},{7,3},{8,12},{9,13},{10,... | collective-permute-start | bytes 516104 | tf_op jit(solution)/shard_map/ppermute | solution.py:625
  32.3 0.7 %collective-permute-start.6 = (bf16[1024,128]{1,0:T(8,128)(2,1)S(1)}, bf16[1024,128]{1,0:T(8,128)(2,1)S(1)}, u32[]{:S(2)}, u32[]{:S(2)}) collective-permute-start(bf16[1024,128]{1,0:T(8,128)(2,1)S(1)} %get-tuple-element.87), channel_id=1, source_target_pairs={{1,2},{3,4},{5,6},{7,8},{9,10},{11,12},{13,14},{2,1},{4,3},{6,5},{... | collective-permute-start | bytes 786440 | tf_op jit(solution)/shard_map/ppermute | solution.py:626
  33.0 2.9 %output_rest.1 = f32[2,2048,128]{2,1,0:T(8,128)} custom-call(bf16[2112,768]{1,0:T(8,128)(2,1)S(1)} %get-tuple-element.80.act_windows, bf16[2304,256]{1,0:T(8,128)(2,1)S(1)} %get-tuple-element.81.taps, f32[2,2048,128]{2,1,0:T(8,128)} %get-tuple-element.82.begun), custom_call_target="tpu_custom_call", output_to_operand_aliasing={{}: (2, {})} | custom-call | flops 1811939328 | bytes 8617984 | tf_op jit(solution)/shard_map/output_rest/pallas_call | solution.py:27
  35.9 1.4 %collective-permute-done.5.arrived = bf16[4,24,896]{2,1,0:T(8,128)(2,1)S(1)} collective-permute-done((bf16[4,24,896]{2,1,0:T(8,128)(2,1)S(1)}, bf16[4,24,896]{2,1,0:T(8,128)(2,1)S(1)}, u32[]{:S(2)}, u32[]{:S(2)}) %collective-permute-start.5) | collective-permute-done | bytes 172064 | tf_op jit(solution)/shard_map/ppermute | solution.py:625
  37.3 1.7 %collective-permute-start.7 = (bf16[24,896]{1,0:T(8,128)(2,1)S(1)}, bf16[24,896]{1,0:T(8,128)(2,1)S(1)}, u32[]{:S(2)}, u32[]{:S(2)}) collective-permute-start(bf16[24,896]{1,0:T(8,128)(2,1)S(1)} %get-tuple-element.91), channel_id=1, source_target_pairs={{0,2},{1,3},{2,0},{3,1},{4,6},{5,7},{6,4},{7,5},{8,10},{9,11},{10,... | collective-permute-start | bytes 129032 | tf_op jit(solution)/shard_map/ppermute | solution.py:644
  39.0 2.6 %collective-permute-start.8 = (bf16[24,896]{1,0:T(8,128)(2,1)S(1)}, bf16[24,896]{1,0:T(8,128)(2,1)S(1)}, u32[]{:S(2)}, u32[]{:S(2)}) collective-permute-start(bf16[24,896]{1,0:T(8,128)(2,1)S(1)} %get-tuple-element.92), channel_id=1, source_target_pairs={{0,8},{1,9},{2,10},{3,11},{4,12},{5,13},{6,14},{7,15},{8,0},{9,1},... | collective-permute-start | bytes 129032 | tf_op jit(solution)/shard_map/ppermute | solution.py:644
  41.6 0.2 collective-permute-start.9
  41.7 0.6 %grad_windows.1.side_windows = bf16[2112,384]{1,0:T(8,128)(2,1)S(1)} custom-call(s32[1]{0:T(128)} %bitcast.me, bf16[2816,128]{1,0:T(8,128)(2,1)S(1)} %collective-permute-done.4.arrived.message, bf16[1024,128]{1,0:T(8,128)(2,1)S(1)} %collective-permute-done.6.outer), custom_call_target="tpu_custom_call" | custom-call | flops 226492416 | bytes 2605060 | tf_op jit(solution)/shard_map/grad_windows/pallas_call | solution.py:27
  42.4 2.9 %grad_volume.1 = f32[2,2048,64]{2,1,0:T(8,128)} custom-call(bf16[2112,384]{1,0:T(8,128)(2,1)S(1)} %get-tuple-element.86.own_windows, bf16[2112,384]{1,0:T(8,128)(2,1)S(1)} %grad_windows.1.side_windows, bf16[384,768]{1,0:T(8,128)(2,1)S(1)} %back_taps.1.taps), custom_call_target="tpu_custom_call" | custom-call | flops 905969664 | bytes 4882432 | tf_op jit(solution)/shard_map/grad_volume/pallas_call | solution.py:27
  45.3 0.0 collective-permute-done.7.refs_0_
  45.3 2.4 %collective-permute-done.9.refs_2_ = bf16[24,896]{1,0:T(8,128)(2,1)S(1)} collective-permute-done((bf16[24,896]{1,0:T(8,128)(2,1)S(1)}, bf16[24,896]{1,0:T(8,128)(2,1)S(1)}, u32[]{:S(2)}, u32[]{:S(2)}) %collective-permute-start.9) | collective-permute-done | bytes 43040 | tf_op jit(solution)/shard_map/ppermute | solution.py:644
  47.7 0.7 %finish.1 = (f32[27,4,64]{2,1,0:T(4,128)}, f32[27,8,64]{2,1,0:T(8,128)}) custom-call(f32[24,896]{1,0:T(8,128)S(1)} %get-tuple-element.90.mine, bf16[24,896]{1,0:T(8,128)(2,1)S(1)} %collective-permute-done.7.refs_0_, bf16[24,896]{1,0:T(8,128)(2,1)S(1)} %collective-permute-done.8.refs_1_, bf16[24,896]{1,0:T(8,128)(2,1)S(1)} %collective-permute-done.9.refs_2_), custom_call_target="tpu_custom_call" | custom-call | bytes 297984 | tf_op jit(solution)/shard_map/finish/pallas_call | solution.py:27
  (6 shorter events, 0.1 us)
Async XLA Ops:
  2.0 6.0 %collective-permute-start = (bf16[2048,128]{1,0:T(8,128)(2,1)S(1)}, bf16[2048,128]{1,0:T(8,128)(2,1)S(1)}, u32[]{:S(2)}, u32[]{:S(2)}) collective-permute-start(bf16[2048,128]{1,0:T(8,128)(2,1)S(1)} %pack_volume.1.own), channel_id=1, source_target_pairs={{0,1},{1,0},{2,3},{3,2},{4,5},{5,4},{6,7},{7,6},{8,9},{9,8},{10,11... | collective-permute-start | bytes 1572872 | tf_op jit(solution)/shard_map/ppermute | solution.py:548
  2.6 14.0 %collective-permute-start.1 = (bf16[2048,128]{1,0:T(8,128)(2,1)S(1)}, bf16[2048,128]{1,0:T(8,128)(2,1)S(1)}, u32[]{:S(2)}, u32[]{:S(2)}) collective-permute-start(bf16[2048,128]{1,0:T(8,128)(2,1)S(1)} %pack_volume.1.own), channel_id=1, source_target_pairs={{1,2},{3,4},{5,6},{7,8},{9,10},{11,12},{13,14},{2,1},{4,3},{6,5},{... | collective-permute-start | bytes 1572872 | tf_op jit(solution)/shard_map/ppermute | solution.py:547
  3.2 4.6 %copy-start = (bf16[3,3,3,64,64]{4,3,2,1,0:T(8,128)(2,1)S(1)}, bf16[3,3,3,64,64]{4,3,2,1,0:T(8,128)(2,1)}, u32[]{:S(2)}) copy-start(bf16[3,3,3,64,64]{4,3,2,1,0:T(8,128)(2,1)} %param.5) | copy-start | bytes 663556
  11.8 11.0 %collective-permute-start.2 = (bf16[2048,128]{1,0:T(8,128)(2,1)S(1)}, bf16[2048,128]{1,0:T(8,128)(2,1)S(1)}, u32[]{:S(2)}, u32[]{:S(2)}) collective-permute-start(bf16[2048,128]{1,0:T(8,128)(2,1)S(1)} %get-tuple-element.61), channel_id=1, source_target_pairs={{0,1},{1,0},{2,3},{3,2},{4,5},{5,4},{6,7},{7,6},{8,9},{9,8},{10,11... | collective-permute-start | bytes 1572872 | tf_op jit(solution)/shard_map/ppermute | solution.py:575
  15.7 7.1 %collective-permute-start.3 = (bf16[1024,128]{1,0:T(8,128)(2,1)S(1)}, bf16[1024,128]{1,0:T(8,128)(2,1)S(1)}, u32[]{:S(2)}, u32[]{:S(2)}) collective-permute-start(bf16[1024,128]{1,0:T(8,128)(2,1)S(1)} %get-tuple-element.62), channel_id=1, source_target_pairs={{1,2},{3,4},{5,6},{7,8},{9,10},{11,12},{13,14},{2,1},{4,3},{6,5},{... | collective-permute-start | bytes 786440 | tf_op jit(solution)/shard_map/ppermute | solution.py:574
  22.8 5.1 %copy-start.1 = (bf16[3,3,3,64,128]{4,3,2,1,0:T(8,128)(2,1)S(1)}, bf16[3,3,3,64,128]{4,3,2,1,0:T(8,128)(2,1)}, u32[]{:S(2)}) copy-start(bf16[3,3,3,64,128]{4,3,2,1,0:T(8,128)(2,1)} %param.6) | copy-start | bytes 1327108
  25.0 4.7 %collective-permute-start.4 = (bf16[2816,128]{1,0:T(8,128)(2,1)S(1)}, bf16[2816,128]{1,0:T(8,128)(2,1)S(1)}, u32[]{:S(2)}, u32[]{:S(2)}) collective-permute-start(bf16[2816,128]{1,0:T(8,128)(2,1)S(1)} %get-tuple-element.67), channel_id=1, source_target_pairs={{0,1},{1,0},{2,3},{3,2},{4,5},{5,4},{6,7},{7,6},{8,9},{9,8},{10,11... | collective-permute-start | bytes 2162696 | tf_op jit(solution)/shard_map/ppermute | solution.py:601
  29.8 7.4 %collective-permute-start.5 = (bf16[4,24,896]{2,1,0:T(8,128)(2,1)S(1)}, bf16[4,24,896]{2,1,0:T(8,128)(2,1)S(1)}, u32[]{:S(2)}, u32[]{:S(2)}) collective-permute-start(bf16[4,24,896]{2,1,0:T(8,128)(2,1)S(1)} %get-tuple-element.76), channel_id=1, source_target_pairs={{0,4},{1,5},{2,6},{3,7},{4,0},{5,1},{6,2},{7,3},{8,12},{9,13},{10,... | collective-permute-start | bytes 516104 | tf_op jit(solution)/shard_map/ppermute | solution.py:625
  32.3 9.4 %collective-permute-start.6 = (bf16[1024,128]{1,0:T(8,128)(2,1)S(1)}, bf16[1024,128]{1,0:T(8,128)(2,1)S(1)}, u32[]{:S(2)}, u32[]{:S(2)}) collective-permute-start(bf16[1024,128]{1,0:T(8,128)(2,1)S(1)} %get-tuple-element.87), channel_id=1, source_target_pairs={{1,2},{3,4},{5,6},{7,8},{9,10},{11,12},{13,14},{2,1},{4,3},{6,5},{... | collective-permute-start | bytes 786440 | tf_op jit(solution)/shard_map/ppermute | solution.py:626
  37.3 8.0 %collective-permute-start.7 = (bf16[24,896]{1,0:T(8,128)(2,1)S(1)}, bf16[24,896]{1,0:T(8,128)(2,1)S(1)}, u32[]{:S(2)}, u32[]{:S(2)}) collective-permute-start(bf16[24,896]{1,0:T(8,128)(2,1)S(1)} %get-tuple-element.91), channel_id=1, source_target_pairs={{0,2},{1,3},{2,0},{3,1},{4,6},{5,7},{6,4},{7,5},{8,10},{9,11},{10,... | collective-permute-start | bytes 129032 | tf_op jit(solution)/shard_map/ppermute | solution.py:644
  39.0 6.3 %collective-permute-start.8 = (bf16[24,896]{1,0:T(8,128)(2,1)S(1)}, bf16[24,896]{1,0:T(8,128)(2,1)S(1)}, u32[]{:S(2)}, u32[]{:S(2)}) collective-permute-start(bf16[24,896]{1,0:T(8,128)(2,1)S(1)} %get-tuple-element.92), channel_id=1, source_target_pairs={{0,8},{1,9},{2,10},{3,11},{4,12},{5,13},{6,14},{7,15},{8,0},{9,1},... | collective-permute-start | bytes 129032 | tf_op jit(solution)/shard_map/ppermute | solution.py:644
  41.6 6.2 %collective-permute-start.9 = (bf16[24,896]{1,0:T(8,128)(2,1)S(1)}, bf16[24,896]{1,0:T(8,128)(2,1)S(1)}, u32[]{:S(2)}, u32[]{:S(2)}) collective-permute-start(bf16[24,896]{1,0:T(8,128)(2,1)S(1)} %get-tuple-element.93), channel_id=1, source_target_pairs={{0,10},{1,11},{2,8},{3,9},{4,14},{5,15},{6,12},{7,13},{8,2},{9,3},... | collective-permute-start | bytes 129032 | tf_op jit(solution)/shard_map/ppermute | solution.py:644

commit v16 on v15

--- a/solution.py
+++ b/solution.py
@@ -216,7 +216,7 @@
         )
 
 
-def back_taps_body(weight, back_taps):
+def back_taps_body(weight, back_taps, turned_taps):
     zero = jnp.zeros((64, 64), BF16)
     for row in range(3):
         for column in range(3):
@@ -227,9 +227,10 @@
                 at = row * 128 + plane * 64
                 for pair in range(2):
                     first = pair * 384 + column * 128
-                    back_taps[at : at + 64, first : first + 128] = jnp.concatenate(
+                    turned_taps[at : at + 64, first : first + 128] = jnp.concatenate(
                         parts[2 * pair : 2 * pair + 2], axis=1
                     )
+    back_taps[...] = turned_taps[...].astype(F32).T.astype(BF16)
 
 
 def hidden_body(
@@ -394,13 +395,16 @@
         kept[at] = total(keep)
 
 
+def others_of(place, places):
+    return [place ^ away for away in [*range(places // 2, places), *range(1, places // 2)]]
+
+
 def spread_body(split_in, owner_bits, me, mine, arrived, kept, *sent):
     place = 0
     for bit in owner_bits:
         place = 2 * place + (me[0] >> bit) % 2
     kept[...] = mine[place] + decoded(arrived[place], split_in)
-    for at, out in enumerate(sent):
-        there = place ^ (at + 1)
+    for there, out in zip(others_of(place, mine.shape[0]), sent):
         out[...] = (mine[there] + decoded(arrived[there], split_in)).astype(BF16)
 
 
@@ -493,7 +497,7 @@
     for at, (start, size) in enumerate(row_blocks(0, output.shape[1])):
         rows = slice(start, start + size + 2 * columns)
         rows = jnp.concatenate([own_windows[rows, :], side_windows[rows, :]], axis=1)
-        terms = lax.dot_general(rows, taps[...], NT, preferred_element_type=F32)
+        terms = jnp.dot(rows, taps[...], preferred_element_type=F32)
         value = terms[:size, :128]
         value = value + terms[columns : columns + size, 128:256]
         value = value + terms[2 * columns : 2 * columns + size, 256:]
@@ -568,7 +572,8 @@
         one_flops, "prepare", (0,), (3,),
     )
     back_taps, = call(
-        back_taps_body, (shape((3 * 128, 768), BF16),), (weight_one,), (), one_flops // 8, "back_taps"
+        back_taps_body, (shape((768, 3 * 128), BF16),), (weight_one,),
+        (pltpu.VMEM((3 * 128, 768), BF16),), one_flops // 8, "back_taps",
     )
     inner, outer, part, back_taps = lax.optimization_barrier((inner, outer, part, back_taps))
     terms_outer = lax.ppermute(outer, "space", across)
@@ -639,8 +644,8 @@
     )
     sent, output, back_windows = lax.optimization_barrier((sent, output, back_windows))
     arrived = []
-    for at, part in enumerate(sent):
-        away = sum(((at + 1) >> i & 1) << bit for i, bit in enumerate(bits[::-1]))
+    for at, part in zip(others_of(0, others + 1), sent):
+        away = sum((at >> i & 1) << bit for i, bit in enumerate(bits[::-1]))
         arrived.append(lax.ppermute(part, "space", [(i, i ^ away) for i in range(count)]))
     grad_windows, = call(
         functools.partial(grad_windows_body, columns), (third,), (me, message, grad_outer),

time: 48.7 us -> 47.6 us (0.977)
  waiting for transfers between devices: 3.92 us -> 2.68 us
    ppermute x3, waiting for transfers between devices: 2.42 us -> 1.18 us  [shards(): lax.ppermute(part, 'space', [(i, i ^ away) for i in range(count)])]
  transfers between devices with their start and end apart: 10 -> 10, of which waited for: 3 -> 3; matrix products, arithmetic and copies ran while one was open for 0% -> 0% of each run, Pallas kernels for 47% -> 48%
where the time goes in v16:
time: 47.6 us; the launch traced here: 47.4 us
  Pallas kernels  27.4 us (58%)
  starting transfers between devices  16.6 us (35%)
  waiting for transfers between devices  2.68 us (6%)
  between operations  0.81 us (2%)
    pallas_call x14, Pallas kernels, call(): pl.pallas_call(body, out_shape=list(outs), in_specs=[pl.BlockSpec(memory_...  27.4 us
    ppermute x3, starting transfers between devices, shards(): lax.ppermute(part, 'space', [(i, i ^ away) for i in range(count)])  4.45 us
    ppermute x1, starting transfers between devices, shards(): terms_inner = lax.ppermute(inner, 'space', within)  3.93 us
    ppermute x1, starting transfers between devices, shards(): message = lax.ppermute(message, 'space', within)  2.93 us
    ppermute x1, starting transfers between devices, shards(): arrived = lax.ppermute(sent, 'space', [(i, i ^ 4) for i in range(count)])  2.52 us
    ppermute x1, waiting for transfers between devices, shards(): arrived = lax.ppermute(sent, 'space', [(i, i ^ 4) for i in range(count)])  1.35 us
    ppermute x3, waiting for transfers between devices, shards(): lax.ppermute(part, 'space', [(i, i ^ away) for i in range(count)])  1.18 us
  transfers between devices with their start and end apart: 10, of which 3 were waited for; matrix products, arithmetic and copies ran while one was open for 0% of the time, Pallas kernels for 48%

profile of v16, /device:TPU:0, one launch (start us, length us, event | category | flops | bytes accessed | tf_op | source)
XLA Modules:
  0.0 47.4 jit_solution(1379708508681829020)
XLA Ops:
  0.6 1.4 %pack_volume.1.own = bf16[2048,128]{1,0:T(8,128)(2,1)S(1)} custom-call(bf16[2,2048,64]{2,1,0:T(8,128)(2,1)} %bitcast.19), custom_call_target="tpu_custom_call" | custom-call | bytes 1048576 | tf_op jit(solution)/shard_map/pack_volume/pallas_call | solution.py:27
  2.0 0.5 %collective-permute-start = (bf16[2048,128]{1,0:T(8,128)(2,1)S(1)}, bf16[2048,128]{1,0:T(8,128)(2,1)S(1)}, u32[]{:S(2)}, u32[]{:S(2)}) collective-permute-start(bf16[2048,128]{1,0:T(8,128)(2,1)S(1)} %pack_volume.1.own), channel_id=1, source_target_pairs={{0,1},{1,0},{2,3},{3,2},{4,5},{5,4},{6,7},{7,6},{8,9},{9,8},{10,11... | collective-permute-start | bytes 1572872 | tf_op jit(solution)/shard_map/ppermute | solution.py:552
  2.6 0.7 %collective-permute-start.1 = (bf16[2048,128]{1,0:T(8,128)(2,1)S(1)}, bf16[2048,128]{1,0:T(8,128)(2,1)S(1)}, u32[]{:S(2)}, u32[]{:S(2)}) collective-permute-start(bf16[2048,128]{1,0:T(8,128)(2,1)S(1)} %pack_volume.1.own), channel_id=1, source_target_pairs={{1,2},{3,4},{5,6},{7,8},{9,10},{11,12},{13,14},{2,1},{4,3},{6,5},{... | collective-permute-start | bytes 1572872 | tf_op jit(solution)/shard_map/ppermute | solution.py:551
  3.2 0.0 copy-start
  3.3 4.6 %grad_act_terms.1 = (f32[2048,128]{1,0:T(8,128)S(1)}, bf16[2048,128]{1,0:T(8,128)(2,1)S(1)}, bf16[1024,128]{1,0:T(8,128)(2,1)S(1)}, bf16[256,2048]{1,0:T(8,128)(2,1)S(1)}) custom-call(s32[1]{0:T(128)} %bitcast.me, bf16[2,2048,128]{2,1,0:T(8,128)(2,1)} %bitcast.20, bf16[27,64,128]{2,1,0:T(8,128)(2,1)} %bitcast.15), custom_call_target="tpu_custom_call" | custom-call | flops 1811939328 | bytes 4374532 | tf_op jit(solution)/shard_map/grad_act_terms/pallas_call | solution.py:27
  7.9 0.4 back_taps.1.taps
  8.2 0.0 collective-permute-done.inner
  8.2 3.7 %prepare.1 = (bf16[2112,384]{1,0:T(8,128)(2,1)S(1)}, bf16[2112,384]{1,0:T(8,128)(2,1)S(1)}, f32[2048,256]{1,0:T(8,128)S(1)}, bf16[1152,256]{1,0:T(8,128)(2,1)S(1)}) custom-call(s32[1]{0:T(128)} %bitcast.me, bf16[2048,128]{1,0:T(8,128)(2,1)S(1)} %pack_volume.1.own, bf16[2048,128]{1,0:T(8,128)(2,1)S(1)} %collective-permute-done.inner, bf16[27,64,64]{2,1,0:T(8,128)(2,1)} %bitcast.13), custom_call_target="tpu_custom_call" | custom-call | flops 905969664 | bytes 7200772 | tf_op jit(solution)/shard_map/prepare/pallas_call | solution.py:27
  12.0 3.9 %collective-permute-start.2 = (bf16[2048,128]{1,0:T(8,128)(2,1)S(1)}, bf16[2048,128]{1,0:T(8,128)(2,1)S(1)}, u32[]{:S(2)}, u32[]{:S(2)}) collective-permute-start(bf16[2048,128]{1,0:T(8,128)(2,1)S(1)} %get-tuple-element.61), channel_id=1, source_target_pairs={{0,1},{1,0},{2,3},{3,2},{4,5},{5,4},{6,7},{7,6},{8,9},{9,8},{10,11... | collective-permute-start | bytes 1572872 | tf_op jit(solution)/shard_map/ppermute | solution.py:580
  15.9 0.8 %collective-permute-start.3 = (bf16[1024,128]{1,0:T(8,128)(2,1)S(1)}, bf16[1024,128]{1,0:T(8,128)(2,1)S(1)}, u32[]{:S(2)}, u32[]{:S(2)}) collective-permute-start(bf16[1024,128]{1,0:T(8,128)(2,1)S(1)} %get-tuple-element.62), channel_id=1, source_target_pairs={{1,2},{3,4},{5,6},{7,8},{9,10},{11,12},{13,14},{2,1},{4,3},{6,5},{... | collective-permute-start | bytes 786440 | tf_op jit(solution)/shard_map/ppermute | solution.py:579
  16.8 0.0 collective-permute-done.1.outer
  16.8 3.5 %hidden.1 = (bf16[2112,768]{1,0:T(8,128)(2,1)S(1)}, f32[2048,128]{1,0:T(8,128)S(1)}, bf16[2112,384]{1,0:T(8,128)(2,1)S(1)}) custom-call(s32[1]{0:T(128)} %bitcast.me, bf16[2048,128]{1,0:T(8,128)(2,1)S(1)} %collective-permute-done.1.outer, f32[2048,256]{1,0:T(8,128)S(1)} %get-tuple-element.56.part, bf16[1152,256]{1,0:T(8,128)(2,1)S(1)} %get-tuple-element.57.outer_taps, ...), custom_call_target="tpu_custom_call" | custom-call | flops 1811939328 | bytes 10747908 | tf_op jit(solution)/shard_map/hidden/pallas_call | solution.py:27
  20.3 2.7 %grad_two_terms.1.other = f32[128,1792]{1,0:T(8,128)S(1)} custom-call(bf16[2112,768]{1,0:T(8,128)(2,1)S(1)} %get-tuple-element.80.act_windows, bf16[256,2048]{1,0:T(8,128)(2,1)S(1)} %get-tuple-element.65.turned), custom_call_target="tpu_custom_call" | custom-call | flops 1811939328 | bytes 5210112 | tf_op jit(solution)/shard_map/grad_two_terms/pallas_call | solution.py:27
  23.0 0.0 collective-permute-done.3.outer
  23.0 0.0 collective-permute-done.2.inner
  23.0 0.0 copy-start.1
  23.0 2.1 %grad_one_terms.1 = (bf16[2048,128]{1,0:T(8,128)(2,1)S(1)}, bf16[1024,128]{1,0:T(8,128)(2,1)S(1)}, bf16[2816,128]{1,0:T(8,128)(2,1)S(1)}, f32[8,24,896]{2,1,0:T(8,128)S(1)}) custom-call(s32[1]{0:T(128)} %bitcast.me, bf16[2112,384]{1,0:T(8,128)(2,1)S(1)} %get-tuple-element.52.own_windows, bf16[2112,384]{1,0:T(8,128)(2,1)S(1)} %get-tuple-element.59.side_windows, ...), custom_call_target="tpu_custom_call" | custom-call | flops 905969664 | bytes 9240580 | tf_op jit(solution)/shard_map/grad_one_terms/pallas_call | solution.py:27
  25.2 2.9 %collective-permute-start.4 = (bf16[2816,128]{1,0:T(8,128)(2,1)S(1)}, bf16[2816,128]{1,0:T(8,128)(2,1)S(1)}, u32[]{:S(2)}, u32[]{:S(2)}) collective-permute-start(bf16[2816,128]{1,0:T(8,128)(2,1)S(1)} %get-tuple-element.67), channel_id=1, source_target_pairs={{0,1},{1,0},{2,3},{3,2},{4,5},{5,4},{6,7},{7,6},{8,9},{9,8},{10,11... | collective-permute-start | bytes 2162696 | tf_op jit(solution)/shard_map/ppermute | solution.py:606
  28.1 1.7 %output_first.1 = (f32[2,2048,128]{2,1,0:T(8,128)}, bf16[2304,256]{1,0:T(8,128)(2,1)S(1)}, bf16[2112,384]{1,0:T(8,128)(2,1)S(1)}) custom-call(bf16[2112,768]{1,0:T(8,128)(2,1)S(1)} %get-tuple-element.80.act_windows, bf16[27,64,128]{2,1,0:T(8,128)(2,1)S(1)} %bitcast.16, bf16[2048,128]{1,0:T(8,128)(2,1)S(1)} %get-tuple-element.68.grad), custom_call_target="tpu_custom_call" | custom-call | flops 1811939328 | bytes 9109504 | tf_op jit(solution)/shard_map/output_first/pallas_call | solution.py:27
  29.8 0.1 collective-permute-done.4.arrived.message
  29.9 0.1 halve.1
  30.0 2.5 %collective-permute-start.5 = (bf16[4,24,896]{2,1,0:T(8,128)(2,1)S(1)}, bf16[4,24,896]{2,1,0:T(8,128)(2,1)S(1)}, u32[]{:S(2)}, u32[]{:S(2)}) collective-permute-start(bf16[4,24,896]{2,1,0:T(8,128)(2,1)S(1)} %get-tuple-element.76), channel_id=1, source_target_pairs={{0,4},{1,5},{2,6},{3,7},{4,0},{5,1},{6,2},{7,3},{8,12},{9,13},{10,... | collective-permute-start | bytes 516104 | tf_op jit(solution)/shard_map/ppermute | solution.py:630
  32.5 0.7 %collective-permute-start.6 = (bf16[1024,128]{1,0:T(8,128)(2,1)S(1)}, bf16[1024,128]{1,0:T(8,128)(2,1)S(1)}, u32[]{:S(2)}, u32[]{:S(2)}) collective-permute-start(bf16[1024,128]{1,0:T(8,128)(2,1)S(1)} %get-tuple-element.87), channel_id=1, source_target_pairs={{1,2},{3,4},{5,6},{7,8},{9,10},{11,12},{13,14},{2,1},{4,3},{6,5},{... | collective-permute-start | bytes 786440 | tf_op jit(solution)/shard_map/ppermute | solution.py:631
  33.2 2.9 %output_rest.1 = f32[2,2048,128]{2,1,0:T(8,128)} custom-call(bf16[2112,768]{1,0:T(8,128)(2,1)S(1)} %get-tuple-element.80.act_windows, bf16[2304,256]{1,0:T(8,128)(2,1)S(1)} %get-tuple-element.81.taps, f32[2,2048,128]{2,1,0:T(8,128)} %get-tuple-element.82.begun), custom_call_target="tpu_custom_call", output_to_operand_aliasing={{}: (2, {})} | custom-call | flops 1811939328 | bytes 8617984 | tf_op jit(solution)/shard_map/output_rest/pallas_call | solution.py:27
  36.1 1.4 %collective-permute-done.5.arrived = bf16[4,24,896]{2,1,0:T(8,128)(2,1)S(1)} collective-permute-done((bf16[4,24,896]{2,1,0:T(8,128)(2,1)S(1)}, bf16[4,24,896]{2,1,0:T(8,128)(2,1)S(1)}, u32[]{:S(2)}, u32[]{:S(2)}) %collective-permute-start.5) | collective-permute-done | bytes 172064 | tf_op jit(solution)/shard_map/ppermute | solution.py:630
  37.5 2.8 %collective-permute-start.7 = (bf16[24,896]{1,0:T(8,128)(2,1)S(1)}, bf16[24,896]{1,0:T(8,128)(2,1)S(1)}, u32[]{:S(2)}, u32[]{:S(2)}) collective-permute-start(bf16[24,896]{1,0:T(8,128)(2,1)S(1)} %get-tuple-element.91), channel_id=1, source_target_pairs={{0,8},{1,9},{2,10},{3,11},{4,12},{5,13},{6,14},{7,15},{8,0},{9,1},... | collective-permute-start | bytes 129032 | tf_op jit(solution)/shard_map/ppermute | solution.py:649
  40.3 1.2 %collective-permute-start.8 = (bf16[24,896]{1,0:T(8,128)(2,1)S(1)}, bf16[24,896]{1,0:T(8,128)(2,1)S(1)}, u32[]{:S(2)}, u32[]{:S(2)}) collective-permute-start(bf16[24,896]{1,0:T(8,128)(2,1)S(1)} %get-tuple-element.92), channel_id=1, source_target_pairs={{0,10},{1,11},{2,8},{3,9},{4,14},{5,15},{6,12},{7,13},{8,2},{9,3},... | collective-permute-start | bytes 129032 | tf_op jit(solution)/shard_map/ppermute | solution.py:649
  41.5 0.4 collective-permute-start.9
  41.9 0.6 %grad_windows.1.side_windows = bf16[2112,384]{1,0:T(8,128)(2,1)S(1)} custom-call(s32[1]{0:T(128)} %bitcast.me, bf16[2816,128]{1,0:T(8,128)(2,1)S(1)} %collective-permute-done.4.arrived.message, bf16[1024,128]{1,0:T(8,128)(2,1)S(1)} %collective-permute-done.6.outer), custom_call_target="tpu_custom_call" | custom-call | flops 226492416 | bytes 2605060 | tf_op jit(solution)/shard_map/grad_windows/pallas_call | solution.py:27
  42.6 2.9 %grad_volume.1 = f32[2,2048,64]{2,1,0:T(8,128)} custom-call(bf16[2112,384]{1,0:T(8,128)(2,1)S(1)} %get-tuple-element.86.own_windows, bf16[2112,384]{1,0:T(8,128)(2,1)S(1)} %grad_windows.1.side_windows, bf16[768,384]{1,0:T(8,128)(2,1)S(1)} %back_taps.1.taps), custom_call_target="tpu_custom_call" | custom-call | flops 905969664 | bytes 4882432 | tf_op jit(solution)/shard_map/grad_volume/pallas_call | solution.py:27
  45.5 1.2 %collective-permute-done.8.refs_1_ = bf16[24,896]{1,0:T(8,128)(2,1)S(1)} collective-permute-done((bf16[24,896]{1,0:T(8,128)(2,1)S(1)}, bf16[24,896]{1,0:T(8,128)(2,1)S(1)}, u32[]{:S(2)}, u32[]{:S(2)}) %collective-permute-start.8) | collective-permute-done | bytes 43040 | tf_op jit(solution)/shard_map/ppermute | solution.py:649
  46.7 0.7 %finish.1 = (f32[27,4,64]{2,1,0:T(4,128)}, f32[27,8,64]{2,1,0:T(8,128)}) custom-call(f32[24,896]{1,0:T(8,128)S(1)} %get-tuple-element.90.mine, bf16[24,896]{1,0:T(8,128)(2,1)S(1)} %collective-permute-done.7.refs_0_, bf16[24,896]{1,0:T(8,128)(2,1)S(1)} %collective-permute-done.8.refs_1_, bf16[24,896]{1,0:T(8,128)(2,1)S(1)} %collective-permute-done.9.refs_2_), custom_call_target="tpu_custom_call" | custom-call | bytes 297984 | tf_op jit(solution)/shard_map/finish/pallas_call | solution.py:27
  (6 shorter events, 0.1 us)
Async XLA Ops:
  2.0 6.2 %collective-permute-start = (bf16[2048,128]{1,0:T(8,128)(2,1)S(1)}, bf16[2048,128]{1,0:T(8,128)(2,1)S(1)}, u32[]{:S(2)}, u32[]{:S(2)}) collective-permute-start(bf16[2048,128]{1,0:T(8,128)(2,1)S(1)} %pack_volume.1.own), channel_id=1, source_target_pairs={{0,1},{1,0},{2,3},{3,2},{4,5},{5,4},{6,7},{7,6},{8,9},{9,8},{10,11... | collective-permute-start | bytes 1572872 | tf_op jit(solution)/shard_map/ppermute | solution.py:552
  2.6 14.2 %collective-permute-start.1 = (bf16[2048,128]{1,0:T(8,128)(2,1)S(1)}, bf16[2048,128]{1,0:T(8,128)(2,1)S(1)}, u32[]{:S(2)}, u32[]{:S(2)}) collective-permute-start(bf16[2048,128]{1,0:T(8,128)(2,1)S(1)} %pack_volume.1.own), channel_id=1, source_target_pairs={{1,2},{3,4},{5,6},{7,8},{9,10},{11,12},{13,14},{2,1},{4,3},{6,5},{... | collective-permute-start | bytes 1572872 | tf_op jit(solution)/shard_map/ppermute | solution.py:551
  3.2 4.6 %copy-start = (bf16[3,3,3,64,64]{4,3,2,1,0:T(8,128)(2,1)S(1)}, bf16[3,3,3,64,64]{4,3,2,1,0:T(8,128)(2,1)}, u32[]{:S(2)}) copy-start(bf16[3,3,3,64,64]{4,3,2,1,0:T(8,128)(2,1)} %param.5) | copy-start | bytes 663556
  12.0 11.0 %collective-permute-start.2 = (bf16[2048,128]{1,0:T(8,128)(2,1)S(1)}, bf16[2048,128]{1,0:T(8,128)(2,1)S(1)}, u32[]{:S(2)}, u32[]{:S(2)}) collective-permute-start(bf16[2048,128]{1,0:T(8,128)(2,1)S(1)} %get-tuple-element.61), channel_id=1, source_target_pairs={{0,1},{1,0},{2,3},{3,2},{4,5},{5,4},{6,7},{7,6},{8,9},{9,8},{10,11... | collective-permute-start | bytes 1572872 | tf_op jit(solution)/shard_map/ppermute | solution.py:580
  15.9 7.1 %collective-permute-start.3 = (bf16[1024,128]{1,0:T(8,128)(2,1)S(1)}, bf16[1024,128]{1,0:T(8,128)(2,1)S(1)}, u32[]{:S(2)}, u32[]{:S(2)}) collective-permute-start(bf16[1024,128]{1,0:T(8,128)(2,1)S(1)} %get-tuple-element.62), channel_id=1, source_target_pairs={{1,2},{3,4},{5,6},{7,8},{9,10},{11,12},{13,14},{2,1},{4,3},{6,5},{... | collective-permute-start | bytes 786440 | tf_op jit(solution)/shard_map/ppermute | solution.py:579
  23.0 5.1 %copy-start.1 = (bf16[3,3,3,64,128]{4,3,2,1,0:T(8,128)(2,1)S(1)}, bf16[3,3,3,64,128]{4,3,2,1,0:T(8,128)(2,1)}, u32[]{:S(2)}) copy-start(bf16[3,3,3,64,128]{4,3,2,1,0:T(8,128)(2,1)} %param.6) | copy-start | bytes 1327108
  25.2 4.8 %collective-permute-start.4 = (bf16[2816,128]{1,0:T(8,128)(2,1)S(1)}, bf16[2816,128]{1,0:T(8,128)(2,1)S(1)}, u32[]{:S(2)}, u32[]{:S(2)}) collective-permute-start(bf16[2816,128]{1,0:T(8,128)(2,1)S(1)} %get-tuple-element.67), channel_id=1, source_target_pairs={{0,1},{1,0},{2,3},{3,2},{4,5},{5,4},{6,7},{7,6},{8,9},{9,8},{10,11... | collective-permute-start | bytes 2162696 | tf_op jit(solution)/shard_map/ppermute | solution.py:606
  30.0 7.4 %collective-permute-start.5 = (bf16[4,24,896]{2,1,0:T(8,128)(2,1)S(1)}, bf16[4,24,896]{2,1,0:T(8,128)(2,1)S(1)}, u32[]{:S(2)}, u32[]{:S(2)}) collective-permute-start(bf16[4,24,896]{2,1,0:T(8,128)(2,1)S(1)} %get-tuple-element.76), channel_id=1, source_target_pairs={{0,4},{1,5},{2,6},{3,7},{4,0},{5,1},{6,2},{7,3},{8,12},{9,13},{10,... | collective-permute-start | bytes 516104 | tf_op jit(solution)/shard_map/ppermute | solution.py:630
  32.5 9.4 %collective-permute-start.6 = (bf16[1024,128]{1,0:T(8,128)(2,1)S(1)}, bf16[1024,128]{1,0:T(8,128)(2,1)S(1)}, u32[]{:S(2)}, u32[]{:S(2)}) collective-permute-start(bf16[1024,128]{1,0:T(8,128)(2,1)S(1)} %get-tuple-element.87), channel_id=1, source_target_pairs={{1,2},{3,4},{5,6},{7,8},{9,10},{11,12},{13,14},{2,1},{4,3},{6,5},{... | collective-permute-start | bytes 786440 | tf_op jit(solution)/shard_map/ppermute | solution.py:631
  37.5 8.0 %collective-permute-start.7 = (bf16[24,896]{1,0:T(8,128)(2,1)S(1)}, bf16[24,896]{1,0:T(8,128)(2,1)S(1)}, u32[]{:S(2)}, u32[]{:S(2)}) collective-permute-start(bf16[24,896]{1,0:T(8,128)(2,1)S(1)} %get-tuple-element.91), channel_id=1, source_target_pairs={{0,8},{1,9},{2,10},{3,11},{4,12},{5,13},{6,14},{7,15},{8,0},{9,1},... | collective-permute-start | bytes 129032 | tf_op jit(solution)/shard_map/ppermute | solution.py:649
  40.3 6.4 %collective-permute-start.8 = (bf16[24,896]{1,0:T(8,128)(2,1)S(1)}, bf16[24,896]{1,0:T(8,128)(2,1)S(1)}, u32[]{:S(2)}, u32[]{:S(2)}) collective-permute-start(bf16[24,896]{1,0:T(8,128)(2,1)S(1)} %get-tuple-element.92), channel_id=1, source_target_pairs={{0,10},{1,11},{2,8},{3,9},{4,14},{5,15},{6,12},{7,13},{8,2},{9,3},... | collective-permute-start | bytes 129032 | tf_op jit(solution)/shard_map/ppermute | solution.py:649
  41.5 5.1 %collective-permute-start.9 = (bf16[24,896]{1,0:T(8,128)(2,1)S(1)}, bf16[24,896]{1,0:T(8,128)(2,1)S(1)}, u32[]{:S(2)}, u32[]{:S(2)}) collective-permute-start(bf16[24,896]{1,0:T(8,128)(2,1)S(1)} %get-tuple-element.93), channel_id=1, source_target_pairs={{0,2},{1,3},{2,0},{3,1},{4,6},{5,7},{6,4},{7,5},{8,10},{9,11},{10,... | collective-permute-start | bytes 129032 | tf_op jit(solution)/shard_map/ppermute | solution.py:649

commit v17 on v16

--- a/solution.py
+++ b/solution.py
@@ -216,7 +216,7 @@
         )
 
 
-def back_taps_body(weight, back_taps, turned_taps):
+def layouts_body(weight, weight_two, back_taps, out_taps, turned_taps):
     zero = jnp.zeros((64, 64), BF16)
     for row in range(3):
         for column in range(3):
@@ -231,6 +231,14 @@
                         parts[2 * pair : 2 * pair + 2], axis=1
                     )
     back_taps[...] = turned_taps[...].astype(F32).T.astype(BF16)
+    for tap in range(9):
+        for at, source in enumerate(PLANES):
+            first = tap * 256 + at * 64
+            for plane in range(2):
+                depth = depth_tap(source, plane)
+                out_taps[first : first + 64, plane * 128 : plane * 128 + 128] = (
+                    jnp.zeros((64, 128), BF16) if depth is None else weight_two[depth * 9 + tap]
+                )
 
 
 def hidden_body(
@@ -292,14 +300,17 @@
         target[first : first + chunk.shape[1], start : start + STEP] = chunk.T.astype(BF16)
 
 
-def grad_two_body(columns, act_windows, turned, terms):
+def grad_two_body(columns, blocks, act_windows, turned, taps, terms, far, output, sems):
     cells = turned.shape[1]
+    copies = output_rows(columns, blocks, act_windows, taps, far, output, sems)
 
     def slices(row, column):
         rows = slice(row * columns, row * columns + cells)
         return act_windows[rows, column * 256 : column * 256 + 256]
 
     kernel_terms(columns, 128, slices, turned, terms)
+    for copy in copies:
+        copy.wait()
 
 
 def coded(value, split):
@@ -443,19 +454,8 @@
 
 
 def output_first_body(
-    columns, blocks, act_windows, weight, grad, far, taps, own_windows, output, sems
+    columns, blocks, act_windows, taps, grad, begun, far, own_windows, output, sems
 ):
-    for row in range(3):
-        for column in range(3):
-            for at, source in enumerate(PLANES):
-                first = row * 768 + column * 256 + at * 64
-                for plane in range(2):
-                    depth = depth_tap(source, plane)
-                    taps[first : first + 64, plane * 128 : plane * 128 + 128] = (
-                        jnp.zeros((64, 128), BF16)
-                        if depth is None
-                        else weight[depth * 9 + row * 3 + column]
-                    )
     copies = output_rows(columns, blocks, act_windows, taps, far, output, sems)
 
     def fill(i, carry):
@@ -475,7 +475,9 @@
         copy.wait()
 
 
-def grad_windows_body(columns, me, message, outer, windows):
+def grad_volume_body(
+    columns, me, own_windows, message, outer, taps, far, side_windows, output, sems
+):
     half = outer.shape[0]
     odd = me[0] % 2 == 1
     before = message.shape[0] - half
@@ -485,14 +487,11 @@
         near = message[pl.ds(before + start, STEP), :].astype(F32)
         below, above = by_side(odd, near, outer[pl.ds(start, STEP), :].astype(F32))
         for first, side in zip((start, start + half), unpacked(above, below)):
-            fill_windows(windows, first, 0, side, columns, 128)
+            fill_windows(side_windows, first, 0, side, columns, 128)
         return carry
 
-    clear_edges(windows, columns)
+    clear_edges(side_windows, columns)
     lax.fori_loop(0, half // STEP, fill, 0)
-
-
-def grad_volume_body(columns, own_windows, side_windows, taps, far, output, sems):
     copies = []
     for at, (start, size) in enumerate(row_blocks(0, output.shape[1])):
         rows = slice(start, start + size + 2 * columns)
@@ -571,11 +570,13 @@
         (pltpu.VMEM((2 * 9 * 128, 256), BF16), pltpu.VMEM(weight_one.shape, BF16), dma),
         one_flops, "prepare", (0,), (3,),
     )
-    back_taps, = call(
-        back_taps_body, (shape((768, 3 * 128), BF16),), (weight_one,),
-        (pltpu.VMEM((3 * 128, 768), BF16),), one_flops // 8, "back_taps",
-    )
-    inner, outer, part, back_taps = lax.optimization_barrier((inner, outer, part, back_taps))
+    back_taps, out_taps = call(
+        layouts_body, (shape((768, 3 * 128), BF16), shape((9 * 256, 256), BF16)),
+        (weight_one, weight_two), (pltpu.VMEM((3 * 128, 768), BF16),), one_flops // 8, "layouts",
+    )
+    inner, outer, part, back_taps, out_taps = lax.optimization_barrier(
+        (inner, outer, part, back_taps, out_taps)
+    )
     terms_outer = lax.ppermute(outer, "space", across)
     terms_inner = lax.ppermute(inner, "space", within)
     act_windows, slope, side_windows = call(
@@ -584,10 +585,16 @@
         (me, vol_outer, part, outer_taps, inner_windows),
         (pltpu.VMEM((slab[0], 384), BF16),), 2 * one_flops, "hidden", (0,),
     )
-    terms_two, = call(
-        functools.partial(grad_two_body, columns),
-        (shape((wide, 2 * lanes), F32),),
-        (act_windows, turned), (), two_flops, "grad_two_terms",
+    half = cells // 2
+    early, middle = [(0, BLOCK)], [(BLOCK, BLOCK), (half, BLOCK // 2)]
+    late = [(half + BLOCK // 2, BLOCK), (cells - BLOCK // 2, BLOCK // 2)]
+    whole = shape((planes, cells, wide), F32)
+    terms_two, output = call(
+        functools.partial(grad_two_body, columns, early),
+        (shape((wide, 2 * lanes), F32), whole),
+        (act_windows, turned, out_taps),
+        (pltpu.VMEM((planes, BLOCK, wide), F32), dma((1,))),
+        two_flops, "grad_two_terms", (), (), (1,),
     )
     groups = lanes // 128
     grad_hidden, outer, message, kept = call(
@@ -604,17 +611,14 @@
         one_flops, "grad_one_terms", (0,),
     )
     message = lax.ppermute(message, "space", within)
-    rest = row_blocks(BLOCK, cells)
-    output, out_taps, back_windows = call(
-        functools.partial(output_first_body, columns, [(0, BLOCK)]),
-        (shape((planes, cells, wide), F32), shape((9 * 256, 256), BF16), third),
-        (act_windows, weight_two, grad_hidden),
-        (pltpu.VMEM((planes, BLOCK, wide), F32), dma((1,))),
-        two_flops, "output_first", (), (), (0,),
-    )
-    message, output, out_taps, back_windows = lax.optimization_barrier(
-        (message, output, out_taps, back_windows)
-    )
+    output, back_windows = call(
+        functools.partial(output_first_body, columns, middle),
+        (whole, third),
+        (act_windows, out_taps, grad_hidden, output),
+        (pltpu.VMEM((planes, BLOCK + BLOCK // 2, wide), F32), dma((2,))),
+        two_flops, "output_first", (), (3,), (0,), {3: 0},
+    )
+    message, output, back_windows = lax.optimization_barrier((message, output, back_windows))
     def halve(bits, bit, split_in, split_out, kept, arrived):
         left = 2 ** (len(bits) - 1)
         sent, kept = call(
@@ -630,10 +634,10 @@
     arrived = lax.ppermute(sent, "space", [(i, i ^ 4) for i in range(count)])
     grad_outer = lax.ppermute(outer, "space", across)
     output, = call(
-        functools.partial(output_rest_body, columns, rest),
-        (shape((planes, cells, wide), F32),),
+        functools.partial(output_rest_body, columns, late),
+        (whole,),
         (act_windows, out_taps, output),
-        (pltpu.VMEM((planes, cells - BLOCK, wide), F32), dma((len(rest),))),
+        (pltpu.VMEM((planes, BLOCK + BLOCK // 2, wide), F32), dma((2,))),
         two_flops, "output_rest", (), (2,), (0,), {2: 0},
     )
     others = 2 ** len(bits) - 1
@@ -647,16 +651,15 @@
     for at, part in zip(others_of(0, others + 1), sent):
         away = sum((at >> i & 1) << bit for i, bit in enumerate(bits[::-1]))
         arrived.append(lax.ppermute(part, "space", [(i, i ^ away) for i in range(count)]))
-    grad_windows, = call(
-        functools.partial(grad_windows_body, columns), (third,), (me, message, grad_outer),
-        (), one_flops // 4, "grad_windows", (0,),
-    )
     grad_volume, = call(
         functools.partial(grad_volume_body, columns),
         (shape((planes, cells, channels), F32),),
-        (back_windows, grad_windows, back_taps),
-        (pltpu.VMEM((planes, cells, channels), F32), dma((cells // BLOCK + 1,))),
-        one_flops, "grad_volume", (), (), (0,),
+        (me, back_windows, message, grad_outer, back_taps),
+        (
+            pltpu.VMEM((slab[0], 384), BF16), pltpu.VMEM((planes, cells, channels), F32),
+            dma((cells // BLOCK + 1,)),
+        ),
+        one_flops, "grad_volume", (0,), (), (0,),
     )
     mine, grad_volume = lax.optimization_barrier((mine, grad_volume))
     grad_one, grad_two = call(

time: 47.6 us -> 48 us (level); the launches traced: 47.4 us -> 47.1 us
  starting transfers between devices: 16.6 us -> 16 us
    ppermute x1, waiting for transfers between devices: 1.35 us -> 2.07 us  [shards(): arrived = lax.ppermute(sent, 'space', [(i, i ^ 4) for i in range(count)])]
    ppermute x3, waiting for transfers between devices: 1.18 us -> 0.65 us  [shards(): lax.ppermute(part, 'space', [(i, i ^ away) for i in range(count)])]
    ppermute x1, starting transfers between devices: 2.52 us -> 2.01 us  [shards(): arrived = lax.ppermute(sent, 'space', [(i, i ^ 4) for i in range(count)])]
    pallas_call x14 -> x13, Pallas kernels: 27.4 us -> 27.5 us  [call(): pl.pallas_call(body, out_shape=list(outs), in_specs=[pl.BlockSpec(memory_...]
  transfers between devices with their start and end apart: 10 -> 10, of which waited for: 3 -> 2; matrix products, arithmetic and copies ran while one was open for 0% -> 0% of each run, Pallas kernels for 48% -> 49%
where the time goes in v17:
time: 48 us; the launch traced here: 47.1 us
  Pallas kernels  27.5 us (57%)
  starting transfers between devices  16 us (33%)
  waiting for transfers between devices  2.73 us (6%)
  between operations  0.82 us (2%)
    pallas_call x13, Pallas kernels, call(): pl.pallas_call(body, out_shape=list(outs), in_specs=[pl.BlockSpec(memory_...  27.5 us
    ppermute x3, starting transfers between devices, shards(): lax.ppermute(part, 'space', [(i, i ^ away) for i in range(count)])  4.45 us
    ppermute x1, starting transfers between devices, shards(): terms_inner = lax.ppermute(inner, 'space', within)  3.93 us
    ppermute x1, starting transfers between devices, shards(): message = lax.ppermute(message, 'space', within)  2.93 us
    ppermute x1, waiting for transfers between devices, shards(): arrived = lax.ppermute(sent, 'space', [(i, i ^ 4) for i in range(count)])  2.07 us
    ppermute x1, starting transfers between devices, shards(): arrived = lax.ppermute(sent, 'space', [(i, i ^ 4) for i in range(count)])  2.01 us
  transfers between devices with their start and end apart: 10, of which 2 were waited for; matrix products, arithmetic and copies ran while one was open for 0% of the time, Pallas kernels for 49%

profile of v17, /device:TPU:0, one launch (start us, length us, event | category | flops | bytes accessed | tf_op | source)
XLA Modules:
  0.0 47.1 jit_solution(15957993567153223311)
XLA Ops:
  0.6 1.4 %pack_volume.1.own = bf16[2048,128]{1,0:T(8,128)(2,1)S(1)} custom-call(bf16[2,2048,64]{2,1,0:T(8,128)(2,1)} %bitcast.19), custom_call_target="tpu_custom_call" | custom-call | bytes 1048576 | tf_op jit(solution)/shard_map/pack_volume/pallas_call | solution.py:27
  2.0 0.5 %collective-permute-start = (bf16[2048,128]{1,0:T(8,128)(2,1)S(1)}, bf16[2048,128]{1,0:T(8,128)(2,1)S(1)}, u32[]{:S(2)}, u32[]{:S(2)}) collective-permute-start(bf16[2048,128]{1,0:T(8,128)(2,1)S(1)} %pack_volume.1.own), channel_id=1, source_target_pairs={{0,1},{1,0},{2,3},{3,2},{4,5},{5,4},{6,7},{7,6},{8,9},{9,8},{10,11... | collective-permute-start | bytes 1572872 | tf_op jit(solution)/shard_map/ppermute | solution.py:551
  2.6 0.7 %collective-permute-start.1 = (bf16[2048,128]{1,0:T(8,128)(2,1)S(1)}, bf16[2048,128]{1,0:T(8,128)(2,1)S(1)}, u32[]{:S(2)}, u32[]{:S(2)}) collective-permute-start(bf16[2048,128]{1,0:T(8,128)(2,1)S(1)} %pack_volume.1.own), channel_id=1, source_target_pairs={{1,2},{3,4},{5,6},{7,8},{9,10},{11,12},{13,14},{2,1},{4,3},{6,5},{... | collective-permute-start | bytes 1572872 | tf_op jit(solution)/shard_map/ppermute | solution.py:550
  3.2 0.0 copy-start
  3.3 0.0 copy-start.1
  3.3 4.6 %grad_act_terms.1 = (f32[2048,128]{1,0:T(8,128)S(1)}, bf16[2048,128]{1,0:T(8,128)(2,1)S(1)}, bf16[1024,128]{1,0:T(8,128)(2,1)S(1)}, bf16[256,2048]{1,0:T(8,128)(2,1)S(1)}) custom-call(s32[1]{0:T(128)} %bitcast.me, bf16[2,2048,128]{2,1,0:T(8,128)(2,1)} %bitcast.20, bf16[27,64,128]{2,1,0:T(8,128)(2,1)} %bitcast.13), custom_call_target="tpu_custom_call" | custom-call | flops 1811939328 | bytes 4374532 | tf_op jit(solution)/shard_map/grad_act_terms/pallas_call | solution.py:27
  7.9 0.5 %layouts.1 = (bf16[768,384]{1,0:T(8,128)(2,1)S(1)}, bf16[2304,256]{1,0:T(8,128)(2,1)S(1)}) custom-call(bf16[27,64,64]{2,1,0:T(8,128)(2,1)S(1)} %bitcast.16, bf16[27,64,128]{2,1,0:T(8,128)(2,1)S(1)} %bitcast.14), custom_call_target="tpu_custom_call" | custom-call | flops 113246208 | bytes 2433024 | tf_op jit(solution)/shard_map/layouts/pallas_call | solution.py:27
  8.4 0.0 collective-permute-done.inner
  8.4 3.7 %prepare.1 = (bf16[2112,384]{1,0:T(8,128)(2,1)S(1)}, bf16[2112,384]{1,0:T(8,128)(2,1)S(1)}, f32[2048,256]{1,0:T(8,128)S(1)}, bf16[1152,256]{1,0:T(8,128)(2,1)S(1)}) custom-call(s32[1]{0:T(128)} %bitcast.me, bf16[2048,128]{1,0:T(8,128)(2,1)S(1)} %pack_volume.1.own, bf16[2048,128]{1,0:T(8,128)(2,1)S(1)} %collective-permute-done.inner, bf16[27,64,64]{2,1,0:T(8,128)(2,1)} %bitcast.15), custom_call_target="tpu_custom_call" | custom-call | flops 905969664 | bytes 7200772 | tf_op jit(solution)/shard_map/prepare/pallas_call | solution.py:27
  12.1 3.9 %collective-permute-start.2 = (bf16[2048,128]{1,0:T(8,128)(2,1)S(1)}, bf16[2048,128]{1,0:T(8,128)(2,1)S(1)}, u32[]{:S(2)}, u32[]{:S(2)}) collective-permute-start(bf16[2048,128]{1,0:T(8,128)(2,1)S(1)} %get-tuple-element.66), channel_id=1, source_target_pairs={{0,1},{1,0},{2,3},{3,2},{4,5},{5,4},{6,7},{7,6},{8,9},{9,8},{10,11... | collective-permute-start | bytes 1572872 | tf_op jit(solution)/shard_map/ppermute | solution.py:581
  16.1 0.8 %collective-permute-start.3 = (bf16[1024,128]{1,0:T(8,128)(2,1)S(1)}, bf16[1024,128]{1,0:T(8,128)(2,1)S(1)}, u32[]{:S(2)}, u32[]{:S(2)}) collective-permute-start(bf16[1024,128]{1,0:T(8,128)(2,1)S(1)} %get-tuple-element.67), channel_id=1, source_target_pairs={{1,2},{3,4},{5,6},{7,8},{9,10},{11,12},{13,14},{2,1},{4,3},{6,5},{... | collective-permute-start | bytes 786440 | tf_op jit(solution)/shard_map/ppermute | solution.py:580
  16.9 0.0 collective-permute-done.1.outer
  16.9 3.5 %hidden.1 = (bf16[2112,768]{1,0:T(8,128)(2,1)S(1)}, f32[2048,128]{1,0:T(8,128)S(1)}, bf16[2112,384]{1,0:T(8,128)(2,1)S(1)}) custom-call(s32[1]{0:T(128)} %bitcast.me, bf16[2048,128]{1,0:T(8,128)(2,1)S(1)} %collective-permute-done.1.outer, f32[2048,256]{1,0:T(8,128)S(1)} %get-tuple-element.61.part, bf16[1152,256]{1,0:T(8,128)(2,1)S(1)} %get-tuple-element.62.outer_taps, ...), custom_call_target="tpu_custom_call" | custom-call | flops 1811939328 | bytes 10747908 | tf_op jit(solution)/shard_map/hidden/pallas_call | solution.py:27
  20.4 3.3 %grad_two_terms.1 = (f32[128,1792]{1,0:T(8,128)S(1)}, f32[2,2048,128]{2,1,0:T(8,128)}) custom-call(bf16[2112,768]{1,0:T(8,128)(2,1)S(1)} %get-tuple-element.87.act_windows, bf16[256,2048]{1,0:T(8,128)(2,1)S(1)} %get-tuple-element.70.turned, bf16[2304,256]{1,0:T(8,128)(2,1)S(1)} %get-tuple-element.71.taps), custom_call_target="tpu_custom_call" | custom-call | flops 1811939328 | bytes 8486912 | tf_op jit(solution)/shard_map/grad_two_terms/pallas_call | solution.py:27
  23.8 0.0 collective-permute-done.2.inner
  23.8 2.1 %grad_one_terms.1 = (bf16[2048,128]{1,0:T(8,128)(2,1)S(1)}, bf16[1024,128]{1,0:T(8,128)(2,1)S(1)}, bf16[2816,128]{1,0:T(8,128)(2,1)S(1)}, f32[8,24,896]{2,1,0:T(8,128)S(1)}) custom-call(s32[1]{0:T(128)} %bitcast.me, bf16[2112,384]{1,0:T(8,128)(2,1)S(1)} %get-tuple-element.55.own_windows, bf16[2112,384]{1,0:T(8,128)(2,1)S(1)} %get-tuple-element.64.side_windows, ...), custom_call_target="tpu_custom_call" | custom-call | flops 905969664 | bytes 9240580 | tf_op jit(solution)/shard_map/grad_one_terms/pallas_call | solution.py:27
  25.9 2.9 %collective-permute-start.4 = (bf16[2816,128]{1,0:T(8,128)(2,1)S(1)}, bf16[2816,128]{1,0:T(8,128)(2,1)S(1)}, u32[]{:S(2)}, u32[]{:S(2)}) collective-permute-start(bf16[2816,128]{1,0:T(8,128)(2,1)S(1)} %get-tuple-element.74), channel_id=1, source_target_pairs={{0,1},{1,0},{2,3},{3,2},{4,5},{5,4},{6,7},{7,6},{8,9},{9,8},{10,11... | collective-permute-start | bytes 2162696 | tf_op jit(solution)/shard_map/ppermute | solution.py:613
  28.9 2.0 %output_first.1 = (f32[2,2048,128]{2,1,0:T(8,128)}, bf16[2112,384]{1,0:T(8,128)(2,1)S(1)}) custom-call(bf16[2112,768]{1,0:T(8,128)(2,1)S(1)} %get-tuple-element.87.act_windows, bf16[2304,256]{1,0:T(8,128)(2,1)S(1)} %get-tuple-element.71.taps, bf16[2048,128]{1,0:T(8,128)(2,1)S(1)} %get-tuple-element.75.grad, ...), custom_call_target="tpu_custom_call", output_to_operand_aliasing={{0}: (3, {})} | custom-call | flops 1811939328 | bytes 10764288 | tf_op jit(solution)/shard_map/output_first/pallas_call | solution.py:27
  30.9 0.0 collective-permute-done.4.arrived.message
  30.9 0.1 halve.1
  31.0 2.0 %collective-permute-start.5 = (bf16[4,24,896]{2,1,0:T(8,128)(2,1)S(1)}, bf16[4,24,896]{2,1,0:T(8,128)(2,1)S(1)}, u32[]{:S(2)}, u32[]{:S(2)}) collective-permute-start(bf16[4,24,896]{2,1,0:T(8,128)(2,1)S(1)} %get-tuple-element.83), channel_id=1, source_target_pairs={{0,4},{1,5},{2,6},{3,7},{4,0},{5,1},{6,2},{7,3},{8,12},{9,13},{10,... | collective-permute-start | bytes 516104 | tf_op jit(solution)/shard_map/ppermute | solution.py:634
  33.0 0.7 %collective-permute-start.6 = (bf16[1024,128]{1,0:T(8,128)(2,1)S(1)}, bf16[1024,128]{1,0:T(8,128)(2,1)S(1)}, u32[]{:S(2)}, u32[]{:S(2)}) collective-permute-start(bf16[1024,128]{1,0:T(8,128)(2,1)S(1)} %get-tuple-element.93), channel_id=1, source_target_pairs={{1,2},{3,4},{5,6},{7,8},{9,10},{11,12},{13,14},{2,1},{4,3},{6,5},{... | collective-permute-start | bytes 786440 | tf_op jit(solution)/shard_map/ppermute | solution.py:635
  33.6 2.0 %output_rest.1 = f32[2,2048,128]{2,1,0:T(8,128)} custom-call(bf16[2112,768]{1,0:T(8,128)(2,1)S(1)} %get-tuple-element.87.act_windows, bf16[2304,256]{1,0:T(8,128)(2,1)S(1)} %get-tuple-element.71.taps, f32[2,2048,128]{2,1,0:T(8,128)} %get-tuple-element.88.begun), custom_call_target="tpu_custom_call", output_to_operand_aliasing={{}: (2, {})} | custom-call | flops 1811939328 | bytes 8617984 | tf_op jit(solution)/shard_map/output_rest/pallas_call | solution.py:27
  35.6 2.1 %collective-permute-done.5.arrived = bf16[4,24,896]{2,1,0:T(8,128)(2,1)S(1)} collective-permute-done((bf16[4,24,896]{2,1,0:T(8,128)(2,1)S(1)}, bf16[4,24,896]{2,1,0:T(8,128)(2,1)S(1)}, u32[]{:S(2)}, u32[]{:S(2)}) %collective-permute-start.5) | collective-permute-done | bytes 172064 | tf_op jit(solution)/shard_map/ppermute | solution.py:634
  37.7 2.8 %collective-permute-start.7 = (bf16[24,896]{1,0:T(8,128)(2,1)S(1)}, bf16[24,896]{1,0:T(8,128)(2,1)S(1)}, u32[]{:S(2)}, u32[]{:S(2)}) collective-permute-start(bf16[24,896]{1,0:T(8,128)(2,1)S(1)} %get-tuple-element.97), channel_id=1, source_target_pairs={{0,8},{1,9},{2,10},{3,11},{4,12},{5,13},{6,14},{7,15},{8,0},{9,1},... | collective-permute-start | bytes 129032 | tf_op jit(solution)/shard_map/ppermute | solution.py:653
  40.6 1.1 %collective-permute-start.8 = (bf16[24,896]{1,0:T(8,128)(2,1)S(1)}, bf16[24,896]{1,0:T(8,128)(2,1)S(1)}, u32[]{:S(2)}, u32[]{:S(2)}) collective-permute-start(bf16[24,896]{1,0:T(8,128)(2,1)S(1)} %get-tuple-element.98), channel_id=1, source_target_pairs={{0,10},{1,11},{2,8},{3,9},{4,14},{5,15},{6,12},{7,13},{8,2},{9,3},... | collective-permute-start | bytes 129032 | tf_op jit(solution)/shard_map/ppermute | solution.py:653
  41.7 0.5 %collective-permute-start.9 = (bf16[24,896]{1,0:T(8,128)(2,1)S(1)}, bf16[24,896]{1,0:T(8,128)(2,1)S(1)}, u32[]{:S(2)}, u32[]{:S(2)}) collective-permute-start(bf16[24,896]{1,0:T(8,128)(2,1)S(1)} %get-tuple-element.99), channel_id=1, source_target_pairs={{0,2},{1,3},{2,0},{3,1},{4,6},{5,7},{6,4},{7,5},{8,10},{9,11},{10,... | collective-permute-start | bytes 129032 | tf_op jit(solution)/shard_map/ppermute | solution.py:653
  42.2 0.0 collective-permute-done.6.outer
  42.2 3.5 %grad_volume.1 = f32[2,2048,64]{2,1,0:T(8,128)} custom-call(s32[1]{0:T(128)} %bitcast.me, bf16[2112,384]{1,0:T(8,128)(2,1)S(1)} %get-tuple-element.92.own_windows, bf16[2816,128]{1,0:T(8,128)(2,1)S(1)} %collective-permute-done.4.arrived.message, bf16[1024,128]{1,0:T(8,128)(2,1)S(1)} %collective-permute-done.6.outer, bf16[768,384]{1,0:T(8,128)(2,1)S(1)} %get-tuple-element.94.taps), custom_call_target="tpu_custom_call" | custom-call | flops 905969664 | bytes 4243460 | tf_op jit(solution)/shard_map/grad_volume/pallas_call | solution.py:27
  45.7 0.0 collective-permute-done.7.refs_0_
  45.7 0.6 %collective-permute-done.8.refs_1_ = bf16[24,896]{1,0:T(8,128)(2,1)S(1)} collective-permute-done((bf16[24,896]{1,0:T(8,128)(2,1)S(1)}, bf16[24,896]{1,0:T(8,128)(2,1)S(1)}, u32[]{:S(2)}, u32[]{:S(2)}) %collective-permute-start.8) | collective-permute-done | bytes 43040 | tf_op jit(solution)/shard_map/ppermute | solution.py:653
  46.4 0.7 %finish.1 = (f32[27,4,64]{2,1,0:T(4,128)}, f32[27,8,64]{2,1,0:T(8,128)}) custom-call(f32[24,896]{1,0:T(8,128)S(1)} %get-tuple-element.96.mine, bf16[24,896]{1,0:T(8,128)(2,1)S(1)} %collective-permute-done.7.refs_0_, bf16[24,896]{1,0:T(8,128)(2,1)S(1)} %collective-permute-done.8.refs_1_, bf16[24,896]{1,0:T(8,128)(2,1)S(1)} %collective-permute-done.9.refs_2_), custom_call_target="tpu_custom_call" | custom-call | bytes 297984 | tf_op jit(solution)/shard_map/finish/pallas_call | solution.py:27
  (5 shorter events, 0.0 us)
Async XLA Ops:
  2.0 6.4 %collective-permute-start = (bf16[2048,128]{1,0:T(8,128)(2,1)S(1)}, bf16[2048,128]{1,0:T(8,128)(2,1)S(1)}, u32[]{:S(2)}, u32[]{:S(2)}) collective-permute-start(bf16[2048,128]{1,0:T(8,128)(2,1)S(1)} %pack_volume.1.own), channel_id=1, source_target_pairs={{0,1},{1,0},{2,3},{3,2},{4,5},{5,4},{6,7},{7,6},{8,9},{9,8},{10,11... | collective-permute-start | bytes 1572872 | tf_op jit(solution)/shard_map/ppermute | solution.py:551
  2.6 14.4 %collective-permute-start.1 = (bf16[2048,128]{1,0:T(8,128)(2,1)S(1)}, bf16[2048,128]{1,0:T(8,128)(2,1)S(1)}, u32[]{:S(2)}, u32[]{:S(2)}) collective-permute-start(bf16[2048,128]{1,0:T(8,128)(2,1)S(1)} %pack_volume.1.own), channel_id=1, source_target_pairs={{1,2},{3,4},{5,6},{7,8},{9,10},{11,12},{13,14},{2,1},{4,3},{6,5},{... | collective-permute-start | bytes 1572872 | tf_op jit(solution)/shard_map/ppermute | solution.py:550
  3.2 4.6 %copy-start = (bf16[3,3,3,64,128]{4,3,2,1,0:T(8,128)(2,1)S(1)}, bf16[3,3,3,64,128]{4,3,2,1,0:T(8,128)(2,1)}, u32[]{:S(2)}) copy-start(bf16[3,3,3,64,128]{4,3,2,1,0:T(8,128)(2,1)} %param.6) | copy-start | bytes 1327108
  3.3 4.6 %copy-start.1 = (bf16[3,3,3,64,64]{4,3,2,1,0:T(8,128)(2,1)S(1)}, bf16[3,3,3,64,64]{4,3,2,1,0:T(8,128)(2,1)}, u32[]{:S(2)}) copy-start(bf16[3,3,3,64,64]{4,3,2,1,0:T(8,128)(2,1)} %param.5) | copy-start | bytes 663556
  12.1 11.7 %collective-permute-start.2 = (bf16[2048,128]{1,0:T(8,128)(2,1)S(1)}, bf16[2048,128]{1,0:T(8,128)(2,1)S(1)}, u32[]{:S(2)}, u32[]{:S(2)}) collective-permute-start(bf16[2048,128]{1,0:T(8,128)(2,1)S(1)} %get-tuple-element.66), channel_id=1, source_target_pairs={{0,1},{1,0},{2,3},{3,2},{4,5},{5,4},{6,7},{7,6},{8,9},{9,8},{10,11... | collective-permute-start | bytes 1572872 | tf_op jit(solution)/shard_map/ppermute | solution.py:581
  16.1 7.7 %collective-permute-start.3 = (bf16[1024,128]{1,0:T(8,128)(2,1)S(1)}, bf16[1024,128]{1,0:T(8,128)(2,1)S(1)}, u32[]{:S(2)}, u32[]{:S(2)}) collective-permute-start(bf16[1024,128]{1,0:T(8,128)(2,1)S(1)} %get-tuple-element.67), channel_id=1, source_target_pairs={{1,2},{3,4},{5,6},{7,8},{9,10},{11,12},{13,14},{2,1},{4,3},{6,5},{... | collective-permute-start | bytes 786440 | tf_op jit(solution)/shard_map/ppermute | solution.py:580
  25.9 4.9 %collective-permute-start.4 = (bf16[2816,128]{1,0:T(8,128)(2,1)S(1)}, bf16[2816,128]{1,0:T(8,128)(2,1)S(1)}, u32[]{:S(2)}, u32[]{:S(2)}) collective-permute-start(bf16[2816,128]{1,0:T(8,128)(2,1)S(1)} %get-tuple-element.74), channel_id=1, source_target_pairs={{0,1},{1,0},{2,3},{3,2},{4,5},{5,4},{6,7},{7,6},{8,9},{9,8},{10,11... | collective-permute-start | bytes 2162696 | tf_op jit(solution)/shard_map/ppermute | solution.py:613
  31.0 6.7 %collective-permute-start.5 = (bf16[4,24,896]{2,1,0:T(8,128)(2,1)S(1)}, bf16[4,24,896]{2,1,0:T(8,128)(2,1)S(1)}, u32[]{:S(2)}, u32[]{:S(2)}) collective-permute-start(bf16[4,24,896]{2,1,0:T(8,128)(2,1)S(1)} %get-tuple-element.83), channel_id=1, source_target_pairs={{0,4},{1,5},{2,6},{3,7},{4,0},{5,1},{6,2},{7,3},{8,12},{9,13},{10,... | collective-permute-start | bytes 516104 | tf_op jit(solution)/shard_map/ppermute | solution.py:634
  33.0 9.2 %collective-permute-start.6 = (bf16[1024,128]{1,0:T(8,128)(2,1)S(1)}, bf16[1024,128]{1,0:T(8,128)(2,1)S(1)}, u32[]{:S(2)}, u32[]{:S(2)}) collective-permute-start(bf16[1024,128]{1,0:T(8,128)(2,1)S(1)} %get-tuple-element.93), channel_id=1, source_target_pairs={{1,2},{3,4},{5,6},{7,8},{9,10},{11,12},{13,14},{2,1},{4,3},{6,5},{... | collective-permute-start | bytes 786440 | tf_op jit(solution)/shard_map/ppermute | solution.py:635
  37.7 8.0 %collective-permute-start.7 = (bf16[24,896]{1,0:T(8,128)(2,1)S(1)}, bf16[24,896]{1,0:T(8,128)(2,1)S(1)}, u32[]{:S(2)}, u32[]{:S(2)}) collective-permute-start(bf16[24,896]{1,0:T(8,128)(2,1)S(1)} %get-tuple-element.97), channel_id=1, source_target_pairs={{0,8},{1,9},{2,10},{3,11},{4,12},{5,13},{6,14},{7,15},{8,0},{9,1},... | collective-permute-start | bytes 129032 | tf_op jit(solution)/shard_map/ppermute | solution.py:653
  40.6 5.8 %collective-permute-start.8 = (bf16[24,896]{1,0:T(8,128)(2,1)S(1)}, bf16[24,896]{1,0:T(8,128)(2,1)S(1)}, u32[]{:S(2)}, u32[]{:S(2)}) collective-permute-start(bf16[24,896]{1,0:T(8,128)(2,1)S(1)} %get-tuple-element.98), channel_id=1, source_target_pairs={{0,10},{1,11},{2,8},{3,9},{4,14},{5,15},{6,12},{7,13},{8,2},{9,3},... | collective-permute-start | bytes 129032 | tf_op jit(solution)/shard_map/ppermute | solution.py:653
  41.7 4.7 %collective-permute-start.9 = (bf16[24,896]{1,0:T(8,128)(2,1)S(1)}, bf16[24,896]{1,0:T(8,128)(2,1)S(1)}, u32[]{:S(2)}, u32[]{:S(2)}) collective-permute-start(bf16[24,896]{1,0:T(8,128)(2,1)S(1)} %get-tuple-element.99), channel_id=1, source_target_pairs={{0,2},{1,3},{2,0},{3,1},{4,6},{5,7},{6,4},{7,5},{8,10},{9,11},{10,... | collective-permute-start | bytes 129032 | tf_op jit(solution)/shard_map/ppermute | solution.py:653

commit v18 on v17

--- a/solution.py
+++ b/solution.py
@@ -632,7 +632,6 @@
     bits, sent, kept = halve(bits, 2, split, 0, kept, message)
     sent, act_windows, outer = lax.optimization_barrier((sent, act_windows, outer))
     arrived = lax.ppermute(sent, "space", [(i, i ^ 4) for i in range(count)])
-    grad_outer = lax.ppermute(outer, "space", across)
     output, = call(
         functools.partial(output_rest_body, columns, late),
         (whole,),
@@ -640,6 +639,8 @@
         (pltpu.VMEM((planes, BLOCK + BLOCK // 2, wide), F32), dma((2,))),
         two_flops, "output_rest", (), (2,), (0,), {2: 0},
     )
+    outer, output = lax.optimization_barrier((outer, output))
+    grad_outer = lax.ppermute(outer, "space", across)
     others = 2 ** len(bits) - 1
     mine, *sent = call(
         functools.partial(spread_body, 0, bits),

time: 48 us -> 50 us (1.042)
  the two profiles are of different devices: /device:TPU:0 before, /device:TPU:19 now
where the time goes in v18:
time: 50 us; the launch traced here: 49.8 us
  Pallas kernels  27.5 us (55%)
  starting transfers between devices  14.9 us (30%)
  waiting for transfers between devices  6.5 us (13%)
  between operations  0.83 us (2%)
    pallas_call x13, Pallas kernels, call(): pl.pallas_call(body, out_shape=list(outs), in_specs=[pl.BlockSpec(memory_...  27.5 us
    ppermute x1, waiting for transfers between devices, shards(): grad_outer = lax.ppermute(outer, 'space', across)  5.86 us
    ppermute x3, starting transfers between devices, shards(): lax.ppermute(part, 'space', [(i, i ^ away) for i in range(count)])  3.61 us
    ppermute x1, starting transfers between devices, shards(): terms_outer = lax.ppermute(outer, 'space', across)  3.33 us
    ppermute x1, starting transfers between devices, shards(): vol_outer = lax.ppermute(own, 'space', across)  3.05 us
    ppermute x1, starting transfers between devices, shards(): grad_outer = lax.ppermute(outer, 'space', across)  2.31 us
    ppermute x1, starting transfers between devices, shards(): arrived = lax.ppermute(sent, 'space', [(i, i ^ 4) for i in range(count)])  1.36 us
  transfers between devices with their start and end apart: 10, of which 3 were waited for; matrix products, arithmetic and copies ran while one was open for 0% of the time, Pallas kernels for 46%

profile of v18, /device:TPU:19, one launch (start us, length us, event | category | flops | bytes accessed | tf_op | source)
XLA Modules:
  0.0 49.8 jit_solution(1891977057777604684)
XLA Ops:
  0.6 1.4 %pack_volume.1.own = bf16[2048,128]{1,0:T(8,128)(2,1)S(1)} custom-call(bf16[2,2048,64]{2,1,0:T(8,128)(2,1)} %bitcast.19), custom_call_target="tpu_custom_call" | custom-call | bytes 1048576 | tf_op jit(solution)/shard_map/pack_volume/pallas_call | solution.py:27
  2.0 0.7 %collective-permute-start = (bf16[2048,128]{1,0:T(8,128)(2,1)S(1)}, bf16[2048,128]{1,0:T(8,128)(2,1)S(1)}, u32[]{:S(2)}, u32[]{:S(2)}) collective-permute-start(bf16[2048,128]{1,0:T(8,128)(2,1)S(1)} %pack_volume.1.own), channel_id=1, source_target_pairs={{0,1},{1,0},{2,3},{3,2},{4,5},{5,4},{6,7},{7,6},{8,9},{9,8},{10,11... | collective-permute-start | bytes 1572872 | tf_op jit(solution)/shard_map/ppermute | solution.py:551
  2.8 3.0 %collective-permute-start.1 = (bf16[2048,128]{1,0:T(8,128)(2,1)S(1)}, bf16[2048,128]{1,0:T(8,128)(2,1)S(1)}, u32[]{:S(2)}, u32[]{:S(2)}) collective-permute-start(bf16[2048,128]{1,0:T(8,128)(2,1)S(1)} %pack_volume.1.own), channel_id=1, source_target_pairs={{1,2},{3,4},{5,6},{7,8},{9,10},{11,12},{13,14},{2,1},{4,3},{6,5},{... | collective-permute-start | bytes 1572872 | tf_op jit(solution)/shard_map/ppermute | solution.py:550
  5.8 0.0 copy-start
  5.8 0.0 copy-start.1
  5.9 4.6 %grad_act_terms.1 = (f32[2048,128]{1,0:T(8,128)S(1)}, bf16[2048,128]{1,0:T(8,128)(2,1)S(1)}, bf16[1024,128]{1,0:T(8,128)(2,1)S(1)}, bf16[256,2048]{1,0:T(8,128)(2,1)S(1)}) custom-call(s32[1]{0:T(128)} %bitcast.me, bf16[2,2048,128]{2,1,0:T(8,128)(2,1)} %bitcast.20, bf16[27,64,128]{2,1,0:T(8,128)(2,1)} %bitcast.13), custom_call_target="tpu_custom_call" | custom-call | flops 1811939328 | bytes 4374532 | tf_op jit(solution)/shard_map/grad_act_terms/pallas_call | solution.py:27
  10.5 0.5 layouts.1
  11.0 0.0 collective-permute-done.inner
  11.0 3.7 %prepare.1 = (bf16[2112,384]{1,0:T(8,128)(2,1)S(1)}, bf16[2112,384]{1,0:T(8,128)(2,1)S(1)}, f32[2048,256]{1,0:T(8,128)S(1)}, bf16[1152,256]{1,0:T(8,128)(2,1)S(1)}) custom-call(s32[1]{0:T(128)} %bitcast.me, bf16[2048,128]{1,0:T(8,128)(2,1)S(1)} %pack_volume.1.own, bf16[2048,128]{1,0:T(8,128)(2,1)S(1)} %collective-permute-done.inner, bf16[27,64,64]{2,1,0:T(8,128)(2,1)} %bitcast.15), custom_call_target="tpu_custom_call" | custom-call | flops 905969664 | bytes 7200772 | tf_op jit(solution)/shard_map/prepare/pallas_call | solution.py:27
  14.7 0.4 collective-permute-start.2
  15.2 3.3 %collective-permute-start.3 = (bf16[1024,128]{1,0:T(8,128)(2,1)S(1)}, bf16[1024,128]{1,0:T(8,128)(2,1)S(1)}, u32[]{:S(2)}, u32[]{:S(2)}) collective-permute-start(bf16[1024,128]{1,0:T(8,128)(2,1)S(1)} %get-tuple-element.69), channel_id=1, source_target_pairs={{1,2},{3,4},{5,6},{7,8},{9,10},{11,12},{13,14},{2,1},{4,3},{6,5},{... | collective-permute-start | bytes 786440 | tf_op jit(solution)/shard_map/ppermute | solution.py:580
  18.5 0.4 collective-permute-done.1.outer
  18.9 3.5 %hidden.1 = (bf16[2112,768]{1,0:T(8,128)(2,1)S(1)}, f32[2048,128]{1,0:T(8,128)S(1)}, bf16[2112,384]{1,0:T(8,128)(2,1)S(1)}) custom-call(s32[1]{0:T(128)} %bitcast.me, bf16[2048,128]{1,0:T(8,128)(2,1)S(1)} %collective-permute-done.1.outer, f32[2048,256]{1,0:T(8,128)S(1)} %get-tuple-element.63.part, bf16[1152,256]{1,0:T(8,128)(2,1)S(1)} %get-tuple-element.64.outer_taps, ...), custom_call_target="tpu_custom_call" | custom-call | flops 1811939328 | bytes 10747908 | tf_op jit(solution)/shard_map/hidden/pallas_call | solution.py:27
  22.4 3.3 %grad_two_terms.1 = (f32[128,1792]{1,0:T(8,128)S(1)}, f32[2,2048,128]{2,1,0:T(8,128)}) custom-call(bf16[2112,768]{1,0:T(8,128)(2,1)S(1)} %get-tuple-element.90.act_windows, bf16[256,2048]{1,0:T(8,128)(2,1)S(1)} %get-tuple-element.72.turned, bf16[2304,256]{1,0:T(8,128)(2,1)S(1)} %get-tuple-element.73.taps), custom_call_target="tpu_custom_call" | custom-call | flops 1811939328 | bytes 8486912 | tf_op jit(solution)/shard_map/grad_two_terms/pallas_call | solution.py:27
  25.7 0.0 collective-permute-done.3.outer
  25.7 0.0 collective-permute-done.2.inner
  25.8 2.1 %grad_one_terms.1 = (bf16[2048,128]{1,0:T(8,128)(2,1)S(1)}, bf16[1024,128]{1,0:T(8,128)(2,1)S(1)}, bf16[2816,128]{1,0:T(8,128)(2,1)S(1)}, f32[8,24,896]{2,1,0:T(8,128)S(1)}) custom-call(s32[1]{0:T(128)} %bitcast.me, bf16[2112,384]{1,0:T(8,128)(2,1)S(1)} %get-tuple-element.57.own_windows, bf16[2112,384]{1,0:T(8,128)(2,1)S(1)} %get-tuple-element.66.side_windows, ...), custom_call_target="tpu_custom_call" | custom-call | flops 905969664 | bytes 9240580 | tf_op jit(solution)/shard_map/grad_one_terms/pallas_call | solution.py:27
  27.9 0.1 collective-permute-start.4
  28.0 2.0 %output_first.1 = (f32[2,2048,128]{2,1,0:T(8,128)}, bf16[2112,384]{1,0:T(8,128)(2,1)S(1)}) custom-call(bf16[2112,768]{1,0:T(8,128)(2,1)S(1)} %get-tuple-element.90.act_windows, bf16[2304,256]{1,0:T(8,128)(2,1)S(1)} %get-tuple-element.73.taps, bf16[2048,128]{1,0:T(8,128)(2,1)S(1)} %get-tuple-element.77.grad, ...), custom_call_target="tpu_custom_call", output_to_operand_aliasing={{0}: (3, {})} | custom-call | flops 1811939328 | bytes 10764288 | tf_op jit(solution)/shard_map/output_first/pallas_call | solution.py:27
  30.0 0.2 collective-permute-done.4.arrived.message
  30.1 0.1 halve.1
  30.2 1.4 %collective-permute-start.5 = (bf16[4,24,896]{2,1,0:T(8,128)(2,1)S(1)}, bf16[4,24,896]{2,1,0:T(8,128)(2,1)S(1)}, u32[]{:S(2)}, u32[]{:S(2)}) collective-permute-start(bf16[4,24,896]{2,1,0:T(8,128)(2,1)S(1)} %get-tuple-element.85), channel_id=1, source_target_pairs={{0,4},{1,5},{2,6},{3,7},{4,0},{5,1},{6,2},{7,3},{8,12},{9,13},{10,... | collective-permute-start | bytes 516104 | tf_op jit(solution)/shard_map/ppermute | solution.py:634
  31.6 2.0 %output_rest.1 = f32[2,2048,128]{2,1,0:T(8,128)} custom-call(bf16[2112,768]{1,0:T(8,128)(2,1)S(1)} %get-tuple-element.90.act_windows, bf16[2304,256]{1,0:T(8,128)(2,1)S(1)} %get-tuple-element.73.taps, f32[2,2048,128]{2,1,0:T(8,128)} %get-tuple-element.91.begun), custom_call_target="tpu_custom_call", output_to_operand_aliasing={{}: (2, {})} | custom-call | flops 1811939328 | bytes 8617984 | tf_op jit(solution)/shard_map/output_rest/pallas_call | solution.py:27
  33.6 2.3 %collective-permute-start.6 = (bf16[1024,128]{1,0:T(8,128)(2,1)S(1)}, bf16[1024,128]{1,0:T(8,128)(2,1)S(1)}, u32[]{:S(2)}, u32[]{:S(2)}) collective-permute-start(bf16[1024,128]{1,0:T(8,128)(2,1)S(1)} %get-tuple-element.97), channel_id=1, source_target_pairs={{1,2},{3,4},{5,6},{7,8},{9,10},{11,12},{13,14},{2,1},{4,3},{6,5},{... | collective-permute-start | bytes 786440 | tf_op jit(solution)/shard_map/ppermute | solution.py:643
  35.9 0.0 collective-permute-done.5.arrived
  36.0 1.1 %collective-permute-start.7 = (bf16[24,896]{1,0:T(8,128)(2,1)S(1)}, bf16[24,896]{1,0:T(8,128)(2,1)S(1)}, u32[]{:S(2)}, u32[]{:S(2)}) collective-permute-start(bf16[24,896]{1,0:T(8,128)(2,1)S(1)} %get-tuple-element.101), channel_id=1, source_target_pairs={{0,8},{1,9},{2,10},{3,11},{4,12},{5,13},{6,14},{7,15},{8,0},{9,1},... | collective-permute-start | bytes 129032 | tf_op jit(solution)/shard_map/ppermute | solution.py:654
  37.1 2.4 %collective-permute-start.8 = (bf16[24,896]{1,0:T(8,128)(2,1)S(1)}, bf16[24,896]{1,0:T(8,128)(2,1)S(1)}, u32[]{:S(2)}, u32[]{:S(2)}) collective-permute-start(bf16[24,896]{1,0:T(8,128)(2,1)S(1)} %get-tuple-element.102), channel_id=1, source_target_pairs={{0,10},{1,11},{2,8},{3,9},{4,14},{5,15},{6,12},{7,13},{8,2},{9,3},... | collective-permute-start | bytes 129032 | tf_op jit(solution)/shard_map/ppermute | solution.py:654
  39.5 0.1 collective-permute-start.9
  39.6 5.9 %collective-permute-done.6.outer = bf16[1024,128]{1,0:T(8,128)(2,1)S(1)} collective-permute-done((bf16[1024,128]{1,0:T(8,128)(2,1)S(1)}, bf16[1024,128]{1,0:T(8,128)(2,1)S(1)}, u32[]{:S(2)}, u32[]{:S(2)}) %collective-permute-start.6) | collective-permute-done | bytes 262176 | tf_op jit(solution)/shard_map/ppermute | solution.py:643
  45.5 3.5 %grad_volume.1 = f32[2,2048,64]{2,1,0:T(8,128)} custom-call(s32[1]{0:T(128)} %bitcast.me, bf16[2112,384]{1,0:T(8,128)(2,1)S(1)} %get-tuple-element.96.own_windows, bf16[2816,128]{1,0:T(8,128)(2,1)S(1)} %collective-permute-done.4.arrived.message, bf16[1024,128]{1,0:T(8,128)(2,1)S(1)} %collective-permute-done.6.outer, bf16[768,384]{1,0:T(8,128)(2,1)S(1)} %get-tuple-element.98.taps), custom_call_target="tpu_custom_call" | custom-call | flops 905969664 | bytes 4243460 | tf_op jit(solution)/shard_map/grad_volume/pallas_call | solution.py:27
  49.0 0.0 collective-permute-done.9.refs_2_
  49.0 0.7 %finish.1 = (f32[27,4,64]{2,1,0:T(4,128)}, f32[27,8,64]{2,1,0:T(8,128)}) custom-call(f32[24,896]{1,0:T(8,128)S(1)} %get-tuple-element.100.mine, bf16[24,896]{1,0:T(8,128)(2,1)S(1)} %collective-permute-done.7.refs_0_, bf16[24,896]{1,0:T(8,128)(2,1)S(1)} %collective-permute-done.8.refs_1_, bf16[24,896]{1,0:T(8,128)(2,1)S(1)} %collective-permute-done.9.refs_2_), custom_call_target="tpu_custom_call" | custom-call | bytes 297984 | tf_op jit(solution)/shard_map/finish/pallas_call | solution.py:27
  (5 shorter events, 0.0 us)
Async XLA Ops:
  2.0 8.9 %collective-permute-start = (bf16[2048,128]{1,0:T(8,128)(2,1)S(1)}, bf16[2048,128]{1,0:T(8,128)(2,1)S(1)}, u32[]{:S(2)}, u32[]{:S(2)}) collective-permute-start(bf16[2048,128]{1,0:T(8,128)(2,1)S(1)} %pack_volume.1.own), channel_id=1, source_target_pairs={{0,1},{1,0},{2,3},{3,2},{4,5},{5,4},{6,7},{7,6},{8,9},{9,8},{10,11... | collective-permute-start | bytes 1572872 | tf_op jit(solution)/shard_map/ppermute | solution.py:551
  2.8 16.1 %collective-permute-start.1 = (bf16[2048,128]{1,0:T(8,128)(2,1)S(1)}, bf16[2048,128]{1,0:T(8,128)(2,1)S(1)}, u32[]{:S(2)}, u32[]{:S(2)}) collective-permute-start(bf16[2048,128]{1,0:T(8,128)(2,1)S(1)} %pack_volume.1.own), channel_id=1, source_target_pairs={{1,2},{3,4},{5,6},{7,8},{9,10},{11,12},{13,14},{2,1},{4,3},{6,5},{... | collective-permute-start | bytes 1572872 | tf_op jit(solution)/shard_map/ppermute | solution.py:550
  5.8 4.6 %copy-start = (bf16[3,3,3,64,128]{4,3,2,1,0:T(8,128)(2,1)S(1)}, bf16[3,3,3,64,128]{4,3,2,1,0:T(8,128)(2,1)}, u32[]{:S(2)}) copy-start(bf16[3,3,3,64,128]{4,3,2,1,0:T(8,128)(2,1)} %param.6) | copy-start | bytes 1327108
  5.8 4.6 %copy-start.1 = (bf16[3,3,3,64,64]{4,3,2,1,0:T(8,128)(2,1)S(1)}, bf16[3,3,3,64,64]{4,3,2,1,0:T(8,128)(2,1)}, u32[]{:S(2)}) copy-start(bf16[3,3,3,64,64]{4,3,2,1,0:T(8,128)(2,1)} %param.5) | copy-start | bytes 663556
  14.7 11.0 %collective-permute-start.2 = (bf16[2048,128]{1,0:T(8,128)(2,1)S(1)}, bf16[2048,128]{1,0:T(8,128)(2,1)S(1)}, u32[]{:S(2)}, u32[]{:S(2)}) collective-permute-start(bf16[2048,128]{1,0:T(8,128)(2,1)S(1)} %get-tuple-element.68), channel_id=1, source_target_pairs={{0,1},{1,0},{2,3},{3,2},{4,5},{5,4},{6,7},{7,6},{8,9},{9,8},{10,11... | collective-permute-start | bytes 1572872 | tf_op jit(solution)/shard_map/ppermute | solution.py:581
  15.2 10.6 %collective-permute-start.3 = (bf16[1024,128]{1,0:T(8,128)(2,1)S(1)}, bf16[1024,128]{1,0:T(8,128)(2,1)S(1)}, u32[]{:S(2)}, u32[]{:S(2)}) collective-permute-start(bf16[1024,128]{1,0:T(8,128)(2,1)S(1)} %get-tuple-element.69), channel_id=1, source_target_pairs={{1,2},{3,4},{5,6},{7,8},{9,10},{11,12},{13,14},{2,1},{4,3},{6,5},{... | collective-permute-start | bytes 786440 | tf_op jit(solution)/shard_map/ppermute | solution.py:580
  27.9 2.3 %collective-permute-start.4 = (bf16[2816,128]{1,0:T(8,128)(2,1)S(1)}, bf16[2816,128]{1,0:T(8,128)(2,1)S(1)}, u32[]{:S(2)}, u32[]{:S(2)}) collective-permute-start(bf16[2816,128]{1,0:T(8,128)(2,1)S(1)} %get-tuple-element.76), channel_id=1, source_target_pairs={{0,1},{1,0},{2,3},{3,2},{4,5},{5,4},{6,7},{7,6},{8,9},{9,8},{10,11... | collective-permute-start | bytes 2162696 | tf_op jit(solution)/shard_map/ppermute | solution.py:613
  30.2 5.7 %collective-permute-start.5 = (bf16[4,24,896]{2,1,0:T(8,128)(2,1)S(1)}, bf16[4,24,896]{2,1,0:T(8,128)(2,1)S(1)}, u32[]{:S(2)}, u32[]{:S(2)}) collective-permute-start(bf16[4,24,896]{2,1,0:T(8,128)(2,1)S(1)} %get-tuple-element.85), channel_id=1, source_target_pairs={{0,4},{1,5},{2,6},{3,7},{4,0},{5,1},{6,2},{7,3},{8,12},{9,13},{10,... | collective-permute-start | bytes 516104 | tf_op jit(solution)/shard_map/ppermute | solution.py:634
  33.6 11.9 %collective-permute-start.6 = (bf16[1024,128]{1,0:T(8,128)(2,1)S(1)}, bf16[1024,128]{1,0:T(8,128)(2,1)S(1)}, u32[]{:S(2)}, u32[]{:S(2)}) collective-permute-start(bf16[1024,128]{1,0:T(8,128)(2,1)S(1)} %get-tuple-element.97), channel_id=1, source_target_pairs={{1,2},{3,4},{5,6},{7,8},{9,10},{11,12},{13,14},{2,1},{4,3},{6,5},{... | collective-permute-start | bytes 786440 | tf_op jit(solution)/shard_map/ppermute | solution.py:643
  36.0 13.0 %collective-permute-start.7 = (bf16[24,896]{1,0:T(8,128)(2,1)S(1)}, bf16[24,896]{1,0:T(8,128)(2,1)S(1)}, u32[]{:S(2)}, u32[]{:S(2)}) collective-permute-start(bf16[24,896]{1,0:T(8,128)(2,1)S(1)} %get-tuple-element.101), channel_id=1, source_target_pairs={{0,8},{1,9},{2,10},{3,11},{4,12},{5,13},{6,14},{7,15},{8,0},{9,1},... | collective-permute-start | bytes 129032 | tf_op jit(solution)/shard_map/ppermute | solution.py:654
  37.1 11.9 %collective-permute-start.8 = (bf16[24,896]{1,0:T(8,128)(2,1)S(1)}, bf16[24,896]{1,0:T(8,128)(2,1)S(1)}, u32[]{:S(2)}, u32[]{:S(2)}) collective-permute-start(bf16[24,896]{1,0:T(8,128)(2,1)S(1)} %get-tuple-element.102), channel_id=1, source_target_pairs={{0,10},{1,11},{2,8},{3,9},{4,14},{5,15},{6,12},{7,13},{8,2},{9,3},... | collective-permute-start | bytes 129032 | tf_op jit(solution)/shard_map/ppermute | solution.py:654
  39.5 9.5 %collective-permute-start.9 = (bf16[24,896]{1,0:T(8,128)(2,1)S(1)}, bf16[24,896]{1,0:T(8,128)(2,1)S(1)}, u32[]{:S(2)}, u32[]{:S(2)}) collective-permute-start(bf16[24,896]{1,0:T(8,128)(2,1)S(1)} %get-tuple-element.103), channel_id=1, source_target_pairs={{0,2},{1,3},{2,0},{3,1},{4,6},{5,7},{6,4},{7,5},{8,10},{9,11},{10,... | collective-permute-start | bytes 129032 | tf_op jit(solution)/shard_map/ppermute | solution.py:654

commit v19 on v17

--- a/solution.py
+++ b/solution.py
@@ -453,7 +453,7 @@
     return copies
 
 
-def output_first_body(
+def output_rest_body(
     columns, blocks, act_windows, taps, grad, begun, far, own_windows, output, sems
 ):
     copies = output_rows(columns, blocks, act_windows, taps, far, output, sems)
@@ -467,11 +467,6 @@
     clear_edges(own_windows, columns)
     lax.fori_loop(0, grad.shape[0] // STEP, fill, 0)
     for copy in copies:
-        copy.wait()
-
-
-def output_rest_body(columns, blocks, act_windows, taps, begun, far, output, sems):
-    for copy in output_rows(columns, blocks, act_windows, taps, far, output, sems):
         copy.wait()
 
 
@@ -585,9 +580,7 @@
         (me, vol_outer, part, outer_taps, inner_windows),
         (pltpu.VMEM((slab[0], 384), BF16),), 2 * one_flops, "hidden", (0,),
     )
-    half = cells // 2
-    early, middle = [(0, BLOCK)], [(BLOCK, BLOCK), (half, BLOCK // 2)]
-    late = [(half + BLOCK // 2, BLOCK), (cells - BLOCK // 2, BLOCK // 2)]
+    early, rest = [(0, BLOCK)], row_blocks(BLOCK, cells)
     whole = shape((planes, cells, wide), F32)
     terms_two, output = call(
         functools.partial(grad_two_body, columns, early),
@@ -611,14 +604,6 @@
         one_flops, "grad_one_terms", (0,),
     )
     message = lax.ppermute(message, "space", within)
-    output, back_windows = call(
-        functools.partial(output_first_body, columns, middle),
-        (whole, third),
-        (act_windows, out_taps, grad_hidden, output),
-        (pltpu.VMEM((planes, BLOCK + BLOCK // 2, wide), F32), dma((2,))),
-        two_flops, "output_first", (), (3,), (0,), {3: 0},
-    )
-    message, output, back_windows = lax.optimization_barrier((message, output, back_windows))
     def halve(bits, bit, split_in, split_out, kept, arrived):
         left = 2 ** (len(bits) - 1)
         sent, kept = call(
@@ -630,21 +615,21 @@
 
     bits = list(range(count.bit_length() - 2, 0, -1))
     bits, sent, kept = halve(bits, 2, split, 0, kept, message)
-    sent, act_windows, outer = lax.optimization_barrier((sent, act_windows, outer))
+    sent, act_windows = lax.optimization_barrier((sent, act_windows))
     arrived = lax.ppermute(sent, "space", [(i, i ^ 4) for i in range(count)])
     grad_outer = lax.ppermute(outer, "space", across)
-    output, = call(
-        functools.partial(output_rest_body, columns, late),
-        (whole,),
-        (act_windows, out_taps, output),
-        (pltpu.VMEM((planes, BLOCK + BLOCK // 2, wide), F32), dma((2,))),
-        two_flops, "output_rest", (), (2,), (0,), {2: 0},
+    output, back_windows = call(
+        functools.partial(output_rest_body, columns, rest),
+        (whole, third),
+        (act_windows, out_taps, grad_hidden, output),
+        (pltpu.VMEM((planes, cells - BLOCK, wide), F32), dma((len(rest),))),
+        two_flops, "output_rest", (), (3,), (0,), {3: 0},
     )
     others = 2 ** len(bits) - 1
     mine, *sent = call(
         functools.partial(spread_body, 0, bits),
         (shape((chunk, lanes), F32), *[shape((chunk, lanes), BF16)] * others),
-        (me, kept, arrived), flops=16 * two_flops, name="spread", smem=(0,),
+        (me, kept, arrived), name="spread", smem=(0,),
     )
     sent, output, back_windows = lax.optimization_barrier((sent, output, back_windows))
     arrived = []

time: 48 us -> 51.6 us (1.075); the launches traced: 47.1 us -> 51.4 us
  waiting for transfers between devices: 2.73 us -> 6.79 us
  starting transfers between devices: 16 us -> 17.4 us
  Pallas kernels: 27.5 us -> 26.4 us
    ppermute x1, waiting for transfers between devices: 2.07 us -> 4.89 us  [shards(): arrived = lax.ppermute(sent, 'space', [(i, i ^ 4) for i in range(count)])]
    ppermute x1, starting transfers between devices: 2.01 us -> 3.16 us  [shards(): arrived = lax.ppermute(sent, 'space', [(i, i ^ 4) for i in range(count)])]
    ppermute x1, waiting for transfers between devices: 0.01 us -> 1.14 us  [shards(): message = lax.ppermute(message, 'space', within)]
    pallas_call x13 -> x12, Pallas kernels: 27.5 us -> 26.4 us  [call(): pl.pallas_call(body, out_shape=list(outs), in_specs=[pl.BlockSpec(memory_...]
  transfers between devices with their start and end apart: 10 -> 10, of which waited for: 2 -> 3; matrix products, arithmetic and copies ran while one was open for 0% -> 0% of each run, Pallas kernels for 49% -> 43%
where the time goes in v19:
time: 51.6 us; the launch traced here: 51.4 us
  Pallas kernels  26.4 us (51%)
  starting transfers between devices  17.4 us (34%)
  waiting for transfers between devices  6.79 us (13%)
  between operations  0.81 us (2%)
    pallas_call x12, Pallas kernels, call(): pl.pallas_call(body, out_shape=list(outs), in_specs=[pl.BlockSpec(memory_...  26.4 us
    ppermute x1, waiting for transfers between devices, shards(): arrived = lax.ppermute(sent, 'space', [(i, i ^ 4) for i in range(count)])  4.89 us
    ppermute x3, starting transfers between devices, shards(): lax.ppermute(part, 'space', [(i, i ^ away) for i in range(count)])  4.64 us
    ppermute x1, starting transfers between devices, shards(): terms_inner = lax.ppermute(inner, 'space', within)  3.93 us
    ppermute x1, starting transfers between devices, shards(): arrived = lax.ppermute(sent, 'space', [(i, i ^ 4) for i in range(count)])  3.16 us
    ppermute x1, starting transfers between devices, shards(): message = lax.ppermute(message, 'space', within)  2.93 us
    ppermute x1, waiting for transfers between devices, shards(): message = lax.ppermute(message, 'space', within)  1.14 us
  transfers between devices with their start and end apart: 10, of which 3 were waited for; matrix products, arithmetic and copies ran while one was open for 0% of the time, Pallas kernels for 43%

profile of v19, /device:TPU:0, one launch (start us, length us, event | category | flops | bytes accessed | tf_op | source)
XLA Modules:
  0.0 51.4 jit_solution(4475342876418484771)
XLA Ops:
  0.6 1.4 %pack_volume.1.own = bf16[2048,128]{1,0:T(8,128)(2,1)S(1)} custom-call(bf16[2,2048,64]{2,1,0:T(8,128)(2,1)} %bitcast.19), custom_call_target="tpu_custom_call" | custom-call | bytes 1048576 | tf_op jit(solution)/shard_map/pack_volume/pallas_call | solution.py:27
  2.0 0.5 %collective-permute-start = (bf16[2048,128]{1,0:T(8,128)(2,1)S(1)}, bf16[2048,128]{1,0:T(8,128)(2,1)S(1)}, u32[]{:S(2)}, u32[]{:S(2)}) collective-permute-start(bf16[2048,128]{1,0:T(8,128)(2,1)S(1)} %pack_volume.1.own), channel_id=1, source_target_pairs={{0,1},{1,0},{2,3},{3,2},{4,5},{5,4},{6,7},{7,6},{8,9},{9,8},{10,11... | collective-permute-start | bytes 1572872 | tf_op jit(solution)/shard_map/ppermute | solution.py:546
  2.6 0.7 %collective-permute-start.1 = (bf16[2048,128]{1,0:T(8,128)(2,1)S(1)}, bf16[2048,128]{1,0:T(8,128)(2,1)S(1)}, u32[]{:S(2)}, u32[]{:S(2)}) collective-permute-start(bf16[2048,128]{1,0:T(8,128)(2,1)S(1)} %pack_volume.1.own), channel_id=1, source_target_pairs={{1,2},{3,4},{5,6},{7,8},{9,10},{11,12},{13,14},{2,1},{4,3},{6,5},{... | collective-permute-start | bytes 1572872 | tf_op jit(solution)/shard_map/ppermute | solution.py:545
  3.2 0.0 copy-start
  3.3 0.0 copy-start.1
  3.3 4.6 %grad_act_terms.1 = (f32[2048,128]{1,0:T(8,128)S(1)}, bf16[2048,128]{1,0:T(8,128)(2,1)S(1)}, bf16[1024,128]{1,0:T(8,128)(2,1)S(1)}, bf16[256,2048]{1,0:T(8,128)(2,1)S(1)}) custom-call(s32[1]{0:T(128)} %bitcast.me, bf16[2,2048,128]{2,1,0:T(8,128)(2,1)} %bitcast.20, bf16[27,64,128]{2,1,0:T(8,128)(2,1)} %bitcast.13), custom_call_target="tpu_custom_call" | custom-call | flops 1811939328 | bytes 4374532 | tf_op jit(solution)/shard_map/grad_act_terms/pallas_call | solution.py:27
  7.9 0.5 layouts.1
  8.4 0.0 collective-permute-done.inner
  8.4 3.7 %prepare.1 = (bf16[2112,384]{1,0:T(8,128)(2,1)S(1)}, bf16[2112,384]{1,0:T(8,128)(2,1)S(1)}, f32[2048,256]{1,0:T(8,128)S(1)}, bf16[1152,256]{1,0:T(8,128)(2,1)S(1)}) custom-call(s32[1]{0:T(128)} %bitcast.me, bf16[2048,128]{1,0:T(8,128)(2,1)S(1)} %pack_volume.1.own, bf16[2048,128]{1,0:T(8,128)(2,1)S(1)} %collective-permute-done.inner, bf16[27,64,64]{2,1,0:T(8,128)(2,1)} %bitcast.15), custom_call_target="tpu_custom_call" | custom-call | flops 905969664 | bytes 7200772 | tf_op jit(solution)/shard_map/prepare/pallas_call | solution.py:27
  12.1 3.9 %collective-permute-start.2 = (bf16[2048,128]{1,0:T(8,128)(2,1)S(1)}, bf16[2048,128]{1,0:T(8,128)(2,1)S(1)}, u32[]{:S(2)}, u32[]{:S(2)}) collective-permute-start(bf16[2048,128]{1,0:T(8,128)(2,1)S(1)} %get-tuple-element.62), channel_id=1, source_target_pairs={{0,1},{1,0},{2,3},{3,2},{4,5},{5,4},{6,7},{7,6},{8,9},{9,8},{10,11... | collective-permute-start | bytes 1572872 | tf_op jit(solution)/shard_map/ppermute | solution.py:576
  16.1 0.8 %collective-permute-start.3 = (bf16[1024,128]{1,0:T(8,128)(2,1)S(1)}, bf16[1024,128]{1,0:T(8,128)(2,1)S(1)}, u32[]{:S(2)}, u32[]{:S(2)}) collective-permute-start(bf16[1024,128]{1,0:T(8,128)(2,1)S(1)} %get-tuple-element.63), channel_id=1, source_target_pairs={{1,2},{3,4},{5,6},{7,8},{9,10},{11,12},{13,14},{2,1},{4,3},{6,5},{... | collective-permute-start | bytes 786440 | tf_op jit(solution)/shard_map/ppermute | solution.py:575
  16.9 0.0 collective-permute-done.1.outer
  16.9 3.5 %hidden.1 = (bf16[2112,768]{1,0:T(8,128)(2,1)S(1)}, f32[2048,128]{1,0:T(8,128)S(1)}, bf16[2112,384]{1,0:T(8,128)(2,1)S(1)}) custom-call(s32[1]{0:T(128)} %bitcast.me, bf16[2048,128]{1,0:T(8,128)(2,1)S(1)} %collective-permute-done.1.outer, f32[2048,256]{1,0:T(8,128)S(1)} %get-tuple-element.57.part, bf16[1152,256]{1,0:T(8,128)(2,1)S(1)} %get-tuple-element.58.outer_taps, ...), custom_call_target="tpu_custom_call" | custom-call | flops 1811939328 | bytes 10747908 | tf_op jit(solution)/shard_map/hidden/pallas_call | solution.py:27
  20.4 3.3 %grad_two_terms.1 = (f32[128,1792]{1,0:T(8,128)S(1)}, f32[2,2048,128]{2,1,0:T(8,128)}) custom-call(bf16[2112,768]{1,0:T(8,128)(2,1)S(1)} %get-tuple-element.77.act_windows, bf16[256,2048]{1,0:T(8,128)(2,1)S(1)} %get-tuple-element.66.turned, bf16[2304,256]{1,0:T(8,128)(2,1)S(1)} %get-tuple-element.67.taps), custom_call_target="tpu_custom_call" | custom-call | flops 1811939328 | bytes 8486912 | tf_op jit(solution)/shard_map/grad_two_terms/pallas_call | solution.py:27
  23.8 0.0 collective-permute-done.3.outer
  23.8 0.0 collective-permute-done.2.inner
  23.8 2.1 %grad_one_terms.1 = (bf16[2048,128]{1,0:T(8,128)(2,1)S(1)}, bf16[1024,128]{1,0:T(8,128)(2,1)S(1)}, bf16[2816,128]{1,0:T(8,128)(2,1)S(1)}, f32[8,24,896]{2,1,0:T(8,128)S(1)}) custom-call(s32[1]{0:T(128)} %bitcast.me, bf16[2112,384]{1,0:T(8,128)(2,1)S(1)} %get-tuple-element.51.own_windows, bf16[2112,384]{1,0:T(8,128)(2,1)S(1)} %get-tuple-element.60.side_windows, ...), custom_call_target="tpu_custom_call" | custom-call | flops 905969664 | bytes 9240580 | tf_op jit(solution)/shard_map/grad_one_terms/pallas_call | solution.py:27
  25.9 2.9 %collective-permute-start.4 = (bf16[2816,128]{1,0:T(8,128)(2,1)S(1)}, bf16[2816,128]{1,0:T(8,128)(2,1)S(1)}, u32[]{:S(2)}, u32[]{:S(2)}) collective-permute-start(bf16[2816,128]{1,0:T(8,128)(2,1)S(1)} %get-tuple-element.70), channel_id=1, source_target_pairs={{0,1},{1,0},{2,3},{3,2},{4,5},{5,4},{6,7},{7,6},{8,9},{9,8},{10,11... | collective-permute-start | bytes 2162696 | tf_op jit(solution)/shard_map/ppermute | solution.py:606
  28.9 0.7 %collective-permute-start.6 = (bf16[1024,128]{1,0:T(8,128)(2,1)S(1)}, bf16[1024,128]{1,0:T(8,128)(2,1)S(1)}, u32[]{:S(2)}, u32[]{:S(2)}) collective-permute-start(bf16[1024,128]{1,0:T(8,128)(2,1)S(1)} %get-tuple-element.85), channel_id=1, source_target_pairs={{1,2},{3,4},{5,6},{7,8},{9,10},{11,12},{13,14},{2,1},{4,3},{6,5},{... | collective-permute-start | bytes 786440 | tf_op jit(solution)/shard_map/ppermute | solution.py:620
  29.6 1.1 %collective-permute-done.4.arrived.message = bf16[2816,128]{1,0:T(8,128)(2,1)S(1)} collective-permute-done((bf16[2816,128]{1,0:T(8,128)(2,1)S(1)}, bf16[2816,128]{1,0:T(8,128)(2,1)S(1)}, u32[]{:S(2)}, u32[]{:S(2)}) %collective-permute-start.4) | collective-permute-done | bytes 720928 | tf_op jit(solution)/shard_map/ppermute | solution.py:606
  30.7 0.1 halve.1
  30.8 3.2 %collective-permute-start.5 = (bf16[4,24,896]{2,1,0:T(8,128)(2,1)S(1)}, bf16[4,24,896]{2,1,0:T(8,128)(2,1)S(1)}, u32[]{:S(2)}, u32[]{:S(2)}) collective-permute-start(bf16[4,24,896]{2,1,0:T(8,128)(2,1)S(1)} %get-tuple-element.73), channel_id=1, source_target_pairs={{0,4},{1,5},{2,6},{3,7},{4,0},{5,1},{6,2},{7,3},{8,12},{9,13},{10,... | collective-permute-start | bytes 516104 | tf_op jit(solution)/shard_map/ppermute | solution.py:619
  33.9 2.9 %output_rest.1 = (f32[2,2048,128]{2,1,0:T(8,128)}, bf16[2112,384]{1,0:T(8,128)(2,1)S(1)}) custom-call(bf16[2112,768]{1,0:T(8,128)(2,1)S(1)} %get-tuple-element.77.act_windows, bf16[2304,256]{1,0:T(8,128)(2,1)S(1)} %get-tuple-element.67.taps, bf16[2048,128]{1,0:T(8,128)(2,1)S(1)} %get-tuple-element.78.grad, ...), custom_call_target="tpu_custom_call", output_to_operand_aliasing={{0}: (3, {})} | custom-call | flops 1811939328 | bytes 10764288 | tf_op jit(solution)/shard_map/output_rest/pallas_call | solution.py:27
  36.8 4.9 %collective-permute-done.5.arrived = bf16[4,24,896]{2,1,0:T(8,128)(2,1)S(1)} collective-permute-done((bf16[4,24,896]{2,1,0:T(8,128)(2,1)S(1)}, bf16[4,24,896]{2,1,0:T(8,128)(2,1)S(1)}, u32[]{:S(2)}, u32[]{:S(2)}) %collective-permute-start.5) | collective-permute-done | bytes 172064 | tf_op jit(solution)/shard_map/ppermute | solution.py:619
  41.7 3.1 %collective-permute-start.7 = (bf16[24,896]{1,0:T(8,128)(2,1)S(1)}, bf16[24,896]{1,0:T(8,128)(2,1)S(1)}, u32[]{:S(2)}, u32[]{:S(2)}) collective-permute-start(bf16[24,896]{1,0:T(8,128)(2,1)S(1)} %get-tuple-element.89), channel_id=1, source_target_pairs={{0,8},{1,9},{2,10},{3,11},{4,12},{5,13},{6,14},{7,15},{8,0},{9,1},... | collective-permute-start | bytes 129032 | tf_op jit(solution)/shard_map/ppermute | solution.py:638
  44.8 0.0 collective-permute-start.8
  44.8 1.5 %collective-permute-start.9 = (bf16[24,896]{1,0:T(8,128)(2,1)S(1)}, bf16[24,896]{1,0:T(8,128)(2,1)S(1)}, u32[]{:S(2)}, u32[]{:S(2)}) collective-permute-start(bf16[24,896]{1,0:T(8,128)(2,1)S(1)} %get-tuple-element.91), channel_id=1, source_target_pairs={{0,2},{1,3},{2,0},{3,1},{4,6},{5,7},{6,4},{7,5},{8,10},{9,11},{10,... | collective-permute-start | bytes 129032 | tf_op jit(solution)/shard_map/ppermute | solution.py:638
  46.4 0.0 collective-permute-done.6.outer
  46.4 3.5 %grad_volume.1 = f32[2,2048,64]{2,1,0:T(8,128)} custom-call(s32[1]{0:T(128)} %bitcast.me, bf16[2112,384]{1,0:T(8,128)(2,1)S(1)} %get-tuple-element.84.own_windows, bf16[2816,128]{1,0:T(8,128)(2,1)S(1)} %collective-permute-done.4.arrived.message, bf16[1024,128]{1,0:T(8,128)(2,1)S(1)} %collective-permute-done.6.outer, bf16[768,384]{1,0:T(8,128)(2,1)S(1)} %get-tuple-element.86.taps), custom_call_target="tpu_custom_call" | custom-call | flops 905969664 | bytes 4243460 | tf_op jit(solution)/shard_map/grad_volume/pallas_call | solution.py:27
  49.9 0.0 collective-permute-done.7.refs_0_
  49.9 0.7 %collective-permute-done.8.refs_1_ = bf16[24,896]{1,0:T(8,128)(2,1)S(1)} collective-permute-done((bf16[24,896]{1,0:T(8,128)(2,1)S(1)}, bf16[24,896]{1,0:T(8,128)(2,1)S(1)}, u32[]{:S(2)}, u32[]{:S(2)}) %collective-permute-start.8) | collective-permute-done | bytes 43040 | tf_op jit(solution)/shard_map/ppermute | solution.py:638
  50.7 0.7 %finish.1 = (f32[27,4,64]{2,1,0:T(4,128)}, f32[27,8,64]{2,1,0:T(8,128)}) custom-call(f32[24,896]{1,0:T(8,128)S(1)} %get-tuple-element.88.mine, bf16[24,896]{1,0:T(8,128)(2,1)S(1)} %collective-permute-done.7.refs_0_, bf16[24,896]{1,0:T(8,128)(2,1)S(1)} %collective-permute-done.8.refs_1_, bf16[24,896]{1,0:T(8,128)(2,1)S(1)} %collective-permute-done.9.refs_2_), custom_call_target="tpu_custom_call" | custom-call | bytes 297984 | tf_op jit(solution)/shard_map/finish/pallas_call | solution.py:27
  (4 shorter events, 0.0 us)
Async XLA Ops:
  2.0 6.4 %collective-permute-start = (bf16[2048,128]{1,0:T(8,128)(2,1)S(1)}, bf16[2048,128]{1,0:T(8,128)(2,1)S(1)}, u32[]{:S(2)}, u32[]{:S(2)}) collective-permute-start(bf16[2048,128]{1,0:T(8,128)(2,1)S(1)} %pack_volume.1.own), channel_id=1, source_target_pairs={{0,1},{1,0},{2,3},{3,2},{4,5},{5,4},{6,7},{7,6},{8,9},{9,8},{10,11... | collective-permute-start | bytes 1572872 | tf_op jit(solution)/shard_map/ppermute | solution.py:546
  2.6 14.4 %collective-permute-start.1 = (bf16[2048,128]{1,0:T(8,128)(2,1)S(1)}, bf16[2048,128]{1,0:T(8,128)(2,1)S(1)}, u32[]{:S(2)}, u32[]{:S(2)}) collective-permute-start(bf16[2048,128]{1,0:T(8,128)(2,1)S(1)} %pack_volume.1.own), channel_id=1, source_target_pairs={{1,2},{3,4},{5,6},{7,8},{9,10},{11,12},{13,14},{2,1},{4,3},{6,5},{... | collective-permute-start | bytes 1572872 | tf_op jit(solution)/shard_map/ppermute | solution.py:545
  3.2 4.6 %copy-start = (bf16[3,3,3,64,128]{4,3,2,1,0:T(8,128)(2,1)S(1)}, bf16[3,3,3,64,128]{4,3,2,1,0:T(8,128)(2,1)}, u32[]{:S(2)}) copy-start(bf16[3,3,3,64,128]{4,3,2,1,0:T(8,128)(2,1)} %param.6) | copy-start | bytes 1327108
  3.3 4.6 %copy-start.1 = (bf16[3,3,3,64,64]{4,3,2,1,0:T(8,128)(2,1)S(1)}, bf16[3,3,3,64,64]{4,3,2,1,0:T(8,128)(2,1)}, u32[]{:S(2)}) copy-start(bf16[3,3,3,64,64]{4,3,2,1,0:T(8,128)(2,1)} %param.5) | copy-start | bytes 663556
  12.1 11.7 %collective-permute-start.2 = (bf16[2048,128]{1,0:T(8,128)(2,1)S(1)}, bf16[2048,128]{1,0:T(8,128)(2,1)S(1)}, u32[]{:S(2)}, u32[]{:S(2)}) collective-permute-start(bf16[2048,128]{1,0:T(8,128)(2,1)S(1)} %get-tuple-element.62), channel_id=1, source_target_pairs={{0,1},{1,0},{2,3},{3,2},{4,5},{5,4},{6,7},{7,6},{8,9},{9,8},{10,11... | collective-permute-start | bytes 1572872 | tf_op jit(solution)/shard_map/ppermute | solution.py:576
  16.1 7.7 %collective-permute-start.3 = (bf16[1024,128]{1,0:T(8,128)(2,1)S(1)}, bf16[1024,128]{1,0:T(8,128)(2,1)S(1)}, u32[]{:S(2)}, u32[]{:S(2)}) collective-permute-start(bf16[1024,128]{1,0:T(8,128)(2,1)S(1)} %get-tuple-element.63), channel_id=1, source_target_pairs={{1,2},{3,4},{5,6},{7,8},{9,10},{11,12},{13,14},{2,1},{4,3},{6,5},{... | collective-permute-start | bytes 786440 | tf_op jit(solution)/shard_map/ppermute | solution.py:575
  25.9 4.8 %collective-permute-start.4 = (bf16[2816,128]{1,0:T(8,128)(2,1)S(1)}, bf16[2816,128]{1,0:T(8,128)(2,1)S(1)}, u32[]{:S(2)}, u32[]{:S(2)}) collective-permute-start(bf16[2816,128]{1,0:T(8,128)(2,1)S(1)} %get-tuple-element.70), channel_id=1, source_target_pairs={{0,1},{1,0},{2,3},{3,2},{4,5},{5,4},{6,7},{7,6},{8,9},{9,8},{10,11... | collective-permute-start | bytes 2162696 | tf_op jit(solution)/shard_map/ppermute | solution.py:606
  28.9 17.5 %collective-permute-start.6 = (bf16[1024,128]{1,0:T(8,128)(2,1)S(1)}, bf16[1024,128]{1,0:T(8,128)(2,1)S(1)}, u32[]{:S(2)}, u32[]{:S(2)}) collective-permute-start(bf16[1024,128]{1,0:T(8,128)(2,1)S(1)} %get-tuple-element.85), channel_id=1, source_target_pairs={{1,2},{3,4},{5,6},{7,8},{9,10},{11,12},{13,14},{2,1},{4,3},{6,5},{... | collective-permute-start | bytes 786440 | tf_op jit(solution)/shard_map/ppermute | solution.py:620
  30.8 10.9 %collective-permute-start.5 = (bf16[4,24,896]{2,1,0:T(8,128)(2,1)S(1)}, bf16[4,24,896]{2,1,0:T(8,128)(2,1)S(1)}, u32[]{:S(2)}, u32[]{:S(2)}) collective-permute-start(bf16[4,24,896]{2,1,0:T(8,128)(2,1)S(1)} %get-tuple-element.73), channel_id=1, source_target_pairs={{0,4},{1,5},{2,6},{3,7},{4,0},{5,1},{6,2},{7,3},{8,12},{9,13},{10,... | collective-permute-start | bytes 516104 | tf_op jit(solution)/shard_map/ppermute | solution.py:619
  41.7 8.2 %collective-permute-start.7 = (bf16[24,896]{1,0:T(8,128)(2,1)S(1)}, bf16[24,896]{1,0:T(8,128)(2,1)S(1)}, u32[]{:S(2)}, u32[]{:S(2)}) collective-permute-start(bf16[24,896]{1,0:T(8,128)(2,1)S(1)} %get-tuple-element.89), channel_id=1, source_target_pairs={{0,8},{1,9},{2,10},{3,11},{4,12},{5,13},{6,14},{7,15},{8,0},{9,1},... | collective-permute-start | bytes 129032 | tf_op jit(solution)/shard_map/ppermute | solution.py:638
  44.8 5.8 %collective-permute-start.8 = (bf16[24,896]{1,0:T(8,128)(2,1)S(1)}, bf16[24,896]{1,0:T(8,128)(2,1)S(1)}, u32[]{:S(2)}, u32[]{:S(2)}) collective-permute-start(bf16[24,896]{1,0:T(8,128)(2,1)S(1)} %get-tuple-element.90), channel_id=1, source_target_pairs={{0,10},{1,11},{2,8},{3,9},{4,14},{5,15},{6,12},{7,13},{8,2},{9,3},... | collective-permute-start | bytes 129032 | tf_op jit(solution)/shard_map/ppermute | solution.py:638
  44.8 5.8 %collective-permute-start.9 = (bf16[24,896]{1,0:T(8,128)(2,1)S(1)}, bf16[24,896]{1,0:T(8,128)(2,1)S(1)}, u32[]{:S(2)}, u32[]{:S(2)}) collective-permute-start(bf16[24,896]{1,0:T(8,128)(2,1)S(1)} %get-tuple-element.91), channel_id=1, source_target_pairs={{0,2},{1,3},{2,0},{3,1},{4,6},{5,7},{6,4},{7,5},{8,10},{9,11},{10,... | collective-permute-start | bytes 129032 | tf_op jit(solution)/shard_map/ppermute | solution.py:638

commit v20 on v17

--- a/solution.py
+++ b/solution.py
@@ -334,11 +334,10 @@
 
 def grad_one_body(
     columns, count, me, own_windows, side_windows, act_terms, inner, outer, slope, other,
-    grad, to_outer, message, kept, turned, terms,
+    grad, to_inner, to_outer, message, kept, turned, terms,
 ):
     cells = grad.shape[0]
     odd = me[0] % 2 == 1
-    before = message.shape[0] - cells // 2
     for start in range(0, cells // 2, STEP):
         low, high = slice(start, start + STEP), slice(start + cells // 2, start + cells // 2 + STEP)
         near = inner[low, :].astype(F32) + inner[high, :].astype(F32)
@@ -351,9 +350,7 @@
             turned[:, rows] = value.T.astype(BF16)
             sides.append(value)
         lower, upper = packed(*sides)
-        message[before + start : before + start + STEP, :] = jnp.where(
-            odd, lower, upper
-        ).astype(BF16)
+        to_inner[low, :] = jnp.where(odd, lower, upper).astype(BF16)
         to_outer[low, :] = jnp.where(odd, upper, lower).astype(BF16)
     def slices(row, column):
         rows = slice(row * columns, row * columns + cells)
@@ -476,16 +473,15 @@
 
 
 def grad_volume_body(
-    columns, me, own_windows, message, outer, taps, far, side_windows, output, sems
+    columns, me, own_windows, inner, outer, taps, far, side_windows, output, sems
 ):
     half = outer.shape[0]
     odd = me[0] % 2 == 1
-    before = message.shape[0] - half
 
     def fill(i, carry):
         start = pl.multiple_of(i * STEP, STEP)
-        near = message[pl.ds(before + start, STEP), :].astype(F32)
-        below, above = by_side(odd, near, outer[pl.ds(start, STEP), :].astype(F32))
+        rows = pl.ds(start, STEP)
+        below, above = by_side(odd, inner[rows, :].astype(F32), outer[rows, :].astype(F32))
         for first, side in zip((start, start + half), unpacked(above, below)):
             fill_windows(side_windows, first, 0, side, columns, 128)
         return carry
@@ -585,9 +581,7 @@
         (me, vol_outer, part, outer_taps, inner_windows),
         (pltpu.VMEM((slab[0], 384), BF16),), 2 * one_flops, "hidden", (0,),
     )
-    half = cells // 2
-    early, middle = [(0, BLOCK)], [(BLOCK, BLOCK), (half, BLOCK // 2)]
-    late = [(half + BLOCK // 2, BLOCK), (cells - BLOCK // 2, BLOCK // 2)]
+    early, middle, late = [(0, BLOCK)], [(BLOCK, BLOCK)], row_blocks(2 * BLOCK, cells)
     whole = shape((planes, cells, wide), F32)
     terms_two, output = call(
         functools.partial(grad_two_body, columns, early),
@@ -597,11 +591,11 @@
         two_flops, "grad_two_terms", (), (), (1,),
     )
     groups = lanes // 128
-    grad_hidden, outer, message, kept = call(
+    grad_hidden, inner, outer, message, kept = call(
         functools.partial(grad_one_body, columns, count),
         (
-            flat, pack,
-            shape((count // 2 * groups * (chunk + split) + cells // 2, 128), BF16),
+            flat, pack, pack,
+            shape((count // 2 * groups * (chunk + split), 128), BF16),
             shape((count // 2, chunk, lanes), F32),
         ),
         (
@@ -615,7 +609,7 @@
         functools.partial(output_first_body, columns, middle),
         (whole, third),
         (act_windows, out_taps, grad_hidden, output),
-        (pltpu.VMEM((planes, BLOCK + BLOCK // 2, wide), F32), dma((2,))),
+        (pltpu.VMEM((planes, BLOCK, wide), F32), dma((1,))),
         two_flops, "output_first", (), (3,), (0,), {3: 0},
     )
     message, output, back_windows = lax.optimization_barrier((message, output, back_windows))
@@ -630,14 +624,15 @@
 
     bits = list(range(count.bit_length() - 2, 0, -1))
     bits, sent, kept = halve(bits, 2, split, 0, kept, message)
-    sent, act_windows, outer = lax.optimization_barrier((sent, act_windows, outer))
+    sent, act_windows, inner, outer = lax.optimization_barrier((sent, act_windows, inner, outer))
     arrived = lax.ppermute(sent, "space", [(i, i ^ 4) for i in range(count)])
     grad_outer = lax.ppermute(outer, "space", across)
+    grad_inner = lax.ppermute(inner, "space", within)
     output, = call(
         functools.partial(output_rest_body, columns, late),
         (whole,),
         (act_windows, out_taps, output),
-        (pltpu.VMEM((planes, BLOCK + BLOCK // 2, wide), F32), dma((2,))),
+        (pltpu.VMEM((planes, cells - 2 * BLOCK, wide), F32), dma((len(late),))),
         two_flops, "output_rest", (), (2,), (0,), {2: 0},
     )
     others = 2 ** len(bits) - 1
@@ -654,7 +649,7 @@
     grad_volume, = call(
         functools.partial(grad_volume_body, columns),
         (shape((planes, cells, channels), F32),),
-        (me, back_windows, message, grad_outer, back_taps),
+        (me, back_windows, grad_inner, grad_outer, back_taps),
         (
             pltpu.VMEM((slab[0], 384), BF16), pltpu.VMEM((planes, cells, channels), F32),
             dma((cells // BLOCK + 1,)),

time: 48 us -> 48.2 us (level)
  the two profiles are of different devices: /device:TPU:0 before, /device:TPU:17 now
where the time goes in v20:
time: 48.2 us; the launch traced here: 48 us
  Pallas kernels  27.5 us (57%)
  starting transfers between devices  15.1 us (31%)
  waiting for transfers between devices  4.49 us (9%)
  between operations  0.84 us (2%)
    pallas_call x13, Pallas kernels, call(): pl.pallas_call(body, out_shape=list(outs), in_specs=[pl.BlockSpec(memory_...  27.5 us
    ppermute x1, waiting for transfers between devices, shards(): grad_outer = lax.ppermute(outer, 'space', across)  3.89 us
    ppermute x3, starting transfers between devices, shards(): lax.ppermute(part, 'space', [(i, i ^ away) for i in range(count)])  3.61 us
    ppermute x1, starting transfers between devices, shards(): terms_outer = lax.ppermute(outer, 'space', across)  3.36 us
    ppermute x1, starting transfers between devices, shards(): vol_outer = lax.ppermute(own, 'space', across)  3.05 us
    ppermute x1, starting transfers between devices, shards(): grad_outer = lax.ppermute(outer, 'space', across)  1.91 us
    ppermute x1, starting transfers between devices, shards(): arrived = lax.ppermute(sent, 'space', [(i, i ^ 4) for i in range(count)])  1.36 us
  transfers between devices with their start and end apart: 11, of which 3 were waited for; matrix products, arithmetic and copies ran while one was open for 0% of the time, Pallas kernels for 48%

profile of v20, /device:TPU:17, one launch (start us, length us, event | category | flops | bytes accessed | tf_op | source)
XLA Modules:
  0.0 48.0 jit_solution(14845878428142426369)
XLA Ops:
  0.6 1.4 %pack_volume.1.own = bf16[2048,128]{1,0:T(8,128)(2,1)S(1)} custom-call(bf16[2,2048,64]{2,1,0:T(8,128)(2,1)} %bitcast.19), custom_call_target="tpu_custom_call" | custom-call | bytes 1048576 | tf_op jit(solution)/shard_map/pack_volume/pallas_call | solution.py:27
  2.0 0.7 %collective-permute-start = (bf16[2048,128]{1,0:T(8,128)(2,1)S(1)}, bf16[2048,128]{1,0:T(8,128)(2,1)S(1)}, u32[]{:S(2)}, u32[]{:S(2)}) collective-permute-start(bf16[2048,128]{1,0:T(8,128)(2,1)S(1)} %pack_volume.1.own), channel_id=1, source_target_pairs={{0,1},{1,0},{2,3},{3,2},{4,5},{5,4},{6,7},{7,6},{8,9},{9,8},{10,11... | collective-permute-start | bytes 1572872 | tf_op jit(solution)/shard_map/ppermute | solution.py:547
  2.8 3.0 %collective-permute-start.1 = (bf16[2048,128]{1,0:T(8,128)(2,1)S(1)}, bf16[2048,128]{1,0:T(8,128)(2,1)S(1)}, u32[]{:S(2)}, u32[]{:S(2)}) collective-permute-start(bf16[2048,128]{1,0:T(8,128)(2,1)S(1)} %pack_volume.1.own), channel_id=1, source_target_pairs={{1,2},{3,4},{5,6},{7,8},{9,10},{11,12},{13,14},{2,1},{4,3},{6,5},{... | collective-permute-start | bytes 1572872 | tf_op jit(solution)/shard_map/ppermute | solution.py:546
  5.8 0.0 copy-start
  5.8 0.0 copy-start.1
  5.9 4.6 %grad_act_terms.1 = (f32[2048,128]{1,0:T(8,128)S(1)}, bf16[2048,128]{1,0:T(8,128)(2,1)S(1)}, bf16[1024,128]{1,0:T(8,128)(2,1)S(1)}, bf16[256,2048]{1,0:T(8,128)(2,1)S(1)}) custom-call(s32[1]{0:T(128)} %bitcast.me, bf16[2,2048,128]{2,1,0:T(8,128)(2,1)} %bitcast.20, bf16[27,64,128]{2,1,0:T(8,128)(2,1)} %bitcast.13), custom_call_target="tpu_custom_call" | custom-call | flops 1811939328 | bytes 4374532 | tf_op jit(solution)/shard_map/grad_act_terms/pallas_call | solution.py:27
  10.5 0.5 layouts.1
  11.0 0.0 collective-permute-done.inner
  11.0 3.7 %prepare.1 = (bf16[2112,384]{1,0:T(8,128)(2,1)S(1)}, bf16[2112,384]{1,0:T(8,128)(2,1)S(1)}, f32[2048,256]{1,0:T(8,128)S(1)}, bf16[1152,256]{1,0:T(8,128)(2,1)S(1)}) custom-call(s32[1]{0:T(128)} %bitcast.me, bf16[2048,128]{1,0:T(8,128)(2,1)S(1)} %pack_volume.1.own, bf16[2048,128]{1,0:T(8,128)(2,1)S(1)} %collective-permute-done.inner, bf16[27,64,64]{2,1,0:T(8,128)(2,1)} %bitcast.15), custom_call_target="tpu_custom_call" | custom-call | flops 905969664 | bytes 7200772 | tf_op jit(solution)/shard_map/prepare/pallas_call | solution.py:27
  14.7 0.4 collective-permute-start.2
  15.1 3.4 %collective-permute-start.3 = (bf16[1024,128]{1,0:T(8,128)(2,1)S(1)}, bf16[1024,128]{1,0:T(8,128)(2,1)S(1)}, u32[]{:S(2)}, u32[]{:S(2)}) collective-permute-start(bf16[1024,128]{1,0:T(8,128)(2,1)S(1)} %get-tuple-element.69), channel_id=1, source_target_pairs={{1,2},{3,4},{5,6},{7,8},{9,10},{11,12},{13,14},{2,1},{4,3},{6,5},{... | collective-permute-start | bytes 786440 | tf_op jit(solution)/shard_map/ppermute | solution.py:576
  18.5 0.4 collective-permute-done.1.outer
  18.9 3.5 %hidden.1 = (bf16[2112,768]{1,0:T(8,128)(2,1)S(1)}, f32[2048,128]{1,0:T(8,128)S(1)}, bf16[2112,384]{1,0:T(8,128)(2,1)S(1)}) custom-call(s32[1]{0:T(128)} %bitcast.me, bf16[2048,128]{1,0:T(8,128)(2,1)S(1)} %collective-permute-done.1.outer, f32[2048,256]{1,0:T(8,128)S(1)} %get-tuple-element.63.part, bf16[1152,256]{1,0:T(8,128)(2,1)S(1)} %get-tuple-element.64.outer_taps, ...), custom_call_target="tpu_custom_call" | custom-call | flops 1811939328 | bytes 10747908 | tf_op jit(solution)/shard_map/hidden/pallas_call | solution.py:27
  22.4 3.3 %grad_two_terms.1 = (f32[128,1792]{1,0:T(8,128)S(1)}, f32[2,2048,128]{2,1,0:T(8,128)}) custom-call(bf16[2112,768]{1,0:T(8,128)(2,1)S(1)} %get-tuple-element.90.act_windows, bf16[256,2048]{1,0:T(8,128)(2,1)S(1)} %get-tuple-element.72.turned, bf16[2304,256]{1,0:T(8,128)(2,1)S(1)} %get-tuple-element.73.taps), custom_call_target="tpu_custom_call" | custom-call | flops 1811939328 | bytes 8486912 | tf_op jit(solution)/shard_map/grad_two_terms/pallas_call | solution.py:27
  25.7 0.0 collective-permute-done.2.inner
  25.8 2.1 %grad_one_terms.1 = (bf16[2048,128]{1,0:T(8,128)(2,1)S(1)}, bf16[1024,128]{1,0:T(8,128)(2,1)S(1)}, bf16[1024,128]{1,0:T(8,128)(2,1)S(1)}, bf16[1792,128]{1,0:T(8,128)(2,1)S(1)}, f32[8,24,896]{2,1,0:T(8,128)S(1)}) custom-call(s32[1]{0:T(128)} %bitcast.me, bf16[2112,384]{1,0:T(8,128)(2,1)S(1)} %get-tuple-element.57.own_windows, ...), custom_call_target="tpu_custom_call" | custom-call | flops 905969664 | bytes 9240580 | tf_op jit(solution)/shard_map/grad_one_terms/pallas_call | solution.py:27
  27.9 0.1 collective-permute-start.4
  28.0 1.6 %output_first.1 = (f32[2,2048,128]{2,1,0:T(8,128)}, bf16[2112,384]{1,0:T(8,128)(2,1)S(1)}) custom-call(bf16[2112,768]{1,0:T(8,128)(2,1)S(1)} %get-tuple-element.90.act_windows, bf16[2304,256]{1,0:T(8,128)(2,1)S(1)} %get-tuple-element.73.taps, bf16[2048,128]{1,0:T(8,128)(2,1)S(1)} %get-tuple-element.77.grad, ...), custom_call_target="tpu_custom_call", output_to_operand_aliasing={{0}: (3, {})} | custom-call | flops 1811939328 | bytes 10764288 | tf_op jit(solution)/shard_map/output_first/pallas_call | solution.py:27
  29.6 0.2 collective-permute-done.4.arrived
  29.8 0.1 halve.1
  29.9 1.4 %collective-permute-start.5 = (bf16[4,24,896]{2,1,0:T(8,128)(2,1)S(1)}, bf16[4,24,896]{2,1,0:T(8,128)(2,1)S(1)}, u32[]{:S(2)}, u32[]{:S(2)}) collective-permute-start(bf16[4,24,896]{2,1,0:T(8,128)(2,1)S(1)} %get-tuple-element.86), channel_id=1, source_target_pairs={{0,4},{1,5},{2,6},{3,7},{4,0},{5,1},{6,2},{7,3},{8,12},{9,13},{10,... | collective-permute-start | bytes 516104 | tf_op jit(solution)/shard_map/ppermute | solution.py:628
  31.2 0.6 %collective-permute-start.6 = (bf16[1024,128]{1,0:T(8,128)(2,1)S(1)}, bf16[1024,128]{1,0:T(8,128)(2,1)S(1)}, u32[]{:S(2)}, u32[]{:S(2)}) collective-permute-start(bf16[1024,128]{1,0:T(8,128)(2,1)S(1)} %get-tuple-element.96), channel_id=1, source_target_pairs={{0,1},{1,0},{2,3},{3,2},{4,5},{5,4},{6,7},{7,6},{8,9},{9,8},{10,11... | collective-permute-start | bytes 786440 | tf_op jit(solution)/shard_map/ppermute | solution.py:630
  31.8 1.9 %collective-permute-start.7 = (bf16[1024,128]{1,0:T(8,128)(2,1)S(1)}, bf16[1024,128]{1,0:T(8,128)(2,1)S(1)}, u32[]{:S(2)}, u32[]{:S(2)}) collective-permute-start(bf16[1024,128]{1,0:T(8,128)(2,1)S(1)} %get-tuple-element.97), channel_id=1, source_target_pairs={{1,2},{3,4},{5,6},{7,8},{9,10},{11,12},{13,14},{2,1},{4,3},{6,5},{... | collective-permute-start | bytes 786440 | tf_op jit(solution)/shard_map/ppermute | solution.py:629
  33.7 2.4 %output_rest.1 = f32[2,2048,128]{2,1,0:T(8,128)} custom-call(bf16[2112,768]{1,0:T(8,128)(2,1)S(1)} %get-tuple-element.90.act_windows, bf16[2304,256]{1,0:T(8,128)(2,1)S(1)} %get-tuple-element.73.taps, f32[2,2048,128]{2,1,0:T(8,128)} %get-tuple-element.91.begun), custom_call_target="tpu_custom_call", output_to_operand_aliasing={{}: (2, {})} | custom-call | flops 1811939328 | bytes 8617984 | tf_op jit(solution)/shard_map/output_rest/pallas_call | solution.py:27
  36.1 0.0 collective-permute-done.5.arrived
  36.1 0.1 spread.1
  36.2 1.0 %collective-permute-start.8 = (bf16[24,896]{1,0:T(8,128)(2,1)S(1)}, bf16[24,896]{1,0:T(8,128)(2,1)S(1)}, u32[]{:S(2)}, u32[]{:S(2)}) collective-permute-start(bf16[24,896]{1,0:T(8,128)(2,1)S(1)} %get-tuple-element.101), channel_id=1, source_target_pairs={{0,8},{1,9},{2,10},{3,11},{4,12},{5,13},{6,14},{7,15},{8,0},{9,1},... | collective-permute-start | bytes 129032 | tf_op jit(solution)/shard_map/ppermute | solution.py:648
  37.1 2.4 %collective-permute-start.9 = (bf16[24,896]{1,0:T(8,128)(2,1)S(1)}, bf16[24,896]{1,0:T(8,128)(2,1)S(1)}, u32[]{:S(2)}, u32[]{:S(2)}) collective-permute-start(bf16[24,896]{1,0:T(8,128)(2,1)S(1)} %get-tuple-element.102), channel_id=1, source_target_pairs={{0,10},{1,11},{2,8},{3,9},{4,14},{5,15},{6,12},{7,13},{8,2},{9,3},... | collective-permute-start | bytes 129032 | tf_op jit(solution)/shard_map/ppermute | solution.py:648
  39.5 0.2 collective-permute-start.10
  39.8 3.9 %collective-permute-done.7.outer = bf16[1024,128]{1,0:T(8,128)(2,1)S(1)} collective-permute-done((bf16[1024,128]{1,0:T(8,128)(2,1)S(1)}, bf16[1024,128]{1,0:T(8,128)(2,1)S(1)}, u32[]{:S(2)}, u32[]{:S(2)}) %collective-permute-start.7) | collective-permute-done | bytes 262176 | tf_op jit(solution)/shard_map/ppermute | solution.py:629
  43.7 3.5 %grad_volume.1 = f32[2,2048,64]{2,1,0:T(8,128)} custom-call(s32[1]{0:T(128)} %bitcast.me, bf16[2112,384]{1,0:T(8,128)(2,1)S(1)} %get-tuple-element.95.own_windows, bf16[1024,128]{1,0:T(8,128)(2,1)S(1)} %collective-permute-done.6.inner, bf16[1024,128]{1,0:T(8,128)(2,1)S(1)} %collective-permute-done.7.outer, bf16[768,384]{1,0:T(8,128)(2,1)S(1)} %get-tuple-element.98.taps), custom_call_target="tpu_custom_call" | custom-call | flops 905969664 | bytes 3784708 | tf_op jit(solution)/shard_map/grad_volume/pallas_call | solution.py:27
  47.2 0.7 %finish.1 = (f32[27,4,64]{2,1,0:T(4,128)}, f32[27,8,64]{2,1,0:T(8,128)}) custom-call(f32[24,896]{1,0:T(8,128)S(1)} %get-tuple-element.100.mine, bf16[24,896]{1,0:T(8,128)(2,1)S(1)} %collective-permute-done.8.refs_0_, bf16[24,896]{1,0:T(8,128)(2,1)S(1)} %collective-permute-done.9.refs_1_, bf16[24,896]{1,0:T(8,128)(2,1)S(1)} %collective-permute-done.10.refs_2_), custom_call_target="tpu_custom_call" | custom-call | bytes 297984 | tf_op jit(solution)/shard_map/finish/pallas_call | solution.py:27
  (7 shorter events, 0.0 us)
Async XLA Ops:
  2.0 8.9 %collective-permute-start = (bf16[2048,128]{1,0:T(8,128)(2,1)S(1)}, bf16[2048,128]{1,0:T(8,128)(2,1)S(1)}, u32[]{:S(2)}, u32[]{:S(2)}) collective-permute-start(bf16[2048,128]{1,0:T(8,128)(2,1)S(1)} %pack_volume.1.own), channel_id=1, source_target_pairs={{0,1},{1,0},{2,3},{3,2},{4,5},{5,4},{6,7},{7,6},{8,9},{9,8},{10,11... | collective-permute-start | bytes 1572872 | tf_op jit(solution)/shard_map/ppermute | solution.py:547
  2.8 16.1 %collective-permute-start.1 = (bf16[2048,128]{1,0:T(8,128)(2,1)S(1)}, bf16[2048,128]{1,0:T(8,128)(2,1)S(1)}, u32[]{:S(2)}, u32[]{:S(2)}) collective-permute-start(bf16[2048,128]{1,0:T(8,128)(2,1)S(1)} %pack_volume.1.own), channel_id=1, source_target_pairs={{1,2},{3,4},{5,6},{7,8},{9,10},{11,12},{13,14},{2,1},{4,3},{6,5},{... | collective-permute-start | bytes 1572872 | tf_op jit(solution)/shard_map/ppermute | solution.py:546
  5.8 4.6 %copy-start = (bf16[3,3,3,64,128]{4,3,2,1,0:T(8,128)(2,1)S(1)}, bf16[3,3,3,64,128]{4,3,2,1,0:T(8,128)(2,1)}, u32[]{:S(2)}) copy-start(bf16[3,3,3,64,128]{4,3,2,1,0:T(8,128)(2,1)} %param.6) | copy-start | bytes 1327108
  5.8 4.6 %copy-start.1 = (bf16[3,3,3,64,64]{4,3,2,1,0:T(8,128)(2,1)S(1)}, bf16[3,3,3,64,64]{4,3,2,1,0:T(8,128)(2,1)}, u32[]{:S(2)}) copy-start(bf16[3,3,3,64,64]{4,3,2,1,0:T(8,128)(2,1)} %param.5) | copy-start | bytes 663556
  14.7 11.0 %collective-permute-start.2 = (bf16[2048,128]{1,0:T(8,128)(2,1)S(1)}, bf16[2048,128]{1,0:T(8,128)(2,1)S(1)}, u32[]{:S(2)}, u32[]{:S(2)}) collective-permute-start(bf16[2048,128]{1,0:T(8,128)(2,1)S(1)} %get-tuple-element.68), channel_id=1, source_target_pairs={{0,1},{1,0},{2,3},{3,2},{4,5},{5,4},{6,7},{7,6},{8,9},{9,8},{10,11... | collective-permute-start | bytes 1572872 | tf_op jit(solution)/shard_map/ppermute | solution.py:577
  15.1 10.6 %collective-permute-start.3 = (bf16[1024,128]{1,0:T(8,128)(2,1)S(1)}, bf16[1024,128]{1,0:T(8,128)(2,1)S(1)}, u32[]{:S(2)}, u32[]{:S(2)}) collective-permute-start(bf16[1024,128]{1,0:T(8,128)(2,1)S(1)} %get-tuple-element.69), channel_id=1, source_target_pairs={{1,2},{3,4},{5,6},{7,8},{9,10},{11,12},{13,14},{2,1},{4,3},{6,5},{... | collective-permute-start | bytes 786440 | tf_op jit(solution)/shard_map/ppermute | solution.py:576
  27.9 1.9 %collective-permute-start.4 = (bf16[1792,128]{1,0:T(8,128)(2,1)S(1)}, bf16[1792,128]{1,0:T(8,128)(2,1)S(1)}, u32[]{:S(2)}, u32[]{:S(2)}) collective-permute-start(bf16[1792,128]{1,0:T(8,128)(2,1)S(1)} %get-tuple-element.76), channel_id=1, source_target_pairs={{0,1},{1,0},{2,3},{3,2},{4,5},{5,4},{6,7},{7,6},{8,9},{9,8},{10,11... | collective-permute-start | bytes 1376264 | tf_op jit(solution)/shard_map/ppermute | solution.py:607
  29.9 6.2 %collective-permute-start.5 = (bf16[4,24,896]{2,1,0:T(8,128)(2,1)S(1)}, bf16[4,24,896]{2,1,0:T(8,128)(2,1)S(1)}, u32[]{:S(2)}, u32[]{:S(2)}) collective-permute-start(bf16[4,24,896]{2,1,0:T(8,128)(2,1)S(1)} %get-tuple-element.86), channel_id=1, source_target_pairs={{0,4},{1,5},{2,6},{3,7},{4,0},{5,1},{6,2},{7,3},{8,12},{9,13},{10,... | collective-permute-start | bytes 516104 | tf_op jit(solution)/shard_map/ppermute | solution.py:628
  31.2 8.6 %collective-permute-start.6 = (bf16[1024,128]{1,0:T(8,128)(2,1)S(1)}, bf16[1024,128]{1,0:T(8,128)(2,1)S(1)}, u32[]{:S(2)}, u32[]{:S(2)}) collective-permute-start(bf16[1024,128]{1,0:T(8,128)(2,1)S(1)} %get-tuple-element.96), channel_id=1, source_target_pairs={{0,1},{1,0},{2,3},{3,2},{4,5},{5,4},{6,7},{7,6},{8,9},{9,8},{10,11... | collective-permute-start | bytes 786440 | tf_op jit(solution)/shard_map/ppermute | solution.py:630
  31.8 11.9 %collective-permute-start.7 = (bf16[1024,128]{1,0:T(8,128)(2,1)S(1)}, bf16[1024,128]{1,0:T(8,128)(2,1)S(1)}, u32[]{:S(2)}, u32[]{:S(2)}) collective-permute-start(bf16[1024,128]{1,0:T(8,128)(2,1)S(1)} %get-tuple-element.97), channel_id=1, source_target_pairs={{1,2},{3,4},{5,6},{7,8},{9,10},{11,12},{13,14},{2,1},{4,3},{6,5},{... | collective-permute-start | bytes 786440 | tf_op jit(solution)/shard_map/ppermute | solution.py:629
  36.2 11.0 %collective-permute-start.8 = (bf16[24,896]{1,0:T(8,128)(2,1)S(1)}, bf16[24,896]{1,0:T(8,128)(2,1)S(1)}, u32[]{:S(2)}, u32[]{:S(2)}) collective-permute-start(bf16[24,896]{1,0:T(8,128)(2,1)S(1)} %get-tuple-element.101), channel_id=1, source_target_pairs={{0,8},{1,9},{2,10},{3,11},{4,12},{5,13},{6,14},{7,15},{8,0},{9,1},... | collective-permute-start | bytes 129032 | tf_op jit(solution)/shard_map/ppermute | solution.py:648
  37.1 10.1 %collective-permute-start.9 = (bf16[24,896]{1,0:T(8,128)(2,1)S(1)}, bf16[24,896]{1,0:T(8,128)(2,1)S(1)}, u32[]{:S(2)}, u32[]{:S(2)}) collective-permute-start(bf16[24,896]{1,0:T(8,128)(2,1)S(1)} %get-tuple-element.102), channel_id=1, source_target_pairs={{0,10},{1,11},{2,8},{3,9},{4,14},{5,15},{6,12},{7,13},{8,2},{9,3},... | collective-permute-start | bytes 129032 | tf_op jit(solution)/shard_map/ppermute | solution.py:648
  39.5 7.7 %collective-permute-start.10 = (bf16[24,896]{1,0:T(8,128)(2,1)S(1)}, bf16[24,896]{1,0:T(8,128)(2,1)S(1)}, u32[]{:S(2)}, u32[]{:S(2)}) collective-permute-start(bf16[24,896]{1,0:T(8,128)(2,1)S(1)} %get-tuple-element.103), channel_id=1, source_target_pairs={{0,2},{1,3},{2,0},{3,1},{4,6},{5,7},{6,4},{7,5},{8,10},{9,11},{10,... | collective-permute-start | bytes 129032 | tf_op jit(solution)/shard_map/ppermute | solution.py:648

commit v21 on v20

--- a/solution.py
+++ b/solution.py
@@ -624,10 +624,9 @@
 
     bits = list(range(count.bit_length() - 2, 0, -1))
     bits, sent, kept = halve(bits, 2, split, 0, kept, message)
-    sent, act_windows, inner, outer = lax.optimization_barrier((sent, act_windows, inner, outer))
+    sent, act_windows, outer = lax.optimization_barrier((sent, act_windows, outer))
     arrived = lax.ppermute(sent, "space", [(i, i ^ 4) for i in range(count)])
     grad_outer = lax.ppermute(outer, "space", across)
-    grad_inner = lax.ppermute(inner, "space", within)
     output, = call(
         functools.partial(output_rest_body, columns, late),
         (whole,),
@@ -641,7 +640,10 @@
         (shape((chunk, lanes), F32), *[shape((chunk, lanes), BF16)] * others),
         (me, kept, arrived), flops=16 * two_flops, name="spread", smem=(0,),
     )
-    sent, output, back_windows = lax.optimization_barrier((sent, output, back_windows))
+    sent, output, back_windows, inner = lax.optimization_barrier(
+        (sent, output, back_windows, inner)
+    )
+    grad_inner = lax.ppermute(inner, "space", within)
     arrived = []
     for at, part in zip(others_of(0, others + 1), sent):
         away = sum((at >> i & 1) << bit for i, bit in enumerate(bits[::-1]))

time: 48.2 us -> 48.1 us (level)
  the two profiles are of different devices: /device:TPU:17 before, /device:TPU:0 now
where the time goes in v21:
time: 48.1 us; the launch traced here: 47.9 us
  Pallas kernels  27.5 us (57%)
  starting transfers between devices  17 us (35%)
  waiting for transfers between devices  2.57 us (5%)
  between operations  0.83 us (2%)
    pallas_call x13, Pallas kernels, call(): pl.pallas_call(body, out_shape=list(outs), in_specs=[pl.BlockSpec(memory_...  27.5 us
    ppermute x3, starting transfers between devices, shards(): lax.ppermute(part, 'space', [(i, i ^ away) for i in range(count)])  4.39 us
    ppermute x1, starting transfers between devices, shards(): terms_inner = lax.ppermute(inner, 'space', within)  3.93 us
    ppermute x1, starting transfers between devices, shards(): message = lax.ppermute(message, 'space', within)  2.93 us
    ppermute x1, starting transfers between devices, shards(): arrived = lax.ppermute(sent, 'space', [(i, i ^ 4) for i in range(count)])  2.01 us
    ppermute x1, waiting for transfers between devices, shards(): arrived = lax.ppermute(sent, 'space', [(i, i ^ 4) for i in range(count)])  1.7 us
    ppermute x1, starting transfers between devices, shards(): grad_inner = lax.ppermute(inner, 'space', within)  0.98 us
  transfers between devices with their start and end apart: 11, of which 2 were waited for; matrix products, arithmetic and copies ran while one was open for 0% of the time, Pallas kernels for 48%

profile of v21, /device:TPU:0, one launch (start us, length us, event | category | flops | bytes accessed | tf_op | source)
XLA Modules:
  0.0 47.9 jit_solution(733806474195074729)
XLA Ops:
  0.6 1.4 %pack_volume.1.own = bf16[2048,128]{1,0:T(8,128)(2,1)S(1)} custom-call(bf16[2,2048,64]{2,1,0:T(8,128)(2,1)} %bitcast.19), custom_call_target="tpu_custom_call" | custom-call | bytes 1048576 | tf_op jit(solution)/shard_map/pack_volume/pallas_call | solution.py:27
  2.0 0.5 %collective-permute-start = (bf16[2048,128]{1,0:T(8,128)(2,1)S(1)}, bf16[2048,128]{1,0:T(8,128)(2,1)S(1)}, u32[]{:S(2)}, u32[]{:S(2)}) collective-permute-start(bf16[2048,128]{1,0:T(8,128)(2,1)S(1)} %pack_volume.1.own), channel_id=1, source_target_pairs={{0,1},{1,0},{2,3},{3,2},{4,5},{5,4},{6,7},{7,6},{8,9},{9,8},{10,11... | collective-permute-start | bytes 1572872 | tf_op jit(solution)/shard_map/ppermute | solution.py:547
  2.6 0.7 %collective-permute-start.1 = (bf16[2048,128]{1,0:T(8,128)(2,1)S(1)}, bf16[2048,128]{1,0:T(8,128)(2,1)S(1)}, u32[]{:S(2)}, u32[]{:S(2)}) collective-permute-start(bf16[2048,128]{1,0:T(8,128)(2,1)S(1)} %pack_volume.1.own), channel_id=1, source_target_pairs={{1,2},{3,4},{5,6},{7,8},{9,10},{11,12},{13,14},{2,1},{4,3},{6,5},{... | collective-permute-start | bytes 1572872 | tf_op jit(solution)/shard_map/ppermute | solution.py:546
  3.2 0.0 copy-start
  3.3 0.0 copy-start.1
  3.3 4.6 %grad_act_terms.1 = (f32[2048,128]{1,0:T(8,128)S(1)}, bf16[2048,128]{1,0:T(8,128)(2,1)S(1)}, bf16[1024,128]{1,0:T(8,128)(2,1)S(1)}, bf16[256,2048]{1,0:T(8,128)(2,1)S(1)}) custom-call(s32[1]{0:T(128)} %bitcast.me, bf16[2,2048,128]{2,1,0:T(8,128)(2,1)} %bitcast.20, bf16[27,64,128]{2,1,0:T(8,128)(2,1)} %bitcast.13), custom_call_target="tpu_custom_call" | custom-call | flops 1811939328 | bytes 4374532 | tf_op jit(solution)/shard_map/grad_act_terms/pallas_call | solution.py:27
  7.9 0.5 layouts.1
  8.4 0.0 collective-permute-done.inner
  8.4 3.7 %prepare.1 = (bf16[2112,384]{1,0:T(8,128)(2,1)S(1)}, bf16[2112,384]{1,0:T(8,128)(2,1)S(1)}, f32[2048,256]{1,0:T(8,128)S(1)}, bf16[1152,256]{1,0:T(8,128)(2,1)S(1)}) custom-call(s32[1]{0:T(128)} %bitcast.me, bf16[2048,128]{1,0:T(8,128)(2,1)S(1)} %pack_volume.1.own, bf16[2048,128]{1,0:T(8,128)(2,1)S(1)} %collective-permute-done.inner, bf16[27,64,64]{2,1,0:T(8,128)(2,1)} %bitcast.15), custom_call_target="tpu_custom_call" | custom-call | flops 905969664 | bytes 7200772 | tf_op jit(solution)/shard_map/prepare/pallas_call | solution.py:27
  12.1 3.9 %collective-permute-start.2 = (bf16[2048,128]{1,0:T(8,128)(2,1)S(1)}, bf16[2048,128]{1,0:T(8,128)(2,1)S(1)}, u32[]{:S(2)}, u32[]{:S(2)}) collective-permute-start(bf16[2048,128]{1,0:T(8,128)(2,1)S(1)} %get-tuple-element.68), channel_id=1, source_target_pairs={{0,1},{1,0},{2,3},{3,2},{4,5},{5,4},{6,7},{7,6},{8,9},{9,8},{10,11... | collective-permute-start | bytes 1572872 | tf_op jit(solution)/shard_map/ppermute | solution.py:577
  16.1 0.8 %collective-permute-start.3 = (bf16[1024,128]{1,0:T(8,128)(2,1)S(1)}, bf16[1024,128]{1,0:T(8,128)(2,1)S(1)}, u32[]{:S(2)}, u32[]{:S(2)}) collective-permute-start(bf16[1024,128]{1,0:T(8,128)(2,1)S(1)} %get-tuple-element.69), channel_id=1, source_target_pairs={{1,2},{3,4},{5,6},{7,8},{9,10},{11,12},{13,14},{2,1},{4,3},{6,5},{... | collective-permute-start | bytes 786440 | tf_op jit(solution)/shard_map/ppermute | solution.py:576
  16.9 0.0 collective-permute-done.1.outer
  16.9 3.5 %hidden.1 = (bf16[2112,768]{1,0:T(8,128)(2,1)S(1)}, f32[2048,128]{1,0:T(8,128)S(1)}, bf16[2112,384]{1,0:T(8,128)(2,1)S(1)}) custom-call(s32[1]{0:T(128)} %bitcast.me, bf16[2048,128]{1,0:T(8,128)(2,1)S(1)} %collective-permute-done.1.outer, f32[2048,256]{1,0:T(8,128)S(1)} %get-tuple-element.63.part, bf16[1152,256]{1,0:T(8,128)(2,1)S(1)} %get-tuple-element.64.outer_taps, ...), custom_call_target="tpu_custom_call" | custom-call | flops 1811939328 | bytes 10747908 | tf_op jit(solution)/shard_map/hidden/pallas_call | solution.py:27
  20.4 3.3 %grad_two_terms.1 = (f32[128,1792]{1,0:T(8,128)S(1)}, f32[2,2048,128]{2,1,0:T(8,128)}) custom-call(bf16[2112,768]{1,0:T(8,128)(2,1)S(1)} %get-tuple-element.89.act_windows, bf16[256,2048]{1,0:T(8,128)(2,1)S(1)} %get-tuple-element.72.turned, bf16[2304,256]{1,0:T(8,128)(2,1)S(1)} %get-tuple-element.73.taps), custom_call_target="tpu_custom_call" | custom-call | flops 1811939328 | bytes 8486912 | tf_op jit(solution)/shard_map/grad_two_terms/pallas_call | solution.py:27
  23.8 0.0 collective-permute-done.3.outer
  23.8 2.1 %grad_one_terms.1 = (bf16[2048,128]{1,0:T(8,128)(2,1)S(1)}, bf16[1024,128]{1,0:T(8,128)(2,1)S(1)}, bf16[1024,128]{1,0:T(8,128)(2,1)S(1)}, bf16[1792,128]{1,0:T(8,128)(2,1)S(1)}, f32[8,24,896]{2,1,0:T(8,128)S(1)}) custom-call(s32[1]{0:T(128)} %bitcast.me, bf16[2112,384]{1,0:T(8,128)(2,1)S(1)} %get-tuple-element.57.own_windows, ...), custom_call_target="tpu_custom_call" | custom-call | flops 905969664 | bytes 9240580 | tf_op jit(solution)/shard_map/grad_one_terms/pallas_call | solution.py:27
  25.9 2.9 %collective-permute-start.4 = (bf16[1792,128]{1,0:T(8,128)(2,1)S(1)}, bf16[1792,128]{1,0:T(8,128)(2,1)S(1)}, u32[]{:S(2)}, u32[]{:S(2)}) collective-permute-start(bf16[1792,128]{1,0:T(8,128)(2,1)S(1)} %get-tuple-element.76), channel_id=1, source_target_pairs={{0,1},{1,0},{2,3},{3,2},{4,5},{5,4},{6,7},{7,6},{8,9},{9,8},{10,11... | collective-permute-start | bytes 1376264 | tf_op jit(solution)/shard_map/ppermute | solution.py:607
  28.9 1.6 %output_first.1 = (f32[2,2048,128]{2,1,0:T(8,128)}, bf16[2112,384]{1,0:T(8,128)(2,1)S(1)}) custom-call(bf16[2112,768]{1,0:T(8,128)(2,1)S(1)} %get-tuple-element.89.act_windows, bf16[2304,256]{1,0:T(8,128)(2,1)S(1)} %get-tuple-element.73.taps, bf16[2048,128]{1,0:T(8,128)(2,1)S(1)} %get-tuple-element.77.grad, ...), custom_call_target="tpu_custom_call", output_to_operand_aliasing={{0}: (3, {})} | custom-call | flops 1811939328 | bytes 10764288 | tf_op jit(solution)/shard_map/output_first/pallas_call | solution.py:27
  30.5 0.1 halve.1
  30.6 2.0 %collective-permute-start.5 = (bf16[4,24,896]{2,1,0:T(8,128)(2,1)S(1)}, bf16[4,24,896]{2,1,0:T(8,128)(2,1)S(1)}, u32[]{:S(2)}, u32[]{:S(2)}) collective-permute-start(bf16[4,24,896]{2,1,0:T(8,128)(2,1)S(1)} %get-tuple-element.85), channel_id=1, source_target_pairs={{0,4},{1,5},{2,6},{3,7},{4,0},{5,1},{6,2},{7,3},{8,12},{9,13},{10,... | collective-permute-start | bytes 516104 | tf_op jit(solution)/shard_map/ppermute | solution.py:628
  32.6 0.7 %collective-permute-start.7 = (bf16[1024,128]{1,0:T(8,128)(2,1)S(1)}, bf16[1024,128]{1,0:T(8,128)(2,1)S(1)}, u32[]{:S(2)}, u32[]{:S(2)}) collective-permute-start(bf16[1024,128]{1,0:T(8,128)(2,1)S(1)} %get-tuple-element.97), channel_id=1, source_target_pairs={{1,2},{3,4},{5,6},{7,8},{9,10},{11,12},{13,14},{2,1},{4,3},{6,5},{... | collective-permute-start | bytes 786440 | tf_op jit(solution)/shard_map/ppermute | solution.py:629
  33.2 2.4 %output_rest.1 = f32[2,2048,128]{2,1,0:T(8,128)} custom-call(bf16[2112,768]{1,0:T(8,128)(2,1)S(1)} %get-tuple-element.89.act_windows, bf16[2304,256]{1,0:T(8,128)(2,1)S(1)} %get-tuple-element.73.taps, f32[2,2048,128]{2,1,0:T(8,128)} %get-tuple-element.90.begun), custom_call_target="tpu_custom_call", output_to_operand_aliasing={{}: (2, {})} | custom-call | flops 1811939328 | bytes 8617984 | tf_op jit(solution)/shard_map/output_rest/pallas_call | solution.py:27
  35.6 1.7 %collective-permute-done.5.arrived = bf16[4,24,896]{2,1,0:T(8,128)(2,1)S(1)} collective-permute-done((bf16[4,24,896]{2,1,0:T(8,128)(2,1)S(1)}, bf16[4,24,896]{2,1,0:T(8,128)(2,1)S(1)}, u32[]{:S(2)}, u32[]{:S(2)}) %collective-permute-start.5) | collective-permute-done | bytes 172064 | tf_op jit(solution)/shard_map/ppermute | solution.py:628
  37.4 1.0 %collective-permute-start.6 = (bf16[1024,128]{1,0:T(8,128)(2,1)S(1)}, bf16[1024,128]{1,0:T(8,128)(2,1)S(1)}, u32[]{:S(2)}, u32[]{:S(2)}) collective-permute-start(bf16[1024,128]{1,0:T(8,128)(2,1)S(1)} %get-tuple-element.96), channel_id=1, source_target_pairs={{0,1},{1,0},{2,3},{3,2},{4,5},{5,4},{6,7},{7,6},{8,9},{9,8},{10,11... | collective-permute-start | bytes 786440 | tf_op jit(solution)/shard_map/ppermute | solution.py:646
  38.3 1.9 %collective-permute-start.8 = (bf16[24,896]{1,0:T(8,128)(2,1)S(1)}, bf16[24,896]{1,0:T(8,128)(2,1)S(1)}, u32[]{:S(2)}, u32[]{:S(2)}) collective-permute-start(bf16[24,896]{1,0:T(8,128)(2,1)S(1)} %get-tuple-element.101), channel_id=1, source_target_pairs={{0,8},{1,9},{2,10},{3,11},{4,12},{5,13},{6,14},{7,15},{8,0},{9,1},... | collective-permute-start | bytes 129032 | tf_op jit(solution)/shard_map/ppermute | solution.py:650
  40.3 1.1 %collective-permute-start.9 = (bf16[24,896]{1,0:T(8,128)(2,1)S(1)}, bf16[24,896]{1,0:T(8,128)(2,1)S(1)}, u32[]{:S(2)}, u32[]{:S(2)}) collective-permute-start(bf16[24,896]{1,0:T(8,128)(2,1)S(1)} %get-tuple-element.102), channel_id=1, source_target_pairs={{0,10},{1,11},{2,8},{3,9},{4,14},{5,15},{6,12},{7,13},{8,2},{9,3},... | collective-permute-start | bytes 129032 | tf_op jit(solution)/shard_map/ppermute | solution.py:650
  41.4 1.4 %collective-permute-start.10 = (bf16[24,896]{1,0:T(8,128)(2,1)S(1)}, bf16[24,896]{1,0:T(8,128)(2,1)S(1)}, u32[]{:S(2)}, u32[]{:S(2)}) collective-permute-start(bf16[24,896]{1,0:T(8,128)(2,1)S(1)} %get-tuple-element.103), channel_id=1, source_target_pairs={{0,2},{1,3},{2,0},{3,1},{4,6},{5,7},{6,4},{7,5},{8,10},{9,11},{10,... | collective-permute-start | bytes 129032 | tf_op jit(solution)/shard_map/ppermute | solution.py:650
  42.7 0.0 collective-permute-done.7.outer
  42.7 0.0 collective-permute-done.6.inner
  42.7 3.5 %grad_volume.1 = f32[2,2048,64]{2,1,0:T(8,128)} custom-call(s32[1]{0:T(128)} %bitcast.me, bf16[2112,384]{1,0:T(8,128)(2,1)S(1)} %get-tuple-element.95.own_windows, bf16[1024,128]{1,0:T(8,128)(2,1)S(1)} %collective-permute-done.6.inner, bf16[1024,128]{1,0:T(8,128)(2,1)S(1)} %collective-permute-done.7.outer, bf16[768,384]{1,0:T(8,128)(2,1)S(1)} %get-tuple-element.98.taps), custom_call_target="tpu_custom_call" | custom-call | flops 905969664 | bytes 3784708 | tf_op jit(solution)/shard_map/grad_volume/pallas_call | solution.py:27
  46.3 0.9 %collective-permute-done.9.refs_1_ = bf16[24,896]{1,0:T(8,128)(2,1)S(1)} collective-permute-done((bf16[24,896]{1,0:T(8,128)(2,1)S(1)}, bf16[24,896]{1,0:T(8,128)(2,1)S(1)}, u32[]{:S(2)}, u32[]{:S(2)}) %collective-permute-start.9) | collective-permute-done | bytes 43040 | tf_op jit(solution)/shard_map/ppermute | solution.py:650
  47.1 0.7 %finish.1 = (f32[27,4,64]{2,1,0:T(4,128)}, f32[27,8,64]{2,1,0:T(8,128)}) custom-call(f32[24,896]{1,0:T(8,128)S(1)} %get-tuple-element.100.mine, bf16[24,896]{1,0:T(8,128)(2,1)S(1)} %collective-permute-done.8.refs_0_, bf16[24,896]{1,0:T(8,128)(2,1)S(1)} %collective-permute-done.9.refs_1_, bf16[24,896]{1,0:T(8,128)(2,1)S(1)} %collective-permute-done.10.refs_2_), custom_call_target="tpu_custom_call" | custom-call | bytes 297984 | tf_op jit(solution)/shard_map/finish/pallas_call | solution.py:27
  (7 shorter events, 0.1 us)
Async XLA Ops:
  2.0 6.4 %collective-permute-start = (bf16[2048,128]{1,0:T(8,128)(2,1)S(1)}, bf16[2048,128]{1,0:T(8,128)(2,1)S(1)}, u32[]{:S(2)}, u32[]{:S(2)}) collective-permute-start(bf16[2048,128]{1,0:T(8,128)(2,1)S(1)} %pack_volume.1.own), channel_id=1, source_target_pairs={{0,1},{1,0},{2,3},{3,2},{4,5},{5,4},{6,7},{7,6},{8,9},{9,8},{10,11... | collective-permute-start | bytes 1572872 | tf_op jit(solution)/shard_map/ppermute | solution.py:547
  2.6 14.4 %collective-permute-start.1 = (bf16[2048,128]{1,0:T(8,128)(2,1)S(1)}, bf16[2048,128]{1,0:T(8,128)(2,1)S(1)}, u32[]{:S(2)}, u32[]{:S(2)}) collective-permute-start(bf16[2048,128]{1,0:T(8,128)(2,1)S(1)} %pack_volume.1.own), channel_id=1, source_target_pairs={{1,2},{3,4},{5,6},{7,8},{9,10},{11,12},{13,14},{2,1},{4,3},{6,5},{... | collective-permute-start | bytes 1572872 | tf_op jit(solution)/shard_map/ppermute | solution.py:546
  3.2 4.6 %copy-start = (bf16[3,3,3,64,128]{4,3,2,1,0:T(8,128)(2,1)S(1)}, bf16[3,3,3,64,128]{4,3,2,1,0:T(8,128)(2,1)}, u32[]{:S(2)}) copy-start(bf16[3,3,3,64,128]{4,3,2,1,0:T(8,128)(2,1)} %param.6) | copy-start | bytes 1327108
  3.3 4.6 %copy-start.1 = (bf16[3,3,3,64,64]{4,3,2,1,0:T(8,128)(2,1)S(1)}, bf16[3,3,3,64,64]{4,3,2,1,0:T(8,128)(2,1)}, u32[]{:S(2)}) copy-start(bf16[3,3,3,64,64]{4,3,2,1,0:T(8,128)(2,1)} %param.5) | copy-start | bytes 663556
  12.1 11.7 %collective-permute-start.2 = (bf16[2048,128]{1,0:T(8,128)(2,1)S(1)}, bf16[2048,128]{1,0:T(8,128)(2,1)S(1)}, u32[]{:S(2)}, u32[]{:S(2)}) collective-permute-start(bf16[2048,128]{1,0:T(8,128)(2,1)S(1)} %get-tuple-element.68), channel_id=1, source_target_pairs={{0,1},{1,0},{2,3},{3,2},{4,5},{5,4},{6,7},{7,6},{8,9},{9,8},{10,11... | collective-permute-start | bytes 1572872 | tf_op jit(solution)/shard_map/ppermute | solution.py:577
  16.1 7.7 %collective-permute-start.3 = (bf16[1024,128]{1,0:T(8,128)(2,1)S(1)}, bf16[1024,128]{1,0:T(8,128)(2,1)S(1)}, u32[]{:S(2)}, u32[]{:S(2)}) collective-permute-start(bf16[1024,128]{1,0:T(8,128)(2,1)S(1)} %get-tuple-element.69), channel_id=1, source_target_pairs={{1,2},{3,4},{5,6},{7,8},{9,10},{11,12},{13,14},{2,1},{4,3},{6,5},{... | collective-permute-start | bytes 786440 | tf_op jit(solution)/shard_map/ppermute | solution.py:576
  25.9 4.5 %collective-permute-start.4 = (bf16[1792,128]{1,0:T(8,128)(2,1)S(1)}, bf16[1792,128]{1,0:T(8,128)(2,1)S(1)}, u32[]{:S(2)}, u32[]{:S(2)}) collective-permute-start(bf16[1792,128]{1,0:T(8,128)(2,1)S(1)} %get-tuple-element.76), channel_id=1, source_target_pairs={{0,1},{1,0},{2,3},{3,2},{4,5},{5,4},{6,7},{7,6},{8,9},{9,8},{10,11... | collective-permute-start | bytes 1376264 | tf_op jit(solution)/shard_map/ppermute | solution.py:607
  30.6 6.8 %collective-permute-start.5 = (bf16[4,24,896]{2,1,0:T(8,128)(2,1)S(1)}, bf16[4,24,896]{2,1,0:T(8,128)(2,1)S(1)}, u32[]{:S(2)}, u32[]{:S(2)}) collective-permute-start(bf16[4,24,896]{2,1,0:T(8,128)(2,1)S(1)} %get-tuple-element.85), channel_id=1, source_target_pairs={{0,4},{1,5},{2,6},{3,7},{4,0},{5,1},{6,2},{7,3},{8,12},{9,13},{10,... | collective-permute-start | bytes 516104 | tf_op jit(solution)/shard_map/ppermute | solution.py:628
  32.6 10.2 %collective-permute-start.7 = (bf16[1024,128]{1,0:T(8,128)(2,1)S(1)}, bf16[1024,128]{1,0:T(8,128)(2,1)S(1)}, u32[]{:S(2)}, u32[]{:S(2)}) collective-permute-start(bf16[1024,128]{1,0:T(8,128)(2,1)S(1)} %get-tuple-element.97), channel_id=1, source_target_pairs={{1,2},{3,4},{5,6},{7,8},{9,10},{11,12},{13,14},{2,1},{4,3},{6,5},{... | collective-permute-start | bytes 786440 | tf_op jit(solution)/shard_map/ppermute | solution.py:629
  37.4 5.4 %collective-permute-start.6 = (bf16[1024,128]{1,0:T(8,128)(2,1)S(1)}, bf16[1024,128]{1,0:T(8,128)(2,1)S(1)}, u32[]{:S(2)}, u32[]{:S(2)}) collective-permute-start(bf16[1024,128]{1,0:T(8,128)(2,1)S(1)} %get-tuple-element.96), channel_id=1, source_target_pairs={{0,1},{1,0},{2,3},{3,2},{4,5},{5,4},{6,7},{7,6},{8,9},{9,8},{10,11... | collective-permute-start | bytes 786440 | tf_op jit(solution)/shard_map/ppermute | solution.py:646
  38.3 7.9 %collective-permute-start.8 = (bf16[24,896]{1,0:T(8,128)(2,1)S(1)}, bf16[24,896]{1,0:T(8,128)(2,1)S(1)}, u32[]{:S(2)}, u32[]{:S(2)}) collective-permute-start(bf16[24,896]{1,0:T(8,128)(2,1)S(1)} %get-tuple-element.101), channel_id=1, source_target_pairs={{0,8},{1,9},{2,10},{3,11},{4,12},{5,13},{6,14},{7,15},{8,0},{9,1},... | collective-permute-start | bytes 129032 | tf_op jit(solution)/shard_map/ppermute | solution.py:650
  40.3 6.9 %collective-permute-start.9 = (bf16[24,896]{1,0:T(8,128)(2,1)S(1)}, bf16[24,896]{1,0:T(8,128)(2,1)S(1)}, u32[]{:S(2)}, u32[]{:S(2)}) collective-permute-start(bf16[24,896]{1,0:T(8,128)(2,1)S(1)} %get-tuple-element.102), channel_id=1, source_target_pairs={{0,10},{1,11},{2,8},{3,9},{4,14},{5,15},{6,12},{7,13},{8,2},{9,3},... | collective-permute-start | bytes 129032 | tf_op jit(solution)/shard_map/ppermute | solution.py:650
  41.4 5.8 %collective-permute-start.10 = (bf16[24,896]{1,0:T(8,128)(2,1)S(1)}, bf16[24,896]{1,0:T(8,128)(2,1)S(1)}, u32[]{:S(2)}, u32[]{:S(2)}) collective-permute-start(bf16[24,896]{1,0:T(8,128)(2,1)S(1)} %get-tuple-element.103), channel_id=1, source_target_pairs={{0,2},{1,3},{2,0},{3,1},{4,6},{5,7},{6,4},{7,5},{8,10},{9,11},{10,... | collective-permute-start | bytes 129032 | tf_op jit(solution)/shard_map/ppermute | solution.py:650

commit v22 on v16

--- a/solution.py
+++ b/solution.py
@@ -545,7 +545,7 @@
     )
     own, = call(
         pack_body, (flat,), (far_volume,),
-        (pltpu.VMEM((planes, cells, channels), BF16), dma((4,))),
+        (pltpu.VMEM((planes, cells, channels), BF16), dma((8,))),
         name="pack_volume", apart=(0,),
     )
     vol_outer = lax.ppermute(own, "space", across)

time: 47.6 us -> 47.9 us (level)
  no operation moved by 1% of the time
where the time goes in v22:
time: 47.9 us; the launch traced here: 47.7 us
  Pallas kernels  27.6 us (58%)
  starting transfers between devices  16.6 us (35%)
  waiting for transfers between devices  2.66 us (6%)
  between operations  0.81 us (2%)
    pallas_call x14, Pallas kernels, call(): pl.pallas_call(body, out_shape=list(outs), in_specs=[pl.BlockSpec(memory_...  27.6 us
    ppermute x3, starting transfers between devices, shards(): lax.ppermute(part, 'space', [(i, i ^ away) for i in range(count)])  4.45 us
    ppermute x1, starting transfers between devices, shards(): terms_inner = lax.ppermute(inner, 'space', within)  3.93 us
    ppermute x1, starting transfers between devices, shards(): message = lax.ppermute(message, 'space', within)  2.93 us
    ppermute x1, starting transfers between devices, shards(): arrived = lax.ppermute(sent, 'space', [(i, i ^ 4) for i in range(count)])  2.54 us
    ppermute x1, waiting for transfers between devices, shards(): arrived = lax.ppermute(sent, 'space', [(i, i ^ 4) for i in range(count)])  1.35 us
    ppermute x3, waiting for transfers between devices, shards(): lax.ppermute(part, 'space', [(i, i ^ away) for i in range(count)])  1.16 us
  transfers between devices with their start and end apart: 10, of which 3 were waited for; matrix products, arithmetic and copies ran while one was open for 0% of the time, Pallas kernels for 48%

profile of v22, /device:TPU:0, one launch (start us, length us, event | category | flops | bytes accessed | tf_op | source)
XLA Modules:
  0.0 47.7 jit_solution(270845653596594044)
XLA Ops:
  0.6 1.7 %pack_volume.1.own = bf16[2048,128]{1,0:T(8,128)(2,1)S(1)} custom-call(bf16[2,2048,64]{2,1,0:T(8,128)(2,1)} %bitcast.19), custom_call_target="tpu_custom_call" | custom-call | bytes 1048576 | tf_op jit(solution)/shard_map/pack_volume/pallas_call | solution.py:27
  2.3 0.5 %collective-permute-start = (bf16[2048,128]{1,0:T(8,128)(2,1)S(1)}, bf16[2048,128]{1,0:T(8,128)(2,1)S(1)}, u32[]{:S(2)}, u32[]{:S(2)}) collective-permute-start(bf16[2048,128]{1,0:T(8,128)(2,1)S(1)} %pack_volume.1.own), channel_id=1, source_target_pairs={{0,1},{1,0},{2,3},{3,2},{4,5},{5,4},{6,7},{7,6},{8,9},{9,8},{10,11... | collective-permute-start | bytes 1572872 | tf_op jit(solution)/shard_map/ppermute | solution.py:552
  2.8 0.7 %collective-permute-start.1 = (bf16[2048,128]{1,0:T(8,128)(2,1)S(1)}, bf16[2048,128]{1,0:T(8,128)(2,1)S(1)}, u32[]{:S(2)}, u32[]{:S(2)}) collective-permute-start(bf16[2048,128]{1,0:T(8,128)(2,1)S(1)} %pack_volume.1.own), channel_id=1, source_target_pairs={{1,2},{3,4},{5,6},{7,8},{9,10},{11,12},{13,14},{2,1},{4,3},{6,5},{... | collective-permute-start | bytes 1572872 | tf_op jit(solution)/shard_map/ppermute | solution.py:551
  3.5 0.0 copy-start
  3.5 4.6 %grad_act_terms.1 = (f32[2048,128]{1,0:T(8,128)S(1)}, bf16[2048,128]{1,0:T(8,128)(2,1)S(1)}, bf16[1024,128]{1,0:T(8,128)(2,1)S(1)}, bf16[256,2048]{1,0:T(8,128)(2,1)S(1)}) custom-call(s32[1]{0:T(128)} %bitcast.me, bf16[2,2048,128]{2,1,0:T(8,128)(2,1)} %bitcast.20, bf16[27,64,128]{2,1,0:T(8,128)(2,1)} %bitcast.15), custom_call_target="tpu_custom_call" | custom-call | flops 1811939328 | bytes 4374532 | tf_op jit(solution)/shard_map/grad_act_terms/pallas_call | solution.py:27
  8.1 0.4 back_taps.1.taps
  8.5 0.0 collective-permute-done.inner
  8.5 3.7 %prepare.1 = (bf16[2112,384]{1,0:T(8,128)(2,1)S(1)}, bf16[2112,384]{1,0:T(8,128)(2,1)S(1)}, f32[2048,256]{1,0:T(8,128)S(1)}, bf16[1152,256]{1,0:T(8,128)(2,1)S(1)}) custom-call(s32[1]{0:T(128)} %bitcast.me, bf16[2048,128]{1,0:T(8,128)(2,1)S(1)} %pack_volume.1.own, bf16[2048,128]{1,0:T(8,128)(2,1)S(1)} %collective-permute-done.inner, bf16[27,64,64]{2,1,0:T(8,128)(2,1)} %bitcast.13), custom_call_target="tpu_custom_call" | custom-call | flops 905969664 | bytes 7200772 | tf_op jit(solution)/shard_map/prepare/pallas_call | solution.py:27
  12.2 3.9 %collective-permute-start.2 = (bf16[2048,128]{1,0:T(8,128)(2,1)S(1)}, bf16[2048,128]{1,0:T(8,128)(2,1)S(1)}, u32[]{:S(2)}, u32[]{:S(2)}) collective-permute-start(bf16[2048,128]{1,0:T(8,128)(2,1)S(1)} %get-tuple-element.61), channel_id=1, source_target_pairs={{0,1},{1,0},{2,3},{3,2},{4,5},{5,4},{6,7},{7,6},{8,9},{9,8},{10,11... | collective-permute-start | bytes 1572872 | tf_op jit(solution)/shard_map/ppermute | solution.py:580
  16.2 0.8 %collective-permute-start.3 = (bf16[1024,128]{1,0:T(8,128)(2,1)S(1)}, bf16[1024,128]{1,0:T(8,128)(2,1)S(1)}, u32[]{:S(2)}, u32[]{:S(2)}) collective-permute-start(bf16[1024,128]{1,0:T(8,128)(2,1)S(1)} %get-tuple-element.62), channel_id=1, source_target_pairs={{1,2},{3,4},{5,6},{7,8},{9,10},{11,12},{13,14},{2,1},{4,3},{6,5},{... | collective-permute-start | bytes 786440 | tf_op jit(solution)/shard_map/ppermute | solution.py:579
  17.0 3.5 %hidden.1 = (bf16[2112,768]{1,0:T(8,128)(2,1)S(1)}, f32[2048,128]{1,0:T(8,128)S(1)}, bf16[2112,384]{1,0:T(8,128)(2,1)S(1)}) custom-call(s32[1]{0:T(128)} %bitcast.me, bf16[2048,128]{1,0:T(8,128)(2,1)S(1)} %collective-permute-done.1.outer, f32[2048,256]{1,0:T(8,128)S(1)} %get-tuple-element.56.part, bf16[1152,256]{1,0:T(8,128)(2,1)S(1)} %get-tuple-element.57.outer_taps, ...), custom_call_target="tpu_custom_call" | custom-call | flops 1811939328 | bytes 10747908 | tf_op jit(solution)/shard_map/hidden/pallas_call | solution.py:27
  20.6 2.7 %grad_two_terms.1.other = f32[128,1792]{1,0:T(8,128)S(1)} custom-call(bf16[2112,768]{1,0:T(8,128)(2,1)S(1)} %get-tuple-element.80.act_windows, bf16[256,2048]{1,0:T(8,128)(2,1)S(1)} %get-tuple-element.65.turned), custom_call_target="tpu_custom_call" | custom-call | flops 1811939328 | bytes 5210112 | tf_op jit(solution)/shard_map/grad_two_terms/pallas_call | solution.py:27
  23.3 0.0 collective-permute-done.2.inner
  23.3 0.0 copy-start.1
  23.3 2.1 %grad_one_terms.1 = (bf16[2048,128]{1,0:T(8,128)(2,1)S(1)}, bf16[1024,128]{1,0:T(8,128)(2,1)S(1)}, bf16[2816,128]{1,0:T(8,128)(2,1)S(1)}, f32[8,24,896]{2,1,0:T(8,128)S(1)}) custom-call(s32[1]{0:T(128)} %bitcast.me, bf16[2112,384]{1,0:T(8,128)(2,1)S(1)} %get-tuple-element.52.own_windows, bf16[2112,384]{1,0:T(8,128)(2,1)S(1)} %get-tuple-element.59.side_windows, ...), custom_call_target="tpu_custom_call" | custom-call | flops 905969664 | bytes 9240580 | tf_op jit(solution)/shard_map/grad_one_terms/pallas_call | solution.py:27
  25.4 2.9 %collective-permute-start.4 = (bf16[2816,128]{1,0:T(8,128)(2,1)S(1)}, bf16[2816,128]{1,0:T(8,128)(2,1)S(1)}, u32[]{:S(2)}, u32[]{:S(2)}) collective-permute-start(bf16[2816,128]{1,0:T(8,128)(2,1)S(1)} %get-tuple-element.67), channel_id=1, source_target_pairs={{0,1},{1,0},{2,3},{3,2},{4,5},{5,4},{6,7},{7,6},{8,9},{9,8},{10,11... | collective-permute-start | bytes 2162696 | tf_op jit(solution)/shard_map/ppermute | solution.py:606
  28.4 1.7 %output_first.1 = (f32[2,2048,128]{2,1,0:T(8,128)}, bf16[2304,256]{1,0:T(8,128)(2,1)S(1)}, bf16[2112,384]{1,0:T(8,128)(2,1)S(1)}) custom-call(bf16[2112,768]{1,0:T(8,128)(2,1)S(1)} %get-tuple-element.80.act_windows, bf16[27,64,128]{2,1,0:T(8,128)(2,1)S(1)} %bitcast.16, bf16[2048,128]{1,0:T(8,128)(2,1)S(1)} %get-tuple-element.68.grad), custom_call_target="tpu_custom_call" | custom-call | flops 1811939328 | bytes 9109504 | tf_op jit(solution)/shard_map/output_first/pallas_call | solution.py:27
  30.1 0.1 collective-permute-done.4.arrived.message
  30.2 0.1 halve.1
  30.3 2.5 %collective-permute-start.5 = (bf16[4,24,896]{2,1,0:T(8,128)(2,1)S(1)}, bf16[4,24,896]{2,1,0:T(8,128)(2,1)S(1)}, u32[]{:S(2)}, u32[]{:S(2)}) collective-permute-start(bf16[4,24,896]{2,1,0:T(8,128)(2,1)S(1)} %get-tuple-element.76), channel_id=1, source_target_pairs={{0,4},{1,5},{2,6},{3,7},{4,0},{5,1},{6,2},{7,3},{8,12},{9,13},{10,... | collective-permute-start | bytes 516104 | tf_op jit(solution)/shard_map/ppermute | solution.py:630
  32.8 0.7 %collective-permute-start.6 = (bf16[1024,128]{1,0:T(8,128)(2,1)S(1)}, bf16[1024,128]{1,0:T(8,128)(2,1)S(1)}, u32[]{:S(2)}, u32[]{:S(2)}) collective-permute-start(bf16[1024,128]{1,0:T(8,128)(2,1)S(1)} %get-tuple-element.87), channel_id=1, source_target_pairs={{1,2},{3,4},{5,6},{7,8},{9,10},{11,12},{13,14},{2,1},{4,3},{6,5},{... | collective-permute-start | bytes 786440 | tf_op jit(solution)/shard_map/ppermute | solution.py:631
  33.5 2.9 %output_rest.1 = f32[2,2048,128]{2,1,0:T(8,128)} custom-call(bf16[2112,768]{1,0:T(8,128)(2,1)S(1)} %get-tuple-element.80.act_windows, bf16[2304,256]{1,0:T(8,128)(2,1)S(1)} %get-tuple-element.81.taps, f32[2,2048,128]{2,1,0:T(8,128)} %get-tuple-element.82.begun), custom_call_target="tpu_custom_call", output_to_operand_aliasing={{}: (2, {})} | custom-call | flops 1811939328 | bytes 8617984 | tf_op jit(solution)/shard_map/output_rest/pallas_call | solution.py:27
  36.4 1.4 %collective-permute-done.5.arrived = bf16[4,24,896]{2,1,0:T(8,128)(2,1)S(1)} collective-permute-done((bf16[4,24,896]{2,1,0:T(8,128)(2,1)S(1)}, bf16[4,24,896]{2,1,0:T(8,128)(2,1)S(1)}, u32[]{:S(2)}, u32[]{:S(2)}) %collective-permute-start.5) | collective-permute-done | bytes 172064 | tf_op jit(solution)/shard_map/ppermute | solution.py:630
  37.8 2.8 %collective-permute-start.7 = (bf16[24,896]{1,0:T(8,128)(2,1)S(1)}, bf16[24,896]{1,0:T(8,128)(2,1)S(1)}, u32[]{:S(2)}, u32[]{:S(2)}) collective-permute-start(bf16[24,896]{1,0:T(8,128)(2,1)S(1)} %get-tuple-element.91), channel_id=1, source_target_pairs={{0,8},{1,9},{2,10},{3,11},{4,12},{5,13},{6,14},{7,15},{8,0},{9,1},... | collective-permute-start | bytes 129032 | tf_op jit(solution)/shard_map/ppermute | solution.py:649
  40.6 1.2 %collective-permute-start.8 = (bf16[24,896]{1,0:T(8,128)(2,1)S(1)}, bf16[24,896]{1,0:T(8,128)(2,1)S(1)}, u32[]{:S(2)}, u32[]{:S(2)}) collective-permute-start(bf16[24,896]{1,0:T(8,128)(2,1)S(1)} %get-tuple-element.92), channel_id=1, source_target_pairs={{0,10},{1,11},{2,8},{3,9},{4,14},{5,15},{6,12},{7,13},{8,2},{9,3},... | collective-permute-start | bytes 129032 | tf_op jit(solution)/shard_map/ppermute | solution.py:649
  41.8 0.4 collective-permute-start.9
  42.2 0.0 collective-permute-done.6.outer
  42.2 0.6 %grad_windows.1.side_windows = bf16[2112,384]{1,0:T(8,128)(2,1)S(1)} custom-call(s32[1]{0:T(128)} %bitcast.me, bf16[2816,128]{1,0:T(8,128)(2,1)S(1)} %collective-permute-done.4.arrived.message, bf16[1024,128]{1,0:T(8,128)(2,1)S(1)} %collective-permute-done.6.outer), custom_call_target="tpu_custom_call" | custom-call | flops 226492416 | bytes 2605060 | tf_op jit(solution)/shard_map/grad_windows/pallas_call | solution.py:27
  42.9 2.9 %grad_volume.1 = f32[2,2048,64]{2,1,0:T(8,128)} custom-call(bf16[2112,384]{1,0:T(8,128)(2,1)S(1)} %get-tuple-element.86.own_windows, bf16[2112,384]{1,0:T(8,128)(2,1)S(1)} %grad_windows.1.side_windows, bf16[768,384]{1,0:T(8,128)(2,1)S(1)} %back_taps.1.taps), custom_call_target="tpu_custom_call" | custom-call | flops 905969664 | bytes 4882432 | tf_op jit(solution)/shard_map/grad_volume/pallas_call | solution.py:27
  45.8 0.0 collective-permute-done.7.refs_0_
  45.8 1.2 %collective-permute-done.8.refs_1_ = bf16[24,896]{1,0:T(8,128)(2,1)S(1)} collective-permute-done((bf16[24,896]{1,0:T(8,128)(2,1)S(1)}, bf16[24,896]{1,0:T(8,128)(2,1)S(1)}, u32[]{:S(2)}, u32[]{:S(2)}) %collective-permute-start.8) | collective-permute-done | bytes 43040 | tf_op jit(solution)/shard_map/ppermute | solution.py:649
  46.9 0.7 %finish.1 = (f32[27,4,64]{2,1,0:T(4,128)}, f32[27,8,64]{2,1,0:T(8,128)}) custom-call(f32[24,896]{1,0:T(8,128)S(1)} %get-tuple-element.90.mine, bf16[24,896]{1,0:T(8,128)(2,1)S(1)} %collective-permute-done.7.refs_0_, bf16[24,896]{1,0:T(8,128)(2,1)S(1)} %collective-permute-done.8.refs_1_, bf16[24,896]{1,0:T(8,128)(2,1)S(1)} %collective-permute-done.9.refs_2_), custom_call_target="tpu_custom_call" | custom-call | bytes 297984 | tf_op jit(solution)/shard_map/finish/pallas_call | solution.py:27
  (6 shorter events, 0.1 us)
Async XLA Ops:
  2.3 6.2 %collective-permute-start = (bf16[2048,128]{1,0:T(8,128)(2,1)S(1)}, bf16[2048,128]{1,0:T(8,128)(2,1)S(1)}, u32[]{:S(2)}, u32[]{:S(2)}) collective-permute-start(bf16[2048,128]{1,0:T(8,128)(2,1)S(1)} %pack_volume.1.own), channel_id=1, source_target_pairs={{0,1},{1,0},{2,3},{3,2},{4,5},{5,4},{6,7},{7,6},{8,9},{9,8},{10,11... | collective-permute-start | bytes 1572872 | tf_op jit(solution)/shard_map/ppermute | solution.py:552
  2.8 14.2 %collective-permute-start.1 = (bf16[2048,128]{1,0:T(8,128)(2,1)S(1)}, bf16[2048,128]{1,0:T(8,128)(2,1)S(1)}, u32[]{:S(2)}, u32[]{:S(2)}) collective-permute-start(bf16[2048,128]{1,0:T(8,128)(2,1)S(1)} %pack_volume.1.own), channel_id=1, source_target_pairs={{1,2},{3,4},{5,6},{7,8},{9,10},{11,12},{13,14},{2,1},{4,3},{6,5},{... | collective-permute-start | bytes 1572872 | tf_op jit(solution)/shard_map/ppermute | solution.py:551
  3.5 4.6 %copy-start = (bf16[3,3,3,64,64]{4,3,2,1,0:T(8,128)(2,1)S(1)}, bf16[3,3,3,64,64]{4,3,2,1,0:T(8,128)(2,1)}, u32[]{:S(2)}) copy-start(bf16[3,3,3,64,64]{4,3,2,1,0:T(8,128)(2,1)} %param.5) | copy-start | bytes 663556
  12.2 11.0 %collective-permute-start.2 = (bf16[2048,128]{1,0:T(8,128)(2,1)S(1)}, bf16[2048,128]{1,0:T(8,128)(2,1)S(1)}, u32[]{:S(2)}, u32[]{:S(2)}) collective-permute-start(bf16[2048,128]{1,0:T(8,128)(2,1)S(1)} %get-tuple-element.61), channel_id=1, source_target_pairs={{0,1},{1,0},{2,3},{3,2},{4,5},{5,4},{6,7},{7,6},{8,9},{9,8},{10,11... | collective-permute-start | bytes 1572872 | tf_op jit(solution)/shard_map/ppermute | solution.py:580
  16.2 7.1 %collective-permute-start.3 = (bf16[1024,128]{1,0:T(8,128)(2,1)S(1)}, bf16[1024,128]{1,0:T(8,128)(2,1)S(1)}, u32[]{:S(2)}, u32[]{:S(2)}) collective-permute-start(bf16[1024,128]{1,0:T(8,128)(2,1)S(1)} %get-tuple-element.62), channel_id=1, source_target_pairs={{1,2},{3,4},{5,6},{7,8},{9,10},{11,12},{13,14},{2,1},{4,3},{6,5},{... | collective-permute-start | bytes 786440 | tf_op jit(solution)/shard_map/ppermute | solution.py:579
  23.3 5.1 %copy-start.1 = (bf16[3,3,3,64,128]{4,3,2,1,0:T(8,128)(2,1)S(1)}, bf16[3,3,3,64,128]{4,3,2,1,0:T(8,128)(2,1)}, u32[]{:S(2)}) copy-start(bf16[3,3,3,64,128]{4,3,2,1,0:T(8,128)(2,1)} %param.6) | copy-start | bytes 1327108
  25.4 4.8 %collective-permute-start.4 = (bf16[2816,128]{1,0:T(8,128)(2,1)S(1)}, bf16[2816,128]{1,0:T(8,128)(2,1)S(1)}, u32[]{:S(2)}, u32[]{:S(2)}) collective-permute-start(bf16[2816,128]{1,0:T(8,128)(2,1)S(1)} %get-tuple-element.67), channel_id=1, source_target_pairs={{0,1},{1,0},{2,3},{3,2},{4,5},{5,4},{6,7},{7,6},{8,9},{9,8},{10,11... | collective-permute-start | bytes 2162696 | tf_op jit(solution)/shard_map/ppermute | solution.py:606
  30.3 7.4 %collective-permute-start.5 = (bf16[4,24,896]{2,1,0:T(8,128)(2,1)S(1)}, bf16[4,24,896]{2,1,0:T(8,128)(2,1)S(1)}, u32[]{:S(2)}, u32[]{:S(2)}) collective-permute-start(bf16[4,24,896]{2,1,0:T(8,128)(2,1)S(1)} %get-tuple-element.76), channel_id=1, source_target_pairs={{0,4},{1,5},{2,6},{3,7},{4,0},{5,1},{6,2},{7,3},{8,12},{9,13},{10,... | collective-permute-start | bytes 516104 | tf_op jit(solution)/shard_map/ppermute | solution.py:630
  32.8 9.4 %collective-permute-start.6 = (bf16[1024,128]{1,0:T(8,128)(2,1)S(1)}, bf16[1024,128]{1,0:T(8,128)(2,1)S(1)}, u32[]{:S(2)}, u32[]{:S(2)}) collective-permute-start(bf16[1024,128]{1,0:T(8,128)(2,1)S(1)} %get-tuple-element.87), channel_id=1, source_target_pairs={{1,2},{3,4},{5,6},{7,8},{9,10},{11,12},{13,14},{2,1},{4,3},{6,5},{... | collective-permute-start | bytes 786440 | tf_op jit(solution)/shard_map/ppermute | solution.py:631
  37.8 8.0 %collective-permute-start.7 = (bf16[24,896]{1,0:T(8,128)(2,1)S(1)}, bf16[24,896]{1,0:T(8,128)(2,1)S(1)}, u32[]{:S(2)}, u32[]{:S(2)}) collective-permute-start(bf16[24,896]{1,0:T(8,128)(2,1)S(1)} %get-tuple-element.91), channel_id=1, source_target_pairs={{0,8},{1,9},{2,10},{3,11},{4,12},{5,13},{6,14},{7,15},{8,0},{9,1},... | collective-permute-start | bytes 129032 | tf_op jit(solution)/shard_map/ppermute | solution.py:649
  40.6 6.4 %collective-permute-start.8 = (bf16[24,896]{1,0:T(8,128)(2,1)S(1)}, bf16[24,896]{1,0:T(8,128)(2,1)S(1)}, u32[]{:S(2)}, u32[]{:S(2)}) collective-permute-start(bf16[24,896]{1,0:T(8,128)(2,1)S(1)} %get-tuple-element.92), channel_id=1, source_target_pairs={{0,10},{1,11},{2,8},{3,9},{4,14},{5,15},{6,12},{7,13},{8,2},{9,3},... | collective-permute-start | bytes 129032 | tf_op jit(solution)/shard_map/ppermute | solution.py:649
  41.8 5.1 %collective-permute-start.9 = (bf16[24,896]{1,0:T(8,128)(2,1)S(1)}, bf16[24,896]{1,0:T(8,128)(2,1)S(1)}, u32[]{:S(2)}, u32[]{:S(2)}) collective-permute-start(bf16[24,896]{1,0:T(8,128)(2,1)S(1)} %get-tuple-element.93), channel_id=1, source_target_pairs={{0,2},{1,3},{2,0},{3,1},{4,6},{5,7},{6,4},{7,5},{8,10},{9,11},{10,... | collective-permute-start | bytes 129032 | tf_op jit(solution)/shard_map/ppermute | solution.py:649
